TPU v7x, 32 devices: a whole 2x2x4 slice. The times are simulated.
32 devices in a mesh: row: 4 (over y, x), col: 8 (over z, core).
Axes of the slice: x: 2, y: 2, z: 4, core: 2. Of those that a mesh axis runs over, the one named last changes fastest.
Arguments:
- features: bfloat16 [4096, 512], P(('col', 'row')), may hold values from -6 to 6
- tile_vals: bfloat16 [4, 1024, 128, 128], P('row', 'col')
- tile_row: int32 [4, 1024], P('row', 'col'), may hold values from 0 to 7
- tile_col: int32 [4, 1024], P('row', 'col'), may hold values from 0 to 3
- tile_count: int32 [4, 8], P('row', 'col'), may hold values from 1 to 128, as said below
- node_type: int32 [4096], P(('row', 'col')), may hold values from 0 to 7
- type_gain: float32 [8, 512], replicated, may hold values from 0.1 to 1.9
- w_in: bfloat16 [512, 1024], replicated, may hold values from -0.25 to 0.25
- w_out: bfloat16 [1024, 512], replicated, may hold values from -0.1875 to 0.1875
- cotangent: bfloat16 [4096, 512], P(('row', 'col')), may hold values from -6 to 6
Outputs:
- mixed: bfloat16 [4096, 512], P(('row', 'col'))
- grad_x: float32 [4096, 512], P(('col', 'row'))
- grad_w_in: float32 [512, 1024], replicated
- grad_w_out: float32 [1024, 512], replicated
- grad_gain: float32 [8, 512], replicated
Inputs may be any that keep to these rules, and one draw needn't show every extreme that they name: Slots 0 to tile_count - 1 of a grid cell's list are live; some grid cell has all 128 slots live in every draw.
All inputs are finite; a program needn't handle non-finite values.
Results may differ from a plain program's by a relative error of at most 0.0056.
Values may be sent and summed in bfloat16 or wider, within the bound.
No kernel may reach another device: no remote copies, remote signals or barrier semaphores. Data moves between devices by JAX's collectives and lax.ppermute only.
A program may use at most 128 MiB of HBM per device.

v0:
```python
import jax
import jax.numpy as jnp
from jax import lax
from jax.sharding import PartitionSpec as P

F = 512
TYPES = 8
TILE = 128


def sweep(weights_all, row_ids_all, col_ids_all, live_count, sources, target, forward, lower):
    span = target.shape[0]
    rounds = weights_all.shape[0] // 16

    def advance(block_index, totals):
        first_slot = block_index * 16
        weights_now = lax.dynamic_slice_in_dim(weights_all, first_slot, 16, 0)
        row_ids = lax.dynamic_slice_in_dim(row_ids_all, first_slot, 16, 0)
        col_ids = lax.dynamic_slice_in_dim(col_ids_all, first_slot, 16, 0)
        living = first_slot + jnp.arange(16, dtype=jnp.int32) < live_count
        if forward:
            pieces = sources[col_ids]
            product = jnp.einsum(
                "sab,sbf->saf", weights_now, pieces, preferred_element_type=jnp.float32
            )
            destination = row_ids - lower
        else:
            pieces = sources[row_ids]
            product = jnp.einsum(
                "sab,saf->sbf", weights_now, pieces, preferred_element_type=jnp.float32
            )
            destination = col_ids - lower
        inside = living & (destination >= 0) & (destination < span)
        product = jnp.where(inside[:, None, None], product, 0.0)
        placed = jnp.clip(destination, 0, span - 1)
        return totals.at[placed].add(product)

    return lax.fori_loop(0, rounds, advance, target)


def shards(
    features,
    tile_vals,
    tile_row,
    tile_col,
    tile_count,
    node_type,
    type_gain,
    w_in,
    w_out,
    cotangent,
):
    row_count = lax.axis_size("row")
    col_count = lax.axis_size("col")
    total_nodes = TILE * row_count * col_count
    weights_all = tile_vals[0]
    row_ids_all = tile_row[0]
    col_ids_all = tile_col[0]
    live_count = tile_count[0, 0]
    gathered = lax.all_gather(features, "row", axis=0, tiled=True).reshape(row_count, TILE, F)
    totals = sweep(
        weights_all,
        row_ids_all,
        col_ids_all,
        live_count,
        gathered,
        jnp.zeros((col_count, TILE, F), jnp.float32),
        True,
        0,
    )
    aggregate = lax.psum_scatter(
        totals.reshape(col_count * TILE, F), "col", scatter_dimension=0, tiled=True
    )
    center = jnp.mean(aggregate, axis=-1, keepdims=True)
    spread = jnp.mean(jnp.square(aggregate - center), axis=-1, keepdims=True)
    inverse = lax.rsqrt(spread + 1e-05)
    normed = (aggregate - center) * inverse
    onehot = (node_type[:, None] == jnp.arange(TYPES, dtype=jnp.int32)[None, :]).astype(jnp.float32)
    gains = jnp.dot(onehot, type_gain, precision=lax.Precision.HIGHEST)
    scaled = (normed * gains).astype(jnp.bfloat16)
    hidden = jnp.dot(scaled, w_in, preferred_element_type=jnp.float32)
    activated = jax.nn.silu(hidden).astype(jnp.bfloat16)
    branch = jnp.dot(activated, w_out, preferred_element_type=jnp.float32)
    mixed = (aggregate + branch).astype(jnp.bfloat16)
    upstream = cotangent.astype(jnp.float32)
    grad_out_w = jnp.dot(activated.T, cotangent, preferred_element_type=jnp.float32)
    grad_act = jnp.dot(cotangent, w_out.T, preferred_element_type=jnp.float32)
    sigmoid_h = jax.nn.sigmoid(hidden)
    grad_hidden = (grad_act * sigmoid_h * (1.0 + hidden * (1.0 - sigmoid_h))).astype(jnp.bfloat16)
    grad_in_w = jnp.dot(scaled.T, grad_hidden, preferred_element_type=jnp.float32)
    grad_scaled = jnp.dot(grad_hidden, w_in.T, preferred_element_type=jnp.float32)
    grad_gain = jnp.dot(onehot.T, grad_scaled * normed, precision=lax.Precision.HIGHEST)
    grad_normed = grad_scaled * gains
    grad_agg = upstream + inverse * (
        grad_normed
        - jnp.mean(grad_normed, axis=-1, keepdims=True)
        - normed * jnp.mean(grad_normed * normed, axis=-1, keepdims=True)
    )
    grad_rows = grad_agg.astype(jnp.bfloat16)
    reduced = lax.psum((grad_in_w, grad_out_w, grad_gain), ("row", "col"))
    grad_sources = lax.all_gather(grad_rows, "col", axis=0, tiled=True).reshape(col_count, TILE, F)
    back = sweep(
        weights_all,
        row_ids_all,
        col_ids_all,
        live_count,
        grad_sources,
        jnp.zeros((row_count, TILE, F), jnp.float32),
        False,
        0,
    )
    grad_x = lax.psum_scatter(
        back.reshape(row_count * TILE, F), "row", scatter_dimension=0, tiled=True
    )
    factor = float(total_nodes) ** (-0.5)
    return (mixed, grad_x, reduced[0] * factor, reduced[1] * factor, reduced[2] * factor)


def solution(mesh):
    return jax.shard_map(
        shards,
        mesh=mesh,
        in_specs=(
            P(("col", "row"), None),
            P("row", "col", None, None),
            P("row", "col"),
            P("row", "col"),
            P("row", "col"),
            P(("row", "col")),
            P(),
            P(),
            P(),
            P(("row", "col"), None),
        ),
        out_specs=(P(("row", "col"), None), P(("col", "row"), None), P(), P(), P()),
        check_vma=False,
    )
```

profile of v0, /device:TPU:0, one launch (start us, length us, event | category | flops | bytes accessed | tf_op | source)
XLA Modules:
  0.0 385.9 jit_solution(3873174497072866127)
XLA Ops:
  7.2 13.3 %all_gather.6 = bf16[512,512]{1,0:T(8,128)(2,1)} all-gather(bf16[128,512]{1,0:T(8,128)(2,1)} %param.14), channel_id=1, replica_groups=mesh['row'=4,'col'=8] {'row'}, dimensions={0}, use_global_device_ids=true | all-gather | bytes 655360 | tf_op jit(solution)/shard_map/all_gather | solution.py:60
  20.8 115.3 %while.26 = (s32[]{:T(128)}, f32[8,128,512]{2,1,0:T(8,128)S(1)}, s32[128]{0:T(128)S(1)}, s32[]{:T(128)}, bf16[128,128,128]{2,1,0:T(8,128)(2,1)}, /*index=5*/s32[...) while((s32[]{:T(128)}, f32[8,128,512]{2,1,0:T(8,128)S(1)}, ...), condition=%wide.region_2.3_spmd, body=%wide.region_0.2_spmd.sunk | while | flops 270533856 | bytes 23597784 | solution.py:38
  20.9 3.0 gather_fusion
  24.7 4.4 %convolution_select_fusion.4 = f32[16,128,512]{2,1,0:T(8,128)} fusion(bf16[16,128,512]{2,1,0:T(8,128)(2,1)} %gather_fusion, pred[16]{0:T(512)(128)(4,1)S(1)} %compare_and_fusion.4, bf16[128,128,128]{2,1,0:T(8,128)(2,1)} %get-tuple-element.424, s32[]{:T(128)S(6)} %select_n.75), kind=kOutput, calls=%fused_computation.4.clone.1 | convolution fusion | flops 269484032 | bytes 6815764 | tf_op jit(solution)/shard_map/while/body/eval_jaxpr/sab,sbf->saf/dot_general | solution.py:23
  29.1 6.1 %scatter_fusion = f32[8,128,512]{2,1,0:T(8,128)S(1)} fusion(f32[8,128,512]{2,1,0:T(8,128)S(1)} %get-tuple-element.410, s32[16]{0:T(128)S(1)} %get-tuple-element.387, f32[16,128,512]{2,1,0:T(8,128)} %convolution_select_fusion.4), kind=kCustom, calls=%fused_computation.2.clone.1 | custom fusion | flops 1048576 | bytes 12582976 | tf_op jit(solution)/shard_map/while/body/eval_jaxpr/scatter-add | solution.py:36
  35.3 3.0 gather_fusion
  39.1 4.4 %convolution_select_fusion.4 = f32[16,128,512]{2,1,0:T(8,128)} fusion(bf16[16,128,512]{2,1,0:T(8,128)(2,1)} %gather_fusion, pred[16]{0:T(512)(128)(4,1)S(1)} %compare_and_fusion.4, bf16[128,128,128]{2,1,0:T(8,128)(2,1)} %get-tuple-element.424, s32[]{:T(128)S(6)} %select_n.75), kind=kOutput, calls=%fused_computation.4.clone.1 | convolution fusion | flops 269484032 | bytes 6815764 | tf_op jit(solution)/shard_map/while/body/eval_jaxpr/sab,sbf->saf/dot_general | solution.py:23
  43.5 6.1 %scatter_fusion = f32[8,128,512]{2,1,0:T(8,128)S(1)} fusion(f32[8,128,512]{2,1,0:T(8,128)S(1)} %get-tuple-element.410, s32[16]{0:T(128)S(1)} %get-tuple-element.387, f32[16,128,512]{2,1,0:T(8,128)} %convolution_select_fusion.4), kind=kCustom, calls=%fused_computation.2.clone.1 | custom fusion | flops 1048576 | bytes 12582976 | tf_op jit(solution)/shard_map/while/body/eval_jaxpr/scatter-add | solution.py:36
  49.7 3.0 gather_fusion
  53.5 4.4 %convolution_select_fusion.4 = f32[16,128,512]{2,1,0:T(8,128)} fusion(bf16[16,128,512]{2,1,0:T(8,128)(2,1)} %gather_fusion, pred[16]{0:T(512)(128)(4,1)S(1)} %compare_and_fusion.4, bf16[128,128,128]{2,1,0:T(8,128)(2,1)} %get-tuple-element.424, s32[]{:T(128)S(6)} %select_n.75), kind=kOutput, calls=%fused_computation.4.clone.1 | convolution fusion | flops 269484032 | bytes 6815764 | tf_op jit(solution)/shard_map/while/body/eval_jaxpr/sab,sbf->saf/dot_general | solution.py:23
  57.9 6.1 %scatter_fusion = f32[8,128,512]{2,1,0:T(8,128)S(1)} fusion(f32[8,128,512]{2,1,0:T(8,128)S(1)} %get-tuple-element.410, s32[16]{0:T(128)S(1)} %get-tuple-element.387, f32[16,128,512]{2,1,0:T(8,128)} %convolution_select_fusion.4), kind=kCustom, calls=%fused_computation.2.clone.1 | custom fusion | flops 1048576 | bytes 12582976 | tf_op jit(solution)/shard_map/while/body/eval_jaxpr/scatter-add | solution.py:36
  64.1 3.0 gather_fusion
  67.9 4.4 %convolution_select_fusion.4 = f32[16,128,512]{2,1,0:T(8,128)} fusion(bf16[16,128,512]{2,1,0:T(8,128)(2,1)} %gather_fusion, pred[16]{0:T(512)(128)(4,1)S(1)} %compare_and_fusion.4, bf16[128,128,128]{2,1,0:T(8,128)(2,1)} %get-tuple-element.424, s32[]{:T(128)S(6)} %select_n.75), kind=kOutput, calls=%fused_computation.4.clone.1 | convolution fusion | flops 269484032 | bytes 6815764 | tf_op jit(solution)/shard_map/while/body/eval_jaxpr/sab,sbf->saf/dot_general | solution.py:23
  72.3 6.1 %scatter_fusion = f32[8,128,512]{2,1,0:T(8,128)S(1)} fusion(f32[8,128,512]{2,1,0:T(8,128)S(1)} %get-tuple-element.410, s32[16]{0:T(128)S(1)} %get-tuple-element.387, f32[16,128,512]{2,1,0:T(8,128)} %convolution_select_fusion.4), kind=kCustom, calls=%fused_computation.2.clone.1 | custom fusion | flops 1048576 | bytes 12582976 | tf_op jit(solution)/shard_map/while/body/eval_jaxpr/scatter-add | solution.py:36
  78.5 3.0 gather_fusion
  82.3 4.4 %convolution_select_fusion.4 = f32[16,128,512]{2,1,0:T(8,128)} fusion(bf16[16,128,512]{2,1,0:T(8,128)(2,1)} %gather_fusion, pred[16]{0:T(512)(128)(4,1)S(1)} %compare_and_fusion.4, bf16[128,128,128]{2,1,0:T(8,128)(2,1)} %get-tuple-element.424, s32[]{:T(128)S(6)} %select_n.75), kind=kOutput, calls=%fused_computation.4.clone.1 | convolution fusion | flops 269484032 | bytes 6815764 | tf_op jit(solution)/shard_map/while/body/eval_jaxpr/sab,sbf->saf/dot_general | solution.py:23
  86.7 6.1 %scatter_fusion = f32[8,128,512]{2,1,0:T(8,128)S(1)} fusion(f32[8,128,512]{2,1,0:T(8,128)S(1)} %get-tuple-element.410, s32[16]{0:T(128)S(1)} %get-tuple-element.387, f32[16,128,512]{2,1,0:T(8,128)} %convolution_select_fusion.4), kind=kCustom, calls=%fused_computation.2.clone.1 | custom fusion | flops 1048576 | bytes 12582976 | tf_op jit(solution)/shard_map/while/body/eval_jaxpr/scatter-add | solution.py:36
  92.9 3.0 gather_fusion
  96.7 4.4 %convolution_select_fusion.4 = f32[16,128,512]{2,1,0:T(8,128)} fusion(bf16[16,128,512]{2,1,0:T(8,128)(2,1)} %gather_fusion, pred[16]{0:T(512)(128)(4,1)S(1)} %compare_and_fusion.4, bf16[128,128,128]{2,1,0:T(8,128)(2,1)} %get-tuple-element.424, s32[]{:T(128)S(6)} %select_n.75), kind=kOutput, calls=%fused_computation.4.clone.1 | convolution fusion | flops 269484032 | bytes 6815764 | tf_op jit(solution)/shard_map/while/body/eval_jaxpr/sab,sbf->saf/dot_general | solution.py:23
  101.1 6.1 %scatter_fusion = f32[8,128,512]{2,1,0:T(8,128)S(1)} fusion(f32[8,128,512]{2,1,0:T(8,128)S(1)} %get-tuple-element.410, s32[16]{0:T(128)S(1)} %get-tuple-element.387, f32[16,128,512]{2,1,0:T(8,128)} %convolution_select_fusion.4), kind=kCustom, calls=%fused_computation.2.clone.1 | custom fusion | flops 1048576 | bytes 12582976 | tf_op jit(solution)/shard_map/while/body/eval_jaxpr/scatter-add | solution.py:36
  107.4 3.0 gather_fusion
  111.1 4.4 %convolution_select_fusion.4 = f32[16,128,512]{2,1,0:T(8,128)} fusion(bf16[16,128,512]{2,1,0:T(8,128)(2,1)} %gather_fusion, pred[16]{0:T(512)(128)(4,1)S(1)} %compare_and_fusion.4, bf16[128,128,128]{2,1,0:T(8,128)(2,1)} %get-tuple-element.424, s32[]{:T(128)S(6)} %select_n.75), kind=kOutput, calls=%fused_computation.4.clone.1 | convolution fusion | flops 269484032 | bytes 6815764 | tf_op jit(solution)/shard_map/while/body/eval_jaxpr/sab,sbf->saf/dot_general | solution.py:23
  115.5 6.2 %scatter_fusion = f32[8,128,512]{2,1,0:T(8,128)S(1)} fusion(f32[8,128,512]{2,1,0:T(8,128)S(1)} %get-tuple-element.410, s32[16]{0:T(128)S(1)} %get-tuple-element.387, f32[16,128,512]{2,1,0:T(8,128)} %convolution_select_fusion.4), kind=kCustom, calls=%fused_computation.2.clone.1 | custom fusion | flops 1048576 | bytes 12582976 | tf_op jit(solution)/shard_map/while/body/eval_jaxpr/scatter-add | solution.py:36
  121.8 3.0 gather_fusion
  125.6 4.4 %convolution_select_fusion.4 = f32[16,128,512]{2,1,0:T(8,128)} fusion(bf16[16,128,512]{2,1,0:T(8,128)(2,1)} %gather_fusion, pred[16]{0:T(512)(128)(4,1)S(1)} %compare_and_fusion.4, bf16[128,128,128]{2,1,0:T(8,128)(2,1)} %get-tuple-element.424, s32[]{:T(128)S(6)} %select_n.75), kind=kOutput, calls=%fused_computation.4.clone.1 | convolution fusion | flops 269484032 | bytes 6815764 | tf_op jit(solution)/shard_map/while/body/eval_jaxpr/sab,sbf->saf/dot_general | solution.py:23
  129.9 6.2 %scatter_fusion = f32[8,128,512]{2,1,0:T(8,128)S(1)} fusion(f32[8,128,512]{2,1,0:T(8,128)S(1)} %get-tuple-element.410, s32[16]{0:T(128)S(1)} %get-tuple-element.387, f32[16,128,512]{2,1,0:T(8,128)} %convolution_select_fusion.4), kind=kCustom, calls=%fused_computation.2.clone.1 | custom fusion | flops 1048576 | bytes 12582976 | tf_op jit(solution)/shard_map/while/body/eval_jaxpr/scatter-add | solution.py:36
  136.2 1.3 copy-done.2
  137.5 36.3 %reduce-scatter.3.cloned.1.call-done = f32[128,512]{1,0:T(8,128)} async-done(((f32[1024,512]{1,0:T(8,128)}), f32[128,512]{1,0:T(8,128)}) %reduce-scatter.3.cloned.1.call-update) | async-done | bytes 262160 | tf_op jit(solution)/shard_map/reduce_scatter | solution.py:71
  174.9 1.2 multiply_reduce_fusion.1
  176.2 1.3 multiply_convert_fusion.1
  180.2 6.4 %copy.15 = bf16[1,128,128,128]{2,3,1,0:T(8,128)(2,1)} copy(bf16[1,128,128,128]{3,2,1,0:T(8,128)(2,1)} %bitcast.31) | data formatting | bytes 8388608 | tf_op args[1]
  186.6 1.8 fusion.17
  188.4 1.8 fusion.14
  190.3 10.7 %all-gather.2.cloned.1.call-done = bf16[1024,512]{1,0:T(8,128)(2,1)} async-done(((bf16[128,512]{1,0:T(8,128)(2,1)}), bf16[1024,512]{1,0:T(8,128)(2,1)}) %all-gather.2.cloned.1.call-update) | async-done | bytes 1048592 | tf_op jit(solution)/shard_map/all_gather | solution.py:101
  201.1 117.5 %while.27 = (s32[]{:T(128)}, f32[4,128,512]{2,1,0:T(8,128)S(1)}, s32[128]{0:T(128)S(1)}, s32[]{:T(128)}, bf16[128,128,128]{1,2,0:T(8,128)(2,1)}, /*index=5*/s32[...) while((s32[]{:T(128)}, f32[4,128,512]{2,1,0:T(8,128)S(1)}, ...), condition=%wide.region_10.11_spmd, body=%wide.region_8.10_spmd.sunk | while | flops 270533856 | bytes 23597784 | solution.py:38
  201.2 3.2 gather_fusion.1
  205.2 4.4 %convolution_select_fusion.5 = f32[16,128,512]{2,1,0:T(8,128)} fusion(bf16[16,128,512]{2,1,0:T(8,128)(2,1)} %gather_fusion.1, pred[16]{0:T(512)(128)(4,1)S(1)} %compare_and_fusion.5, bf16[128,128,128]{1,2,0:T(8,128)(2,1)} %get-tuple-element.457, s32[]{:T(128)S(6)} %select_n.78), kind=kOutput, calls=%fused_computation.11.clone.1 | convolution fusion | flops 269484032 | bytes 6815764 | tf_op jit(solution)/shard_map/while/body/eval_jaxpr/sab,saf->sbf/dot_general | solution.py:29
  209.6 6.1 %scatter_fusion.1 = f32[4,128,512]{2,1,0:T(8,128)S(1)} fusion(f32[4,128,512]{2,1,0:T(8,128)S(1)} %get-tuple-element.443, s32[16]{0:T(128)S(1)} %get-tuple-element.396, f32[16,128,512]{2,1,0:T(8,128)} %convolution_select_fusion.5), kind=kCustom, calls=%fused_computation.3.clone.1 | custom fusion | flops 1048576 | bytes 12582976 | tf_op jit(solution)/shard_map/while/body/eval_jaxpr/scatter-add | solution.py:36
  215.9 3.2 gather_fusion.1
  219.9 4.5 %convolution_select_fusion.5 = f32[16,128,512]{2,1,0:T(8,128)} fusion(bf16[16,128,512]{2,1,0:T(8,128)(2,1)} %gather_fusion.1, pred[16]{0:T(512)(128)(4,1)S(1)} %compare_and_fusion.5, bf16[128,128,128]{1,2,0:T(8,128)(2,1)} %get-tuple-element.457, s32[]{:T(128)S(6)} %select_n.78), kind=kOutput, calls=%fused_computation.11.clone.1 | convolution fusion | flops 269484032 | bytes 6815764 | tf_op jit(solution)/shard_map/while/body/eval_jaxpr/sab,saf->sbf/dot_general | solution.py:29
  224.3 6.2 %scatter_fusion.1 = f32[4,128,512]{2,1,0:T(8,128)S(1)} fusion(f32[4,128,512]{2,1,0:T(8,128)S(1)} %get-tuple-element.443, s32[16]{0:T(128)S(1)} %get-tuple-element.396, f32[16,128,512]{2,1,0:T(8,128)} %convolution_select_fusion.5), kind=kCustom, calls=%fused_computation.3.clone.1 | custom fusion | flops 1048576 | bytes 12582976 | tf_op jit(solution)/shard_map/while/body/eval_jaxpr/scatter-add | solution.py:36
  230.6 3.2 gather_fusion.1
  234.6 4.5 %convolution_select_fusion.5 = f32[16,128,512]{2,1,0:T(8,128)} fusion(bf16[16,128,512]{2,1,0:T(8,128)(2,1)} %gather_fusion.1, pred[16]{0:T(512)(128)(4,1)S(1)} %compare_and_fusion.5, bf16[128,128,128]{1,2,0:T(8,128)(2,1)} %get-tuple-element.457, s32[]{:T(128)S(6)} %select_n.78), kind=kOutput, calls=%fused_computation.11.clone.1 | convolution fusion | flops 269484032 | bytes 6815764 | tf_op jit(solution)/shard_map/while/body/eval_jaxpr/sab,saf->sbf/dot_general | solution.py:29
  239.1 6.1 %scatter_fusion.1 = f32[4,128,512]{2,1,0:T(8,128)S(1)} fusion(f32[4,128,512]{2,1,0:T(8,128)S(1)} %get-tuple-element.443, s32[16]{0:T(128)S(1)} %get-tuple-element.396, f32[16,128,512]{2,1,0:T(8,128)} %convolution_select_fusion.5), kind=kCustom, calls=%fused_computation.3.clone.1 | custom fusion | flops 1048576 | bytes 12582976 | tf_op jit(solution)/shard_map/while/body/eval_jaxpr/scatter-add | solution.py:36
  245.3 3.3 gather_fusion.1
  249.4 4.4 %convolution_select_fusion.5 = f32[16,128,512]{2,1,0:T(8,128)} fusion(bf16[16,128,512]{2,1,0:T(8,128)(2,1)} %gather_fusion.1, pred[16]{0:T(512)(128)(4,1)S(1)} %compare_and_fusion.5, bf16[128,128,128]{1,2,0:T(8,128)(2,1)} %get-tuple-element.457, s32[]{:T(128)S(6)} %select_n.78), kind=kOutput, calls=%fused_computation.11.clone.1 | convolution fusion | flops 269484032 | bytes 6815764 | tf_op jit(solution)/shard_map/while/body/eval_jaxpr/sab,saf->sbf/dot_general | solution.py:29
  253.8 6.1 %scatter_fusion.1 = f32[4,128,512]{2,1,0:T(8,128)S(1)} fusion(f32[4,128,512]{2,1,0:T(8,128)S(1)} %get-tuple-element.443, s32[16]{0:T(128)S(1)} %get-tuple-element.396, f32[16,128,512]{2,1,0:T(8,128)} %convolution_select_fusion.5), kind=kCustom, calls=%fused_computation.3.clone.1 | custom fusion | flops 1048576 | bytes 12582976 | tf_op jit(solution)/shard_map/while/body/eval_jaxpr/scatter-add | solution.py:36
  260.1 3.2 gather_fusion.1
  264.0 4.4 %convolution_select_fusion.5 = f32[16,128,512]{2,1,0:T(8,128)} fusion(bf16[16,128,512]{2,1,0:T(8,128)(2,1)} %gather_fusion.1, pred[16]{0:T(512)(128)(4,1)S(1)} %compare_and_fusion.5, bf16[128,128,128]{1,2,0:T(8,128)(2,1)} %get-tuple-element.457, s32[]{:T(128)S(6)} %select_n.78), kind=kOutput, calls=%fused_computation.11.clone.1 | convolution fusion | flops 269484032 | bytes 6815764 | tf_op jit(solution)/shard_map/while/body/eval_jaxpr/sab,saf->sbf/dot_general | solution.py:29
  268.5 6.2 %scatter_fusion.1 = f32[4,128,512]{2,1,0:T(8,128)S(1)} fusion(f32[4,128,512]{2,1,0:T(8,128)S(1)} %get-tuple-element.443, s32[16]{0:T(128)S(1)} %get-tuple-element.396, f32[16,128,512]{2,1,0:T(8,128)} %convolution_select_fusion.5), kind=kCustom, calls=%fused_computation.3.clone.1 | custom fusion | flops 1048576 | bytes 12582976 | tf_op jit(solution)/shard_map/while/body/eval_jaxpr/scatter-add | solution.py:36
  274.7 3.2 gather_fusion.1
  278.7 4.4 %convolution_select_fusion.5 = f32[16,128,512]{2,1,0:T(8,128)} fusion(bf16[16,128,512]{2,1,0:T(8,128)(2,1)} %gather_fusion.1, pred[16]{0:T(512)(128)(4,1)S(1)} %compare_and_fusion.5, bf16[128,128,128]{1,2,0:T(8,128)(2,1)} %get-tuple-element.457, s32[]{:T(128)S(6)} %select_n.78), kind=kOutput, calls=%fused_computation.11.clone.1 | convolution fusion | flops 269484032 | bytes 6815764 | tf_op jit(solution)/shard_map/while/body/eval_jaxpr/sab,saf->sbf/dot_general | solution.py:29
  283.1 6.1 %scatter_fusion.1 = f32[4,128,512]{2,1,0:T(8,128)S(1)} fusion(f32[4,128,512]{2,1,0:T(8,128)S(1)} %get-tuple-element.443, s32[16]{0:T(128)S(1)} %get-tuple-element.396, f32[16,128,512]{2,1,0:T(8,128)} %convolution_select_fusion.5), kind=kCustom, calls=%fused_computation.3.clone.1 | custom fusion | flops 1048576 | bytes 12582976 | tf_op jit(solution)/shard_map/while/body/eval_jaxpr/scatter-add | solution.py:36
  289.4 3.2 gather_fusion.1
  293.3 4.4 %convolution_select_fusion.5 = f32[16,128,512]{2,1,0:T(8,128)} fusion(bf16[16,128,512]{2,1,0:T(8,128)(2,1)} %gather_fusion.1, pred[16]{0:T(512)(128)(4,1)S(1)} %compare_and_fusion.5, bf16[128,128,128]{1,2,0:T(8,128)(2,1)} %get-tuple-element.457, s32[]{:T(128)S(6)} %select_n.78), kind=kOutput, calls=%fused_computation.11.clone.1 | convolution fusion | flops 269484032 | bytes 6815764 | tf_op jit(solution)/shard_map/while/body/eval_jaxpr/sab,saf->sbf/dot_general | solution.py:29
  297.8 6.2 %scatter_fusion.1 = f32[4,128,512]{2,1,0:T(8,128)S(1)} fusion(f32[4,128,512]{2,1,0:T(8,128)S(1)} %get-tuple-element.443, s32[16]{0:T(128)S(1)} %get-tuple-element.396, f32[16,128,512]{2,1,0:T(8,128)} %convolution_select_fusion.5), kind=kCustom, calls=%fused_computation.3.clone.1 | custom fusion | flops 1048576 | bytes 12582976 | tf_op jit(solution)/shard_map/while/body/eval_jaxpr/scatter-add | solution.py:36
  304.1 3.2 gather_fusion.1
  308.0 4.4 %convolution_select_fusion.5 = f32[16,128,512]{2,1,0:T(8,128)} fusion(bf16[16,128,512]{2,1,0:T(8,128)(2,1)} %gather_fusion.1, pred[16]{0:T(512)(128)(4,1)S(1)} %compare_and_fusion.5, bf16[128,128,128]{1,2,0:T(8,128)(2,1)} %get-tuple-element.457, s32[]{:T(128)S(6)} %select_n.78), kind=kOutput, calls=%fused_computation.11.clone.1 | convolution fusion | flops 269484032 | bytes 6815764 | tf_op jit(solution)/shard_map/while/body/eval_jaxpr/sab,saf->sbf/dot_general | solution.py:29
  312.5 6.1 %scatter_fusion.1 = f32[4,128,512]{2,1,0:T(8,128)S(1)} fusion(f32[4,128,512]{2,1,0:T(8,128)S(1)} %get-tuple-element.443, s32[16]{0:T(128)S(1)} %get-tuple-element.396, f32[16,128,512]{2,1,0:T(8,128)} %convolution_select_fusion.5), kind=kCustom, calls=%fused_computation.3.clone.1 | custom fusion | flops 1048576 | bytes 12582976 | tf_op jit(solution)/shard_map/while/body/eval_jaxpr/scatter-add | solution.py:36
  319.9 40.6 %psum.23 = f32[8,512]{1,0:T(8,128)S(1)} all-reduce(f32[8,512]{1,0:T(8,128)S(1)} %fusion.7), channel_id=1, replica_groups=mesh['row'=4,'col'=8] {'row','col'}, use_global_device_ids=true, to_apply=%region_14.15 | all-reduce | flops 4096 | bytes 32768 | tf_op jit(solution)/shard_map/psum | solution.py:100
  361.1 2.2 fusion.6
  363.3 3.4 broadcast_multiply_fusion.1
  366.7 1.5 broadcast_multiply_fusion
  368.3 11.1 %reduce-scatter.5.cloned.1.call-done = f32[128,512]{1,0:T(8,128)} async-done(((f32[512,512]{1,0:T(8,128)}), f32[128,512]{1,0:T(8,128)}) %reduce-scatter.5.cloned.1.call-update) | async-done | bytes 262160 | tf_op jit(solution)/shard_map/reduce_scatter | solution.py:112
  (90 shorter events, 19.2 us)
Async XLA Ops:
  7.2 170.3 %copy-start = (bf16[512,1024]{1,0:T(8,128)(2,1)S(1)}, bf16[512,1024]{1,0:T(8,128)(2,1)}, u32[]{:S(2)}) copy-start(bf16[512,1024]{1,0:T(8,128)(2,1)} %param.21) | copy-start | bytes 3145732
  7.2 13.6 %copy-start.6 = (s32[1,128]{1,0:T(1,128)S(1)}, s32[1,128]{1,0:T(1,128)}, u32[]{:S(2)}) copy-start(s32[1,128]{1,0:T(1,128)} %param.16) | copy-start | bytes 1540
  7.2 13.6 %copy-start.7 = (s32[1,128]{1,0:T(1,128)S(1)}, s32[1,128]{1,0:T(1,128)}, u32[]{:S(2)}) copy-start(s32[1,128]{1,0:T(1,128)} %param.17) | copy-start | bytes 1540
  7.2 166.7 %reduce-scatter.3.cloned.1.call-start = ((), (), s32[]{:S(2)}) async-start(), calls=%async_computation.2 | async-start | bytes 2359296 | tf_op jit(solution)/shard_map/reduce_scatter | solution.py:71
  136.1 1.3 copy-start.2
  136.2 40.0 %copy-start.8 = (f32[8,512]{1,0:T(8,128)S(1)}, f32[8,512]{1,0:T(8,128)}, u32[]{:S(2)}) copy-start(f32[8,512]{1,0:T(8,128)} %param.20) | copy-start | bytes 49156
  136.2 40.0 %copy-start.9 = (s32[128]{0:T(128)S(1)}, s32[128]{0:T(128)}, u32[]{:S(2)}) copy-start(s32[128]{0:T(128)} %param.19) | copy-start | bytes 1540
  136.2 41.6 %copy-start.5 = (bf16[128,512]{1,0:T(8,128)(2,1)S(1)}, bf16[128,512]{1,0:T(8,128)(2,1)}, u32[]{:S(2)}) copy-start(bf16[128,512]{1,0:T(8,128)(2,1)} %param.23) | copy-start | bytes 393220
  137.5 63.5 %all-gather.2.cloned.1.call-start = ((), (), s32[]{:S(2)}) async-start(), calls=%async_computation.3 | async-start | bytes 1179648 | tf_op jit(solution)/shard_map/all_gather | solution.py:101
  174.9 2.9 copy-start.10
  177.8 1.0 copy-start.3
  180.2 183.1 %all-reduce.3.cloned.1.call-start = ((), (), s32[]{:S(2)}) async-start(), calls=%async_computation.5 | async-start | bytes 8388608 | tf_op jit(solution)/shard_map/psum | solution.py:100
  190.3 189.1 %reduce-scatter.5.cloned.1.call-start = ((), (), s32[]{:S(2)}) async-start(), calls=%async_computation.4 | async-start | bytes 1310720 | tf_op jit(solution)/shard_map/reduce_scatter | solution.py:112
  318.6 1.0 copy-start.1
  363.3 3.5 copy-start.4
Sparse Core Ops, SparseCore 0:
  137.6 36.2 reduce-scatter.2
  180.3 20.6 all-gather.1
  207.3 142.0 all-reduce.2
  352.7 26.6 reduce-scatter.4
where the time goes:
time: 389 us; the launch traced here: 386 us
  other arithmetic  120 us (31%)
  matrix products  79.5 us (20%)
  local copies, waits for them, and re-layouts  59.8 us (15%)
  waiting for transfers between devices  58.2 us (15%)
  blocking collectives  53.8 us (14%)
  between operations  14 us (4%)
    scatter-add x16, other arithmetic, advance(): return totals.at[placed].add(product)  98.2 us
    psum x1, blocking collectives, shards(): reduced = lax.psum((grad_in_w, grad_out_w, grad_gain), ('row', 'col'))  40.6 us
    reduce_scatter x1, waiting for transfers between devices, shards(): lax.psum_scatter(totals.reshape(col_count * TILE, F), 'col', scatter_dime...  36.3 us
    dot_general x8, matrix products, advance(): jnp.einsum('sab,saf->sbf', weights_now, pieces, preferred_element_type=jn...  35.6 us
    dot_general x8, matrix products, advance(): jnp.einsum('sab,sbf->saf', weights_now, pieces, preferred_element_type=jn...  35.2 us
    gather x8, local copies, waits for them, and re-layouts, advance(): pieces = sources[row_ids]  26 us
    gather x8, local copies, waits for them, and re-layouts, advance(): pieces = sources[col_ids]  24.3 us
    all_gather x1, blocking collectives, shards(): lax.all_gather(features, 'row', axis=0, tiled=True)  13.3 us
  transfers between devices with their start and end apart: 4, of which 3 were waited for; matrix products, arithmetic and copies ran while one was open for 35% of the time, Pallas kernels for 0%

commit v1 on v0

v1 whole, which is shorter than its diff:
```python
import jax
import jax.numpy as jnp
import numpy as np
from jax import lax
from jax.experimental import pallas as pl
from jax.experimental.pallas import tpu as pltpu
from jax.sharding import PartitionSpec as P

F = 512
TYPES = 8
TILE = 128
BF = jnp.bfloat16
FP = jnp.float32
AXES = ("row", "col")


def reversed_bits(value, bits):
    out = 0
    for b in range(bits):
        out |= ((value >> b) & 1) << (bits - 1 - b)
    return out


def exchange(x, rows, cols, row_masks, z_masks):
    pairs = []
    for r in range(rows):
        for c in range(cols):
            core = c & 1
            pairs.append((r * cols + c, (r ^ row_masks[core]) * cols + (c ^ (2 * z_masks[core]))))
    return lax.ppermute(x, AXES, pairs)


def swap_cores(x, rows, cols):
    return lax.ppermute(x, AXES, [(i, i ^ 1) for i in range(rows * cols)])


def rounded(x):
    return lax.reduce_precision(x, 8, 7).astype(BF)


def split(x):
    high = lax.reduce_precision(x, 8, 7)
    return jnp.concatenate([high.astype(BF), rounded(x - high)], axis=0)


def joined(x):
    x = x.astype(FP)
    return x[:TYPES] + x[TYPES:]


def build(tile_vals, tile_row, tile_col, live_count, row_order, col_order):
    slots = tile_vals.shape[0]
    n_r, n_c = row_order.shape[0], col_order.shape[0]
    half, wide = n_r // 2, n_c * TILE
    chunk = 16
    rounds = slots // chunk

    def kernel(count_ref, row_ref, col_ref, ro_ref, co_ref, vals_ref, near_ref, near_t_ref, far_ref, far_t_ref, total):
        step = pl.program_id(0)

        @pl.when(step == 0)
        def _():
            total[...] = jnp.zeros_like(total)

        first = step * chunk

        def add(s, carry):
            r, c = row_ref[first + s], col_ref[first + s]
            total[r, c] = total[r, c] + vals_ref[s].astype(FP)
            return carry

        lax.fori_loop(0, jnp.clip(count_ref[0] - first, 0, chunk), add, 0)

        @pl.when(step == rounds - 1)
        def _():
            for side, (out, out_t) in enumerate(((near_ref, near_t_ref), (far_ref, far_t_ref))):

                def emit(p, carry, side=side, out=out, out_t=out_t):
                    r = ro_ref[side * half + p]
                    at = pl.ds(pl.multiple_of(p * TILE, TILE), TILE)
                    for q in range(n_c):
                        value = total[r, co_ref[q]]
                        high = value.astype(BF)
                        out[at, q * TILE : (q + 1) * TILE] = high
                        out[at, wide + q * TILE : wide + (q + 1) * TILE] = (value - high.astype(FP)).astype(BF)
                        out_t[q * TILE : (q + 1) * TILE, at] = value.T.astype(BF)
                    return carry

                lax.fori_loop(0, half, emit, 0)

    dense = n_r * n_c * TILE * TILE
    plain = jax.ShapeDtypeStruct((half * TILE, 2 * wide), BF)
    turned = jax.ShapeDtypeStruct((wide, half * TILE), BF)
    return pl.pallas_call(
        kernel,
        out_shape=(plain, turned, plain, turned),
        grid_spec=pltpu.PrefetchScalarGridSpec(
            num_scalar_prefetch=5,
            grid=(rounds,),
            in_specs=[pl.BlockSpec((chunk, TILE, TILE), lambda i, *_: (i, 0, 0))],
            out_specs=tuple(pl.BlockSpec(x.shape, lambda i, *_: (0, 0)) for x in (plain, turned, plain, turned)),
            scratch_shapes=[pltpu.VMEM((n_r, n_c, TILE, TILE), FP)],
        ),
        compiler_params=pltpu.CompilerParams(vmem_limit_bytes=dense * 11 + 4 * 1024 * 1024),
        cost_estimate=pl.CostEstimate(
            flops=slots * TILE * TILE, bytes_accessed=slots * TILE * TILE * 2 + dense * 6, transcendentals=0
        ),
        name="build_dense",
    )(live_count, tile_row, tile_col, row_order, col_order, tile_vals)


def write_weights(near, far, core, first_order, second_order, factor):
    n_row = first_order.shape[0]
    lanes = near[0].shape[1]
    parts = len(near)
    span = near[0].shape[0] // n_row
    per = F // span

    def kernel(core_ref, f_ref, s_ref, *refs):
        mine, there, (in_ref, out_ref) = refs[:parts], refs[parts : 2 * parts], refs[2 * parts :]

        def put(sources, ref):
            for i, x in enumerate(sources):
                ref[:, i * lanes : (i + 1) * lanes] = x[...].astype(FP) * factor

        @pl.when(core_ref[0] == 0)
        def _():
            put(mine, in_ref)
            put(there, out_ref)

        @pl.when(core_ref[0] != 0)
        def _():
            put(there, in_ref)
            put(mine, out_ref)

    block = pl.BlockSpec((span, lanes), lambda q, *_: (q, 0))
    return pl.pallas_call(
        kernel,
        out_shape=(jax.ShapeDtypeStruct((F, 2 * F), FP), jax.ShapeDtypeStruct((2 * F, F), FP)),
        grid_spec=pltpu.PrefetchScalarGridSpec(
            num_scalar_prefetch=3,
            grid=(n_row,),
            in_specs=[block] * (2 * parts),
            out_specs=(
                pl.BlockSpec((span, F), lambda q, c, f, s: (f[q] % per, f[q] // per)),
                pl.BlockSpec((span, F), lambda q, c, f, s: (s[q], 0)),
            ),
        ),
        cost_estimate=pl.CostEstimate(flops=4 * F * F, bytes_accessed=24 * F * F, transcendentals=0),
        name="write_weights",
    )(core.reshape(1), first_order, second_order, *near, *far)


def tie(*arrays):
    return lax.optimization_barrier(arrays)


def shards(
    features,
    tile_vals,
    tile_row,
    tile_col,
    tile_count,
    node_type,
    type_gain,
    w_in,
    w_out,
    cotangent,
):
    n_row, n_col = lax.axis_size("row"), lax.axis_size("col")
    n_z = n_col // 2
    row_bits, z_bits = n_row.bit_length() - 1, n_z.bit_length() - 1
    total_nodes = TILE * n_row * n_col
    row, col = lax.axis_index("row"), lax.axis_index("col")
    core, z = col & 1, col >> 1

    def row_step(x, step):
        return exchange(x, n_row, n_col, (1 << step, 1 << (row_bits - 1 - step)), (0, 0))

    def z_step(x, step):
        return exchange(x, n_row, n_col, (0, 0), (1 << step, 1 << (z_bits - 1 - step)))

    def dot(a, b, dims):
        return lax.dot_general(a, b, (dims, ((), ())), preferred_element_type=FP)

    z_flip = jnp.array([reversed_bits(p, z_bits) for p in range(n_z)], jnp.int32)
    z_same = jnp.arange(n_z, dtype=jnp.int32)
    row_flip = row ^ jnp.array([reversed_bits(q, row_bits) for q in range(n_row)], jnp.int32)
    row_same = row ^ jnp.arange(n_row, dtype=jnp.int32)
    z_own = jnp.where(core == 0, z_same, z_flip)
    z_other = jnp.where(core == 0, z_flip, z_same)
    row_order = jnp.concatenate([2 * (z ^ z_own) + core, 2 * (z ^ z_other) + (1 - core)])
    col_order = jnp.where(core == 0, row_same, row_flip)

    near, near_t, far, far_t = build(tile_vals[0], tile_row[0], tile_col[0], tile_count[0], row_order, col_order)
    here, there = [features], []
    for step in range(row_bits):
        came = row_step(here[0] if step == 0 else jnp.concatenate(here, axis=0), step)
        there.append(swap_cores(here[-1], n_row, n_col))
        here.append(came)
    there.append(swap_cores(here[-1], n_row, n_col))
    far, far_t = swap_cores(far, n_row, n_col), swap_cores(far_t, n_row, n_col)

    total = dot(near, jnp.concatenate(here + here, axis=0), ((1,), (0,))) + dot(
        far, jnp.concatenate(there + there, axis=0), ((1,), (0,))
    )
    for step in reversed(range(z_bits)):
        mid = total.shape[0] // 2
        came = z_step(rounded(total[mid:]), step)
        total = total[:mid] + came.astype(FP)
    aggregate = total

    center = jnp.mean(aggregate, axis=-1, keepdims=True)
    spread = jnp.mean(jnp.square(aggregate - center), axis=-1, keepdims=True)
    inverse = lax.rsqrt(spread + 1e-05)
    normed = (aggregate - center) * inverse
    onehot = (node_type[:, None] == jnp.arange(TYPES, dtype=jnp.int32)[None, :]).astype(FP)
    gains = jnp.dot(onehot, type_gain, precision=lax.Precision.HIGHEST)
    scaled = (normed * gains).astype(BF)
    hidden = jnp.dot(scaled, w_in, preferred_element_type=FP)
    grad_act = dot(cotangent, w_out, ((1,), (1,)))
    sigmoid_h = jax.nn.sigmoid(hidden)
    activated = (hidden * sigmoid_h).astype(BF)
    grad_hidden = (grad_act * sigmoid_h * (1.0 + hidden * (1.0 - sigmoid_h))).astype(BF)

    for_in = jnp.concatenate([scaled, grad_hidden], axis=1)
    for_out = jnp.concatenate([cotangent, activated], axis=1)
    mine = jnp.where(core == 0, for_in, for_out)
    away = jnp.where(core == 0, for_out, for_in)
    away, activated, grad_hidden = tie(away, activated, grad_hidden)
    pairs = jnp.concatenate([mine, swap_cores(away, n_row, n_col)], axis=0)
    single, double = pairs[:, :F], pairs[:, F:]
    twice = jnp.concatenate([single, single], axis=1)
    left = jnp.where(core == 0, twice, double)
    right = jnp.where(core == 0, double, twice)
    wide = left.shape[1]
    span = wide // n_row
    parts = 2
    lanes = F // parts

    def weight_blocks(places, part):
        out = []
        for q in places:
            start = col_order[q] * span
            a = lax.dynamic_slice_in_dim(left, start, span, 1)
            b = lax.dynamic_slice_in_dim(right, (start // F) * F + part * lanes, lanes, 1)
            out.append(dot(a, b, ((0,), (0,))))
        return jnp.concatenate(out, axis=0)

    sums, outs = [None] * parts, [None] * parts
    for i in range(parts):
        outs[i] = rounded(weight_blocks(range(n_row // 2, n_row), i))
    *outs, activated, grad_hidden = tie(*outs, activated, grad_hidden)
    for i in range(parts):
        sums[i] = weight_blocks(range(n_row // 2), i)

    branch = jnp.dot(activated, w_out, preferred_element_type=FP)
    mixed = (aggregate + branch).astype(BF)
    grad_scaled = dot(grad_hidden, w_in, ((1,), (1,)))
    grad_gain = lax.dot_general(
        onehot, grad_scaled * normed, (((0,), (0,)), ((), ())), precision=lax.Precision.HIGHEST
    )
    grad_normed = grad_scaled * gains
    grad_agg = cotangent.astype(FP) + inverse * (
        grad_normed
        - jnp.mean(grad_normed, axis=-1, keepdims=True)
        - normed * jnp.mean(grad_normed * normed, axis=-1, keepdims=True)
    )
    grad_rows = grad_agg.astype(BF)

    gain = split(grad_gain)
    for step in range(z_bits):
        came = z_step(jnp.concatenate([grad_rows, gain], axis=0), step)
        size = grad_rows.shape[0]
        grad_rows = jnp.concatenate([grad_rows, came[:size]], axis=0)
        gain = split(joined(gain) + joined(came[size:]))
    came = swap_cores(rounded(dot(far_t, grad_rows, ((1,), (0,)))), n_row, n_col)
    low = dot(near_t, grad_rows, ((1,), (0,))) + came.astype(FP)
    for step in reversed(range(row_bits)):
        size = low.shape[0] // 2
        came = row_step(jnp.concatenate([rounded(low[size:]), gain], axis=0), step)
        gain = split(joined(gain) + joined(came[size:]))
        low = low[:size] + came[:size].astype(FP)
    grad_x = low
    factor = float(total_nodes) ** (-0.5)
    grad_gain = (joined(gain) + joined(swap_cores(gain, n_row, n_col))) * factor

    for step in reversed(range(row_bits)):
        for i in range(parts):
            mid = sums[i].shape[0] // 2
            sums[i] = sums[i] + row_step(outs[i], step).astype(FP)
            if step:
                sums[i], outs[i] = sums[i][:mid], rounded(sums[i][mid:])
    for step in range(z_bits):
        for i in range(parts):
            held = rounded(sums[i])
            sums[i] = held.astype(FP) + z_step(held, step).astype(FP)
    owns = [rounded(x) for x in sums]
    others = [[] for _ in range(parts)]
    for step in range(row_bits):
        for i in range(parts):
            came = row_step(owns[i], step)
            if step == row_bits - 1:
                others[i].append(swap_cores(owns[i], n_row, n_col))
                came, mixed, grad_x = tie(came, mixed, grad_x)
                others[i].append(swap_cores(came, n_row, n_col))
            owns[i] = jnp.concatenate([owns[i], came], axis=0)
    others = [jnp.concatenate(x, axis=0) for x in others]
    grad_w_in, grad_w_out = write_weights(owns, others, core, row_same, row_flip, factor)
    return mixed, grad_x, grad_w_in, grad_w_out, grad_gain


def solution(mesh):
    return jax.shard_map(
        shards,
        mesh=mesh,
        in_specs=(
            P(("col", "row"), None),
            P("row", "col", None, None),
            P("row", "col"),
            P("row", "col"),
            P("row", "col"),
            P(("row", "col")),
            P(),
            P(),
            P(),
            P(("row", "col"), None),
        ),
        out_specs=(P(("row", "col"), None), P(("col", "row"), None), P(), P(), P()),
        check_vma=False,
    )
```

time: 389 us -> 105 us (0.27)
  other arithmetic: 120 us -> 8.98 us
  matrix products: 79.5 us -> 8.89 us
  local copies, waits for them, and re-layouts: 59.8 us -> 4.34 us
  blocking collectives: 53.8 us -> 0 us
  starting transfers between devices: 0.16 us -> 34.7 us
  waiting for transfers between devices: 58.2 us -> 36.4 us
  between operations: 14 us -> 4.63 us
  Pallas kernels: 0 us -> 6.97 us
    scatter-add x16 -> x0, other arithmetic: 98.2 us -> none  [advance(): return totals.at[placed].add(product)]
    dot_general x23 -> x17, matrix products: 78.2 us -> 7.86 us  [the longest x14 6.22 us: dot(): return lax.dot_general(a, b, (dims, ((), ())), preferred_element_type=FP)]
    gather x16 -> x0, local copies, waits for them, and re-layouts: 50.3 us -> none  [the longest x8 26 us: advance(): pieces = sources[row_ids]]
    reduce_scatter x2 -> x0, waiting for transfers between devices: 47.4 us -> none  [the longest x1 36.3 us: shards(): lax.psum_scatter(totals.reshape(col_count * TILE, F), 'col', scatter_dime...]
    psum x1 -> x0, blocking collectives: 40.6 us -> none  [shards(): reduced = lax.psum((grad_in_w, grad_out_w, grad_gain), ('row', 'col'))]
    ppermute x0 -> x32, waiting for transfers between devices: none -> 36.4 us  [the longest x20 33.6 us: exchange(): return lax.ppermute(x, AXES, pairs)]
    ppermute x0 -> x32, starting transfers between devices: none -> 34.7 us  [the longest x20 32.8 us: exchange(): return lax.ppermute(x, AXES, pairs)]
    all_gather x1 -> x0, blocking collectives: 13.3 us -> none  [shards(): lax.all_gather(features, 'row', axis=0, tiled=True)]
  transfers between devices with their start and end apart: 4 -> 32, of which waited for: 3 -> 15; matrix products, arithmetic and copies ran while one was open for 35% -> 13% of each run, Pallas kernels for 0% -> 2%
where the time goes in v1:
time: 105 us
  waiting for transfers between devices  36.4 us (35%)
  starting transfers between devices  34.7 us (33%)
  other arithmetic  8.98 us (9%)
  matrix products  8.89 us (8%)
  Pallas kernels  6.97 us (7%)
  between operations  4.63 us (4%)
  local copies, waits for them, and re-layouts  4.34 us (4%)
    ppermute x20, waiting for transfers between devices, exchange(): return lax.ppermute(x, AXES, pairs)  33.6 us
    ppermute x20, starting transfers between devices, exchange(): return lax.ppermute(x, AXES, pairs)  32.8 us
    dot_general x14, matrix products, dot(): return lax.dot_general(a, b, (dims, ((), ())), preferred_element_type=FP)  6.22 us
    pallas_call x1, Pallas kernels, write_weights(): pl.pallas_call(kernel, out_shape=(jax.ShapeDtypeStruct((F, 2 * F), FP), j...  4.98 us
    unnamed x36, local copies, waits for them, and re-layouts  3.68 us
    ppermute x12, waiting for transfers between devices, swap_cores(): return lax.ppermute(x, AXES, [(i, i ^ 1) for i in range(rows * cols)])  2.78 us
  transfers between devices with their start and end apart: 32, of which 15 were waited for; matrix products, arithmetic and copies ran while one was open for 13% of the time, Pallas kernels for 2%

profile of v1, /device:TPU:0, one launch (start us, length us, event | category | flops | bytes accessed | tf_op | source)
XLA Modules:
  0.0 104.9 jit_solution(11201777957047130332)
XLA Ops:
  0.6 3.0 %collective-permute-start = (bf16[128,512]{1,0:T(8,128)(2,1)}, bf16[128,512]{1,0:T(8,128)(2,1)S(1)}, u32[]{:S(2)}, u32[]{:S(2)}) collective-permute-start(bf16[128,512]{1,0:T(8,128)(2,1)} %param.12), channel_id=1, source_target_pairs={{0,8},{1,17},{2,10},{3,19},{4,12},{5,21},{6,14},{7,23},{8,0},{9,25... | collective-permute-start | bytes 393224 | tf_op jit(solution)/shard_map/ppermute | solution.py:30
  3.7 1.2 %broadcast_xor_fusion = (s32[4]{0:T(128)}, s32[4]{0:T(128)S(1)}, s32[4]{0:T(128)S(1)}, s32[4]{0:T(128)S(1)}) fusion(s32[4]{0:T(128)} %constant.88.clone, s32[]{:T(128)S(6)} %axis_index.25, pred[]{:T(512)S(6)} %eq.8, s32[]{:T(128)} %and.26, s32[]{:T(128)S(6)} %shift_right_arithmetic.3, s32[]{:T(128)S(6)} %sub.61), kind=kLoop, calls=%fused_computation.181 | loop fusion | flops 44 | bytes 97 | tf_op jit(solution)/shard_map/xor | solution.py:188
  5.6 2.2 %copy-done.1 = bf16[1,128,128,128]{3,2,1,0:T(8,128)(2,1)S(1)} copy-done((bf16[1,128,128,128]{3,2,1,0:T(8,128)(2,1)S(1)}, bf16[1,128,128,128]{3,2,1,0:T(8,128)(2,1)}, u32[]{:S(2)}) %copy-start.1) | copy-done | bytes 4194328
  7.7 0.7 copy-done.2
  8.4 0.7 copy-done.3
  9.0 2.0 %build_dense.1 = (bf16[512,1024]{1,0:T(8,128)(2,1)S(1)}, bf16[512,512]{1,0:T(8,128)(2,1)S(1)}, bf16[512,1024]{1,0:T(8,128)(2,1)S(1)}, bf16[512,512]{1,0:T(8,128)(2,1)S(1)}) custom-call(s32[1]{0:T(128)} %bitcast.24.count_ref, s32[128]{0:T(128)S(1)} %bitcast.26, s32[128]{0:T(128)S(1)} %bitcast.27, s32[8]{0:T(128)S(1)} %pad_add_fusion.ro_ref, ...), custom_call_target="tpu_custom_call" | custom-call | flops 2097152 | bytes 7340032 | tf_op jit(solution)/shard_map/build_dense/pallas_call | solution.py:94
  11.1 0.5 collective-permute-start.2
  11.6 1.6 %collective-permute-start.1 = (bf16[256,512]{1,0:T(8,128)(2,1)S(1)}, bf16[256,512]{1,0:T(8,128)(2,1)S(1)}, u32[]{:S(2)}, u32[]{:S(2)}) collective-permute-start(bf16[256,512]{1,0:T(8,128)(2,1)S(1)} %pad_maximum_fusion.12), channel_id=1, source_target_pairs={{0,16},{1,9},{2,18},{3,11},{4,20},{5,13},{6,22},{7,15},{8,24},{9,1... | collective-permute-start | bytes 786440 | tf_op jit(solution)/shard_map/ppermute | solution.py:30
  13.3 1.3 %collective-permute-done.4 = bf16[128,512]{1,0:T(8,128)(2,1)S(1)} collective-permute-done((bf16[128,512]{1,0:T(8,128)(2,1)S(1)}, bf16[128,512]{1,0:T(8,128)(2,1)S(1)}, u32[]{:S(2)}, u32[]{:S(2)}) %collective-permute-start.4) | collective-permute-done | bytes 131104 | tf_op jit(solution)/shard_map/ppermute | solution.py:34
  14.6 3.5 %collective-permute-done.1 = bf16[256,512]{1,0:T(8,128)(2,1)S(1)} collective-permute-done((bf16[256,512]{1,0:T(8,128)(2,1)S(1)}, bf16[256,512]{1,0:T(8,128)(2,1)S(1)}, u32[]{:S(2)}, u32[]{:S(2)}) %collective-permute-start.1) | collective-permute-done | bytes 262176 | tf_op jit(solution)/shard_map/ppermute | solution.py:30
  18.1 1.4 %collective-permute-done.5 = bf16[256,512]{1,0:T(8,128)(2,1)S(1)} collective-permute-done((bf16[256,512]{1,0:T(8,128)(2,1)S(1)}, bf16[256,512]{1,0:T(8,128)(2,1)S(1)}, u32[]{:S(2)}, u32[]{:S(2)}) %collective-permute-start.5) | collective-permute-done | bytes 262176 | tf_op jit(solution)/shard_map/ppermute | solution.py:34
  19.7 0.7 fusion.87
  20.4 0.7 convolution_add_fusion.1
  21.2 2.6 %collective-permute-start.6 = (bf16[256,512]{1,0:T(8,128)(2,1)S(1)}, bf16[256,512]{1,0:T(8,128)(2,1)S(1)}, u32[]{:S(2)}, u32[]{:S(2)}) collective-permute-start(bf16[256,512]{1,0:T(8,128)(2,1)S(1)} %fusion.5), channel_id=1, source_target_pairs={{0,4},{1,3},{2,6},{3,1},{4,0},{5,7},{6,2},{7,5},{8,12},{9,11},{10,... | collective-permute-start | bytes 786440 | tf_op jit(solution)/shard_map/ppermute | solution.py:30
  23.8 6.5 %collective-permute-done.6 = bf16[256,512]{1,0:T(8,128)(2,1)S(1)} collective-permute-done((bf16[256,512]{1,0:T(8,128)(2,1)S(1)}, bf16[256,512]{1,0:T(8,128)(2,1)S(1)}, u32[]{:S(2)}, u32[]{:S(2)}) %collective-permute-start.6) | collective-permute-done | bytes 262176 | tf_op jit(solution)/shard_map/ppermute | solution.py:30
  30.4 1.9 %collective-permute-start.7 = (bf16[128,512]{1,0:T(8,128)(2,1)S(1)}, bf16[128,512]{1,0:T(8,128)(2,1)S(1)}, u32[]{:S(2)}, u32[]{:S(2)}) collective-permute-start(bf16[128,512]{1,0:T(8,128)(2,1)S(1)} %fusion.15), channel_id=1, source_target_pairs={{0,2},{1,5},{2,0},{3,7},{4,6},{5,1},{6,4},{7,3},{8,10},{9,13},{10,... | collective-permute-start | bytes 393224 | tf_op jit(solution)/shard_map/ppermute | solution.py:30
  32.3 4.3 %collective-permute-done.7 = bf16[128,512]{1,0:T(8,128)(2,1)S(1)} collective-permute-done((bf16[128,512]{1,0:T(8,128)(2,1)S(1)}, bf16[128,512]{1,0:T(8,128)(2,1)S(1)}, u32[]{:S(2)}, u32[]{:S(2)}) %collective-permute-start.7) | collective-permute-done | bytes 131104 | tf_op jit(solution)/shard_map/ppermute | solution.py:30
  37.0 1.0 multiply_convert_fusion.1
  38.0 0.4 multiply_convert_fusion
  38.4 0.5 fusion.2
  38.9 0.9 broadcast_select_fusion.3
  39.8 0.5 collective-permute-start.23
  40.3 0.6 fusion.86
  43.6 0.5 iota_xor_fusion.f_ref
  45.6 0.2 fusion.26
  45.9 1.0 fusion.3
  46.9 0.6 fusion.80
  47.5 0.3 reduce-precision_convert_fusion.8
  48.0 0.7 collective-permute-start.21
  48.7 1.7 %collective-permute-start.9 = (bf16[512,256]{1,0:T(8,128)(2,1)S(1)}, bf16[512,256]{1,0:T(8,128)(2,1)S(1)}, u32[]{:S(2)}, u32[]{:S(2)}) collective-permute-start(bf16[512,256]{1,0:T(8,128)(2,1)S(1)} %get-tuple-element.29), channel_id=1, source_target_pairs={{0,16},{1,9},{2,18},{3,11},{4,20},{5,13},{6,22},{7,15},{8,24},{9,1... | collective-permute-start | bytes 786440 | tf_op jit(solution)/shard_map/ppermute | solution.py:30
  50.3 0.3 collective-permute-start.15
  50.9 0.2 fusion.30
  51.2 3.5 %collective-permute-done.21 = bf16[144,512]{1,0:T(8,128)(2,1)S(1)} collective-permute-done((bf16[144,512]{1,0:T(8,128)(2,1)S(1)}, bf16[144,512]{1,0:T(8,128)(2,1)S(1)}, u32[]{:S(2)}, u32[]{:S(2)}) %collective-permute-start.21) | collective-permute-done | bytes 147488 | tf_op jit(solution)/shard_map/ppermute | solution.py:30
  54.8 1.6 %collective-permute-start.22 = (bf16[272,512]{1,0:T(8,128)(2,1)S(1)}, bf16[272,512]{1,0:T(8,128)(2,1)S(1)}, u32[]{:S(2)}, u32[]{:S(2)}) collective-permute-start(bf16[272,512]{1,0:T(8,128)(2,1)S(1)} %pad_maximum_fusion.9), channel_id=1, source_target_pairs={{0,4},{1,3},{2,6},{3,1},{4,0},{5,7},{6,2},{7,5},{8,12},{9,11},{10,... | collective-permute-start | bytes 835592 | tf_op jit(solution)/shard_map/ppermute | solution.py:30
  56.5 1.2 %collective-permute-start.10 = (bf16[256,256]{1,0:T(8,128)(2,1)S(1)}, bf16[256,256]{1,0:T(8,128)(2,1)S(1)}, u32[]{:S(2)}, u32[]{:S(2)}) collective-permute-start(bf16[256,256]{1,0:T(8,128)(2,1)S(1)} %fusion.12), channel_id=1, source_target_pairs={{0,8},{1,17},{2,10},{3,19},{4,12},{5,21},{6,14},{7,23},{8,0},{9,25... | collective-permute-start | bytes 393224 | tf_op jit(solution)/shard_map/ppermute | solution.py:30
  57.9 2.2 %collective-permute-start.16 = (bf16[256,256]{1,0:T(8,128)(2,1)S(1)}, bf16[256,256]{1,0:T(8,128)(2,1)S(1)}, u32[]{:S(2)}, u32[]{:S(2)}) collective-permute-start(bf16[256,256]{1,0:T(8,128)(2,1)S(1)} %fusion.9), channel_id=1, source_target_pairs={{0,8},{1,17},{2,10},{3,19},{4,12},{5,21},{6,14},{7,23},{8,0},{9,25... | collective-permute-start | bytes 393224 | tf_op jit(solution)/shard_map/ppermute | solution.py:30
  60.1 1.4 %collective-permute-done.10 = bf16[256,256]{1,0:T(8,128)(2,1)S(1)} collective-permute-done((bf16[256,256]{1,0:T(8,128)(2,1)S(1)}, bf16[256,256]{1,0:T(8,128)(2,1)S(1)}, u32[]{:S(2)}, u32[]{:S(2)}) %collective-permute-start.10) | collective-permute-done | bytes 131104 | tf_op jit(solution)/shard_map/ppermute | solution.py:30
  61.5 2.5 %collective-permute-start.11 = (bf16[256,256]{1,0:T(8,128)(2,1)S(1)}, bf16[256,256]{1,0:T(8,128)(2,1)S(1)}, u32[]{:S(2)}, u32[]{:S(2)}) collective-permute-start(bf16[256,256]{1,0:T(8,128)(2,1)S(1)} %fusion.14), channel_id=1, source_target_pairs={{0,2},{1,5},{2,0},{3,7},{4,6},{5,1},{6,4},{7,3},{8,10},{9,13},{10,... | collective-permute-start | bytes 393224 | tf_op jit(solution)/shard_map/ppermute | solution.py:30
  64.1 1.4 %collective-permute-start.17 = (bf16[256,256]{1,0:T(8,128)(2,1)S(1)}, bf16[256,256]{1,0:T(8,128)(2,1)S(1)}, u32[]{:S(2)}, u32[]{:S(2)}) collective-permute-start(bf16[256,256]{1,0:T(8,128)(2,1)S(1)} %fusion.11), channel_id=1, source_target_pairs={{0,2},{1,5},{2,0},{3,7},{4,6},{5,1},{6,4},{7,3},{8,10},{9,13},{10,... | collective-permute-start | bytes 393224 | tf_op jit(solution)/shard_map/ppermute | solution.py:30
  65.4 2.0 %collective-permute-done.22 = bf16[272,512]{1,0:T(8,128)(2,1)S(1)} collective-permute-done((bf16[272,512]{1,0:T(8,128)(2,1)S(1)}, bf16[272,512]{1,0:T(8,128)(2,1)S(1)}, u32[]{:S(2)}, u32[]{:S(2)}) %collective-permute-start.22) | collective-permute-done | bytes 278560 | tf_op jit(solution)/shard_map/ppermute | solution.py:30
  67.5 1.5 %fusion = bf16[512,512]{1,0:T(8,128)(2,1)S(1)} fusion(bf16[512,512]{1,0:T(8,128)(2,1)} %collective-permute-done.23, bf16[256,512]{1,0:T(8,128)(2,1)S(1)} %slice.202, bf16[128,512]{1,0:T(8,128)(2,1)S(1)} %slice.196, bf16[128,512]{1,0:T(8,128)(2,1)S(1)} %add_convert_fusion), kind=kOutput, calls=%fused_computation.3 | convolution fusion | flops 270532608 | bytes 1572864 | tf_op jit(solution)/shard_map/dot_general | solution.py:184
  69.1 0.6 collective-permute-start.12
  69.7 2.1 %collective-permute-done.17 = bf16[256,256]{1,0:T(8,128)(2,1)S(1)} collective-permute-done((bf16[256,256]{1,0:T(8,128)(2,1)S(1)}, bf16[256,256]{1,0:T(8,128)(2,1)S(1)}, u32[]{:S(2)}, u32[]{:S(2)}) %collective-permute-start.17) | collective-permute-done | bytes 131104 | tf_op jit(solution)/shard_map/ppermute | solution.py:30
  71.8 1.2 %collective-permute-start.18 = (bf16[256,256]{1,0:T(8,128)(2,1)S(1)}, bf16[256,256]{1,0:T(8,128)(2,1)S(1)}, u32[]{:S(2)}, u32[]{:S(2)}) collective-permute-start(bf16[256,256]{1,0:T(8,128)(2,1)S(1)} %reduce-precision_convert_fusion.1), channel_id=1, source_target_pairs={{0,4},{1,3},{2,6},{3,1},{4,0},{5,7},{6,2},{7,5},{8,12},{9,11},{10,... | collective-permute-start | bytes 393224 | tf_op jit(solution)/shard_map/ppermute | solution.py:30
  73.0 2.2 %collective-permute-done.12 = bf16[256,256]{1,0:T(8,128)(2,1)S(1)} collective-permute-done((bf16[256,256]{1,0:T(8,128)(2,1)S(1)}, bf16[256,256]{1,0:T(8,128)(2,1)S(1)}, u32[]{:S(2)}, u32[]{:S(2)}) %collective-permute-start.12) | collective-permute-done | bytes 131104 | tf_op jit(solution)/shard_map/ppermute | solution.py:30
  75.2 4.8 %collective-permute-start.13 = (bf16[256,256]{1,0:T(8,128)(2,1)S(1)}, bf16[256,256]{1,0:T(8,128)(2,1)S(1)}, u32[]{:S(2)}, u32[]{:S(2)}) collective-permute-start(bf16[256,256]{1,0:T(8,128)(2,1)S(1)} %reduce-precision_convert_fusion.2), channel_id=1, source_target_pairs={{0,8},{1,17},{2,10},{3,19},{4,12},{5,21},{6,14},{7,23},{8,0},{9,25... | collective-permute-start | bytes 393224 | tf_op jit(solution)/shard_map/ppermute | solution.py:30
  80.0 0.4 convolution_add_fusion
  80.5 1.6 %collective-permute-start.25 = (bf16[272,512]{1,0:T(8,128)(2,1)S(1)}, bf16[272,512]{1,0:T(8,128)(2,1)S(1)}, u32[]{:S(2)}, u32[]{:S(2)}) collective-permute-start(bf16[272,512]{1,0:T(8,128)(2,1)S(1)} %pad_maximum_fusion.10), channel_id=1, source_target_pairs={{0,16},{1,9},{2,18},{3,11},{4,20},{5,13},{6,22},{7,15},{8,24},{9,1... | collective-permute-start | bytes 835592 | tf_op jit(solution)/shard_map/ppermute | solution.py:30
  82.2 0.6 collective-permute-start.19
  82.7 1.5 %collective-permute-done.13 = bf16[256,256]{1,0:T(8,128)(2,1)S(1)} collective-permute-done((bf16[256,256]{1,0:T(8,128)(2,1)S(1)}, bf16[256,256]{1,0:T(8,128)(2,1)S(1)}, u32[]{:S(2)}, u32[]{:S(2)}) %collective-permute-start.13) | collective-permute-done | bytes 131104 | tf_op jit(solution)/shard_map/ppermute | solution.py:30
  84.3 1.7 %collective-permute-start.14 = (bf16[512,256]{1,0:T(8,128)(2,1)S(1)}, bf16[512,256]{1,0:T(8,128)(2,1)S(1)}, u32[]{:S(2)}, u32[]{:S(2)}) collective-permute-start(bf16[512,256]{1,0:T(8,128)(2,1)S(1)} %pad_maximum_fusion.13), channel_id=1, source_target_pairs={{0,16},{1,9},{2,18},{3,11},{4,20},{5,13},{6,22},{7,15},{8,24},{9,1... | collective-permute-start | bytes 786440 | tf_op jit(solution)/shard_map/ppermute | solution.py:30
  86.1 1.1 %collective-permute-done.25 = bf16[272,512]{1,0:T(8,128)(2,1)S(1)} collective-permute-done((bf16[272,512]{1,0:T(8,128)(2,1)S(1)}, bf16[272,512]{1,0:T(8,128)(2,1)S(1)}, u32[]{:S(2)}, u32[]{:S(2)}) %collective-permute-start.25) | collective-permute-done | bytes 278560 | tf_op jit(solution)/shard_map/ppermute | solution.py:30
  87.3 0.8 collective-permute-start.26
  88.3 0.8 collective-permute-start.20
  89.1 4.7 %collective-permute-done.26 = bf16[144,512]{1,0:T(8,128)(2,1)S(1)} collective-permute-done((bf16[144,512]{1,0:T(8,128)(2,1)S(1)}, bf16[144,512]{1,0:T(8,128)(2,1)S(1)}, u32[]{:S(2)}, u32[]{:S(2)}) %collective-permute-start.26) | collective-permute-done | bytes 147488 | tf_op jit(solution)/shard_map/ppermute | solution.py:30
  93.8 0.7 slice_add_fusion.2
  94.5 0.6 collective-permute-done.20
  95.4 0.4 collective-permute-start.30
  95.9 0.9 pad_maximum_fusion.4.refs_1_
  96.8 0.8 pad_maximum_fusion.3.refs_0_
  97.6 0.6 fusion.58
  98.2 0.8 pad_maximum_fusion.6.refs_3_
  99.1 0.9 pad_maximum_fusion.5.refs_2_
  99.9 5.0 %write_weights.1 = (f32[512,1024]{1,0:T(8,128)}, f32[1024,512]{1,0:T(8,128)}) custom-call(s32[1]{0:T(128)} %bitcast.8.core_ref, s32[4]{0:T(128)} %iota_xor_fusion.f_ref, s32[4]{0:T(128)} %get-tuple-element.64.s_ref, bf16[1024,256]{1,0:T(8,128)(2,1)} %pad_maximum_fusion.3.refs_0_, bf16[1024,256]{1,0:T(8,128)(2,1)} %pad_maximum_fusion.4.refs_1_, ...), custom_call_target="tpu_custom_call" | custom-call | flops 1048576 | bytes 6291456 | tf_op jit(solution)/shard_map/write_weights/pallas_call | solution.py:137
  (122 shorter events, 4.0 us)
Async XLA Ops:
  0.6 37.4 %copy-start = (bf16[512,1024]{1,0:T(8,128)(2,1)S(1)}, bf16[512,1024]{1,0:T(8,128)(2,1)}, u32[]{:S(2)}) copy-start(bf16[512,1024]{1,0:T(8,128)(2,1)} %param.19) | copy-start | bytes 3145732
  0.6 10.9 %collective-permute-start = (bf16[128,512]{1,0:T(8,128)(2,1)}, bf16[128,512]{1,0:T(8,128)(2,1)S(1)}, u32[]{:S(2)}, u32[]{:S(2)}) collective-permute-start(bf16[128,512]{1,0:T(8,128)(2,1)} %param.12), channel_id=1, source_target_pairs={{0,8},{1,17},{2,10},{3,19},{4,12},{5,21},{6,14},{7,23},{8,0},{9,25... | collective-permute-start | bytes 393224 | tf_op jit(solution)/shard_map/ppermute | solution.py:30
  3.6 9.6 %collective-permute-start.3 = (bf16[128,512]{1,0:T(8,128)(2,1)}, bf16[128,512]{1,0:T(8,128)(2,1)S(1)}, u32[]{:S(2)}, u32[]{:S(2)}) collective-permute-start(bf16[128,512]{1,0:T(8,128)(2,1)} %param.12), channel_id=1, source_target_pairs={{0,1},{1,0},{2,3},{3,2},{4,5},{5,4},{6,7},{7,6},{8,9},{9,8},{10,11... | collective-permute-start | bytes 393224 | tf_op jit(solution)/shard_map/ppermute | solution.py:34
  5.5 2.2 %copy-start.1 = (bf16[1,128,128,128]{3,2,1,0:T(8,128)(2,1)S(1)}, bf16[1,128,128,128]{3,2,1,0:T(8,128)(2,1)}, u32[]{:S(2)}) copy-start(bf16[1,128,128,128]{3,2,1,0:T(8,128)(2,1)} %param.13) | copy-start | bytes 12582916
  7.7 0.7 copy-start.2
  8.4 0.7 copy-start.3
  9.0 2.5 %copy-start.4 = (bf16[128,512]{1,0:T(8,128)(2,1)S(1)}, bf16[128,512]{1,0:T(8,128)(2,1)}, u32[]{:S(2)}) copy-start(bf16[128,512]{1,0:T(8,128)(2,1)} %param.12) | copy-start | bytes 393220
  11.1 8.6 %collective-permute-start.2 = (bf16[512,1024]{1,0:T(8,128)(2,1)S(1)}, bf16[512,1024]{1,0:T(8,128)(2,1)S(1)}, u32[]{:S(2)}, u32[]{:S(2)}) collective-permute-start(bf16[512,1024]{1,0:T(8,128)(2,1)S(1)} %get-tuple-element.25), channel_id=1, source_target_pairs={{0,1},{1,0},{2,3},{3,2},{4,5},{5,4},{6,7},{7,6},{8,9},{9,8},{10,11... | collective-permute-start | bytes 3145736 | tf_op jit(solution)/shard_map/ppermute | solution.py:34
  11.6 6.4 %collective-permute-start.1 = (bf16[256,512]{1,0:T(8,128)(2,1)S(1)}, bf16[256,512]{1,0:T(8,128)(2,1)S(1)}, u32[]{:S(2)}, u32[]{:S(2)}) collective-permute-start(bf16[256,512]{1,0:T(8,128)(2,1)S(1)} %pad_maximum_fusion.12), channel_id=1, source_target_pairs={{0,16},{1,9},{2,18},{3,11},{4,20},{5,13},{6,22},{7,15},{8,24},{9,1... | collective-permute-start | bytes 786440 | tf_op jit(solution)/shard_map/ppermute | solution.py:30
  13.2 1.3 %collective-permute-start.4 = (bf16[128,512]{1,0:T(8,128)(2,1)S(1)}, bf16[128,512]{1,0:T(8,128)(2,1)S(1)}, u32[]{:S(2)}, u32[]{:S(2)}) collective-permute-start(bf16[128,512]{1,0:T(8,128)(2,1)S(1)} %collective-permute-done), channel_id=1, source_target_pairs={{0,1},{1,0},{2,3},{3,2},{4,5},{5,4},{6,7},{7,6},{8,9},{9,8},{10,11... | collective-permute-start | bytes 393224 | tf_op jit(solution)/shard_map/ppermute | solution.py:34
  18.1 1.5 %collective-permute-start.5 = (bf16[256,512]{1,0:T(8,128)(2,1)S(1)}, bf16[256,512]{1,0:T(8,128)(2,1)S(1)}, u32[]{:S(2)}, u32[]{:S(2)}) collective-permute-start(bf16[256,512]{1,0:T(8,128)(2,1)S(1)} %collective-permute-done.1), channel_id=1, source_target_pairs={{0,1},{1,0},{2,3},{3,2},{4,5},{5,4},{6,7},{7,6},{8,9},{9,8},{10,11... | collective-permute-start | bytes 786440 | tf_op jit(solution)/shard_map/ppermute | solution.py:34
  21.1 15.9 %copy-start.11 = (f32[8,512]{1,0:T(8,128)S(1)}, f32[8,512]{1,0:T(8,128)}, u32[]{:S(2)}) copy-start(f32[8,512]{1,0:T(8,128)} %param.18) | copy-start | bytes 49156
  21.1 15.9 %copy-start.12 = (s32[128]{0:T(128)S(1)}, s32[128]{0:T(128)}, u32[]{:S(2)}) copy-start(s32[128]{0:T(128)} %param.17) | copy-start | bytes 1540
  21.2 9.1 %collective-permute-start.6 = (bf16[256,512]{1,0:T(8,128)(2,1)S(1)}, bf16[256,512]{1,0:T(8,128)(2,1)S(1)}, u32[]{:S(2)}, u32[]{:S(2)}) collective-permute-start(bf16[256,512]{1,0:T(8,128)(2,1)S(1)} %fusion.5), channel_id=1, source_target_pairs={{0,4},{1,3},{2,6},{3,1},{4,0},{5,7},{6,2},{7,5},{8,12},{9,11},{10,... | collective-permute-start | bytes 786440 | tf_op jit(solution)/shard_map/ppermute | solution.py:30
  30.4 6.2 %collective-permute-start.7 = (bf16[128,512]{1,0:T(8,128)(2,1)S(1)}, bf16[128,512]{1,0:T(8,128)(2,1)S(1)}, u32[]{:S(2)}, u32[]{:S(2)}) collective-permute-start(bf16[128,512]{1,0:T(8,128)(2,1)S(1)} %fusion.15), channel_id=1, source_target_pairs={{0,2},{1,5},{2,0},{3,7},{4,6},{5,1},{6,4},{7,3},{8,10},{9,13},{10,... | collective-permute-start | bytes 393224 | tf_op jit(solution)/shard_map/ppermute | solution.py:30
  36.8 1.6 %copy-start.5 = (bf16[1024,512]{1,0:T(8,128)(2,1)S(1)}, bf16[1024,512]{1,0:T(8,128)(2,1)}, u32[]{:S(2)}) copy-start(bf16[1024,512]{1,0:T(8,128)(2,1)} %param.20) | copy-start | bytes 3145732
  36.8 1.6 %copy-start.10 = (bf16[128,512]{1,0:T(8,128)(2,1)S(1)}, bf16[128,512]{1,0:T(8,128)(2,1)}, u32[]{:S(2)}) copy-start(bf16[128,512]{1,0:T(8,128)(2,1)} %param.21) | copy-start | bytes 393220
  38.9 0.9 copy-start.8
  39.8 4.3 %collective-permute-start.8 = (bf16[128,1536]{1,0:T(8,128)(2,1)}, bf16[128,1536]{1,0:T(8,128)(2,1)S(1)}, u32[]{:S(2)}, u32[]{:S(2)}) collective-permute-start(bf16[128,1536]{1,0:T(8,128)(2,1)} %get-tuple-element.26), channel_id=1, source_target_pairs={{0,1},{1,0},{2,3},{3,2},{4,5},{5,4},{6,7},{7,6},{8,9},{9,8},{10,11... | collective-permute-start | bytes 1179656 | tf_op jit(solution)/shard_map/ppermute | solution.py:34
  39.8 27.6 %collective-permute-start.23 = (bf16[512,512]{1,0:T(8,128)(2,1)S(1)}, bf16[512,512]{1,0:T(8,128)(2,1)}, u32[]{:S(2)}, u32[]{:S(2)}) collective-permute-start(bf16[512,512]{1,0:T(8,128)(2,1)S(1)} %get-tuple-element.34), channel_id=1, source_target_pairs={{0,1},{1,0},{2,3},{3,2},{4,5},{5,4},{6,7},{7,6},{8,9},{9,8},{10,11... | collective-permute-start | bytes 1572872 | tf_op jit(solution)/shard_map/ppermute | solution.py:34
  44.6 1.3 %copy-start.6 = (bf16[1024,512]{1,0:T(8,128)(2,1)S(1)}, bf16[1024,512]{1,0:T(8,128)(2,1)}, u32[]{:S(2)}) copy-start(bf16[1024,512]{1,0:T(8,128)(2,1)} %param.20) | copy-start | bytes 3145732
  45.3 1.5 %copy-start.7 = (f32[128,512]{1,0:T(8,128)S(1)}, f32[128,512]{1,0:T(8,128)}, u32[]{:S(2)}) copy-start(f32[128,512]{1,0:T(8,128)} %get-tuple-element.73) | copy-start | bytes 786436
  45.3 1.5 %copy-start.9 = (bf16[128,1024]{1,0:T(8,128)(2,1)S(1)}, bf16[128,1024]{1,0:T(8,128)(2,1)}, u32[]{:S(2)}) copy-start(bf16[128,1024]{1,0:T(8,128)(2,1)} %copy-done.8) | copy-start | bytes 786436
  48.0 6.7 %collective-permute-start.21 = (bf16[144,512]{1,0:T(8,128)(2,1)S(1)}, bf16[144,512]{1,0:T(8,128)(2,1)S(1)}, u32[]{:S(2)}, u32[]{:S(2)}) collective-permute-start(bf16[144,512]{1,0:T(8,128)(2,1)S(1)} %pad_maximum_fusion.17), channel_id=1, source_target_pairs={{0,2},{1,5},{2,0},{3,7},{4,6},{5,1},{6,4},{7,3},{8,10},{9,13},{10,... | collective-permute-start | bytes 442376 | tf_op jit(solution)/shard_map/ppermute | solution.py:30
  48.7 7.7 %collective-permute-start.9 = (bf16[512,256]{1,0:T(8,128)(2,1)S(1)}, bf16[512,256]{1,0:T(8,128)(2,1)S(1)}, u32[]{:S(2)}, u32[]{:S(2)}) collective-permute-start(bf16[512,256]{1,0:T(8,128)(2,1)S(1)} %get-tuple-element.29), channel_id=1, source_target_pairs={{0,16},{1,9},{2,18},{3,11},{4,20},{5,13},{6,22},{7,15},{8,24},{9,1... | collective-permute-start | bytes 786440 | tf_op jit(solution)/shard_map/ppermute | solution.py:30
  50.3 7.5 %collective-permute-start.15 = (bf16[512,256]{1,0:T(8,128)(2,1)S(1)}, bf16[512,256]{1,0:T(8,128)(2,1)S(1)}, u32[]{:S(2)}, u32[]{:S(2)}) collective-permute-start(bf16[512,256]{1,0:T(8,128)(2,1)S(1)} %get-tuple-element.30), channel_id=1, source_target_pairs={{0,16},{1,9},{2,18},{3,11},{4,20},{5,13},{6,22},{7,15},{8,24},{9,1... | collective-permute-start | bytes 786440 | tf_op jit(solution)/shard_map/ppermute | solution.py:30
  54.8 12.6 %collective-permute-start.22 = (bf16[272,512]{1,0:T(8,128)(2,1)S(1)}, bf16[272,512]{1,0:T(8,128)(2,1)S(1)}, u32[]{:S(2)}, u32[]{:S(2)}) collective-permute-start(bf16[272,512]{1,0:T(8,128)(2,1)S(1)} %pad_maximum_fusion.9), channel_id=1, source_target_pairs={{0,4},{1,3},{2,6},{3,1},{4,0},{5,7},{6,2},{7,5},{8,12},{9,11},{10,... | collective-permute-start | bytes 835592 | tf_op jit(solution)/shard_map/ppermute | solution.py:30
  56.5 5.0 %collective-permute-start.10 = (bf16[256,256]{1,0:T(8,128)(2,1)S(1)}, bf16[256,256]{1,0:T(8,128)(2,1)S(1)}, u32[]{:S(2)}, u32[]{:S(2)}) collective-permute-start(bf16[256,256]{1,0:T(8,128)(2,1)S(1)} %fusion.12), channel_id=1, source_target_pairs={{0,8},{1,17},{2,10},{3,19},{4,12},{5,21},{6,14},{7,23},{8,0},{9,25... | collective-permute-start | bytes 393224 | tf_op jit(solution)/shard_map/ppermute | solution.py:30
  57.9 6.1 %collective-permute-start.16 = (bf16[256,256]{1,0:T(8,128)(2,1)S(1)}, bf16[256,256]{1,0:T(8,128)(2,1)S(1)}, u32[]{:S(2)}, u32[]{:S(2)}) collective-permute-start(bf16[256,256]{1,0:T(8,128)(2,1)S(1)} %fusion.9), channel_id=1, source_target_pairs={{0,8},{1,17},{2,10},{3,19},{4,12},{5,21},{6,14},{7,23},{8,0},{9,25... | collective-permute-start | bytes 393224 | tf_op jit(solution)/shard_map/ppermute | solution.py:30
  61.5 7.5 %collective-permute-start.11 = (bf16[256,256]{1,0:T(8,128)(2,1)S(1)}, bf16[256,256]{1,0:T(8,128)(2,1)S(1)}, u32[]{:S(2)}, u32[]{:S(2)}) collective-permute-start(bf16[256,256]{1,0:T(8,128)(2,1)S(1)} %fusion.14), channel_id=1, source_target_pairs={{0,2},{1,5},{2,0},{3,7},{4,6},{5,1},{6,4},{7,3},{8,10},{9,13},{10,... | collective-permute-start | bytes 393224 | tf_op jit(solution)/shard_map/ppermute | solution.py:30
  64.1 7.7 %collective-permute-start.17 = (bf16[256,256]{1,0:T(8,128)(2,1)S(1)}, bf16[256,256]{1,0:T(8,128)(2,1)S(1)}, u32[]{:S(2)}, u32[]{:S(2)}) collective-permute-start(bf16[256,256]{1,0:T(8,128)(2,1)S(1)} %fusion.11), channel_id=1, source_target_pairs={{0,2},{1,5},{2,0},{3,7},{4,6},{5,1},{6,4},{7,3},{8,10},{9,13},{10,... | collective-permute-start | bytes 393224 | tf_op jit(solution)/shard_map/ppermute | solution.py:30
  69.0 11.1 %collective-permute-start.24 = (bf16[512,512]{1,0:T(8,128)(2,1)S(1)}, bf16[512,512]{1,0:T(8,128)(2,1)S(1)}, u32[]{:S(2)}, u32[]{:S(2)}) collective-permute-start(bf16[512,512]{1,0:T(8,128)(2,1)S(1)} %fusion), channel_id=1, source_target_pairs={{0,1},{1,0},{2,3},{3,2},{4,5},{5,4},{6,7},{7,6},{8,9},{9,8},{10,11... | collective-permute-start | bytes 1572872 | tf_op jit(solution)/shard_map/ppermute | solution.py:34
  69.1 6.0 %collective-permute-start.12 = (bf16[256,256]{1,0:T(8,128)(2,1)S(1)}, bf16[256,256]{1,0:T(8,128)(2,1)S(1)}, u32[]{:S(2)}, u32[]{:S(2)}) collective-permute-start(bf16[256,256]{1,0:T(8,128)(2,1)S(1)} %reduce-precision_convert_fusion.3), channel_id=1, source_target_pairs={{0,4},{1,3},{2,6},{3,1},{4,0},{5,7},{6,2},{7,5},{8,12},{9,11},{10,... | collective-permute-start | bytes 393224 | tf_op jit(solution)/shard_map/ppermute | solution.py:30
  71.8 10.3 %collective-permute-start.18 = (bf16[256,256]{1,0:T(8,128)(2,1)S(1)}, bf16[256,256]{1,0:T(8,128)(2,1)S(1)}, u32[]{:S(2)}, u32[]{:S(2)}) collective-permute-start(bf16[256,256]{1,0:T(8,128)(2,1)S(1)} %reduce-precision_convert_fusion.1), channel_id=1, source_target_pairs={{0,4},{1,3},{2,6},{3,1},{4,0},{5,7},{6,2},{7,5},{8,12},{9,11},{10,... | collective-permute-start | bytes 393224 | tf_op jit(solution)/shard_map/ppermute | solution.py:30
  75.2 9.1 %collective-permute-start.13 = (bf16[256,256]{1,0:T(8,128)(2,1)S(1)}, bf16[256,256]{1,0:T(8,128)(2,1)S(1)}, u32[]{:S(2)}, u32[]{:S(2)}) collective-permute-start(bf16[256,256]{1,0:T(8,128)(2,1)S(1)} %reduce-precision_convert_fusion.2), channel_id=1, source_target_pairs={{0,8},{1,17},{2,10},{3,19},{4,12},{5,21},{6,14},{7,23},{8,0},{9,25... | collective-permute-start | bytes 393224 | tf_op jit(solution)/shard_map/ppermute | solution.py:30
  80.5 6.6 %collective-permute-start.25 = (bf16[272,512]{1,0:T(8,128)(2,1)S(1)}, bf16[272,512]{1,0:T(8,128)(2,1)S(1)}, u32[]{:S(2)}, u32[]{:S(2)}) collective-permute-start(bf16[272,512]{1,0:T(8,128)(2,1)S(1)} %pad_maximum_fusion.10), channel_id=1, source_target_pairs={{0,16},{1,9},{2,18},{3,11},{4,20},{5,13},{6,22},{7,15},{8,24},{9,1... | collective-permute-start | bytes 835592 | tf_op jit(solution)/shard_map/ppermute | solution.py:30
  82.2 6.0 %collective-permute-start.19 = (bf16[256,256]{1,0:T(8,128)(2,1)S(1)}, bf16[256,256]{1,0:T(8,128)(2,1)S(1)}, u32[]{:S(2)}, u32[]{:S(2)}) collective-permute-start(bf16[256,256]{1,0:T(8,128)(2,1)S(1)} %reduce-precision_convert_fusion), channel_id=1, source_target_pairs={{0,8},{1,17},{2,10},{3,19},{4,12},{5,21},{6,14},{7,23},{8,0},{9,25... | collective-permute-start | bytes 393224 | tf_op jit(solution)/shard_map/ppermute | solution.py:30
  84.3 14.0 %collective-permute-start.29 = (bf16[512,256]{1,0:T(8,128)(2,1)S(1)}, bf16[512,256]{1,0:T(8,128)(2,1)S(1)}, u32[]{:S(2)}, u32[]{:S(2)}) collective-permute-start(bf16[512,256]{1,0:T(8,128)(2,1)S(1)} %pad_maximum_fusion.13), channel_id=1, source_target_pairs={{0,1},{1,0},{2,3},{3,2},{4,5},{5,4},{6,7},{7,6},{8,9},{9,8},{10,11... | collective-permute-start | bytes 786440 | tf_op jit(solution)/shard_map/ppermute | solution.py:34
  84.3 10.8 %collective-permute-start.14 = (bf16[512,256]{1,0:T(8,128)(2,1)S(1)}, bf16[512,256]{1,0:T(8,128)(2,1)S(1)}, u32[]{:S(2)}, u32[]{:S(2)}) collective-permute-start(bf16[512,256]{1,0:T(8,128)(2,1)S(1)} %pad_maximum_fusion.13), channel_id=1, source_target_pairs={{0,16},{1,9},{2,18},{3,11},{4,20},{5,13},{6,22},{7,15},{8,24},{9,1... | collective-permute-start | bytes 786440 | tf_op jit(solution)/shard_map/ppermute | solution.py:30
  87.3 6.5 %collective-permute-start.26 = (bf16[144,512]{1,0:T(8,128)(2,1)S(1)}, bf16[144,512]{1,0:T(8,128)(2,1)S(1)}, u32[]{:S(2)}, u32[]{:S(2)}) collective-permute-start(bf16[144,512]{1,0:T(8,128)(2,1)S(1)} %pad_maximum_fusion.18), channel_id=1, source_target_pairs={{0,8},{1,17},{2,10},{3,19},{4,12},{5,21},{6,14},{7,23},{8,0},{9,25... | collective-permute-start | bytes 442376 | tf_op jit(solution)/shard_map/ppermute | solution.py:30
  88.2 10.9 %collective-permute-start.27 = (bf16[512,256]{1,0:T(8,128)(2,1)S(1)}, bf16[512,256]{1,0:T(8,128)(2,1)S(1)}, u32[]{:S(2)}, u32[]{:S(2)}) collective-permute-start(bf16[512,256]{1,0:T(8,128)(2,1)S(1)} %pad_maximum_fusion.14), channel_id=1, source_target_pairs={{0,1},{1,0},{2,3},{3,2},{4,5},{5,4},{6,7},{7,6},{8,9},{9,8},{10,11... | collective-permute-start | bytes 786440 | tf_op jit(solution)/shard_map/ppermute | solution.py:34
  88.3 6.9 %collective-permute-start.20 = (bf16[512,256]{1,0:T(8,128)(2,1)S(1)}, bf16[512,256]{1,0:T(8,128)(2,1)S(1)}, u32[]{:S(2)}, u32[]{:S(2)}) collective-permute-start(bf16[512,256]{1,0:T(8,128)(2,1)S(1)} %pad_maximum_fusion.14), channel_id=1, source_target_pairs={{0,16},{1,9},{2,18},{3,11},{4,20},{5,13},{6,22},{7,15},{8,24},{9,1... | collective-permute-start | bytes 786440 | tf_op jit(solution)/shard_map/ppermute | solution.py:30
  95.2 2.4 %collective-permute-start.31 = (bf16[16,512]{1,0:T(8,128)(2,1)S(1)}, bf16[16,512]{1,0:T(8,128)(2,1)S(1)}, u32[]{:S(2)}, u32[]{:S(2)}) collective-permute-start(bf16[16,512]{1,0:T(8,128)(2,1)S(1)} %get-tuple-element.61), channel_id=1, source_target_pairs={{0,1},{1,0},{2,3},{3,2},{4,5},{5,4},{6,7},{7,6},{8,9},{9,8},{10,11... | collective-permute-start | bytes 49160 | tf_op jit(solution)/shard_map/ppermute | solution.py:34
  95.4 2.8 %collective-permute-start.30 = (bf16[512,256]{1,0:T(8,128)(2,1)S(1)}, bf16[512,256]{1,0:T(8,128)(2,1)S(1)}, u32[]{:S(2)}, u32[]{:S(2)}) collective-permute-start(bf16[512,256]{1,0:T(8,128)(2,1)S(1)} %collective-permute-done.14), channel_id=1, source_target_pairs={{0,1},{1,0},{2,3},{3,2},{4,5},{5,4},{6,7},{7,6},{8,9},{9,8},{10,11... | collective-permute-start | bytes 786440 | tf_op jit(solution)/shard_map/ppermute | solution.py:34
  95.8 3.3 %collective-permute-start.28 = (bf16[512,256]{1,0:T(8,128)(2,1)S(1)}, bf16[512,256]{1,0:T(8,128)(2,1)S(1)}, u32[]{:S(2)}, u32[]{:S(2)}) collective-permute-start(bf16[512,256]{1,0:T(8,128)(2,1)S(1)} %collective-permute-done.20), channel_id=1, source_target_pairs={{0,1},{1,0},{2,3},{3,2},{4,5},{5,4},{6,7},{7,6},{8,9},{9,8},{10,11... | collective-permute-start | bytes 786440 | tf_op jit(solution)/shard_map/ppermute | solution.py:34

commit v2 on v1

v2 whole, which is shorter than its diff:
```python
import jax
import jax.numpy as jnp
import numpy as np
from jax import lax
from jax.experimental import pallas as pl
from jax.experimental.pallas import tpu as pltpu
from jax.sharding import PartitionSpec as P

F = 512
TYPES = 8
TILE = 128
BF = jnp.bfloat16
FP = jnp.float32
AXES = ("row", "col")


def reversed_bits(value, bits):
    out = 0
    for b in range(bits):
        out |= ((value >> b) & 1) << (bits - 1 - b)
    return out


def exchange(x, rows, cols, row_masks, z_masks):
    pairs = []
    for r in range(rows):
        for c in range(cols):
            core = c & 1
            pairs.append((r * cols + c, (r ^ row_masks[core]) * cols + (c ^ (2 * z_masks[core]))))
    return lax.ppermute(x, AXES, pairs)


def swap_cores(x, rows, cols):
    return lax.ppermute(x, AXES, [(i, i ^ 1) for i in range(rows * cols)])


def rounded(x):
    return lax.reduce_precision(x, 8, 7).astype(BF)


def split(x):
    high = lax.reduce_precision(x, 8, 7)
    return jnp.concatenate([high.astype(BF), rounded(x - high)], axis=0)


def joined(x):
    x = x.astype(FP)
    return x[:TYPES] + x[TYPES:]


def build(tile_vals, tile_row, tile_col, tile_count, n_row, n_col):
    slots = tile_vals.shape[1]
    n_z = n_col // 2
    wide, half = n_row * TILE, n_z * TILE
    chunk = 16
    rounds = slots // chunk

    def kernel(count_ref, row_ref, col_ref, vals_ref, near_ref, far_ref, total, held, sems):
        copies = []
        for i in range(rounds):
            at = pl.ds(i * chunk, chunk)
            copies.append(pltpu.make_async_copy(vals_ref.at[0, at], held.at[at], sems.at[i]))
            copies[i].start()
        row, col = lax.axis_index("row"), lax.axis_index("col")
        core, z = col & 1, col >> 1
        total[...] = jnp.zeros_like(total)
        count = count_ref[0, 0]

        def add(s, carry):
            r, c = row_ref[0, s], col_ref[0, s]
            total[r, c] = total[r, c] + held[s].astype(FP)
            return carry

        for i in range(rounds):
            copies[i].wait()
            lax.fori_loop(i * chunk, jnp.clip(count, i * chunk, (i + 1) * chunk), add, 0)

        for side, out in enumerate((near_ref, far_ref)):
            whose = core ^ side

            def emit(p, carry, out=out, whose=whose):
                r = 2 * (z ^ jnp.where(whose == 0, p, reversed_bits(p, n_z.bit_length() - 1))) + whose
                at = pl.ds(pl.multiple_of(p * TILE, TILE), TILE)
                for q in range(n_row):
                    value = total[r, row ^ jnp.where(core == 0, q, reversed_bits(q, n_row.bit_length() - 1))]
                    high = value.astype(BF)
                    out[at, q * TILE : (q + 1) * TILE] = high
                    out[at, wide + q * TILE : wide + (q + 1) * TILE] = (value - high.astype(FP)).astype(BF)
                return carry

            lax.fori_loop(0, n_z, emit, 0)

    dense = n_row * n_col * TILE * TILE
    result = jax.ShapeDtypeStruct((half, 2 * wide), BF)
    smem = pl.BlockSpec(memory_space=pltpu.SMEM)
    return pl.pallas_call(
        kernel,
        out_shape=(result, result),
        in_specs=[smem, smem, smem, pl.BlockSpec(memory_space=pltpu.HBM)],
        scratch_shapes=[
            pltpu.VMEM((n_col, n_row, TILE, TILE), FP),
            pltpu.VMEM((slots, TILE, TILE), BF),
            pltpu.SemaphoreType.DMA((rounds,)),
        ],
        compiler_params=pltpu.CompilerParams(vmem_limit_bytes=dense * 9 + 8 * 1024 * 1024),
        cost_estimate=pl.CostEstimate(
            flops=slots * TILE * TILE, bytes_accessed=slots * TILE * TILE * 2 + dense * 4, transcendentals=0
        ),
        name="build_dense",
    )(tile_count, tile_row, tile_col, tile_vals)


def write_weights(near, far, held, first_place, n_row, factor):
    parts = len(near)
    rows, lanes = near[0].shape
    span = 2 * F // n_row
    places = rows // span
    per = F // span

    def kernel(*refs):
        mine, there = refs[:parts], refs[parts : 2 * parts]
        in_ref, out_ref, wide_in, wide_out, sems = refs[-5:]
        core, row = lax.axis_index("col") & 1, lax.axis_index("row")

        def put(sources, ref, at):
            for i, x in enumerate(sources):
                ref[at, i * lanes : (i + 1) * lanes] = x[at, :].astype(FP) * factor

        copies = []
        for j in range(places):
            q = first_place + j
            at = pl.ds(j * span, span)

            @pl.when(core == 0)
            def _(at=at):
                put(mine, wide_in, at)
                put(there, wide_out, at)

            @pl.when(core != 0)
            def _(at=at):
                put(there, wide_in, at)
                put(mine, wide_out, at)

            g = row ^ q
            to = in_ref.at[
                pl.ds(pl.multiple_of((g % per) * span, span), span), pl.ds(pl.multiple_of((g // per) * F, F), F)
            ]
            copies.append(pltpu.make_async_copy(wide_in.at[at], to, sems.at[2 * j]))
            copies[-1].start()
            g = row ^ reversed_bits(q, n_row.bit_length() - 1)
            to = out_ref.at[pl.ds(pl.multiple_of(g * span, span), span)]
            copies.append(pltpu.make_async_copy(wide_out.at[at], to, sems.at[2 * j + 1]))
            copies[-1].start()
        for copy in copies:
            copy.wait()

    vmem, hbm = pl.BlockSpec(memory_space=pltpu.VMEM), pl.BlockSpec(memory_space=pltpu.HBM)
    return pl.pallas_call(
        kernel,
        out_shape=(jax.ShapeDtypeStruct((F, 2 * F), FP), jax.ShapeDtypeStruct((2 * F, F), FP)),
        in_specs=[vmem] * (2 * parts) + [hbm] * len(held),
        out_specs=(hbm, hbm),
        input_output_aliases={2 * parts + i: i for i in range(len(held))},
        scratch_shapes=[
            pltpu.VMEM((rows, F), FP),
            pltpu.VMEM((rows, F), FP),
            pltpu.SemaphoreType.DMA((2 * places,)),
        ],
        compiler_params=pltpu.CompilerParams(vmem_limit_bytes=16 * 1024 * 1024),
        cost_estimate=pl.CostEstimate(flops=4 * rows * F, bytes_accessed=12 * rows * F, transcendentals=0),
        name="write_weights",
    )(*near, *far, *held)


def tie(*arrays):
    return lax.optimization_barrier(arrays)


def shards(
    features,
    tile_vals,
    tile_row,
    tile_col,
    tile_count,
    node_type,
    type_gain,
    w_in,
    w_out,
    cotangent,
):
    n_row, n_col = lax.axis_size("row"), lax.axis_size("col")
    n_z = n_col // 2
    row_bits, z_bits = n_row.bit_length() - 1, n_z.bit_length() - 1
    total_nodes = TILE * n_row * n_col
    row, col = lax.axis_index("row"), lax.axis_index("col")
    core, z = col & 1, col >> 1

    def row_step(x, step):
        return exchange(x, n_row, n_col, (1 << step, 1 << (row_bits - 1 - step)), (0, 0))

    def z_step(x, step):
        return exchange(x, n_row, n_col, (0, 0), (1 << step, 1 << (z_bits - 1 - step)))

    def dot(a, b, dims):
        return lax.dot_general(a, b, (dims, ((), ())), preferred_element_type=FP)

    def place(q):
        return row ^ jnp.where(core == 0, q, reversed_bits(q, row_bits))

    here, there = [features], []
    for step in range(row_bits):
        came = row_step(here[0] if step == 0 else jnp.concatenate(here, axis=0), step)
        if step == 0:
            came, tile_count = tie(came, tile_count)
        there.append(swap_cores(here[-1], n_row, n_col))
        here.append(came)
    there.append(swap_cores(here[-1], n_row, n_col))
    near, far = build(tile_vals, tile_row, tile_col, tile_count, n_row, n_col)
    far = swap_cores(far, n_row, n_col)

    total = dot(near, jnp.concatenate(here + here, axis=0), ((1,), (0,)))
    total, there[-1] = tie(total, there[-1])
    total = total + dot(far, jnp.concatenate(there + there, axis=0), ((1,), (0,)))
    for step in reversed(range(z_bits)):
        mid = total.shape[0] // 2
        came = z_step(rounded(total[mid:]), step)
        total = total[:mid] + came.astype(FP)
    aggregate = total

    center = jnp.mean(aggregate, axis=-1, keepdims=True)
    spread = jnp.mean(jnp.square(aggregate - center), axis=-1, keepdims=True)
    inverse = lax.rsqrt(spread + 1e-05)
    normed = (aggregate - center) * inverse
    onehot = (node_type[:, None] == jnp.arange(TYPES, dtype=jnp.int32)[None, :]).astype(FP)
    gains = jnp.dot(onehot, type_gain, precision=lax.Precision.HIGHEST)
    scaled = (normed * gains).astype(BF)
    hidden = jnp.dot(scaled, w_in, preferred_element_type=FP)
    grad_act = dot(cotangent, w_out, ((1,), (1,)))
    sigmoid_h = jax.nn.sigmoid(hidden)
    activated = (hidden * sigmoid_h).astype(BF)
    grad_hidden = (grad_act * sigmoid_h * (1.0 + hidden * (1.0 - sigmoid_h))).astype(BF)

    for_in = jnp.concatenate([scaled, grad_hidden], axis=1)
    for_out = jnp.concatenate([cotangent, activated], axis=1)
    mine = jnp.where(core == 0, for_in, for_out)
    away = jnp.where(core == 0, for_out, for_in)
    mine, grad_hidden = tie(mine, grad_hidden)
    met = swap_cores(away, n_row, n_col)

    grad_scaled = dot(grad_hidden, w_in, ((1,), (1,)))
    grad_gain = lax.dot_general(
        onehot, grad_scaled * normed, (((0,), (0,)), ((), ())), precision=lax.Precision.HIGHEST
    )
    grad_normed = grad_scaled * gains
    grad_agg = cotangent.astype(FP) + inverse * (
        grad_normed
        - jnp.mean(grad_normed, axis=-1, keepdims=True)
        - normed * jnp.mean(grad_normed * normed, axis=-1, keepdims=True)
    )
    grad_rows = grad_agg.astype(BF)
    gain = split(grad_gain)
    met, grad_rows, gain = tie(met, grad_rows, gain)
    pairs = jnp.concatenate([mine, met], axis=0)
    single, double = pairs[:, :F], pairs[:, F:]
    twice = jnp.concatenate([single, single], axis=1)
    left = jnp.where(core == 0, twice, double)
    right = jnp.where(core == 0, double, twice)
    wide = left.shape[1]
    span = wide // n_row
    parts = 2
    lanes = F // parts

    def weight_blocks(places, part):
        out = []
        for q in places:
            start = place(q) * span
            a = lax.dynamic_slice_in_dim(left, start, span, 1)
            b = lax.dynamic_slice_in_dim(right, (start // F) * F + part * lanes, lanes, 1)
            out.append(dot(a, b, ((0,), (0,))))
        return jnp.concatenate(out, axis=0)

    sums, outs = [None] * parts, [None] * parts
    for i in range(parts):
        outs[i] = rounded(weight_blocks(range(n_row // 2, n_row), i))
    *outs, activated = tie(*outs, activated)
    for i in range(parts):
        sums[i] = weight_blocks(range(n_row // 2), i)
    branch = jnp.dot(activated, w_out, preferred_element_type=FP)
    mixed = (aggregate + branch).astype(BF)

    for step in range(z_bits):
        came = z_step(jnp.concatenate([grad_rows, gain], axis=0), step)
        size = grad_rows.shape[0]
        grad_rows = jnp.concatenate([grad_rows, came[:size]], axis=0)
        gain = split(joined(gain) + joined(came[size:]))
    own = n_row * TILE
    came = swap_cores(rounded(dot(far[:, :own], grad_rows, ((0,), (0,)))), n_row, n_col)
    low = dot(near[:, :own], grad_rows, ((0,), (0,))) + came.astype(FP)
    for step in reversed(range(row_bits)):
        size = low.shape[0] // 2
        came = row_step(jnp.concatenate([rounded(low[size:]), gain], axis=0), step)
        gain = split(joined(gain) + joined(came[size:]))
        low = low[:size] + came[:size].astype(FP)
    grad_x = low
    factor = float(total_nodes) ** (-0.5)
    grad_gain = (joined(gain) + joined(swap_cores(gain, n_row, n_col))) * factor

    for step in reversed(range(row_bits)):
        for i in range(parts):
            mid = sums[i].shape[0] // 2
            sums[i] = sums[i] + row_step(outs[i], step).astype(FP)
            if step:
                sums[i], outs[i] = sums[i][:mid], rounded(sums[i][mid:])
    for step in range(z_bits):
        for i in range(parts):
            held = rounded(sums[i])
            sums[i] = held.astype(FP) + z_step(held, step).astype(FP)
    owns = [rounded(x) for x in sums]
    for step in range(row_bits - 1):
        for i in range(parts):
            owns[i] = jnp.concatenate([owns[i], row_step(owns[i], step)], axis=0)
    came = [row_step(x, row_bits - 1) for x in owns]
    others = [swap_cores(x, n_row, n_col) for x in owns]
    weights = write_weights(owns, others, [], 0, n_row, factor)
    *came, mixed, grad_x = tie(*came, mixed, grad_x)
    others = [swap_cores(x, n_row, n_col) for x in came]
    grad_w_in, grad_w_out = write_weights(came, others, weights, n_row // 2, n_row, factor)
    return mixed, grad_x, grad_w_in, grad_w_out, grad_gain


def solution(mesh):
    return jax.shard_map(
        shards,
        mesh=mesh,
        in_specs=(
            P(("col", "row"), None),
            P("row", "col", None, None),
            P("row", "col"),
            P("row", "col"),
            P("row", "col"),
            P(("row", "col")),
            P(),
            P(),
            P(),
            P(("row", "col"), None),
        ),
        out_specs=(P(("row", "col"), None), P(("col", "row"), None), P(), P(), P()),
        check_vma=False,
    )
```

time: 105 us -> 91.6 us (0.87)
  other arithmetic: 8.98 us -> 3.27 us
  waiting for transfers between devices: 36.4 us -> 32.9 us
  between operations: 4.63 us -> 2.01 us
  Pallas kernels: 6.97 us -> 4.55 us
  starting transfers between devices: 34.7 us -> 36.9 us
  matrix products: 8.89 us -> 7.21 us
    concatenate x7 -> x3, other arithmetic: 3.49 us -> 0.04 us  [the longest x2 0.04 us: shards(): owns[i] = jnp.concatenate([owns[i], row_step(owns[i], step)], axis=0)]
    ppermute x20, waiting for transfers between devices: 33.6 us -> 30.6 us  [exchange(): return lax.ppermute(x, AXES, pairs)]
    ppermute x20, starting transfers between devices: 32.8 us -> 35.3 us  [exchange(): return lax.ppermute(x, AXES, pairs)]
    pallas_call x1 -> x2, Pallas kernels: 4.98 us -> 2.86 us  [write_weights(): pl.pallas_call(kernel, out_shape=(jax.ShapeDtypeStruct((F, 2 * F), FP), j...]
    xor x2 -> x0, other arithmetic: 1.7 us -> none  [the longest x1 1.16 us: shards(): row ^ jnp.array([reversed_bits(q, row_bits) for q in range(n_row)], jnp.i...]
    ppermute x12 -> x11, waiting for transfers between devices: 2.78 us -> 2.32 us  [swap_cores(): return lax.ppermute(x, AXES, [(i, i ^ 1) for i in range(rows * cols)])]
    unnamed x36 -> x33, local copies, waits for them, and re-layouts: 3.68 us -> 4.01 us
  transfers between devices with their start and end apart: 32 -> 31, of which waited for: 15 -> 17; matrix products, arithmetic and copies ran while one was open for 13% -> 8% of each run, Pallas kernels for 2% -> 3%
where the time goes in v2:
time: 91.6 us; the launch traced here: 91 us
  starting transfers between devices  36.9 us (40%)
  waiting for transfers between devices  32.9 us (36%)
  matrix products  7.21 us (8%)
  Pallas kernels  4.55 us (5%)
  local copies, waits for them, and re-layouts  4.12 us (4%)
  other arithmetic  3.27 us (4%)
  between operations  2.01 us (2%)
    ppermute x20, starting transfers between devices, exchange(): return lax.ppermute(x, AXES, pairs)  35.3 us
    ppermute x20, waiting for transfers between devices, exchange(): return lax.ppermute(x, AXES, pairs)  30.6 us
    dot_general x14, matrix products, dot(): return lax.dot_general(a, b, (dims, ((), ())), preferred_element_type=FP)  5.24 us
    unnamed x33, local copies, waits for them, and re-layouts  4.01 us
    pallas_call x2, Pallas kernels, write_weights(): pl.pallas_call(kernel, out_shape=(jax.ShapeDtypeStruct((F, 2 * F), FP), j...  2.86 us
    ppermute x11, waiting for transfers between devices, swap_cores(): return lax.ppermute(x, AXES, [(i, i ^ 1) for i in range(rows * cols)])  2.32 us
  transfers between devices with their start and end apart: 31, of which 17 were waited for; matrix products, arithmetic and copies ran while one was open for 8% of the time, Pallas kernels for 3%

profile of v2, /device:TPU:0, one launch (start us, length us, event | category | flops | bytes accessed | tf_op | source)
XLA Modules:
  0.0 91.0 jit_solution(7145506502179629633)
XLA Ops:
  0.6 3.0 %collective-permute-start = (bf16[128,512]{1,0:T(8,128)(2,1)}, bf16[128,512]{1,0:T(8,128)(2,1)S(1)}, u32[]{:S(2)}, u32[]{:S(2)}) collective-permute-start(bf16[128,512]{1,0:T(8,128)(2,1)} %param.10), channel_id=1, source_target_pairs={{0,8},{1,17},{2,10},{3,19},{4,12},{5,21},{6,14},{7,23},{8,0},{9,25... | collective-permute-start | bytes 393224 | tf_op jit(solution)/shard_map/ppermute | solution.py:30
  4.3 2.2 %copy-done.1 = bf16[1,128,128,128]{3,2,1,0:T(8,128)(2,1)S(1)} copy-done((bf16[1,128,128,128]{3,2,1,0:T(8,128)(2,1)S(1)}, bf16[1,128,128,128]{3,2,1,0:T(8,128)(2,1)}, u32[]{:S(2)}) %copy-start.1) | copy-done | bytes 4194328
  6.5 0.7 copy-done.2
  7.2 0.7 copy-done.3
  7.8 1.7 %build_dense.1 = (bf16[512,1024]{1,0:T(8,128)(2,1)S(1)}, bf16[512,1024]{1,0:T(8,128)(2,1)S(1)}) custom-call(s32[1,1]{1,0:T(1,128)S(6)} %copy.32.count_ref, s32[1,128]{1,0:T(1,128)S(1)} %copy-done.2, s32[1,128]{1,0:T(1,128)S(1)} %copy-done.3, bf16[1,128,128,128]{3,2,1,0:T(8,128)(2,1)S(1)} %copy-done.1), custom_call_target="tpu_custom_call" | custom-call | flops 2097152 | bytes 6291456 | tf_op jit(solution)/shard_map/build_dense/pallas_call | solution.py:96
  9.5 0.6 collective-permute-start.3
  10.3 2.4 %collective-permute-start.1 = (bf16[256,512]{1,0:T(8,128)(2,1)S(1)}, bf16[256,512]{1,0:T(8,128)(2,1)S(1)}, u32[]{:S(2)}, u32[]{:S(2)}) collective-permute-start(bf16[256,512]{1,0:T(8,128)(2,1)S(1)} %pad_maximum_fusion.6), channel_id=1, source_target_pairs={{0,16},{1,9},{2,18},{3,11},{4,20},{5,13},{6,22},{7,15},{8,24},{9,1... | collective-permute-start | bytes 786440 | tf_op jit(solution)/shard_map/ppermute | solution.py:30
  12.8 4.3 %collective-permute-done.1 = bf16[256,512]{1,0:T(8,128)(2,1)S(1)} collective-permute-done((bf16[256,512]{1,0:T(8,128)(2,1)S(1)}, bf16[256,512]{1,0:T(8,128)(2,1)S(1)}, u32[]{:S(2)}, u32[]{:S(2)}) %collective-permute-start.1) | collective-permute-done | bytes 262176 | tf_op jit(solution)/shard_map/ppermute | solution.py:30
  17.2 0.7 fusion.82
  17.9 0.8 collective-permute-done.2
  18.8 0.7 fusion.83
  19.8 3.1 %collective-permute-start.6 = (bf16[256,512]{1,0:T(8,128)(2,1)S(1)}, bf16[256,512]{1,0:T(8,128)(2,1)S(1)}, u32[]{:S(2)}, u32[]{:S(2)}) collective-permute-start(bf16[256,512]{1,0:T(8,128)(2,1)S(1)} %fusion.6), channel_id=1, source_target_pairs={{0,4},{1,3},{2,6},{3,1},{4,0},{5,7},{6,2},{7,5},{8,12},{9,11},{10,... | collective-permute-start | bytes 786440 | tf_op jit(solution)/shard_map/ppermute | solution.py:30
  22.8 5.5 %collective-permute-done.6 = bf16[256,512]{1,0:T(8,128)(2,1)S(1)} collective-permute-done((bf16[256,512]{1,0:T(8,128)(2,1)S(1)}, bf16[256,512]{1,0:T(8,128)(2,1)S(1)}, u32[]{:S(2)}, u32[]{:S(2)}) %collective-permute-start.6) | collective-permute-done | bytes 262176 | tf_op jit(solution)/shard_map/ppermute | solution.py:30
  28.4 2.9 %collective-permute-start.7 = (bf16[128,512]{1,0:T(8,128)(2,1)S(1)}, bf16[128,512]{1,0:T(8,128)(2,1)S(1)}, u32[]{:S(2)}, u32[]{:S(2)}) collective-permute-start(bf16[128,512]{1,0:T(8,128)(2,1)S(1)} %fusion.17), channel_id=1, source_target_pairs={{0,2},{1,5},{2,0},{3,7},{4,6},{5,1},{6,4},{7,3},{8,10},{9,13},{10,... | collective-permute-start | bytes 393224 | tf_op jit(solution)/shard_map/ppermute | solution.py:30
  31.4 4.3 %collective-permute-done.7 = bf16[128,512]{1,0:T(8,128)(2,1)S(1)} collective-permute-done((bf16[128,512]{1,0:T(8,128)(2,1)S(1)}, bf16[128,512]{1,0:T(8,128)(2,1)S(1)}, u32[]{:S(2)}, u32[]{:S(2)}) %collective-permute-start.7) | collective-permute-done | bytes 131104 | tf_op jit(solution)/shard_map/ppermute | solution.py:30
  36.0 0.3 multiply_convert_fusion.1
  36.4 0.4 multiply_convert_fusion
  36.7 0.3 copy-done.5
  37.0 0.5 fusion.2
  37.7 0.6 fusion.76
  38.2 0.3 reduce-precision_convert_fusion.8
  38.9 1.5 %collective-permute-done.8 = bf16[128,1536]{1,0:T(8,128)(2,1)S(1)} collective-permute-done((bf16[128,1536]{1,0:T(8,128)(2,1)S(1)}, bf16[128,1536]{1,0:T(8,128)(2,1)S(1)}, u32[]{:S(2)}, u32[]{:S(2)}) %collective-permute-start.8) | collective-permute-done | bytes 393248 | tf_op jit(solution)/shard_map/ppermute | solution.py:34
  40.4 0.7 collective-permute-start.21
  41.2 0.2 broadcast_select_fusion.1
  41.4 0.2 fusion.22
  41.7 0.2 fusion.34
  41.9 0.2 fusion.26
  42.1 0.2 fusion.30
  42.4 0.2 fusion.24
  42.6 0.2 fusion.28
  42.9 1.0 %fusion.3 = bf16[128,512]{1,0:T(8,128)(2,1)} fusion(f32[128,512]{1,0:T(8,128)S(1)} %get-tuple-element.61, bf16[128,1024]{1,0:T(8,128)(2,1)S(1)} %get-tuple-element.38, bf16[1024,512]{1,0:T(8,128)(2,1)S(1)} %copy-done.5), kind=kOutput, calls=%fused_computation.7 | convolution fusion | flops 134348800 | bytes 1703936 | tf_op jit(solution)/shard_map/dot_general | solution.py:288
  43.9 2.0 %collective-permute-start.9 = (bf16[512,256]{1,0:T(8,128)(2,1)S(1)}, bf16[512,256]{1,0:T(8,128)(2,1)S(1)}, u32[]{:S(2)}, u32[]{:S(2)}) collective-permute-start(bf16[512,256]{1,0:T(8,128)(2,1)S(1)} %fusion.7), channel_id=1, source_target_pairs={{0,16},{1,9},{2,18},{3,11},{4,20},{5,13},{6,22},{7,15},{8,24},{9,1... | collective-permute-start | bytes 786440 | tf_op jit(solution)/shard_map/ppermute | solution.py:30
  46.2 0.2 fusion.32
  46.4 0.7 collective-permute-done.21
  47.3 2.4 %collective-permute-start.22 = (bf16[272,512]{1,0:T(8,128)(2,1)S(1)}, bf16[272,512]{1,0:T(8,128)(2,1)S(1)}, u32[]{:S(2)}, u32[]{:S(2)}) collective-permute-start(bf16[272,512]{1,0:T(8,128)(2,1)S(1)} %pad_maximum_fusion.4), channel_id=1, source_target_pairs={{0,4},{1,3},{2,6},{3,1},{4,0},{5,7},{6,2},{7,5},{8,12},{9,11},{10,... | collective-permute-start | bytes 835592 | tf_op jit(solution)/shard_map/ppermute | solution.py:30
  49.7 0.6 collective-permute-done.9
  50.4 0.5 collective-permute-start.10
  50.9 2.2 %collective-permute-done.15 = bf16[512,256]{1,0:T(8,128)(2,1)S(1)} collective-permute-done((bf16[512,256]{1,0:T(8,128)(2,1)S(1)}, bf16[512,256]{1,0:T(8,128)(2,1)S(1)}, u32[]{:S(2)}, u32[]{:S(2)}) %collective-permute-start.15) | collective-permute-done | bytes 262176 | tf_op jit(solution)/shard_map/ppermute | solution.py:30
  53.2 0.5 collective-permute-start.16
  53.7 1.7 %collective-permute-done.10 = bf16[256,256]{1,0:T(8,128)(2,1)S(1)} collective-permute-done((bf16[256,256]{1,0:T(8,128)(2,1)S(1)}, bf16[256,256]{1,0:T(8,128)(2,1)S(1)}, u32[]{:S(2)}, u32[]{:S(2)}) %collective-permute-start.10) | collective-permute-done | bytes 131104 | tf_op jit(solution)/shard_map/ppermute | solution.py:30
  55.4 1.4 %collective-permute-start.11 = (bf16[256,256]{1,0:T(8,128)(2,1)S(1)}, bf16[256,256]{1,0:T(8,128)(2,1)S(1)}, u32[]{:S(2)}, u32[]{:S(2)}) collective-permute-start(bf16[256,256]{1,0:T(8,128)(2,1)S(1)} %fusion.16), channel_id=1, source_target_pairs={{0,2},{1,5},{2,0},{3,7},{4,6},{5,1},{6,4},{7,3},{8,10},{9,13},{10,... | collective-permute-start | bytes 393224 | tf_op jit(solution)/shard_map/ppermute | solution.py:30
  56.8 1.4 %collective-permute-done.16 = bf16[256,256]{1,0:T(8,128)(2,1)S(1)} collective-permute-done((bf16[256,256]{1,0:T(8,128)(2,1)S(1)}, bf16[256,256]{1,0:T(8,128)(2,1)S(1)}, u32[]{:S(2)}, u32[]{:S(2)}) %collective-permute-start.16) | collective-permute-done | bytes 131104 | tf_op jit(solution)/shard_map/ppermute | solution.py:30
  58.2 1.4 %collective-permute-start.17 = (bf16[256,256]{1,0:T(8,128)(2,1)S(1)}, bf16[256,256]{1,0:T(8,128)(2,1)S(1)}, u32[]{:S(2)}, u32[]{:S(2)}) collective-permute-start(bf16[256,256]{1,0:T(8,128)(2,1)S(1)} %fusion.13), channel_id=1, source_target_pairs={{0,2},{1,5},{2,0},{3,7},{4,6},{5,1},{6,4},{7,3},{8,10},{9,13},{10,... | collective-permute-start | bytes 393224 | tf_op jit(solution)/shard_map/ppermute | solution.py:30
  59.7 0.5 fusion
  60.3 0.8 collective-permute-done.11
  61.1 3.2 %collective-permute-start.12 = (bf16[256,256]{1,0:T(8,128)(2,1)S(1)}, bf16[256,256]{1,0:T(8,128)(2,1)S(1)}, u32[]{:S(2)}, u32[]{:S(2)}) collective-permute-start(bf16[256,256]{1,0:T(8,128)(2,1)S(1)} %reduce-precision_convert_fusion.3), channel_id=1, source_target_pairs={{0,4},{1,3},{2,6},{3,1},{4,0},{5,7},{6,2},{7,5},{8,12},{9,11},{10,... | collective-permute-start | bytes 393224 | tf_op jit(solution)/shard_map/ppermute | solution.py:30
  64.3 5.0 %collective-permute-start.18 = (bf16[256,256]{1,0:T(8,128)(2,1)S(1)}, bf16[256,256]{1,0:T(8,128)(2,1)S(1)}, u32[]{:S(2)}, u32[]{:S(2)}) collective-permute-start(bf16[256,256]{1,0:T(8,128)(2,1)S(1)} %reduce-precision_convert_fusion.1), channel_id=1, source_target_pairs={{0,4},{1,3},{2,6},{3,1},{4,0},{5,7},{6,2},{7,5},{8,12},{9,11},{10,... | collective-permute-start | bytes 393224 | tf_op jit(solution)/shard_map/ppermute | solution.py:30
  69.3 0.9 %collective-permute-start.13 = (bf16[256,256]{1,0:T(8,128)(2,1)S(1)}, bf16[256,256]{1,0:T(8,128)(2,1)S(1)}, u32[]{:S(2)}, u32[]{:S(2)}) collective-permute-start(bf16[256,256]{1,0:T(8,128)(2,1)S(1)} %reduce-precision_convert_fusion.2), channel_id=1, source_target_pairs={{0,8},{1,17},{2,10},{3,19},{4,12},{5,21},{6,14},{7,23},{8,0},{9,25... | collective-permute-start | bytes 393224 | tf_op jit(solution)/shard_map/ppermute | solution.py:30
  70.3 0.5 convolution_add_fusion
  70.8 1.3 %collective-permute-start.24 = (bf16[272,512]{1,0:T(8,128)(2,1)S(1)}, bf16[272,512]{1,0:T(8,128)(2,1)S(1)}, u32[]{:S(2)}, u32[]{:S(2)}) collective-permute-start(bf16[272,512]{1,0:T(8,128)(2,1)S(1)} %pad_maximum_fusion.5), channel_id=1, source_target_pairs={{0,16},{1,9},{2,18},{3,11},{4,20},{5,13},{6,22},{7,15},{8,24},{9,1... | collective-permute-start | bytes 835592 | tf_op jit(solution)/shard_map/ppermute | solution.py:30
  72.1 1.8 %collective-permute-done.18 = bf16[256,256]{1,0:T(8,128)(2,1)S(1)} collective-permute-done((bf16[256,256]{1,0:T(8,128)(2,1)S(1)}, bf16[256,256]{1,0:T(8,128)(2,1)S(1)}, u32[]{:S(2)}, u32[]{:S(2)}) %collective-permute-start.18) | collective-permute-done | bytes 131104 | tf_op jit(solution)/shard_map/ppermute | solution.py:30
  74.2 0.4 collective-permute-done.13
  74.7 1.3 %collective-permute-start.14 = (bf16[512,256]{1,0:T(8,128)(2,1)S(1)}, bf16[512,256]{1,0:T(8,128)(2,1)S(1)}, u32[]{:S(2)}, u32[]{:S(2)}) collective-permute-start(bf16[512,256]{1,0:T(8,128)(2,1)S(1)} %pad_maximum_fusion.7.refs_0_), channel_id=1, source_target_pairs={{0,16},{1,9},{2,18},{3,11},{4,20},{5,13},{6,22},{7,15},{8,24},{9,1... | collective-permute-start | bytes 786440 | tf_op jit(solution)/shard_map/ppermute | solution.py:30
  76.0 1.4 %collective-permute-done.24 = bf16[272,512]{1,0:T(8,128)(2,1)S(1)} collective-permute-done((bf16[272,512]{1,0:T(8,128)(2,1)S(1)}, bf16[272,512]{1,0:T(8,128)(2,1)S(1)}, u32[]{:S(2)}, u32[]{:S(2)}) %collective-permute-start.24) | collective-permute-done | bytes 278560 | tf_op jit(solution)/shard_map/ppermute | solution.py:30
  77.6 1.2 %collective-permute-start.25 = (bf16[144,512]{1,0:T(8,128)(2,1)S(1)}, bf16[144,512]{1,0:T(8,128)(2,1)S(1)}, u32[]{:S(2)}, u32[]{:S(2)}) collective-permute-start(bf16[144,512]{1,0:T(8,128)(2,1)S(1)} %pad_maximum_fusion.12), channel_id=1, source_target_pairs={{0,8},{1,17},{2,10},{3,19},{4,12},{5,21},{6,14},{7,23},{8,0},{9,25... | collective-permute-start | bytes 442376 | tf_op jit(solution)/shard_map/ppermute | solution.py:30
  78.8 1.5 %collective-permute-done.19 = bf16[256,256]{1,0:T(8,128)(2,1)S(1)} collective-permute-done((bf16[256,256]{1,0:T(8,128)(2,1)S(1)}, bf16[256,256]{1,0:T(8,128)(2,1)S(1)}, u32[]{:S(2)}, u32[]{:S(2)}) %collective-permute-start.19) | collective-permute-done | bytes 131104 | tf_op jit(solution)/shard_map/ppermute | solution.py:30
  80.4 1.7 %collective-permute-start.20 = (bf16[512,256]{1,0:T(8,128)(2,1)S(1)}, bf16[512,256]{1,0:T(8,128)(2,1)S(1)}, u32[]{:S(2)}, u32[]{:S(2)}) collective-permute-start(bf16[512,256]{1,0:T(8,128)(2,1)S(1)} %pad_maximum_fusion.8.refs_1_), channel_id=1, source_target_pairs={{0,16},{1,9},{2,18},{3,11},{4,20},{5,13},{6,22},{7,15},{8,24},{9,1... | collective-permute-start | bytes 786440 | tf_op jit(solution)/shard_map/ppermute | solution.py:30
  82.1 1.4 %collective-permute-done.25 = bf16[144,512]{1,0:T(8,128)(2,1)S(1)} collective-permute-done((bf16[144,512]{1,0:T(8,128)(2,1)S(1)}, bf16[144,512]{1,0:T(8,128)(2,1)S(1)}, u32[]{:S(2)}, u32[]{:S(2)}) %collective-permute-start.25) | collective-permute-done | bytes 147488 | tf_op jit(solution)/shard_map/ppermute | solution.py:30
  83.4 0.7 slice_add_fusion.2
  84.2 2.7 %collective-permute-done.20.refs_1_ = bf16[512,256]{1,0:T(8,128)(2,1)S(1)} collective-permute-done((bf16[512,256]{1,0:T(8,128)(2,1)S(1)}, bf16[512,256]{1,0:T(8,128)(2,1)S(1)}, u32[]{:S(2)}, u32[]{:S(2)}) %collective-permute-start.20) | collective-permute-done | bytes 262176 | tf_op jit(solution)/shard_map/ppermute | solution.py:30
  86.8 0.5 collective-permute-start.27
  87.5 1.4 %write_weights.2 = (f32[512,1024]{1,0:T(8,128)}, f32[1024,512]{1,0:T(8,128)}) custom-call(bf16[512,256]{1,0:T(8,128)(2,1)S(1)} %pad_maximum_fusion.7.refs_0_, bf16[512,256]{1,0:T(8,128)(2,1)S(1)} %pad_maximum_fusion.8.refs_1_, bf16[512,256]{1,0:T(8,128)(2,1)S(1)} %collective-permute-done.28.refs_2_, bf16[512,256]{1,0:T(8,128)(2,1)S(1)} %collective-permute-done.29.refs_3_), custom_call_target="tpu_custom_call" | custom-call | flops 1048576 | bytes 3145728 | tf_op jit(solution)/shard_map/write_weights/pallas_call | solution.py:158
  89.0 0.6 fusion.60
  89.6 1.4 %write_weights.3 = (f32[512,1024]{1,0:T(8,128)}, f32[1024,512]{1,0:T(8,128)}) custom-call(bf16[512,256]{1,0:T(8,128)(2,1)S(1)} %collective-permute-done.14.refs_0_, bf16[512,256]{1,0:T(8,128)(2,1)S(1)} %collective-permute-done.20.refs_1_, bf16[512,256]{1,0:T(8,128)(2,1)S(1)} %collective-permute-done.26.refs_2_, ...), custom_call_target="tpu_custom_call", output_to_operand_aliasing={{0}: (4, {}), {1}: (5, {})} | custom-call | flops 1048576 | bytes 3145728 | tf_op jit(solution)/shard_map/write_weights/pallas_call | solution.py:158
  (113 shorter events, 3.1 us)
Async XLA Ops:
  0.6 35.7 %copy-start = (bf16[512,1024]{1,0:T(8,128)(2,1)S(1)}, bf16[512,1024]{1,0:T(8,128)(2,1)}, u32[]{:S(2)}) copy-start(bf16[512,1024]{1,0:T(8,128)(2,1)} %param.17) | copy-start | bytes 3145732
  0.6 9.5 %collective-permute-start = (bf16[128,512]{1,0:T(8,128)(2,1)}, bf16[128,512]{1,0:T(8,128)(2,1)S(1)}, u32[]{:S(2)}, u32[]{:S(2)}) collective-permute-start(bf16[128,512]{1,0:T(8,128)(2,1)} %param.10), channel_id=1, source_target_pairs={{0,8},{1,17},{2,10},{3,19},{4,12},{5,21},{6,14},{7,23},{8,0},{9,25... | collective-permute-start | bytes 393224 | tf_op jit(solution)/shard_map/ppermute | solution.py:30
  3.7 9.0 %collective-permute-start.4 = (bf16[128,512]{1,0:T(8,128)(2,1)}, bf16[128,512]{1,0:T(8,128)(2,1)S(1)}, u32[]{:S(2)}, u32[]{:S(2)}) collective-permute-start(bf16[128,512]{1,0:T(8,128)(2,1)} %param.10), channel_id=1, source_target_pairs={{0,1},{1,0},{2,3},{3,2},{4,5},{5,4},{6,7},{7,6},{8,9},{9,8},{10,11... | collective-permute-start | bytes 393224 | tf_op jit(solution)/shard_map/ppermute | solution.py:34
  4.3 2.2 %copy-start.1 = (bf16[1,128,128,128]{3,2,1,0:T(8,128)(2,1)S(1)}, bf16[1,128,128,128]{3,2,1,0:T(8,128)(2,1)}, u32[]{:S(2)}) copy-start(bf16[1,128,128,128]{3,2,1,0:T(8,128)(2,1)} %vals_ref.1) | copy-start | bytes 12582916
  6.5 0.7 copy-start.2
  7.2 0.7 copy-start.3
  7.8 2.3 %copy-start.4 = (bf16[128,512]{1,0:T(8,128)(2,1)S(1)}, bf16[128,512]{1,0:T(8,128)(2,1)}, u32[]{:S(2)}) copy-start(bf16[128,512]{1,0:T(8,128)(2,1)} %param.10) | copy-start | bytes 393220
  9.5 9.3 %collective-permute-start.3 = (bf16[512,1024]{1,0:T(8,128)(2,1)S(1)}, bf16[512,1024]{1,0:T(8,128)(2,1)S(1)}, u32[]{:S(2)}, u32[]{:S(2)}) collective-permute-start(bf16[512,1024]{1,0:T(8,128)(2,1)S(1)} %get-tuple-element.31), channel_id=1, source_target_pairs={{0,1},{1,0},{2,3},{3,2},{4,5},{5,4},{6,7},{7,6},{8,9},{9,8},{10,11... | collective-permute-start | bytes 3145736 | tf_op jit(solution)/shard_map/ppermute | solution.py:34
  10.2 2.6 %collective-permute-start.5 = (bf16[128,512]{1,0:T(8,128)(2,1)S(1)}, bf16[128,512]{1,0:T(8,128)(2,1)S(1)}, u32[]{:S(2)}, u32[]{:S(2)}) collective-permute-start(bf16[128,512]{1,0:T(8,128)(2,1)S(1)} %collective-permute-done), channel_id=1, source_target_pairs={{0,1},{1,0},{2,3},{3,2},{4,5},{5,4},{6,7},{7,6},{8,9},{9,8},{10,11... | collective-permute-start | bytes 393224 | tf_op jit(solution)/shard_map/ppermute | solution.py:34
  10.3 6.8 %collective-permute-start.1 = (bf16[256,512]{1,0:T(8,128)(2,1)S(1)}, bf16[256,512]{1,0:T(8,128)(2,1)S(1)}, u32[]{:S(2)}, u32[]{:S(2)}) collective-permute-start(bf16[256,512]{1,0:T(8,128)(2,1)S(1)} %pad_maximum_fusion.6), channel_id=1, source_target_pairs={{0,16},{1,9},{2,18},{3,11},{4,20},{5,13},{6,22},{7,15},{8,24},{9,1... | collective-permute-start | bytes 786440 | tf_op jit(solution)/shard_map/ppermute | solution.py:30
  17.1 1.6 %collective-permute-start.2 = (bf16[256,512]{1,0:T(8,128)(2,1)S(1)}, bf16[256,512]{1,0:T(8,128)(2,1)S(1)}, u32[]{:S(2)}, u32[]{:S(2)}) collective-permute-start(bf16[256,512]{1,0:T(8,128)(2,1)S(1)} %collective-permute-done.1), channel_id=1, source_target_pairs={{0,1},{1,0},{2,3},{3,2},{4,5},{5,4},{6,7},{7,6},{8,9},{9,8},{10,11... | collective-permute-start | bytes 786440 | tf_op jit(solution)/shard_map/ppermute | solution.py:34
  18.8 1.0 %copy-start.9 = (bf16[512,1024]{1,0:T(8,128)(2,1)}, bf16[512,1024]{1,0:T(8,128)(2,1)S(1)}, u32[]{:S(2)}) copy-start(bf16[512,1024]{1,0:T(8,128)(2,1)S(1)} %collective-permute-done.3) | copy-start | bytes 3145732
  19.8 16.3 %copy-start.7 = (f32[8,512]{1,0:T(8,128)S(1)}, f32[8,512]{1,0:T(8,128)}, u32[]{:S(2)}) copy-start(f32[8,512]{1,0:T(8,128)} %param.16) | copy-start | bytes 49156
  19.8 16.3 %copy-start.8 = (s32[128]{0:T(128)S(1)}, s32[128]{0:T(128)}, u32[]{:S(2)}) copy-start(s32[128]{0:T(128)} %param.15) | copy-start | bytes 1540
  19.8 8.5 %collective-permute-start.6 = (bf16[256,512]{1,0:T(8,128)(2,1)S(1)}, bf16[256,512]{1,0:T(8,128)(2,1)S(1)}, u32[]{:S(2)}, u32[]{:S(2)}) collective-permute-start(bf16[256,512]{1,0:T(8,128)(2,1)S(1)} %fusion.6), channel_id=1, source_target_pairs={{0,4},{1,3},{2,6},{3,1},{4,0},{5,7},{6,2},{7,5},{8,12},{9,11},{10,... | collective-permute-start | bytes 786440 | tf_op jit(solution)/shard_map/ppermute | solution.py:30
  28.4 7.2 %collective-permute-start.7 = (bf16[128,512]{1,0:T(8,128)(2,1)S(1)}, bf16[128,512]{1,0:T(8,128)(2,1)S(1)}, u32[]{:S(2)}, u32[]{:S(2)}) collective-permute-start(bf16[128,512]{1,0:T(8,128)(2,1)S(1)} %fusion.17), channel_id=1, source_target_pairs={{0,2},{1,5},{2,0},{3,7},{4,6},{5,1},{6,4},{7,3},{8,10},{9,13},{10,... | collective-permute-start | bytes 393224 | tf_op jit(solution)/shard_map/ppermute | solution.py:30
  35.8 1.2 %copy-start.5 = (bf16[1024,512]{1,0:T(8,128)(2,1)S(1)}, bf16[1024,512]{1,0:T(8,128)(2,1)}, u32[]{:S(2)}) copy-start(bf16[1024,512]{1,0:T(8,128)(2,1)} %param.18) | copy-start | bytes 3145732
  35.8 1.2 %copy-start.6 = (bf16[128,512]{1,0:T(8,128)(2,1)S(1)}, bf16[128,512]{1,0:T(8,128)(2,1)}, u32[]{:S(2)}) copy-start(bf16[128,512]{1,0:T(8,128)(2,1)} %param.19) | copy-start | bytes 393220
  38.6 1.8 %collective-permute-start.8 = (bf16[128,1536]{1,0:T(8,128)(2,1)S(1)}, bf16[128,1536]{1,0:T(8,128)(2,1)S(1)}, u32[]{:S(2)}, u32[]{:S(2)}) collective-permute-start(bf16[128,1536]{1,0:T(8,128)(2,1)S(1)} %get-tuple-element.64), channel_id=1, source_target_pairs={{0,1},{1,0},{2,3},{3,2},{4,5},{5,4},{6,7},{7,6},{8,9},{9,8},{10,11... | collective-permute-start | bytes 1179656 | tf_op jit(solution)/shard_map/ppermute | solution.py:34
  40.4 6.8 %collective-permute-start.21 = (bf16[144,512]{1,0:T(8,128)(2,1)S(1)}, bf16[144,512]{1,0:T(8,128)(2,1)S(1)}, u32[]{:S(2)}, u32[]{:S(2)}) collective-permute-start(bf16[144,512]{1,0:T(8,128)(2,1)S(1)} %pad_maximum_fusion.11), channel_id=1, source_target_pairs={{0,2},{1,5},{2,0},{3,7},{4,6},{5,1},{6,4},{7,3},{8,10},{9,13},{10,... | collective-permute-start | bytes 442376 | tf_op jit(solution)/shard_map/ppermute | solution.py:30
  43.9 6.4 %collective-permute-start.9 = (bf16[512,256]{1,0:T(8,128)(2,1)S(1)}, bf16[512,256]{1,0:T(8,128)(2,1)S(1)}, u32[]{:S(2)}, u32[]{:S(2)}) collective-permute-start(bf16[512,256]{1,0:T(8,128)(2,1)S(1)} %fusion.7), channel_id=1, source_target_pairs={{0,16},{1,9},{2,18},{3,11},{4,20},{5,13},{6,22},{7,15},{8,24},{9,1... | collective-permute-start | bytes 786440 | tf_op jit(solution)/shard_map/ppermute | solution.py:30
  45.9 7.2 %collective-permute-start.15 = (bf16[512,256]{1,0:T(8,128)(2,1)S(1)}, bf16[512,256]{1,0:T(8,128)(2,1)S(1)}, u32[]{:S(2)}, u32[]{:S(2)}) collective-permute-start(bf16[512,256]{1,0:T(8,128)(2,1)S(1)} %fusion.8), channel_id=1, source_target_pairs={{0,16},{1,9},{2,18},{3,11},{4,20},{5,13},{6,22},{7,15},{8,24},{9,1... | collective-permute-start | bytes 786440 | tf_op jit(solution)/shard_map/ppermute | solution.py:30
  47.3 12.4 %collective-permute-start.22 = (bf16[272,512]{1,0:T(8,128)(2,1)S(1)}, bf16[272,512]{1,0:T(8,128)(2,1)S(1)}, u32[]{:S(2)}, u32[]{:S(2)}) collective-permute-start(bf16[272,512]{1,0:T(8,128)(2,1)S(1)} %pad_maximum_fusion.4), channel_id=1, source_target_pairs={{0,4},{1,3},{2,6},{3,1},{4,0},{5,7},{6,2},{7,5},{8,12},{9,11},{10,... | collective-permute-start | bytes 835592 | tf_op jit(solution)/shard_map/ppermute | solution.py:30
  50.3 9.3 %copy-start.10 = (bf16[512,1024]{1,0:T(8,128)(2,1)S(1)}, bf16[512,1024]{1,0:T(8,128)(2,1)}, u32[]{:S(2)}) copy-start(bf16[512,1024]{1,0:T(8,128)(2,1)} %copy-done.9) | copy-start | bytes 3145732
  50.4 5.0 %collective-permute-start.10 = (bf16[256,256]{1,0:T(8,128)(2,1)S(1)}, bf16[256,256]{1,0:T(8,128)(2,1)S(1)}, u32[]{:S(2)}, u32[]{:S(2)}) collective-permute-start(bf16[256,256]{1,0:T(8,128)(2,1)S(1)} %fusion.14), channel_id=1, source_target_pairs={{0,8},{1,17},{2,10},{3,19},{4,12},{5,21},{6,14},{7,23},{8,0},{9,25... | collective-permute-start | bytes 393224 | tf_op jit(solution)/shard_map/ppermute | solution.py:30
  53.2 5.0 %collective-permute-start.16 = (bf16[256,256]{1,0:T(8,128)(2,1)S(1)}, bf16[256,256]{1,0:T(8,128)(2,1)S(1)}, u32[]{:S(2)}, u32[]{:S(2)}) collective-permute-start(bf16[256,256]{1,0:T(8,128)(2,1)S(1)} %fusion.11), channel_id=1, source_target_pairs={{0,8},{1,17},{2,10},{3,19},{4,12},{5,21},{6,14},{7,23},{8,0},{9,25... | collective-permute-start | bytes 393224 | tf_op jit(solution)/shard_map/ppermute | solution.py:30
  55.4 5.6 %collective-permute-start.11 = (bf16[256,256]{1,0:T(8,128)(2,1)S(1)}, bf16[256,256]{1,0:T(8,128)(2,1)S(1)}, u32[]{:S(2)}, u32[]{:S(2)}) collective-permute-start(bf16[256,256]{1,0:T(8,128)(2,1)S(1)} %fusion.16), channel_id=1, source_target_pairs={{0,2},{1,5},{2,0},{3,7},{4,6},{5,1},{6,4},{7,3},{8,10},{9,13},{10,... | collective-permute-start | bytes 393224 | tf_op jit(solution)/shard_map/ppermute | solution.py:30
  58.2 6.1 %collective-permute-start.17 = (bf16[256,256]{1,0:T(8,128)(2,1)S(1)}, bf16[256,256]{1,0:T(8,128)(2,1)S(1)}, u32[]{:S(2)}, u32[]{:S(2)}) collective-permute-start(bf16[256,256]{1,0:T(8,128)(2,1)S(1)} %fusion.13), channel_id=1, source_target_pairs={{0,2},{1,5},{2,0},{3,7},{4,6},{5,1},{6,4},{7,3},{8,10},{9,13},{10,... | collective-permute-start | bytes 393224 | tf_op jit(solution)/shard_map/ppermute | solution.py:30
  60.2 10.1 %collective-permute-start.23 = (bf16[512,512]{1,0:T(8,128)(2,1)S(1)}, bf16[512,512]{1,0:T(8,128)(2,1)S(1)}, u32[]{:S(2)}, u32[]{:S(2)}) collective-permute-start(bf16[512,512]{1,0:T(8,128)(2,1)S(1)} %fusion), channel_id=1, source_target_pairs={{0,1},{1,0},{2,3},{3,2},{4,5},{5,4},{6,7},{7,6},{8,9},{9,8},{10,11... | collective-permute-start | bytes 1572872 | tf_op jit(solution)/shard_map/ppermute | solution.py:34
  61.1 8.2 %collective-permute-start.12 = (bf16[256,256]{1,0:T(8,128)(2,1)S(1)}, bf16[256,256]{1,0:T(8,128)(2,1)S(1)}, u32[]{:S(2)}, u32[]{:S(2)}) collective-permute-start(bf16[256,256]{1,0:T(8,128)(2,1)S(1)} %reduce-precision_convert_fusion.3), channel_id=1, source_target_pairs={{0,4},{1,3},{2,6},{3,1},{4,0},{5,7},{6,2},{7,5},{8,12},{9,11},{10,... | collective-permute-start | bytes 393224 | tf_op jit(solution)/shard_map/ppermute | solution.py:30
  64.3 9.6 %collective-permute-start.18 = (bf16[256,256]{1,0:T(8,128)(2,1)S(1)}, bf16[256,256]{1,0:T(8,128)(2,1)S(1)}, u32[]{:S(2)}, u32[]{:S(2)}) collective-permute-start(bf16[256,256]{1,0:T(8,128)(2,1)S(1)} %reduce-precision_convert_fusion.1), channel_id=1, source_target_pairs={{0,4},{1,3},{2,6},{3,1},{4,0},{5,7},{6,2},{7,5},{8,12},{9,11},{10,... | collective-permute-start | bytes 393224 | tf_op jit(solution)/shard_map/ppermute | solution.py:30
  69.3 5.2 %collective-permute-start.13 = (bf16[256,256]{1,0:T(8,128)(2,1)S(1)}, bf16[256,256]{1,0:T(8,128)(2,1)S(1)}, u32[]{:S(2)}, u32[]{:S(2)}) collective-permute-start(bf16[256,256]{1,0:T(8,128)(2,1)S(1)} %reduce-precision_convert_fusion.2), channel_id=1, source_target_pairs={{0,8},{1,17},{2,10},{3,19},{4,12},{5,21},{6,14},{7,23},{8,0},{9,25... | collective-permute-start | bytes 393224 | tf_op jit(solution)/shard_map/ppermute | solution.py:30
  70.8 6.6 %collective-permute-start.24 = (bf16[272,512]{1,0:T(8,128)(2,1)S(1)}, bf16[272,512]{1,0:T(8,128)(2,1)S(1)}, u32[]{:S(2)}, u32[]{:S(2)}) collective-permute-start(bf16[272,512]{1,0:T(8,128)(2,1)S(1)} %pad_maximum_fusion.5), channel_id=1, source_target_pairs={{0,16},{1,9},{2,18},{3,11},{4,20},{5,13},{6,22},{7,15},{8,24},{9,1... | collective-permute-start | bytes 835592 | tf_op jit(solution)/shard_map/ppermute | solution.py:30
  74.0 6.3 %collective-permute-start.19 = (bf16[256,256]{1,0:T(8,128)(2,1)S(1)}, bf16[256,256]{1,0:T(8,128)(2,1)S(1)}, u32[]{:S(2)}, u32[]{:S(2)}) collective-permute-start(bf16[256,256]{1,0:T(8,128)(2,1)S(1)} %reduce-precision_convert_fusion), channel_id=1, source_target_pairs={{0,8},{1,17},{2,10},{3,19},{4,12},{5,21},{6,14},{7,23},{8,0},{9,25... | collective-permute-start | bytes 393224 | tf_op jit(solution)/shard_map/ppermute | solution.py:30
  74.6 12.9 %collective-permute-start.28 = (bf16[512,256]{1,0:T(8,128)(2,1)S(1)}, bf16[512,256]{1,0:T(8,128)(2,1)S(1)}, u32[]{:S(2)}, u32[]{:S(2)}) collective-permute-start(bf16[512,256]{1,0:T(8,128)(2,1)S(1)} %pad_maximum_fusion.7.refs_0_), channel_id=1, source_target_pairs={{0,1},{1,0},{2,3},{3,2},{4,5},{5,4},{6,7},{7,6},{8,9},{9,8},{10,11... | collective-permute-start | bytes 786440 | tf_op jit(solution)/shard_map/ppermute | solution.py:34
  74.7 9.5 %collective-permute-start.14 = (bf16[512,256]{1,0:T(8,128)(2,1)S(1)}, bf16[512,256]{1,0:T(8,128)(2,1)S(1)}, u32[]{:S(2)}, u32[]{:S(2)}) collective-permute-start(bf16[512,256]{1,0:T(8,128)(2,1)S(1)} %pad_maximum_fusion.7.refs_0_), channel_id=1, source_target_pairs={{0,16},{1,9},{2,18},{3,11},{4,20},{5,13},{6,22},{7,15},{8,24},{9,1... | collective-permute-start | bytes 786440 | tf_op jit(solution)/shard_map/ppermute | solution.py:30
  77.6 5.8 %collective-permute-start.25 = (bf16[144,512]{1,0:T(8,128)(2,1)S(1)}, bf16[144,512]{1,0:T(8,128)(2,1)S(1)}, u32[]{:S(2)}, u32[]{:S(2)}) collective-permute-start(bf16[144,512]{1,0:T(8,128)(2,1)S(1)} %pad_maximum_fusion.12), channel_id=1, source_target_pairs={{0,8},{1,17},{2,10},{3,19},{4,12},{5,21},{6,14},{7,23},{8,0},{9,25... | collective-permute-start | bytes 442376 | tf_op jit(solution)/shard_map/ppermute | solution.py:30
  80.3 7.2 %collective-permute-start.29 = (bf16[512,256]{1,0:T(8,128)(2,1)S(1)}, bf16[512,256]{1,0:T(8,128)(2,1)S(1)}, u32[]{:S(2)}, u32[]{:S(2)}) collective-permute-start(bf16[512,256]{1,0:T(8,128)(2,1)S(1)} %pad_maximum_fusion.8.refs_1_), channel_id=1, source_target_pairs={{0,1},{1,0},{2,3},{3,2},{4,5},{5,4},{6,7},{7,6},{8,9},{9,8},{10,11... | collective-permute-start | bytes 786440 | tf_op jit(solution)/shard_map/ppermute | solution.py:34
  80.4 6.4 %collective-permute-start.20 = (bf16[512,256]{1,0:T(8,128)(2,1)S(1)}, bf16[512,256]{1,0:T(8,128)(2,1)S(1)}, u32[]{:S(2)}, u32[]{:S(2)}) collective-permute-start(bf16[512,256]{1,0:T(8,128)(2,1)S(1)} %pad_maximum_fusion.8.refs_1_), channel_id=1, source_target_pairs={{0,16},{1,9},{2,18},{3,11},{4,20},{5,13},{6,22},{7,15},{8,24},{9,1... | collective-permute-start | bytes 786440 | tf_op jit(solution)/shard_map/ppermute | solution.py:30
  86.8 2.7 %collective-permute-start.26 = (bf16[512,256]{1,0:T(8,128)(2,1)S(1)}, bf16[512,256]{1,0:T(8,128)(2,1)S(1)}, u32[]{:S(2)}, u32[]{:S(2)}) collective-permute-start(bf16[512,256]{1,0:T(8,128)(2,1)S(1)} %collective-permute-done.14.refs_0_), channel_id=1, source_target_pairs={{0,1},{1,0},{2,3},{3,2},{4,5},{5,4},{6,7},{7,6},{8,9},{9,8},{10,11... | collective-permute-start | bytes 786440 | tf_op jit(solution)/shard_map/ppermute | solution.py:34
  86.8 2.7 %collective-permute-start.27 = (bf16[512,256]{1,0:T(8,128)(2,1)S(1)}, bf16[512,256]{1,0:T(8,128)(2,1)S(1)}, u32[]{:S(2)}, u32[]{:S(2)}) collective-permute-start(bf16[512,256]{1,0:T(8,128)(2,1)S(1)} %collective-permute-done.20.refs_1_), channel_id=1, source_target_pairs={{0,1},{1,0},{2,3},{3,2},{4,5},{5,4},{6,7},{7,6},{8,9},{9,8},{10,11... | collective-permute-start | bytes 786440 | tf_op jit(solution)/shard_map/ppermute | solution.py:34
  87.4 1.5 %collective-permute-start.30 = (bf16[16,512]{1,0:T(8,128)(2,1)S(1)}, bf16[16,512]{1,0:T(8,128)(2,1)S(1)}, u32[]{:S(2)}, u32[]{:S(2)}) collective-permute-start(bf16[16,512]{1,0:T(8,128)(2,1)S(1)} %get-tuple-element.67), channel_id=1, source_target_pairs={{0,1},{1,0},{2,3},{3,2},{4,5},{5,4},{6,7},{7,6},{8,9},{9,8},{10,11... | collective-permute-start | bytes 49160 | tf_op jit(solution)/shard_map/ppermute | solution.py:34

commit v3 on v2

v3 whole, which is shorter than its diff:
```python
import jax
import jax.numpy as jnp
import numpy as np
from jax import lax
from jax.experimental import pallas as pl
from jax.experimental.pallas import tpu as pltpu
from jax.sharding import PartitionSpec as P

F = 512
TYPES = 8
TILE = 128
BF = jnp.bfloat16
FP = jnp.float32
AXES = ("row", "col")


def reversed_bits(value, bits):
    out = 0
    for b in range(bits):
        out |= ((value >> b) & 1) << (bits - 1 - b)
    return out


def exchange(x, rows, cols, row_masks, z_masks):
    pairs = []
    for r in range(rows):
        for c in range(cols):
            core = c & 1
            pairs.append((r * cols + c, (r ^ row_masks[core]) * cols + (c ^ (2 * z_masks[core]))))
    return lax.ppermute(x, AXES, pairs)


def swap_cores(x, rows, cols):
    return lax.ppermute(x, AXES, [(i, i ^ 1) for i in range(rows * cols)])


def rounded(x):
    return lax.reduce_precision(x, 8, 7).astype(BF)


def split(x):
    high = lax.reduce_precision(x, 8, 7)
    return jnp.concatenate([high.astype(BF), rounded(x - high)], axis=0)


def whole(x):
    x = x.astype(FP)
    return x[:TYPES] + x[TYPES:]


def build(tile_vals, tile_row, tile_col, tile_count, n_row, n_col):
    slots = tile_vals.shape[1]
    n_z = n_col // 2
    wide, half = n_row * TILE, n_z * TILE
    chunk = 16
    rounds = slots // chunk

    def kernel(
        count_ref, rows_ref, cols_ref, vals_ref, near_ref, far_ref, total, held, row_ref, col_ref, sems
    ):
        places = [
            pltpu.make_async_copy(rows_ref, row_ref, sems.at[rounds]),
            pltpu.make_async_copy(cols_ref, col_ref, sems.at[rounds + 1]),
        ]
        for copy in places:
            copy.start()
        copies = []
        for i in range(rounds):
            at = pl.ds(i * chunk, chunk)
            copies.append(pltpu.make_async_copy(vals_ref.at[0, at], held.at[at], sems.at[i]))
            copies[i].start()
        row, col = lax.axis_index("row"), lax.axis_index("col")
        core, z = col & 1, col >> 1
        total[...] = jnp.zeros_like(total)
        count = count_ref[0, 0]
        for copy in places:
            copy.wait()

        def add(s, carry):
            r, c = row_ref[0, s], col_ref[0, s]
            total[r, c] = total[r, c] + held[s].astype(FP)
            return carry

        for i in range(rounds):
            copies[i].wait()
            lax.fori_loop(i * chunk, jnp.clip(count, i * chunk, (i + 1) * chunk), add, 0)

        for side, out in enumerate((near_ref, far_ref)):
            whose = core ^ side

            def emit(p, carry, out=out, whose=whose):
                r = 2 * (z ^ jnp.where(whose == 0, p, reversed_bits(p, n_z.bit_length() - 1))) + whose
                at = pl.ds(pl.multiple_of(p * TILE, TILE), TILE)
                for q in range(n_row):
                    value = total[r, row ^ jnp.where(core == 0, q, reversed_bits(q, n_row.bit_length() - 1))]
                    high = value.astype(BF)
                    out[at, q * TILE : (q + 1) * TILE] = high
                    out[at, wide + q * TILE : wide + (q + 1) * TILE] = (value - high.astype(FP)).astype(BF)
                return carry

            lax.fori_loop(0, n_z, emit, 0)

    dense = n_row * n_col * TILE * TILE
    result = jax.ShapeDtypeStruct((half, 2 * wide), BF)
    return pl.pallas_call(
        kernel,
        out_shape=(result, result),
        in_specs=[pl.BlockSpec(memory_space=pltpu.SMEM)] + [pl.BlockSpec(memory_space=pl.ANY)] * 3,
        scratch_shapes=[
            pltpu.VMEM((n_col, n_row, TILE, TILE), FP),
            pltpu.VMEM((slots, TILE, TILE), BF),
            pltpu.SMEM((1, slots), jnp.int32),
            pltpu.SMEM((1, slots), jnp.int32),
            pltpu.SemaphoreType.DMA((rounds + 2,)),
        ],
        compiler_params=pltpu.CompilerParams(vmem_limit_bytes=dense * 9 + 8 * 1024 * 1024),
        cost_estimate=pl.CostEstimate(
            flops=slots * TILE * TILE, bytes_accessed=slots * TILE * TILE * 2 + dense * 4, transcendentals=0
        ),
        name="build_dense",
    )(tile_count, *(pltpu.with_memory_space_constraint(x, pltpu.HBM) for x in (tile_row, tile_col, tile_vals)))


def write_weights(near, far, held, gains, first_place, n_row, factor):
    parts = len(near)
    rows, lanes = near[0].shape
    span = 2 * F // n_row
    places = rows // span
    per = F // span

    def kernel(*refs):
        mine, there = refs[:parts], refs[parts : 2 * parts]
        in_ref, out_ref = refs[-5 - len(gains) // 2 :][:2]
        wide_in, wide_out, sems = refs[-3:]
        core, row = lax.axis_index("col") & 1, lax.axis_index("row")

        def put(sources, ref, at):
            for i, x in enumerate(sources):
                ref[at, i * lanes : (i + 1) * lanes] = x[at, :].astype(FP) * factor

        copies = []
        for j in range(places):
            q = first_place + j
            at = pl.ds(j * span, span)

            @pl.when(core == 0)
            def _(at=at):
                put(mine, wide_in, at)
                put(there, wide_out, at)

            @pl.when(core != 0)
            def _(at=at):
                put(there, wide_in, at)
                put(mine, wide_out, at)

            g = row ^ q
            to = in_ref.at[
                pl.ds(pl.multiple_of((g % per) * span, span), span), pl.ds(pl.multiple_of((g // per) * F, F), F)
            ]
            copies.append(pltpu.make_async_copy(wide_in.at[at], to, sems.at[2 * j]))
            copies[-1].start()
            g = row ^ reversed_bits(q, n_row.bit_length() - 1)
            to = out_ref.at[pl.ds(pl.multiple_of(g * span, span), span)]
            copies.append(pltpu.make_async_copy(wide_out.at[at], to, sems.at[2 * j + 1]))
            copies[-1].start()
        if gains:
            one, two = (x[...].astype(FP) for x in refs[2 * parts + len(held) :][:2])
            refs[-4][...] = ((one[:TYPES] + one[TYPES:]) + (two[:TYPES] + two[TYPES:])) * factor
        for copy in copies:
            copy.wait()

    vmem, hbm = pl.BlockSpec(memory_space=pltpu.VMEM), pl.BlockSpec(memory_space=pltpu.HBM)
    return pl.pallas_call(
        kernel,
        out_shape=(jax.ShapeDtypeStruct((F, 2 * F), FP), jax.ShapeDtypeStruct((2 * F, F), FP))
        + (jax.ShapeDtypeStruct((TYPES, F), FP),) * (len(gains) // 2),
        in_specs=[vmem] * (2 * parts) + [hbm] * len(held) + [vmem] * len(gains),
        out_specs=(hbm, hbm) + (vmem,) * (len(gains) // 2),
        input_output_aliases={2 * parts + i: i for i in range(len(held))},
        scratch_shapes=[
            pltpu.VMEM((rows, F), FP),
            pltpu.VMEM((rows, F), FP),
            pltpu.SemaphoreType.DMA((2 * places,)),
        ],
        compiler_params=pltpu.CompilerParams(vmem_limit_bytes=16 * 1024 * 1024),
        cost_estimate=pl.CostEstimate(flops=4 * rows * F, bytes_accessed=12 * rows * F, transcendentals=0),
        name="write_weights",
    )(*near, *far, *held, *gains)


def node_gradients(grad_hidden, w_in, aggregate, gains, cotangent, picked):
    rows = cotangent.shape[0]

    def kernel(gh_ref, w_ref, agg_ref, gains_ref, cot_ref, picked_ref, out_ref):
        aggregate = agg_ref[...]
        center = jnp.mean(aggregate, axis=-1, keepdims=True)
        spread = jnp.mean(jnp.square(aggregate - center), axis=-1, keepdims=True)
        inverse = lax.rsqrt(spread + 1e-05)
        normed = (aggregate - center) * inverse
        grad_scaled = lax.dot_general(
            gh_ref[...], w_ref[...], (((1,), (1,)), ((), ())), preferred_element_type=FP
        )
        grad_normed = grad_scaled * gains_ref[...]
        grad_agg = cot_ref[...].astype(FP) + inverse * (
            grad_normed
            - jnp.mean(grad_normed, axis=-1, keepdims=True)
            - normed * jnp.mean(grad_normed * normed, axis=-1, keepdims=True)
        )
        out_ref[:rows] = grad_agg.astype(BF)
        gain = jnp.dot(
            picked_ref[...], grad_scaled * normed, precision=lax.Precision.HIGHEST, preferred_element_type=FP
        )
        high = gain.astype(BF).astype(FP)
        out_ref[rows:] = jnp.concatenate([high, gain - high], axis=0).astype(BF)

    return pl.pallas_call(
        kernel,
        out_shape=jax.ShapeDtypeStruct((rows + 2 * TYPES, F), BF),
        in_specs=[pl.BlockSpec(memory_space=pltpu.VMEM)] * 6,
        out_specs=pl.BlockSpec(memory_space=pltpu.VMEM),
        compiler_params=pltpu.CompilerParams(vmem_limit_bytes=8 * 1024 * 1024),
        cost_estimate=pl.CostEstimate(flops=4 * rows * F * F, bytes_accessed=4 * F * F, transcendentals=rows),
        name="node_gradients",
    )(grad_hidden, w_in, aggregate, gains, cotangent, picked)


def weight_blocks(mine, met, places, n_row, parts, dtype, through=()):
    span = 2 * F // n_row
    per = F // span
    lanes = F // parts
    rows = len(places) * span

    def kernel(mine_ref, met_ref, *refs):
        outs = refs[len(through) : len(through) + parts]
        core, row = lax.axis_index("col") & 1, lax.axis_index("row")

        def block(left, right):
            total = None
            for ref in (mine_ref, met_ref):
                term = lax.dot_general(
                    ref[:, left], ref[:, right], (((0,), (0,)), ((), ())), preferred_element_type=FP
                )
                total = term if total is None else total + term
            return total

        def put(j, value):
            for i, out in enumerate(outs):
                out[j * span : (j + 1) * span, :] = value[:, i * lanes : (i + 1) * lanes].astype(dtype)

        for j, q in enumerate(places):

            @pl.when(core == 0)
            def _(j=j, q=q):
                g = row ^ q
                left = pl.ds(pl.multiple_of((g % per) * span, span), span)
                right = pl.ds(pl.multiple_of(F + (g // per) * F, F), F)
                put(j, block(left, right))

            @pl.when(core != 0)
            def _(j=j, q=q):
                g = row ^ reversed_bits(q, n_row.bit_length() - 1)
                left = pl.ds(pl.multiple_of(F + g * span, span), span)
                put(j, block(left, slice(0, F)))

    return pl.pallas_call(
        kernel,
        out_shape=tuple(jax.ShapeDtypeStruct((rows, lanes), dtype) for _ in range(parts))
        + tuple(jax.ShapeDtypeStruct(x.shape, x.dtype) for x in through),
        in_specs=[pl.BlockSpec(memory_space=pltpu.VMEM)] * 2 + [pl.BlockSpec(memory_space=pl.ANY)] * len(through),
        out_specs=(pl.BlockSpec(memory_space=pltpu.VMEM),) * parts
        + (pl.BlockSpec(memory_space=pl.ANY),) * len(through),
        input_output_aliases={2 + i: parts + i for i in range(len(through))},
        compiler_params=pltpu.CompilerParams(vmem_limit_bytes=8 * 1024 * 1024),
        cost_estimate=pl.CostEstimate(
            flops=4 * TILE * rows * F, bytes_accessed=8 * TILE * F + 4 * rows * F, transcendentals=0
        ),
        name="weight_blocks",
    )(mine, met, *through)


def mix(aggregate, activated, w_out, after):
    def kernel(agg_ref, act_ref, w_ref, after_ref, out_ref):
        branch = jnp.dot(act_ref[...], w_ref[...], preferred_element_type=FP)
        out_ref[...] = (agg_ref[...] + branch).astype(BF)

    vmem = pl.BlockSpec(memory_space=pltpu.VMEM)
    return pl.pallas_call(
        kernel,
        out_shape=jax.ShapeDtypeStruct(aggregate.shape, BF),
        in_specs=[vmem, vmem, vmem, pl.BlockSpec(memory_space=pl.ANY)],
        out_specs=vmem,
        compiler_params=pltpu.CompilerParams(vmem_limit_bytes=8 * 1024 * 1024),
        cost_estimate=pl.CostEstimate(flops=0, bytes_accessed=0, transcendentals=0),
        name="mix",
    )(aggregate, activated, w_out, after)


def small_call(kernel, name, outs, operands, after=()):
    n, m = len(operands), len(after)

    def body(*refs):
        kernel(*refs[:n], *refs[n + m :])

    moved = sum(x.size * x.dtype.itemsize for x in (*operands, *outs))
    vmem = pl.BlockSpec(memory_space=pltpu.VMEM)
    return pl.pallas_call(
        body,
        out_shape=tuple(outs),
        in_specs=[vmem] * n + [pl.BlockSpec(memory_space=pl.ANY)] * m,
        out_specs=(vmem,) * len(outs),
        compiler_params=pltpu.CompilerParams(vmem_limit_bytes=2 * moved + 4 * 1024 * 1024),
        cost_estimate=pl.CostEstimate(flops=0, bytes_accessed=0, transcendentals=0),
        name=name,
    )(*operands, *after)


def added(keep, came, halves, after):
    n, lanes = keep.shape
    half = n // 2

    def kernel(keep_ref, came_ref, *outs):
        if halves:
            outs[0][...] = (keep_ref[half:].astype(FP) + came_ref[half:].astype(FP)).astype(BF)
            outs[1][...] = keep_ref[:half].astype(FP) + came_ref[:half].astype(FP)
        else:
            outs[0][...] = (keep_ref[...].astype(FP) + came_ref[...].astype(FP)).astype(BF)

    if halves:
        outs = (jax.ShapeDtypeStruct((half, lanes), BF), jax.ShapeDtypeStruct((half, lanes), FP))
    else:
        outs = (jax.ShapeDtypeStruct((n, lanes), BF),)
    return small_call(kernel, "added", outs, (keep, came), after)


def node_values(keep, came, gains, w_in, w_out, cotangent):
    n = keep.shape[0]

    def kernel(keep_ref, came_ref, gains_ref, w_in_ref, w_out_ref, cot_ref, agg_ref, mine_ref, away_ref, act_ref, gh_ref):
        aggregate = keep_ref[...] + came_ref[...].astype(FP)
        agg_ref[...] = aggregate
        center = jnp.mean(aggregate, axis=-1, keepdims=True)
        spread = jnp.mean(jnp.square(aggregate - center), axis=-1, keepdims=True)
        inverse = lax.rsqrt(spread + 1e-05)
        scaled = ((aggregate - center) * inverse * gains_ref[...]).astype(BF)
        cot = cot_ref[...]
        grad_act = lax.dot_general(cot, w_out_ref[...], (((1,), (1,)), ((), ())), preferred_element_type=FP)
        hidden = jnp.dot(scaled, w_in_ref[...], preferred_element_type=FP)
        sigmoid_h = jax.nn.sigmoid(hidden)
        activated = (hidden * sigmoid_h).astype(BF)
        grad_hidden = (grad_act * sigmoid_h * (1.0 + hidden * (1.0 - sigmoid_h))).astype(BF)
        act_ref[...] = activated
        gh_ref[...] = grad_hidden

        def put(for_in, for_out):
            for_in[:, :F] = scaled
            for_in[:, F:] = grad_hidden
            for_out[:, :F] = cot
            for_out[:, F:] = activated

        first = lax.axis_index("col") & 1 == 0

        @pl.when(first)
        def _():
            put(mine_ref, away_ref)

        @pl.when(jnp.logical_not(first))
        def _():
            put(away_ref, mine_ref)

    outs = (jax.ShapeDtypeStruct((n, F), FP),) + tuple(jax.ShapeDtypeStruct((n, w * F), BF) for w in (3, 3, 2, 2))
    return small_call(kernel, "node_values", outs, (keep, came, gains, w_in, w_out, cotangent))


def shards(
    features,
    tile_vals,
    tile_row,
    tile_col,
    tile_count,
    node_type,
    type_gain,
    w_in,
    w_out,
    cotangent,
):
    n_row, n_col = lax.axis_size("row"), lax.axis_size("col")
    n_z = n_col // 2
    row_bits, z_bits = n_row.bit_length() - 1, n_z.bit_length() - 1
    total_nodes = TILE * n_row * n_col
    row, col = lax.axis_index("row"), lax.axis_index("col")
    core, z = col & 1, col >> 1

    def row_step(x, step):
        return exchange(x, n_row, n_col, (1 << step, 1 << (row_bits - 1 - step)), (0, 0))

    def z_step(x, step):
        return exchange(x, n_row, n_col, (0, 0), (1 << step, 1 << (z_bits - 1 - step)))

    def dot(a, b, dims):
        return lax.dot_general(a, b, (dims, ((), ())), preferred_element_type=FP)

    def place(q):
        return row ^ jnp.where(core == 0, q, reversed_bits(q, row_bits))

    here = [features]
    for q in range(1, n_row):
        here.append(exchange(features, n_row, n_col, (q, reversed_bits(q, row_bits)), (0, 0)))
    there = [swap_cores(features, n_row, n_col), swap_cores(jnp.concatenate(here[1:], axis=0), n_row, n_col)]
    near, far = build(tile_vals, tile_row, tile_col, tile_count, n_row, n_col)
    far = swap_cores(far, n_row, n_col)
    onehot = (node_type[:, None] == jnp.arange(TYPES, dtype=jnp.int32)[None, :]).astype(FP)
    gains = jnp.dot(onehot, type_gain, precision=lax.Precision.HIGHEST)

    mid = near.shape[0] // 2
    here, there = jnp.concatenate(here + here, axis=0), jnp.concatenate(there + there, axis=0)
    sent = rounded(dot(near[mid:], here, ((1,), (0,))) + dot(far[mid:], there, ((1,), (0,))))
    total = dot(near[:mid], here, ((1,), (0,))) + dot(far[:mid], there, ((1,), (0,)))
    for step in reversed(range(z_bits)):
        came = z_step(sent, step)
        if step:
            sent, total = added(total, came, True, ())
    aggregate, mine, away, activated, grad_hidden = node_values(total, came, gains, w_in, w_out, cotangent)

    met = swap_cores(away, n_row, n_col)
    node_rows = node_gradients(grad_hidden, w_in, aggregate, gains, cotangent, onehot.T)
    parts = 2
    sent = list(weight_blocks(mine, met, range(n_row // 2, n_row), n_row, parts, BF))
    *sums, node_rows = weight_blocks(mine, met, range(n_row // 2), n_row, parts, FP, (node_rows,))

    grad_rows, gain = node_rows[:TILE], node_rows[TILE:]
    for step in range(z_bits):
        came = z_step(jnp.concatenate([grad_rows, gain], axis=0), step)
        size = grad_rows.shape[0]
        grad_rows = jnp.concatenate([grad_rows, came[:size]], axis=0)
        gain = split(whole(gain) + whole(came[size:]))
    own = n_row * TILE
    came = swap_cores(rounded(dot(far[:, :own], grad_rows, ((0,), (0,)))), n_row, n_col)
    low = dot(near[:, :own], grad_rows, ((0,), (0,))) + came.astype(FP)
    for step in reversed(range(row_bits)):
        size = low.shape[0] // 2
        came = row_step(jnp.concatenate([rounded(low[size:]), gain], axis=0), step)
        gain = split(whole(gain) + whole(came[size:]))
        low = low[:size] + came[:size].astype(FP)
    grad_x = low

    mixed = None
    for step in reversed(range(row_bits)):
        for i in range(parts):
            mid = sums[i].shape[0] // 2
            came = row_step(sent[i], step)
            if mixed is None:
                mixed = mix(aggregate, activated, w_out, came)
            sums[i] = sums[i] + came.astype(FP)
            if step:
                sums[i], sent[i] = sums[i][:mid], rounded(sums[i][mid:])
    for step in range(z_bits):
        for i in range(parts):
            held = rounded(sums[i])
            sums[i] = held.astype(FP) + z_step(held, step).astype(FP)
    sent = [rounded(x) for x in sums]
    for step in range(row_bits - 1):
        for i in range(parts):
            sent[i] = jnp.concatenate([sent[i], row_step(sent[i], step)], axis=0)
    came = [row_step(x, row_bits - 1) for x in sent]

    factor = float(total_nodes) ** (-0.5)
    others = [swap_cores(x, n_row, n_col) for x in sent]
    weights = write_weights(sent, others, [], [], 0, n_row, factor)
    others = [swap_cores(x, n_row, n_col) for x in came]
    grad_w_in, grad_w_out, grad_gain = write_weights(
        came, others, weights, [gain, swap_cores(gain, n_row, n_col)], n_row // 2, n_row, factor
    )
    return mixed, grad_x, grad_w_in, grad_w_out, grad_gain


def solution(mesh):
    return jax.shard_map(
        shards,
        mesh=mesh,
        in_specs=(
            P(("col", "row"), None),
            P("row", "col", None, None),
            P("row", "col"),
            P("row", "col"),
            P("row", "col"),
            P(("row", "col")),
            P(),
            P(),
            P(),
            P(("row", "col"), None),
        ),
        out_specs=(P(("row", "col"), None), P(("col", "row"), None), P(), P(), P()),
        check_vma=False,
    )
```

time: 91.6 us -> 84.5 us (0.922); the launches traced: 91 us -> 83 us
  Pallas kernels: 4.55 us -> 10 us
  matrix products: 7.21 us -> 2.97 us
  starting transfers between devices: 36.9 us -> 32.8 us
  local copies, waits for them, and re-layouts: 4.12 us -> 0.24 us
  other arithmetic: 3.27 us -> 1.46 us
    pallas_call x1 -> x7, Pallas kernels: 1.69 us -> 6.56 us  [the longest x1 2.74 us: build(): pl.pallas_call(kernel, out_shape=(result, result), in_specs=[pl.BlockSpec...]
    ppermute x20 -> x21, starting transfers between devices: 35.3 us -> 31.2 us  [exchange(): return lax.ppermute(x, AXES, pairs)]
    unnamed x33 -> x22, local copies, waits for them, and re-layouts: 4.01 us -> 0.16 us
    dot_general x14 -> x6, matrix products: 5.24 us -> 2.67 us  [dot(): return lax.dot_general(a, b, (dims, ((), ())), preferred_element_type=FP)]
    dot_general x3 -> x0, matrix products: 1.64 us -> none  [the longest x1 0.97 us: shards(): branch = jnp.dot(activated, w_out, preferred_element_type=FP)]
    ppermute x20 -> x21, waiting for transfers between devices: 30.6 us -> 31 us  [exchange(): return lax.ppermute(x, AXES, pairs)]
    ppermute x11 -> x10, waiting for transfers between devices: 2.32 us -> 2.61 us  [swap_cores(): return lax.ppermute(x, AXES, [(i, i ^ 1) for i in range(rows * cols)])]
  transfers between devices with their start and end apart: 31 -> 31, of which waited for: 17 -> 17; matrix products, arithmetic and copies ran while one was open for 8% -> 5% of each run, Pallas kernels for 3% -> 8%
where the time goes in v3:
time: 84.5 us; the launch traced here: 83 us
  waiting for transfers between devices  33.6 us (40%)
  starting transfers between devices  32.8 us (39%)
  Pallas kernels  10 us (12%)
  matrix products  2.97 us (4%)
  between operations  1.83 us (2%)
  other arithmetic  1.46 us (2%)
    ppermute x21, starting transfers between devices, exchange(): return lax.ppermute(x, AXES, pairs)  31.2 us
    ppermute x21, waiting for transfers between devices, exchange(): return lax.ppermute(x, AXES, pairs)  31 us
    pallas_call x2, Pallas kernels, write_weights(): pl.pallas_call(kernel, out_shape=(jax.ShapeDtypeStruct((F, 2 * F), FP), j...  3.47 us
    pallas_call x1, Pallas kernels, build(): pl.pallas_call(kernel, out_shape=(result, result), in_specs=[pl.BlockSpec...  2.74 us
    dot_general x6, matrix products, dot(): return lax.dot_general(a, b, (dims, ((), ())), preferred_element_type=FP)  2.67 us
    ppermute x10, waiting for transfers between devices, swap_cores(): return lax.ppermute(x, AXES, [(i, i ^ 1) for i in range(rows * cols)])  2.61 us
  transfers between devices with their start and end apart: 31, of which 17 were waited for; matrix products, arithmetic and copies ran while one was open for 5% of the time, Pallas kernels for 8%

profile of v3, /device:TPU:0, one launch (start us, length us, event | category | flops | bytes accessed | tf_op | source)
XLA Modules:
  0.0 83.0 jit_solution(7809368193516285110)
XLA Ops:
  0.6 4.0 %collective-permute-start.2 = (bf16[128,512]{1,0:T(8,128)(2,1)}, bf16[128,512]{1,0:T(8,128)(2,1)S(1)}, u32[]{:S(2)}, u32[]{:S(2)}) collective-permute-start(bf16[128,512]{1,0:T(8,128)(2,1)} %param.10), channel_id=1, source_target_pairs={{0,24},{1,25},{2,26},{3,27},{4,28},{5,29},{6,30},{7,31},{8,16},{9,... | collective-permute-start | bytes 393224 | tf_op jit(solution)/shard_map/ppermute | solution.py:30
  4.6 0.5 collective-permute-start.1
  5.1 0.1 collective-permute-start
  5.9 2.7 %build_dense.1 = (bf16[512,1024]{1,0:T(8,128)(2,1)S(1)}, bf16[512,1024]{1,0:T(8,128)(2,1)S(1)}) custom-call(s32[1,1]{1,0:T(1,128)S(6)} %copy.31.count_ref, s32[1,128]{1,0:T(1,128)} %rows_ref.1, s32[1,128]{1,0:T(1,128)} %cols_ref.1, bf16[1,128,128,128]{3,2,1,0:T(8,128)(2,1)} %vals_ref.1), custom_call_target="tpu_custom_call" | custom-call | flops 2097152 | bytes 6291456 | tf_op jit(solution)/shard_map/build_dense/pallas_call | solution.py:105
  8.7 0.6 collective-permute-start.3
  9.3 1.9 %collective-permute-done.1 = bf16[128,512]{1,0:T(8,128)(2,1)S(1)} collective-permute-done((bf16[128,512]{1,0:T(8,128)(2,1)}, bf16[128,512]{1,0:T(8,128)(2,1)S(1)}, u32[]{:S(2)}, u32[]{:S(2)}) %collective-permute-start.1) | collective-permute-done | bytes 131104 | tf_op jit(solution)/shard_map/ppermute | solution.py:30
  11.1 0.2 collective-permute-done
  11.4 0.1 collective-permute-start.5
  11.6 1.5 %collective-permute-done.5 = bf16[384,512]{1,0:T(8,128)(2,1)S(1)} collective-permute-done((bf16[384,512]{1,0:T(8,128)(2,1)S(1)}, bf16[384,512]{1,0:T(8,128)(2,1)S(1)}, u32[]{:S(2)}, u32[]{:S(2)}) %collective-permute-start.5) | collective-permute-done | bytes 393248 | tf_op jit(solution)/shard_map/ppermute | solution.py:34
  13.3 0.4 fusion.5
  13.7 0.4 fusion.2
  14.2 2.7 %collective-permute-start.6 = (bf16[256,512]{1,0:T(8,128)(2,1)S(1)}, bf16[256,512]{1,0:T(8,128)(2,1)S(1)}, u32[]{:S(2)}, u32[]{:S(2)}) collective-permute-start(bf16[256,512]{1,0:T(8,128)(2,1)S(1)} %fusion.2), channel_id=1, source_target_pairs={{0,4},{1,3},{2,6},{3,1},{4,0},{5,7},{6,2},{7,5},{8,12},{9,11},{10,... | collective-permute-start | bytes 786440 | tf_op jit(solution)/shard_map/ppermute | solution.py:30
  16.8 0.4 fusion.7
  17.3 0.4 convolution_add_fusion.2.refs_0_
  17.7 5.7 %collective-permute-done.6.refs_1_ = bf16[256,512]{1,0:T(8,128)(2,1)S(1)} collective-permute-done((bf16[256,512]{1,0:T(8,128)(2,1)S(1)}, bf16[256,512]{1,0:T(8,128)(2,1)S(1)}, u32[]{:S(2)}, u32[]{:S(2)}) %collective-permute-start.6) | collective-permute-done | bytes 262176 | tf_op jit(solution)/shard_map/ppermute | solution.py:30
  23.5 1.8 %collective-permute-start.7 = (bf16[128,512]{1,0:T(8,128)(2,1)S(1)}, bf16[128,512]{1,0:T(8,128)(2,1)S(1)}, u32[]{:S(2)}, u32[]{:S(2)}) collective-permute-start(bf16[128,512]{1,0:T(8,128)(2,1)S(1)} %get-tuple-element.27), channel_id=1, source_target_pairs={{0,2},{1,5},{2,0},{3,7},{4,6},{5,1},{6,4},{7,3},{8,10},{9,13},{10,... | collective-permute-start | bytes 393224 | tf_op jit(solution)/shard_map/ppermute | solution.py:30
  25.3 0.3 fusion.19.refs_2_.gains_ref
  25.6 4.0 %collective-permute-done.7.refs_1_ = bf16[128,512]{1,0:T(8,128)(2,1)S(1)} collective-permute-done((bf16[128,512]{1,0:T(8,128)(2,1)S(1)}, bf16[128,512]{1,0:T(8,128)(2,1)S(1)}, u32[]{:S(2)}, u32[]{:S(2)}) %collective-permute-start.7) | collective-permute-done | bytes 131104 | tf_op jit(solution)/shard_map/ppermute | solution.py:30
  29.6 0.8 node_values.1
  30.4 0.1 collective-permute-start.8
  30.5 0.8 node_gradients.1.refs_0_
  31.3 0.9 %collective-permute-done.8.met_ref = bf16[128,1536]{1,0:T(8,128)(2,1)S(1)} collective-permute-done((bf16[128,1536]{1,0:T(8,128)(2,1)S(1)}, bf16[128,1536]{1,0:T(8,128)(2,1)S(1)}, u32[]{:S(2)}, u32[]{:S(2)}) %collective-permute-start.8) | collective-permute-done | bytes 393248 | tf_op jit(solution)/shard_map/ppermute | solution.py:34
  32.2 0.6 weight_blocks.3
  32.9 0.7 collective-permute-start.10
  33.6 0.7 weight_blocks.2
  34.2 1.5 %collective-permute-start.9 = (bf16[512,256]{1,0:T(8,128)(2,1)S(1)}, bf16[512,256]{1,0:T(8,128)(2,1)S(1)}, u32[]{:S(2)}, u32[]{:S(2)}) collective-permute-start(bf16[512,256]{1,0:T(8,128)(2,1)S(1)} %get-tuple-element.32), channel_id=1, source_target_pairs={{0,16},{1,9},{2,18},{3,11},{4,20},{5,13},{6,22},{7,15},{8,24},{9,1... | collective-permute-start | bytes 786440 | tf_op jit(solution)/shard_map/ppermute | solution.py:30
  35.7 0.6 collective-permute-start.20
  36.3 3.4 %collective-permute-done.10 = bf16[144,512]{1,0:T(8,128)(2,1)S(1)} collective-permute-done((bf16[144,512]{1,0:T(8,128)(2,1)S(1)}, bf16[144,512]{1,0:T(8,128)(2,1)S(1)}, u32[]{:S(2)}, u32[]{:S(2)}) %collective-permute-start.10) | collective-permute-done | bytes 147488 | tf_op jit(solution)/shard_map/ppermute | solution.py:30
  39.7 1.5 %collective-permute-start.11 = (bf16[272,512]{1,0:T(8,128)(2,1)S(1)}, bf16[272,512]{1,0:T(8,128)(2,1)S(1)}, u32[]{:S(2)}, u32[]{:S(2)}) collective-permute-start(bf16[272,512]{1,0:T(8,128)(2,1)S(1)} %pad_maximum_fusion.2), channel_id=1, source_target_pairs={{0,4},{1,3},{2,6},{3,1},{4,0},{5,7},{6,2},{7,5},{8,12},{9,11},{10,... | collective-permute-start | bytes 835592 | tf_op jit(solution)/shard_map/ppermute | solution.py:30
  41.3 0.1 convert_add_fusion.1
  41.4 1.5 %collective-permute-start.15 = (bf16[256,256]{1,0:T(8,128)(2,1)S(1)}, bf16[256,256]{1,0:T(8,128)(2,1)S(1)}, u32[]{:S(2)}, u32[]{:S(2)}) collective-permute-start(bf16[256,256]{1,0:T(8,128)(2,1)S(1)} %fusion.15), channel_id=1, source_target_pairs={{0,8},{1,17},{2,10},{3,19},{4,12},{5,21},{6,14},{7,23},{8,0},{9,25... | collective-permute-start | bytes 393224 | tf_op jit(solution)/shard_map/ppermute | solution.py:30
  42.9 0.6 collective-permute-done.20
  43.5 0.1 convert_add_fusion
  43.6 1.5 %collective-permute-start.21 = (bf16[256,256]{1,0:T(8,128)(2,1)S(1)}, bf16[256,256]{1,0:T(8,128)(2,1)S(1)}, u32[]{:S(2)}, u32[]{:S(2)}) collective-permute-start(bf16[256,256]{1,0:T(8,128)(2,1)S(1)} %fusion.12), channel_id=1, source_target_pairs={{0,8},{1,17},{2,10},{3,19},{4,12},{5,21},{6,14},{7,23},{8,0},{9,25... | collective-permute-start | bytes 393224 | tf_op jit(solution)/shard_map/ppermute | solution.py:30
  45.1 1.3 %collective-permute-done.15 = bf16[256,256]{1,0:T(8,128)(2,1)S(1)} collective-permute-done((bf16[256,256]{1,0:T(8,128)(2,1)S(1)}, bf16[256,256]{1,0:T(8,128)(2,1)S(1)}, u32[]{:S(2)}, u32[]{:S(2)}) %collective-permute-start.15) | collective-permute-done | bytes 131104 | tf_op jit(solution)/shard_map/ppermute | solution.py:30
  46.4 2.5 %collective-permute-start.16 = (bf16[256,256]{1,0:T(8,128)(2,1)S(1)}, bf16[256,256]{1,0:T(8,128)(2,1)S(1)}, u32[]{:S(2)}, u32[]{:S(2)}) collective-permute-start(bf16[256,256]{1,0:T(8,128)(2,1)S(1)} %fusion.17), channel_id=1, source_target_pairs={{0,2},{1,5},{2,0},{3,7},{4,6},{5,1},{6,4},{7,3},{8,10},{9,13},{10,... | collective-permute-start | bytes 393224 | tf_op jit(solution)/shard_map/ppermute | solution.py:30
  49.0 1.6 %collective-permute-start.22 = (bf16[256,256]{1,0:T(8,128)(2,1)S(1)}, bf16[256,256]{1,0:T(8,128)(2,1)S(1)}, u32[]{:S(2)}, u32[]{:S(2)}) collective-permute-start(bf16[256,256]{1,0:T(8,128)(2,1)S(1)} %fusion.14), channel_id=1, source_target_pairs={{0,2},{1,5},{2,0},{3,7},{4,6},{5,1},{6,4},{7,3},{8,10},{9,13},{10,... | collective-permute-start | bytes 393224 | tf_op jit(solution)/shard_map/ppermute | solution.py:30
  50.6 1.7 %collective-permute-done.11 = bf16[272,512]{1,0:T(8,128)(2,1)S(1)} collective-permute-done((bf16[272,512]{1,0:T(8,128)(2,1)S(1)}, bf16[272,512]{1,0:T(8,128)(2,1)S(1)}, u32[]{:S(2)}, u32[]{:S(2)}) %collective-permute-start.11) | collective-permute-done | bytes 278560 | tf_op jit(solution)/shard_map/ppermute | solution.py:30
  52.3 0.5 fusion
  52.7 0.1 collective-permute-start.12
  52.9 0.4 collective-permute-done.16
  53.3 1.8 %collective-permute-start.17 = (bf16[256,256]{1,0:T(8,128)(2,1)S(1)}, bf16[256,256]{1,0:T(8,128)(2,1)S(1)}, u32[]{:S(2)}, u32[]{:S(2)}) collective-permute-start(bf16[256,256]{1,0:T(8,128)(2,1)S(1)} %reduce-precision_convert_fusion.3), channel_id=1, source_target_pairs={{0,4},{1,3},{2,6},{3,1},{4,0},{5,7},{6,2},{7,5},{8,12},{9,11},{10,... | collective-permute-start | bytes 393224 | tf_op jit(solution)/shard_map/ppermute | solution.py:30
  55.1 0.9 %collective-permute-done.22 = bf16[256,256]{1,0:T(8,128)(2,1)S(1)} collective-permute-done((bf16[256,256]{1,0:T(8,128)(2,1)S(1)}, bf16[256,256]{1,0:T(8,128)(2,1)S(1)}, u32[]{:S(2)}, u32[]{:S(2)}) %collective-permute-start.22) | collective-permute-done | bytes 131104 | tf_op jit(solution)/shard_map/ppermute | solution.py:30
  56.0 1.9 %collective-permute-start.23 = (bf16[256,256]{1,0:T(8,128)(2,1)S(1)}, bf16[256,256]{1,0:T(8,128)(2,1)S(1)}, u32[]{:S(2)}, u32[]{:S(2)}) collective-permute-start(bf16[256,256]{1,0:T(8,128)(2,1)S(1)} %reduce-precision_convert_fusion.1), channel_id=1, source_target_pairs={{0,4},{1,3},{2,6},{3,1},{4,0},{5,7},{6,2},{7,5},{8,12},{9,11},{10,... | collective-permute-start | bytes 393224 | tf_op jit(solution)/shard_map/ppermute | solution.py:30
  57.9 1.4 %collective-permute-done.17 = bf16[256,256]{1,0:T(8,128)(2,1)S(1)} collective-permute-done((bf16[256,256]{1,0:T(8,128)(2,1)S(1)}, bf16[256,256]{1,0:T(8,128)(2,1)S(1)}, u32[]{:S(2)}, u32[]{:S(2)}) %collective-permute-start.17) | collective-permute-done | bytes 131104 | tf_op jit(solution)/shard_map/ppermute | solution.py:30
  59.4 1.5 %collective-permute-start.18 = (bf16[256,256]{1,0:T(8,128)(2,1)S(1)}, bf16[256,256]{1,0:T(8,128)(2,1)S(1)}, u32[]{:S(2)}, u32[]{:S(2)}) collective-permute-start(bf16[256,256]{1,0:T(8,128)(2,1)S(1)} %reduce-precision_convert_fusion.2), channel_id=1, source_target_pairs={{0,8},{1,17},{2,10},{3,19},{4,12},{5,21},{6,14},{7,23},{8,0},{9,25... | collective-permute-start | bytes 393224 | tf_op jit(solution)/shard_map/ppermute | solution.py:30
  60.9 2.2 %collective-permute-done.23 = bf16[256,256]{1,0:T(8,128)(2,1)S(1)} collective-permute-done((bf16[256,256]{1,0:T(8,128)(2,1)S(1)}, bf16[256,256]{1,0:T(8,128)(2,1)S(1)}, u32[]{:S(2)}, u32[]{:S(2)}) %collective-permute-start.23) | collective-permute-done | bytes 131104 | tf_op jit(solution)/shard_map/ppermute | solution.py:30
  63.1 0.5 collective-permute-start.24
  63.7 0.5 convolution_add_fusion
  64.2 1.5 %collective-permute-start.13 = (bf16[272,512]{1,0:T(8,128)(2,1)S(1)}, bf16[272,512]{1,0:T(8,128)(2,1)S(1)}, u32[]{:S(2)}, u32[]{:S(2)}) collective-permute-start(bf16[272,512]{1,0:T(8,128)(2,1)S(1)} %pad_maximum_fusion.3), channel_id=1, source_target_pairs={{0,16},{1,9},{2,18},{3,11},{4,20},{5,13},{6,22},{7,15},{8,24},{9,1... | collective-permute-start | bytes 835592 | tf_op jit(solution)/shard_map/ppermute | solution.py:30
  65.8 0.1 collective-permute-start.28
  65.8 0.6 collective-permute-start.19
  66.5 3.1 %collective-permute-done.24 = bf16[256,256]{1,0:T(8,128)(2,1)S(1)} collective-permute-done((bf16[256,256]{1,0:T(8,128)(2,1)S(1)}, bf16[256,256]{1,0:T(8,128)(2,1)S(1)}, u32[]{:S(2)}, u32[]{:S(2)}) %collective-permute-start.24) | collective-permute-done | bytes 131104 | tf_op jit(solution)/shard_map/ppermute | solution.py:30
  69.6 0.1 collective-permute-start.29
  69.7 1.6 %collective-permute-start.25 = (bf16[512,256]{1,0:T(8,128)(2,1)S(1)}, bf16[512,256]{1,0:T(8,128)(2,1)S(1)}, u32[]{:S(2)}, u32[]{:S(2)}) collective-permute-start(bf16[512,256]{1,0:T(8,128)(2,1)S(1)} %pad_maximum_fusion.5.refs_1_), channel_id=1, source_target_pairs={{0,16},{1,9},{2,18},{3,11},{4,20},{5,13},{6,22},{7,15},{8,24},{9,1... | collective-permute-start | bytes 786440 | tf_op jit(solution)/shard_map/ppermute | solution.py:30
  71.4 1.2 %collective-permute-start.14 = (bf16[144,512]{1,0:T(8,128)(2,1)S(1)}, bf16[144,512]{1,0:T(8,128)(2,1)S(1)}, u32[]{:S(2)}, u32[]{:S(2)}) collective-permute-start(bf16[144,512]{1,0:T(8,128)(2,1)S(1)} %pad_maximum_fusion.8), channel_id=1, source_target_pairs={{0,8},{1,17},{2,10},{3,19},{4,12},{5,21},{6,14},{7,23},{8,0},{9,25... | collective-permute-start | bytes 442376 | tf_op jit(solution)/shard_map/ppermute | solution.py:30
  72.6 1.0 %mix.1 = bf16[128,512]{1,0:T(8,128)(2,1)} custom-call(f32[128,512]{1,0:T(8,128)S(1)} %get-tuple-element.28.agg_ref, bf16[128,1024]{1,0:T(8,128)(2,1)S(1)} %get-tuple-element.29.act_ref, bf16[1024,512]{1,0:T(8,128)(2,1)S(1)} %copy-done.2, bf16[512,256]{1,0:T(8,128)(2,1)S(1)} %collective-permute-done.9.after_ref), custom_call_target="tpu_custom_call" | custom-call | tf_op jit(solution)/shard_map/mix/pallas_call | solution.py:287
  73.6 0.1 collective-permute-start.26
  73.7 4.3 %collective-permute-done.25.refs_1_ = bf16[512,256]{1,0:T(8,128)(2,1)S(1)} collective-permute-done((bf16[512,256]{1,0:T(8,128)(2,1)S(1)}, bf16[512,256]{1,0:T(8,128)(2,1)S(1)}, u32[]{:S(2)}, u32[]{:S(2)}) %collective-permute-start.25) | collective-permute-done | bytes 262176 | tf_op jit(solution)/shard_map/ppermute | solution.py:30
  78.0 1.4 %write_weights.2 = (f32[512,1024]{1,0:T(8,128)}, f32[1024,512]{1,0:T(8,128)}) custom-call(bf16[512,256]{1,0:T(8,128)(2,1)S(1)} %pad_maximum_fusion.4.refs_0_, bf16[512,256]{1,0:T(8,128)(2,1)S(1)} %pad_maximum_fusion.5.refs_1_, bf16[512,256]{1,0:T(8,128)(2,1)S(1)} %collective-permute-done.28.refs_2_, bf16[512,256]{1,0:T(8,128)(2,1)S(1)} %collective-permute-done.29.refs_3_), custom_call_target="tpu_custom_call" | custom-call | flops 1048576 | bytes 3145728 | tf_op jit(solution)/shard_map/write_weights/pallas_call | solution.py:173
  79.6 0.6 collective-permute-start.30
  80.1 0.7 slice_add_fusion.3
  80.8 0.1 collective-permute-done.30.refs_7_
  80.9 2.0 %write_weights.3 = (f32[512,1024]{1,0:T(8,128)}, f32[1024,512]{1,0:T(8,128)}, f32[8,512]{1,0:T(8,128)}) custom-call(bf16[512,256]{1,0:T(8,128)(2,1)S(1)} %collective-permute-done.19.refs_0_, bf16[512,256]{1,0:T(8,128)(2,1)S(1)} %collective-permute-done.25.refs_1_, ...), custom_call_target="tpu_custom_call", output_to_operand_aliasing={{0}: (4, {}), {1}: (5, {})} | custom-call | flops 1048576 | bytes 3145728 | tf_op jit(solution)/shard_map/write_weights/pallas_call | solution.py:173
  (79 shorter events, 0.9 us)
Async XLA Ops:
  0.6 24.7 %copy-start = (f32[8,512]{1,0:T(8,128)S(1)}, f32[8,512]{1,0:T(8,128)}, u32[]{:S(2)}) copy-start(f32[8,512]{1,0:T(8,128)} %param.16) | copy-start | bytes 49156
  0.6 8.6 %collective-permute-start.2 = (bf16[128,512]{1,0:T(8,128)(2,1)}, bf16[128,512]{1,0:T(8,128)(2,1)S(1)}, u32[]{:S(2)}, u32[]{:S(2)}) collective-permute-start(bf16[128,512]{1,0:T(8,128)(2,1)} %param.10), channel_id=1, source_target_pairs={{0,24},{1,25},{2,26},{3,27},{4,28},{5,29},{6,30},{7,31},{8,16},{9,... | collective-permute-start | bytes 393224 | tf_op jit(solution)/shard_map/ppermute | solution.py:30
  4.6 6.5 %collective-permute-start.1 = (bf16[128,512]{1,0:T(8,128)(2,1)}, bf16[128,512]{1,0:T(8,128)(2,1)S(1)}, u32[]{:S(2)}, u32[]{:S(2)}) collective-permute-start(bf16[128,512]{1,0:T(8,128)(2,1)} %param.10), channel_id=1, source_target_pairs={{0,16},{1,9},{2,18},{3,11},{4,20},{5,13},{6,22},{7,15},{8,24},{9,1... | collective-permute-start | bytes 393224 | tf_op jit(solution)/shard_map/ppermute | solution.py:30
  5.1 6.3 %collective-permute-start = (bf16[128,512]{1,0:T(8,128)(2,1)}, bf16[128,512]{1,0:T(8,128)(2,1)S(1)}, u32[]{:S(2)}, u32[]{:S(2)}) collective-permute-start(bf16[128,512]{1,0:T(8,128)(2,1)} %param.10), channel_id=1, source_target_pairs={{0,8},{1,17},{2,10},{3,19},{4,12},{5,21},{6,14},{7,23},{8,0},{9,25... | collective-permute-start | bytes 393224 | tf_op jit(solution)/shard_map/ppermute | solution.py:30
  5.3 6.3 %collective-permute-start.4 = (bf16[128,512]{1,0:T(8,128)(2,1)}, bf16[128,512]{1,0:T(8,128)(2,1)S(1)}, u32[]{:S(2)}, u32[]{:S(2)}) collective-permute-start(bf16[128,512]{1,0:T(8,128)(2,1)} %param.10), channel_id=1, source_target_pairs={{0,1},{1,0},{2,3},{3,2},{4,5},{5,4},{6,7},{7,6},{8,9},{9,8},{10,11... | collective-permute-start | bytes 393224 | tf_op jit(solution)/shard_map/ppermute | solution.py:34
  5.9 3.3 %copy-start.4 = (bf16[128,512]{1,0:T(8,128)(2,1)S(1)}, bf16[128,512]{1,0:T(8,128)(2,1)}, u32[]{:S(2)}) copy-start(bf16[128,512]{1,0:T(8,128)(2,1)} %param.10) | copy-start | bytes 393220
  8.7 4.6 %collective-permute-start.3 = (bf16[512,1024]{1,0:T(8,128)(2,1)S(1)}, bf16[512,1024]{1,0:T(8,128)(2,1)S(1)}, u32[]{:S(2)}, u32[]{:S(2)}) collective-permute-start(bf16[512,1024]{1,0:T(8,128)(2,1)S(1)} %get-tuple-element.25), channel_id=1, source_target_pairs={{0,1},{1,0},{2,3},{3,2},{4,5},{5,4},{6,7},{7,6},{8,9},{9,8},{10,11... | collective-permute-start | bytes 3145736 | tf_op jit(solution)/shard_map/ppermute | solution.py:34
  11.4 1.8 %collective-permute-start.5 = (bf16[384,512]{1,0:T(8,128)(2,1)S(1)}, bf16[384,512]{1,0:T(8,128)(2,1)S(1)}, u32[]{:S(2)}, u32[]{:S(2)}) collective-permute-start(bf16[384,512]{1,0:T(8,128)(2,1)S(1)} %pad_maximum_fusion.1), channel_id=1, source_target_pairs={{0,1},{1,0},{2,3},{3,2},{4,5},{5,4},{6,7},{7,6},{8,9},{9,8},{10,11... | collective-permute-start | bytes 1179656 | tf_op jit(solution)/shard_map/ppermute | solution.py:34
  14.2 9.3 %collective-permute-start.6 = (bf16[256,512]{1,0:T(8,128)(2,1)S(1)}, bf16[256,512]{1,0:T(8,128)(2,1)S(1)}, u32[]{:S(2)}, u32[]{:S(2)}) collective-permute-start(bf16[256,512]{1,0:T(8,128)(2,1)S(1)} %fusion.2), channel_id=1, source_target_pairs={{0,4},{1,3},{2,6},{3,1},{4,0},{5,7},{6,2},{7,5},{8,12},{9,11},{10,... | collective-permute-start | bytes 786440 | tf_op jit(solution)/shard_map/ppermute | solution.py:30
  17.3 8.0 %copy-start.5 = (s32[128]{0:T(128)S(1)}, s32[128]{0:T(128)}, u32[]{:S(2)}) copy-start(s32[128]{0:T(128)} %param.15) | copy-start | bytes 1540
  17.3 12.4 %copy-start.1 = (bf16[512,1024]{1,0:T(8,128)(2,1)S(1)}, bf16[512,1024]{1,0:T(8,128)(2,1)}, u32[]{:S(2)}) copy-start(bf16[512,1024]{1,0:T(8,128)(2,1)} %w_ref.3) | copy-start | bytes 3145732
  17.3 12.4 %copy-start.2 = (bf16[1024,512]{1,0:T(8,128)(2,1)S(1)}, bf16[1024,512]{1,0:T(8,128)(2,1)}, u32[]{:S(2)}) copy-start(bf16[1024,512]{1,0:T(8,128)(2,1)} %w_ref.2) | copy-start | bytes 3145732
  17.3 12.4 %copy-start.3 = (bf16[128,512]{1,0:T(8,128)(2,1)S(1)}, bf16[128,512]{1,0:T(8,128)(2,1)}, u32[]{:S(2)}) copy-start(bf16[128,512]{1,0:T(8,128)(2,1)} %cot_ref.1) | copy-start | bytes 393220
  23.5 6.2 %collective-permute-start.7 = (bf16[128,512]{1,0:T(8,128)(2,1)S(1)}, bf16[128,512]{1,0:T(8,128)(2,1)S(1)}, u32[]{:S(2)}, u32[]{:S(2)}) collective-permute-start(bf16[128,512]{1,0:T(8,128)(2,1)S(1)} %get-tuple-element.27), channel_id=1, source_target_pairs={{0,2},{1,5},{2,0},{3,7},{4,6},{5,1},{6,4},{7,3},{8,10},{9,13},{10,... | collective-permute-start | bytes 393224 | tf_op jit(solution)/shard_map/ppermute | solution.py:30
  30.4 1.8 %collective-permute-start.8 = (bf16[128,1536]{1,0:T(8,128)(2,1)S(1)}, bf16[128,1536]{1,0:T(8,128)(2,1)S(1)}, u32[]{:S(2)}, u32[]{:S(2)}) collective-permute-start(bf16[128,1536]{1,0:T(8,128)(2,1)S(1)} %get-tuple-element.31), channel_id=1, source_target_pairs={{0,1},{1,0},{2,3},{3,2},{4,5},{5,4},{6,7},{7,6},{8,9},{9,8},{10,11... | collective-permute-start | bytes 1179656 | tf_op jit(solution)/shard_map/ppermute | solution.py:34
  32.9 6.8 %collective-permute-start.10 = (bf16[144,512]{1,0:T(8,128)(2,1)S(1)}, bf16[144,512]{1,0:T(8,128)(2,1)S(1)}, u32[]{:S(2)}, u32[]{:S(2)}) collective-permute-start(bf16[144,512]{1,0:T(8,128)(2,1)S(1)} %get-tuple-element.34), channel_id=1, source_target_pairs={{0,2},{1,5},{2,0},{3,7},{4,6},{5,1},{6,4},{7,3},{8,10},{9,13},{10,... | collective-permute-start | bytes 442376 | tf_op jit(solution)/shard_map/ppermute | solution.py:30
  34.2 7.1 %collective-permute-start.9 = (bf16[512,256]{1,0:T(8,128)(2,1)S(1)}, bf16[512,256]{1,0:T(8,128)(2,1)S(1)}, u32[]{:S(2)}, u32[]{:S(2)}) collective-permute-start(bf16[512,256]{1,0:T(8,128)(2,1)S(1)} %get-tuple-element.32), channel_id=1, source_target_pairs={{0,16},{1,9},{2,18},{3,11},{4,20},{5,13},{6,22},{7,15},{8,24},{9,1... | collective-permute-start | bytes 786440 | tf_op jit(solution)/shard_map/ppermute | solution.py:30
  35.7 7.7 %collective-permute-start.20 = (bf16[512,256]{1,0:T(8,128)(2,1)S(1)}, bf16[512,256]{1,0:T(8,128)(2,1)S(1)}, u32[]{:S(2)}, u32[]{:S(2)}) collective-permute-start(bf16[512,256]{1,0:T(8,128)(2,1)S(1)} %get-tuple-element.37), channel_id=1, source_target_pairs={{0,16},{1,9},{2,18},{3,11},{4,20},{5,13},{6,22},{7,15},{8,24},{9,1... | collective-permute-start | bytes 786440 | tf_op jit(solution)/shard_map/ppermute | solution.py:30
  39.7 12.5 %collective-permute-start.11 = (bf16[272,512]{1,0:T(8,128)(2,1)S(1)}, bf16[272,512]{1,0:T(8,128)(2,1)S(1)}, u32[]{:S(2)}, u32[]{:S(2)}) collective-permute-start(bf16[272,512]{1,0:T(8,128)(2,1)S(1)} %pad_maximum_fusion.2), channel_id=1, source_target_pairs={{0,4},{1,3},{2,6},{3,1},{4,0},{5,7},{6,2},{7,5},{8,12},{9,11},{10,... | collective-permute-start | bytes 835592 | tf_op jit(solution)/shard_map/ppermute | solution.py:30
  41.4 5.0 %collective-permute-start.15 = (bf16[256,256]{1,0:T(8,128)(2,1)S(1)}, bf16[256,256]{1,0:T(8,128)(2,1)S(1)}, u32[]{:S(2)}, u32[]{:S(2)}) collective-permute-start(bf16[256,256]{1,0:T(8,128)(2,1)S(1)} %fusion.15), channel_id=1, source_target_pairs={{0,8},{1,17},{2,10},{3,19},{4,12},{5,21},{6,14},{7,23},{8,0},{9,25... | collective-permute-start | bytes 393224 | tf_op jit(solution)/shard_map/ppermute | solution.py:30
  43.6 5.4 %collective-permute-start.21 = (bf16[256,256]{1,0:T(8,128)(2,1)S(1)}, bf16[256,256]{1,0:T(8,128)(2,1)S(1)}, u32[]{:S(2)}, u32[]{:S(2)}) collective-permute-start(bf16[256,256]{1,0:T(8,128)(2,1)S(1)} %fusion.12), channel_id=1, source_target_pairs={{0,8},{1,17},{2,10},{3,19},{4,12},{5,21},{6,14},{7,23},{8,0},{9,25... | collective-permute-start | bytes 393224 | tf_op jit(solution)/shard_map/ppermute | solution.py:30
  46.4 6.8 %collective-permute-start.16 = (bf16[256,256]{1,0:T(8,128)(2,1)S(1)}, bf16[256,256]{1,0:T(8,128)(2,1)S(1)}, u32[]{:S(2)}, u32[]{:S(2)}) collective-permute-start(bf16[256,256]{1,0:T(8,128)(2,1)S(1)} %fusion.17), channel_id=1, source_target_pairs={{0,2},{1,5},{2,0},{3,7},{4,6},{5,1},{6,4},{7,3},{8,10},{9,13},{10,... | collective-permute-start | bytes 393224 | tf_op jit(solution)/shard_map/ppermute | solution.py:30
  49.0 7.0 %collective-permute-start.22 = (bf16[256,256]{1,0:T(8,128)(2,1)S(1)}, bf16[256,256]{1,0:T(8,128)(2,1)S(1)}, u32[]{:S(2)}, u32[]{:S(2)}) collective-permute-start(bf16[256,256]{1,0:T(8,128)(2,1)S(1)} %fusion.14), channel_id=1, source_target_pairs={{0,2},{1,5},{2,0},{3,7},{4,6},{5,1},{6,4},{7,3},{8,10},{9,13},{10,... | collective-permute-start | bytes 393224 | tf_op jit(solution)/shard_map/ppermute | solution.py:30
  52.7 10.9 %collective-permute-start.12 = (bf16[512,512]{1,0:T(8,128)(2,1)S(1)}, bf16[512,512]{1,0:T(8,128)(2,1)S(1)}, u32[]{:S(2)}, u32[]{:S(2)}) collective-permute-start(bf16[512,512]{1,0:T(8,128)(2,1)S(1)} %fusion), channel_id=1, source_target_pairs={{0,1},{1,0},{2,3},{3,2},{4,5},{5,4},{6,7},{7,6},{8,9},{9,8},{10,11... | collective-permute-start | bytes 1572872 | tf_op jit(solution)/shard_map/ppermute | solution.py:34
  53.3 6.0 %collective-permute-start.17 = (bf16[256,256]{1,0:T(8,128)(2,1)S(1)}, bf16[256,256]{1,0:T(8,128)(2,1)S(1)}, u32[]{:S(2)}, u32[]{:S(2)}) collective-permute-start(bf16[256,256]{1,0:T(8,128)(2,1)S(1)} %reduce-precision_convert_fusion.3), channel_id=1, source_target_pairs={{0,4},{1,3},{2,6},{3,1},{4,0},{5,7},{6,2},{7,5},{8,12},{9,11},{10,... | collective-permute-start | bytes 393224 | tf_op jit(solution)/shard_map/ppermute | solution.py:30
  56.0 7.1 %collective-permute-start.23 = (bf16[256,256]{1,0:T(8,128)(2,1)S(1)}, bf16[256,256]{1,0:T(8,128)(2,1)S(1)}, u32[]{:S(2)}, u32[]{:S(2)}) collective-permute-start(bf16[256,256]{1,0:T(8,128)(2,1)S(1)} %reduce-precision_convert_fusion.1), channel_id=1, source_target_pairs={{0,4},{1,3},{2,6},{3,1},{4,0},{5,7},{6,2},{7,5},{8,12},{9,11},{10,... | collective-permute-start | bytes 393224 | tf_op jit(solution)/shard_map/ppermute | solution.py:30
  59.4 6.4 %collective-permute-start.18 = (bf16[256,256]{1,0:T(8,128)(2,1)S(1)}, bf16[256,256]{1,0:T(8,128)(2,1)S(1)}, u32[]{:S(2)}, u32[]{:S(2)}) collective-permute-start(bf16[256,256]{1,0:T(8,128)(2,1)S(1)} %reduce-precision_convert_fusion.2), channel_id=1, source_target_pairs={{0,8},{1,17},{2,10},{3,19},{4,12},{5,21},{6,14},{7,23},{8,0},{9,25... | collective-permute-start | bytes 393224 | tf_op jit(solution)/shard_map/ppermute | solution.py:30
  63.1 6.4 %collective-permute-start.24 = (bf16[256,256]{1,0:T(8,128)(2,1)S(1)}, bf16[256,256]{1,0:T(8,128)(2,1)S(1)}, u32[]{:S(2)}, u32[]{:S(2)}) collective-permute-start(bf16[256,256]{1,0:T(8,128)(2,1)S(1)} %reduce-precision_convert_fusion), channel_id=1, source_target_pairs={{0,8},{1,17},{2,10},{3,19},{4,12},{5,21},{6,14},{7,23},{8,0},{9,25... | collective-permute-start | bytes 393224 | tf_op jit(solution)/shard_map/ppermute | solution.py:30
  64.2 7.0 %collective-permute-start.13 = (bf16[272,512]{1,0:T(8,128)(2,1)S(1)}, bf16[272,512]{1,0:T(8,128)(2,1)S(1)}, u32[]{:S(2)}, u32[]{:S(2)}) collective-permute-start(bf16[272,512]{1,0:T(8,128)(2,1)S(1)} %pad_maximum_fusion.3), channel_id=1, source_target_pairs={{0,16},{1,9},{2,18},{3,11},{4,20},{5,13},{6,22},{7,15},{8,24},{9,1... | collective-permute-start | bytes 835592 | tf_op jit(solution)/shard_map/ppermute | solution.py:30
  65.8 12.3 %collective-permute-start.28 = (bf16[512,256]{1,0:T(8,128)(2,1)S(1)}, bf16[512,256]{1,0:T(8,128)(2,1)S(1)}, u32[]{:S(2)}, u32[]{:S(2)}) collective-permute-start(bf16[512,256]{1,0:T(8,128)(2,1)S(1)} %pad_maximum_fusion.4.refs_0_), channel_id=1, source_target_pairs={{0,1},{1,0},{2,3},{3,2},{4,5},{5,4},{6,7},{7,6},{8,9},{9,8},{10,11... | collective-permute-start | bytes 786440 | tf_op jit(solution)/shard_map/ppermute | solution.py:34
  65.8 7.8 %collective-permute-start.19 = (bf16[512,256]{1,0:T(8,128)(2,1)S(1)}, bf16[512,256]{1,0:T(8,128)(2,1)S(1)}, u32[]{:S(2)}, u32[]{:S(2)}) collective-permute-start(bf16[512,256]{1,0:T(8,128)(2,1)S(1)} %pad_maximum_fusion.4.refs_0_), channel_id=1, source_target_pairs={{0,16},{1,9},{2,18},{3,11},{4,20},{5,13},{6,22},{7,15},{8,24},{9,1... | collective-permute-start | bytes 786440 | tf_op jit(solution)/shard_map/ppermute | solution.py:30
  69.6 8.4 %collective-permute-start.29 = (bf16[512,256]{1,0:T(8,128)(2,1)S(1)}, bf16[512,256]{1,0:T(8,128)(2,1)S(1)}, u32[]{:S(2)}, u32[]{:S(2)}) collective-permute-start(bf16[512,256]{1,0:T(8,128)(2,1)S(1)} %pad_maximum_fusion.5.refs_1_), channel_id=1, source_target_pairs={{0,1},{1,0},{2,3},{3,2},{4,5},{5,4},{6,7},{7,6},{8,9},{9,8},{10,11... | collective-permute-start | bytes 786440 | tf_op jit(solution)/shard_map/ppermute | solution.py:34
  69.7 8.3 %collective-permute-start.25 = (bf16[512,256]{1,0:T(8,128)(2,1)S(1)}, bf16[512,256]{1,0:T(8,128)(2,1)S(1)}, u32[]{:S(2)}, u32[]{:S(2)}) collective-permute-start(bf16[512,256]{1,0:T(8,128)(2,1)S(1)} %pad_maximum_fusion.5.refs_1_), channel_id=1, source_target_pairs={{0,16},{1,9},{2,18},{3,11},{4,20},{5,13},{6,22},{7,15},{8,24},{9,1... | collective-permute-start | bytes 786440 | tf_op jit(solution)/shard_map/ppermute | solution.py:30
  71.4 8.1 %collective-permute-start.14 = (bf16[144,512]{1,0:T(8,128)(2,1)S(1)}, bf16[144,512]{1,0:T(8,128)(2,1)S(1)}, u32[]{:S(2)}, u32[]{:S(2)}) collective-permute-start(bf16[144,512]{1,0:T(8,128)(2,1)S(1)} %pad_maximum_fusion.8), channel_id=1, source_target_pairs={{0,8},{1,17},{2,10},{3,19},{4,12},{5,21},{6,14},{7,23},{8,0},{9,25... | collective-permute-start | bytes 442376 | tf_op jit(solution)/shard_map/ppermute | solution.py:30
  73.6 7.2 %collective-permute-start.26 = (bf16[512,256]{1,0:T(8,128)(2,1)S(1)}, bf16[512,256]{1,0:T(8,128)(2,1)S(1)}, u32[]{:S(2)}, u32[]{:S(2)}) collective-permute-start(bf16[512,256]{1,0:T(8,128)(2,1)S(1)} %collective-permute-done.19.refs_0_), channel_id=1, source_target_pairs={{0,1},{1,0},{2,3},{3,2},{4,5},{5,4},{6,7},{7,6},{8,9},{9,8},{10,11... | collective-permute-start | bytes 786440 | tf_op jit(solution)/shard_map/ppermute | solution.py:34
  78.0 2.8 %collective-permute-start.27 = (bf16[512,256]{1,0:T(8,128)(2,1)S(1)}, bf16[512,256]{1,0:T(8,128)(2,1)S(1)}, u32[]{:S(2)}, u32[]{:S(2)}) collective-permute-start(bf16[512,256]{1,0:T(8,128)(2,1)S(1)} %collective-permute-done.25.refs_1_), channel_id=1, source_target_pairs={{0,1},{1,0},{2,3},{3,2},{4,5},{5,4},{6,7},{7,6},{8,9},{9,8},{10,11... | collective-permute-start | bytes 786440 | tf_op jit(solution)/shard_map/ppermute | solution.py:34
  79.6 1.4 %collective-permute-start.30 = (bf16[16,512]{1,0:T(8,128)(2,1)S(1)}, bf16[16,512]{1,0:T(8,128)(2,1)S(1)}, u32[]{:S(2)}, u32[]{:S(2)}) collective-permute-start(bf16[16,512]{1,0:T(8,128)(2,1)S(1)} %pad_maximum_fusion.9.refs_6_), channel_id=1, source_target_pairs={{0,1},{1,0},{2,3},{3,2},{4,5},{5,4},{6,7},{7,6},{8,9},{9,8},{10,11... | collective-permute-start | bytes 49160 | tf_op jit(solution)/shard_map/ppermute | solution.py:34

commit v4 on v3

--- a/solution.py
+++ b/solution.py
@@ -121,16 +121,19 @@
     )(tile_count, *(pltpu.with_memory_space_constraint(x, pltpu.HBM) for x in (tile_row, tile_col, tile_vals)))
 
 
-def write_weights(near, far, held, gains, first_place, n_row, factor):
+def write_weights(near, far, held, gains, first_place, first_lane, n_row, factor, through=()):
     parts = len(near)
     rows, lanes = near[0].shape
+    width = parts * lanes
     span = 2 * F // n_row
     places = rows // span
     per = F // span
+    n_gain = len(gains) // 2
 
     def kernel(*refs):
         mine, there = refs[:parts], refs[parts : 2 * parts]
-        in_ref, out_ref = refs[-5 - len(gains) // 2 :][:2]
+        outs = refs[2 * parts + len(held) + len(gains) + len(through) :]
+        in_ref, out_ref = outs[:2]
         wide_in, wide_out, sems = refs[-3:]
         core, row = lax.axis_index("col") & 1, lax.axis_index("row")
 
@@ -155,37 +158,43 @@
 
             g = row ^ q
             to = in_ref.at[
-                pl.ds(pl.multiple_of((g % per) * span, span), span), pl.ds(pl.multiple_of((g // per) * F, F), F)
+                pl.ds(pl.multiple_of((g % per) * span, span), span),
+                pl.ds(pl.multiple_of((g // per) * F + first_lane, TILE), width),
             ]
             copies.append(pltpu.make_async_copy(wide_in.at[at], to, sems.at[2 * j]))
             copies[-1].start()
             g = row ^ reversed_bits(q, n_row.bit_length() - 1)
-            to = out_ref.at[pl.ds(pl.multiple_of(g * span, span), span)]
+            to = out_ref.at[pl.ds(pl.multiple_of(g * span, span), span), pl.ds(first_lane, width)]
             copies.append(pltpu.make_async_copy(wide_out.at[at], to, sems.at[2 * j + 1]))
             copies[-1].start()
         if gains:
             one, two = (x[...].astype(FP) for x in refs[2 * parts + len(held) :][:2])
-            refs[-4][...] = ((one[:TYPES] + one[TYPES:]) + (two[:TYPES] + two[TYPES:])) * factor
+            outs[2][...] = ((one[:TYPES] + one[TYPES:]) + (two[:TYPES] + two[TYPES:])) * factor
         for copy in copies:
             copy.wait()
 
     vmem, hbm = pl.BlockSpec(memory_space=pltpu.VMEM), pl.BlockSpec(memory_space=pltpu.HBM)
+    keep = pl.BlockSpec(memory_space=pl.ANY)
+    before = 2 * parts + len(held) + len(gains)
+    aliases = {2 * parts + i: i for i in range(len(held))}
+    aliases.update({before + i: 2 + n_gain + i for i in range(len(through))})
     return pl.pallas_call(
         kernel,
         out_shape=(jax.ShapeDtypeStruct((F, 2 * F), FP), jax.ShapeDtypeStruct((2 * F, F), FP))
-        + (jax.ShapeDtypeStruct((TYPES, F), FP),) * (len(gains) // 2),
-        in_specs=[vmem] * (2 * parts) + [hbm] * len(held) + [vmem] * len(gains),
-        out_specs=(hbm, hbm) + (vmem,) * (len(gains) // 2),
-        input_output_aliases={2 * parts + i: i for i in range(len(held))},
+        + (jax.ShapeDtypeStruct((TYPES, F), FP),) * n_gain
+        + tuple(jax.ShapeDtypeStruct(x.shape, x.dtype) for x in through),
+        in_specs=[vmem] * (2 * parts) + [hbm] * len(held) + [vmem] * len(gains) + [keep] * len(through),
+        out_specs=(hbm, hbm) + (vmem,) * n_gain + (keep,) * len(through),
+        input_output_aliases=aliases,
         scratch_shapes=[
-            pltpu.VMEM((rows, F), FP),
-            pltpu.VMEM((rows, F), FP),
+            pltpu.VMEM((rows, width), FP),
+            pltpu.VMEM((rows, width), FP),
             pltpu.SemaphoreType.DMA((2 * places,)),
         ],
         compiler_params=pltpu.CompilerParams(vmem_limit_bytes=16 * 1024 * 1024),
-        cost_estimate=pl.CostEstimate(flops=4 * rows * F, bytes_accessed=12 * rows * F, transcendentals=0),
+        cost_estimate=pl.CostEstimate(flops=0, bytes_accessed=0, transcendentals=0),
         name="write_weights",
-    )(*near, *far, *held, *gains)
+    )(*near, *far, *held, *gains, *through)
 
 
 def node_gradients(grad_hidden, w_in, aggregate, gains, cotangent, picked):
@@ -224,11 +233,12 @@
     )(grad_hidden, w_in, aggregate, gains, cotangent, picked)
 
 
-def weight_blocks(mine, met, places, n_row, parts, dtype, through=()):
+def weight_blocks(mine, met, places, n_row, lanes, dtype, through=()):
     span = 2 * F // n_row
     per = F // span
-    lanes = F // parts
     rows = len(places) * span
+    parts = len(lanes)
+    low, high = lanes[0][0], lanes[-1][0] + lanes[-1][1]
 
     def kernel(mine_ref, met_ref, *refs):
         outs = refs[len(through) : len(through) + parts]
@@ -244,8 +254,8 @@
             return total
 
         def put(j, value):
-            for i, out in enumerate(outs):
-                out[j * span : (j + 1) * span, :] = value[:, i * lanes : (i + 1) * lanes].astype(dtype)
+            for (start, size), out in zip(lanes, outs):
+                out[j * span : (j + 1) * span, :] = value[:, start - low : start - low + size].astype(dtype)
 
         for j, q in enumerate(places):
 
@@ -253,18 +263,18 @@
             def _(j=j, q=q):
                 g = row ^ q
                 left = pl.ds(pl.multiple_of((g % per) * span, span), span)
-                right = pl.ds(pl.multiple_of(F + (g // per) * F, F), F)
+                right = pl.ds(pl.multiple_of(F + low + (g // per) * F, TILE), high - low)
                 put(j, block(left, right))
 
             @pl.when(core != 0)
             def _(j=j, q=q):
                 g = row ^ reversed_bits(q, n_row.bit_length() - 1)
                 left = pl.ds(pl.multiple_of(F + g * span, span), span)
-                put(j, block(left, slice(0, F)))
+                put(j, block(left, slice(low, high)))
 
     return pl.pallas_call(
         kernel,
-        out_shape=tuple(jax.ShapeDtypeStruct((rows, lanes), dtype) for _ in range(parts))
+        out_shape=tuple(jax.ShapeDtypeStruct((rows, size), dtype) for _, size in lanes)
         + tuple(jax.ShapeDtypeStruct(x.shape, x.dtype) for x in through),
         in_specs=[pl.BlockSpec(memory_space=pltpu.VMEM)] * 2 + [pl.BlockSpec(memory_space=pl.ANY)] * len(through),
         out_specs=(pl.BlockSpec(memory_space=pltpu.VMEM),) * parts
@@ -272,7 +282,7 @@
         input_output_aliases={2 + i: parts + i for i in range(len(through))},
         compiler_params=pltpu.CompilerParams(vmem_limit_bytes=8 * 1024 * 1024),
         cost_estimate=pl.CostEstimate(
-            flops=4 * TILE * rows * F, bytes_accessed=8 * TILE * F + 4 * rows * F, transcendentals=0
+            flops=4 * TILE * rows * (high - low), bytes_accessed=8 * TILE * F + 4 * rows * F, transcendentals=0
         ),
         name="weight_blocks",
     )(mine, met, *through)
@@ -369,6 +379,17 @@
 
     outs = (jax.ShapeDtypeStruct((n, F), FP),) + tuple(jax.ShapeDtypeStruct((n, w * F), BF) for w in (3, 3, 2, 2))
     return small_call(kernel, "node_values", outs, (keep, came, gains, w_in, w_out, cotangent))
+
+
+def joined(held, came, after):
+    n, lanes = held.shape
+
+    def kernel(held_ref, came_ref, out_ref):
+        out_ref[:n] = held_ref[...]
+        out_ref[n:] = came_ref[...]
+
+    outs = (jax.ShapeDtypeStruct((2 * n, lanes), BF),)
+    return small_call(kernel, "joined", outs, (held, came), after)[0]
 
 
 def shards(
@@ -424,8 +445,11 @@
     met = swap_cores(away, n_row, n_col)
     node_rows = node_gradients(grad_hidden, w_in, aggregate, gains, cotangent, onehot.T)
     parts = 2
-    sent = list(weight_blocks(mine, met, range(n_row // 2, n_row), n_row, parts, BF))
-    *sums, node_rows = weight_blocks(mine, met, range(n_row // 2), n_row, parts, FP, (node_rows,))
+    lanes = [(i * F // parts, F // parts) for i in range(parts)]
+    ahead, behind = range(n_row // 2, n_row), range(n_row // 2)
+    first, node_rows = weight_blocks(mine, met, ahead, n_row, lanes[:1], BF, (node_rows,))
+    sent = [first] + [weight_blocks(mine, met, ahead, n_row, [x], BF)[0] for x in lanes[1:]]
+    sums = list(weight_blocks(mine, met, behind, n_row, lanes, FP))
 
     grad_rows, gain = node_rows[:TILE], node_rows[TILE:]
     for step in range(z_bits):
@@ -436,9 +460,11 @@
     own = n_row * TILE
     came = swap_cores(rounded(dot(far[:, :own], grad_rows, ((0,), (0,)))), n_row, n_col)
     low = dot(near[:, :own], grad_rows, ((0,), (0,))) + came.astype(FP)
+    marks = []
     for step in reversed(range(row_bits)):
         size = low.shape[0] // 2
-        came = row_step(jnp.concatenate([rounded(low[size:]), gain], axis=0), step)
+        marks.append(jnp.concatenate([rounded(low[size:]), gain], axis=0))
+        came = row_step(marks[-1], step)
         gain = split(whole(gain) + whole(came[size:]))
         low = low[:size] + came[:size].astype(FP)
     grad_x = low
@@ -455,21 +481,29 @@
                 sums[i], sent[i] = sums[i][:mid], rounded(sums[i][mid:])
     for step in range(z_bits):
         for i in range(parts):
-            held = rounded(sums[i])
-            sums[i] = held.astype(FP) + z_step(held, step).astype(FP)
-    sent = [rounded(x) for x in sums]
+            if step == 0:
+                sent[i] = rounded(sums[i])
+            came = z_step(sent[i], step)
+            if step == 0 and i == parts - 1:
+                sent[i] = added(sent[i], came, False, marks[:1])[0]
+            else:
+                sent[i] = rounded(sent[i].astype(FP) + came.astype(FP))
     for step in range(row_bits - 1):
         for i in range(parts):
-            sent[i] = jnp.concatenate([sent[i], row_step(sent[i], step)], axis=0)
+            came = row_step(sent[i], step)
+            if step == row_bits - 2:
+                sent[i] = joined(sent[i], came, sent[:i] + (marks[-1:] if i == parts - 1 else []))
+            else:
+                sent[i] = jnp.concatenate([sent[i], came], axis=0)
     came = [row_step(x, row_bits - 1) for x in sent]
 
     factor = float(total_nodes) ** (-0.5)
     others = [swap_cores(x, n_row, n_col) for x in sent]
-    weights = write_weights(sent, others, [], [], 0, n_row, factor)
+    gains = [gain, swap_cores(gain, n_row, n_col)]
+    *weights, came[0] = write_weights(sent, others, [], [], 0, 0, n_row, factor, came[:1])
     others = [swap_cores(x, n_row, n_col) for x in came]
-    grad_w_in, grad_w_out, grad_gain = write_weights(
-        came, others, weights, [gain, swap_cores(gain, n_row, n_col)], n_row // 2, n_row, factor
-    )
+    *weights, grad_gain = write_weights(came, others, weights, gains, n_row // 2, 0, n_row, factor)
+    grad_w_in, grad_w_out = weights
     return mixed, grad_x, grad_w_in, grad_w_out, grad_gain
 
 

time: 84.5 us -> 81.3 us (0.962)
  waiting for transfers between devices: 33.6 us -> 31.3 us
  starting transfers between devices: 32.8 us -> 31.8 us
    ppermute x21, waiting for transfers between devices: 31 us -> 27.9 us  [exchange(): return lax.ppermute(x, AXES, pairs)]
  transfers between devices with their start and end apart: 31 -> 31, of which waited for: 17 -> 18; matrix products, arithmetic and copies ran while one was open for 5% -> 5% of each run, Pallas kernels for 8% -> 9%
where the time goes in v4:
time: 81.3 us; the launch traced here: 79.9 us
  starting transfers between devices  31.8 us (39%)
  waiting for transfers between devices  31.3 us (38%)
  Pallas kernels  10.5 us (13%)
  matrix products  2.98 us (4%)
  between operations  1.8 us (2%)
  other arithmetic  1.39 us (2%)
    ppermute x21, starting transfers between devices, exchange(): return lax.ppermute(x, AXES, pairs)  30.4 us
    ppermute x21, waiting for transfers between devices, exchange(): return lax.ppermute(x, AXES, pairs)  27.9 us
    pallas_call x2, Pallas kernels, write_weights(): pl.pallas_call(kernel, out_shape=(jax.ShapeDtypeStruct((F, 2 * F), FP), j...  3.46 us
    ppermute x10, waiting for transfers between devices, swap_cores(): return lax.ppermute(x, AXES, [(i, i ^ 1) for i in range(rows * cols)])  3.42 us
    pallas_call x1, Pallas kernels, build(): pl.pallas_call(kernel, out_shape=(result, result), in_specs=[pl.BlockSpec...  2.74 us
    dot_general x6, matrix products, dot(): return lax.dot_general(a, b, (dims, ((), ())), preferred_element_type=FP)  2.68 us
    pallas_call x3, Pallas kernels, weight_blocks(): pl.pallas_call(kernel, out_shape=tuple((jax.ShapeDtypeStruct((rows, size)...  1.67 us
  transfers between devices with their start and end apart: 31, of which 18 were waited for; matrix products, arithmetic and copies ran while one was open for 5% of the time, Pallas kernels for 9%

profile of v4, /device:TPU:0, one launch (start us, length us, event | category | flops | bytes accessed | tf_op | source)
XLA Modules:
  0.0 79.9 jit_solution(15352186695138611696)
XLA Ops:
  0.6 4.0 %collective-permute-start.2 = (bf16[128,512]{1,0:T(8,128)(2,1)}, bf16[128,512]{1,0:T(8,128)(2,1)S(1)}, u32[]{:S(2)}, u32[]{:S(2)}) collective-permute-start(bf16[128,512]{1,0:T(8,128)(2,1)} %param.10), channel_id=1, source_target_pairs={{0,24},{1,25},{2,26},{3,27},{4,28},{5,29},{6,30},{7,31},{8,16},{9,... | collective-permute-start | bytes 393224 | tf_op jit(solution)/shard_map/ppermute | solution.py:30
  4.6 0.5 collective-permute-start.1
  5.1 0.1 collective-permute-start
  5.9 2.7 %build_dense.1 = (bf16[512,1024]{1,0:T(8,128)(2,1)S(1)}, bf16[512,1024]{1,0:T(8,128)(2,1)S(1)}) custom-call(s32[1,1]{1,0:T(1,128)S(6)} %copy.33.count_ref, s32[1,128]{1,0:T(1,128)} %rows_ref.1, s32[1,128]{1,0:T(1,128)} %cols_ref.1, bf16[1,128,128,128]{3,2,1,0:T(8,128)(2,1)} %vals_ref.1), custom_call_target="tpu_custom_call" | custom-call | flops 2097152 | bytes 6291456 | tf_op jit(solution)/shard_map/build_dense/pallas_call | solution.py:105
  8.7 0.6 collective-permute-start.3
  9.3 1.9 %collective-permute-done.1 = bf16[128,512]{1,0:T(8,128)(2,1)S(1)} collective-permute-done((bf16[128,512]{1,0:T(8,128)(2,1)}, bf16[128,512]{1,0:T(8,128)(2,1)S(1)}, u32[]{:S(2)}, u32[]{:S(2)}) %collective-permute-start.1) | collective-permute-done | bytes 131104 | tf_op jit(solution)/shard_map/ppermute | solution.py:30
  11.1 0.2 collective-permute-done
  11.4 0.1 collective-permute-start.5
  11.6 1.5 %collective-permute-done.5 = bf16[384,512]{1,0:T(8,128)(2,1)S(1)} collective-permute-done((bf16[384,512]{1,0:T(8,128)(2,1)S(1)}, bf16[384,512]{1,0:T(8,128)(2,1)S(1)}, u32[]{:S(2)}, u32[]{:S(2)}) %collective-permute-start.5) | collective-permute-done | bytes 393248 | tf_op jit(solution)/shard_map/ppermute | solution.py:34
  13.3 0.4 fusion.5
  13.7 0.4 fusion.2
  14.2 2.7 %collective-permute-start.6 = (bf16[256,512]{1,0:T(8,128)(2,1)S(1)}, bf16[256,512]{1,0:T(8,128)(2,1)S(1)}, u32[]{:S(2)}, u32[]{:S(2)}) collective-permute-start(bf16[256,512]{1,0:T(8,128)(2,1)S(1)} %fusion.2), channel_id=1, source_target_pairs={{0,4},{1,3},{2,6},{3,1},{4,0},{5,7},{6,2},{7,5},{8,12},{9,11},{10,... | collective-permute-start | bytes 786440 | tf_op jit(solution)/shard_map/ppermute | solution.py:30
  16.8 0.4 fusion.7
  17.3 0.4 convolution_add_fusion.2.refs_0_
  17.7 5.7 %collective-permute-done.6.refs_1_ = bf16[256,512]{1,0:T(8,128)(2,1)S(1)} collective-permute-done((bf16[256,512]{1,0:T(8,128)(2,1)S(1)}, bf16[256,512]{1,0:T(8,128)(2,1)S(1)}, u32[]{:S(2)}, u32[]{:S(2)}) %collective-permute-start.6) | collective-permute-done | bytes 262176 | tf_op jit(solution)/shard_map/ppermute | solution.py:30
  23.5 1.8 %collective-permute-start.7 = (bf16[128,512]{1,0:T(8,128)(2,1)S(1)}, bf16[128,512]{1,0:T(8,128)(2,1)S(1)}, u32[]{:S(2)}, u32[]{:S(2)}) collective-permute-start(bf16[128,512]{1,0:T(8,128)(2,1)S(1)} %get-tuple-element.27), channel_id=1, source_target_pairs={{0,2},{1,5},{2,0},{3,7},{4,6},{5,1},{6,4},{7,3},{8,10},{9,13},{10,... | collective-permute-start | bytes 393224 | tf_op jit(solution)/shard_map/ppermute | solution.py:30
  25.3 0.3 fusion.19.refs_2_.gains_ref
  25.6 4.0 %collective-permute-done.7.refs_1_ = bf16[128,512]{1,0:T(8,128)(2,1)S(1)} collective-permute-done((bf16[128,512]{1,0:T(8,128)(2,1)S(1)}, bf16[128,512]{1,0:T(8,128)(2,1)S(1)}, u32[]{:S(2)}, u32[]{:S(2)}) %collective-permute-start.7) | collective-permute-done | bytes 131104 | tf_op jit(solution)/shard_map/ppermute | solution.py:30
  29.6 0.8 node_values.1
  30.4 0.1 collective-permute-start.8
  30.5 0.8 node_gradients.1.refs_0_
  31.3 0.9 %collective-permute-done.8.met_ref = bf16[128,1536]{1,0:T(8,128)(2,1)S(1)} collective-permute-done((bf16[128,1536]{1,0:T(8,128)(2,1)S(1)}, bf16[128,1536]{1,0:T(8,128)(2,1)S(1)}, u32[]{:S(2)}, u32[]{:S(2)}) %collective-permute-start.8) | collective-permute-done | bytes 393248 | tf_op jit(solution)/shard_map/ppermute | solution.py:34
  32.2 0.5 weight_blocks.3
  32.7 0.7 collective-permute-start.10
  33.4 1.5 %collective-permute-start.9 = (bf16[512,256]{1,0:T(8,128)(2,1)S(1)}, bf16[512,256]{1,0:T(8,128)(2,1)S(1)}, u32[]{:S(2)}, u32[]{:S(2)}) collective-permute-start(bf16[512,256]{1,0:T(8,128)(2,1)S(1)} %get-tuple-element.33), channel_id=1, source_target_pairs={{0,16},{1,9},{2,18},{3,11},{4,20},{5,13},{6,22},{7,15},{8,24},{9,1... | collective-permute-start | bytes 786440 | tf_op jit(solution)/shard_map/ppermute | solution.py:30
  34.9 0.5 weight_blocks.5
  35.4 0.6 collective-permute-start.19
  36.0 0.6 weight_blocks.4
  36.7 2.8 %collective-permute-done.10 = bf16[144,512]{1,0:T(8,128)(2,1)S(1)} collective-permute-done((bf16[144,512]{1,0:T(8,128)(2,1)S(1)}, bf16[144,512]{1,0:T(8,128)(2,1)S(1)}, u32[]{:S(2)}, u32[]{:S(2)}) %collective-permute-start.10) | collective-permute-done | bytes 147488 | tf_op jit(solution)/shard_map/ppermute | solution.py:30
  39.6 1.5 %collective-permute-start.11 = (bf16[272,512]{1,0:T(8,128)(2,1)S(1)}, bf16[272,512]{1,0:T(8,128)(2,1)S(1)}, u32[]{:S(2)}, u32[]{:S(2)}) collective-permute-start(bf16[272,512]{1,0:T(8,128)(2,1)S(1)} %pad_maximum_fusion.2), channel_id=1, source_target_pairs={{0,4},{1,3},{2,6},{3,1},{4,0},{5,7},{6,2},{7,5},{8,12},{9,11},{10,... | collective-permute-start | bytes 835592 | tf_op jit(solution)/shard_map/ppermute | solution.py:30
  41.1 0.1 convert_add_fusion.1
  41.2 1.6 %collective-permute-start.15 = (bf16[256,256]{1,0:T(8,128)(2,1)S(1)}, bf16[256,256]{1,0:T(8,128)(2,1)S(1)}, u32[]{:S(2)}, u32[]{:S(2)}) collective-permute-start(bf16[256,256]{1,0:T(8,128)(2,1)S(1)} %fusion.15), channel_id=1, source_target_pairs={{0,8},{1,17},{2,10},{3,19},{4,12},{5,21},{6,14},{7,23},{8,0},{9,25... | collective-permute-start | bytes 393224 | tf_op jit(solution)/shard_map/ppermute | solution.py:30
  42.9 1.4 %collective-permute-start.20 = (bf16[256,256]{1,0:T(8,128)(2,1)S(1)}, bf16[256,256]{1,0:T(8,128)(2,1)S(1)}, u32[]{:S(2)}, u32[]{:S(2)}) collective-permute-start(bf16[256,256]{1,0:T(8,128)(2,1)S(1)} %fusion.12), channel_id=1, source_target_pairs={{0,8},{1,17},{2,10},{3,19},{4,12},{5,21},{6,14},{7,23},{8,0},{9,25... | collective-permute-start | bytes 393224 | tf_op jit(solution)/shard_map/ppermute | solution.py:30
  44.3 2.0 %collective-permute-done.15 = bf16[256,256]{1,0:T(8,128)(2,1)S(1)} collective-permute-done((bf16[256,256]{1,0:T(8,128)(2,1)S(1)}, bf16[256,256]{1,0:T(8,128)(2,1)S(1)}, u32[]{:S(2)}, u32[]{:S(2)}) %collective-permute-start.15) | collective-permute-done | bytes 131104 | tf_op jit(solution)/shard_map/ppermute | solution.py:30
  46.3 2.5 %collective-permute-start.16 = (bf16[256,256]{1,0:T(8,128)(2,1)S(1)}, bf16[256,256]{1,0:T(8,128)(2,1)S(1)}, u32[]{:S(2)}, u32[]{:S(2)}) collective-permute-start(bf16[256,256]{1,0:T(8,128)(2,1)S(1)} %fusion.17), channel_id=1, source_target_pairs={{0,2},{1,5},{2,0},{3,7},{4,6},{5,1},{6,4},{7,3},{8,10},{9,13},{10,... | collective-permute-start | bytes 393224 | tf_op jit(solution)/shard_map/ppermute | solution.py:30
  48.9 1.6 %collective-permute-start.21 = (bf16[256,256]{1,0:T(8,128)(2,1)S(1)}, bf16[256,256]{1,0:T(8,128)(2,1)S(1)}, u32[]{:S(2)}, u32[]{:S(2)}) collective-permute-start(bf16[256,256]{1,0:T(8,128)(2,1)S(1)} %fusion.14.refs_0_), channel_id=1, source_target_pairs={{0,2},{1,5},{2,0},{3,7},{4,6},{5,1},{6,4},{7,3},{8,10},{9,13},{10,... | collective-permute-start | bytes 393224 | tf_op jit(solution)/shard_map/ppermute | solution.py:30
  50.5 1.9 %collective-permute-done.11 = bf16[272,512]{1,0:T(8,128)(2,1)S(1)} collective-permute-done((bf16[272,512]{1,0:T(8,128)(2,1)S(1)}, bf16[272,512]{1,0:T(8,128)(2,1)S(1)}, u32[]{:S(2)}, u32[]{:S(2)}) %collective-permute-start.11) | collective-permute-done | bytes 278560 | tf_op jit(solution)/shard_map/ppermute | solution.py:30
  52.4 0.5 fusion
  52.9 0.1 collective-permute-start.12
  53.0 0.4 collective-permute-done.16
  53.5 0.8 collective-permute-start.17
  54.3 0.6 collective-permute-done.12
  54.9 0.5 convolution_add_fusion
  55.4 1.5 %collective-permute-start.13 = (bf16[272,512]{1,0:T(8,128)(2,1)S(1)}, bf16[272,512]{1,0:T(8,128)(2,1)S(1)}, u32[]{:S(2)}, u32[]{:S(2)}) collective-permute-start(bf16[272,512]{1,0:T(8,128)(2,1)S(1)} %pad_maximum_fusion.3.refs_2_), channel_id=1, source_target_pairs={{0,16},{1,9},{2,18},{3,11},{4,20},{5,13},{6,22},{7,15},{8,24},{9,1... | collective-permute-start | bytes 835592 | tf_op jit(solution)/shard_map/ppermute | solution.py:30
  57.0 1.7 %collective-permute-start.22 = (bf16[256,256]{1,0:T(8,128)(2,1)S(1)}, bf16[256,256]{1,0:T(8,128)(2,1)S(1)}, u32[]{:S(2)}, u32[]{:S(2)}) collective-permute-start(bf16[256,256]{1,0:T(8,128)(2,1)S(1)} %added.3), channel_id=1, source_target_pairs={{0,4},{1,3},{2,6},{3,1},{4,0},{5,7},{6,2},{7,5},{8,12},{9,11},{10,... | collective-permute-start | bytes 393224 | tf_op jit(solution)/shard_map/ppermute | solution.py:30
  58.7 0.9 %collective-permute-done.17 = bf16[256,256]{1,0:T(8,128)(2,1)S(1)} collective-permute-done((bf16[256,256]{1,0:T(8,128)(2,1)S(1)}, bf16[256,256]{1,0:T(8,128)(2,1)S(1)}, u32[]{:S(2)}, u32[]{:S(2)}) %collective-permute-start.17) | collective-permute-done | bytes 131104 | tf_op jit(solution)/shard_map/ppermute | solution.py:30
  59.6 1.6 %collective-permute-start.18 = (bf16[256,256]{1,0:T(8,128)(2,1)S(1)}, bf16[256,256]{1,0:T(8,128)(2,1)S(1)}, u32[]{:S(2)}, u32[]{:S(2)}) collective-permute-start(bf16[256,256]{1,0:T(8,128)(2,1)S(1)} %reduce-precision_convert_fusion.1.refs_0_), channel_id=1, source_target_pairs={{0,8},{1,17},{2,10},{3,19},{4,12},{5,21},{6,14},{7,23},{8,0},{9,25... | collective-permute-start | bytes 393224 | tf_op jit(solution)/shard_map/ppermute | solution.py:30
  61.1 2.6 %collective-permute-done.22 = bf16[256,256]{1,0:T(8,128)(2,1)S(1)} collective-permute-done((bf16[256,256]{1,0:T(8,128)(2,1)S(1)}, bf16[256,256]{1,0:T(8,128)(2,1)S(1)}, u32[]{:S(2)}, u32[]{:S(2)}) %collective-permute-start.22) | collective-permute-done | bytes 131104 | tf_op jit(solution)/shard_map/ppermute | solution.py:30
  63.8 1.6 %collective-permute-start.23 = (bf16[256,256]{1,0:T(8,128)(2,1)S(1)}, bf16[256,256]{1,0:T(8,128)(2,1)S(1)}, u32[]{:S(2)}, u32[]{:S(2)}) collective-permute-start(bf16[256,256]{1,0:T(8,128)(2,1)S(1)} %reduce-precision_convert_fusion.refs_0_), channel_id=1, source_target_pairs={{0,8},{1,17},{2,10},{3,19},{4,12},{5,21},{6,14},{7,23},{8,0},{9,25... | collective-permute-start | bytes 393224 | tf_op jit(solution)/shard_map/ppermute | solution.py:30
  65.4 0.1 slice_add_fusion
  65.5 0.6 collective-permute-start.14
  66.1 1.0 %mix.1 = bf16[128,512]{1,0:T(8,128)(2,1)} custom-call(f32[128,512]{1,0:T(8,128)S(1)} %get-tuple-element.28.agg_ref, bf16[128,1024]{1,0:T(8,128)(2,1)S(1)} %get-tuple-element.29.act_ref, bf16[1024,512]{1,0:T(8,128)(2,1)S(1)} %copy-done.2, bf16[512,256]{1,0:T(8,128)(2,1)S(1)} %collective-permute-done.9.after_ref), custom_call_target="tpu_custom_call" | custom-call | tf_op jit(solution)/shard_map/mix/pallas_call | solution.py:297
  67.1 1.3 %collective-permute-start.26 = (bf16[512,256]{1,0:T(8,128)(2,1)S(1)}, bf16[512,256]{1,0:T(8,128)(2,1)S(1)}, u32[]{:S(2)}, u32[]{:S(2)}) collective-permute-start(bf16[512,256]{1,0:T(8,128)(2,1)S(1)} %joined.2.refs_2_.refs_0_), channel_id=1, source_target_pairs={{0,16},{1,9},{2,18},{3,11},{4,20},{5,13},{6,22},{7,15},{8,24},{9,1... | collective-permute-start | bytes 786440 | tf_op jit(solution)/shard_map/ppermute | solution.py:30
  68.4 0.9 %collective-permute-done.23.refs_1_ = bf16[256,256]{1,0:T(8,128)(2,1)S(1)} collective-permute-done((bf16[256,256]{1,0:T(8,128)(2,1)S(1)}, bf16[256,256]{1,0:T(8,128)(2,1)S(1)}, u32[]{:S(2)}, u32[]{:S(2)}) %collective-permute-start.23) | collective-permute-done | bytes 131104 | tf_op jit(solution)/shard_map/ppermute | solution.py:30
  69.3 1.0 %collective-permute-start.27 = (bf16[512,256]{1,0:T(8,128)(2,1)S(1)}, bf16[512,256]{1,0:T(8,128)(2,1)S(1)}, u32[]{:S(2)}, u32[]{:S(2)}) collective-permute-start(bf16[512,256]{1,0:T(8,128)(2,1)S(1)} %joined.3.refs_1_), channel_id=1, source_target_pairs={{0,16},{1,9},{2,18},{3,11},{4,20},{5,13},{6,22},{7,15},{8,24},{9,1... | collective-permute-start | bytes 786440 | tf_op jit(solution)/shard_map/ppermute | solution.py:30
  70.3 2.1 %collective-permute-done.14 = bf16[144,512]{1,0:T(8,128)(2,1)S(1)} collective-permute-done((bf16[144,512]{1,0:T(8,128)(2,1)S(1)}, bf16[144,512]{1,0:T(8,128)(2,1)S(1)}, u32[]{:S(2)}, u32[]{:S(2)}) %collective-permute-start.14) | collective-permute-done | bytes 147488 | tf_op jit(solution)/shard_map/ppermute | solution.py:30
  72.5 1.0 %collective-permute-done.26.refs_4_ = bf16[512,256]{1,0:T(8,128)(2,1)S(1)} collective-permute-done((bf16[512,256]{1,0:T(8,128)(2,1)S(1)}, bf16[512,256]{1,0:T(8,128)(2,1)S(1)}, u32[]{:S(2)}, u32[]{:S(2)}) %collective-permute-start.26) | collective-permute-done | bytes 262176 | tf_op jit(solution)/shard_map/ppermute | solution.py:30
  73.5 1.4 %write_weights.2 = (f32[512,1024]{1,0:T(8,128)}, f32[1024,512]{1,0:T(8,128)}, bf16[512,256]{1,0:T(8,128)(2,1)S(1)}) custom-call(bf16[512,256]{1,0:T(8,128)(2,1)S(1)} %joined.2.refs_2_.refs_0_, bf16[512,256]{1,0:T(8,128)(2,1)S(1)} %joined.3.refs_1_, bf16[512,256]{1,0:T(8,128)(2,1)S(1)} %collective-permute-done.24.refs_2_, ...), custom_call_target="tpu_custom_call", output_to_operand_aliasing={{2}: (4, {})} | custom-call | tf_op jit(solution)/shard_map/write_weights/pallas_call | solution.py:181
  75.0 0.1 collective-permute-start.28
  75.0 1.3 %collective-permute-done.27.refs_1_ = bf16[512,256]{1,0:T(8,128)(2,1)S(1)} collective-permute-done((bf16[512,256]{1,0:T(8,128)(2,1)S(1)}, bf16[512,256]{1,0:T(8,128)(2,1)S(1)}, u32[]{:S(2)}, u32[]{:S(2)}) %collective-permute-start.27) | collective-permute-done | bytes 262176 | tf_op jit(solution)/shard_map/ppermute | solution.py:30
  76.3 0.5 collective-permute-start.30
  76.8 0.7 slice_add_fusion.3
  77.6 0.3 collective-permute-done.30.refs_7_
  77.9 2.0 %write_weights.3 = (f32[512,1024]{1,0:T(8,128)}, f32[1024,512]{1,0:T(8,128)}, f32[8,512]{1,0:T(8,128)}) custom-call(bf16[512,256]{1,0:T(8,128)(2,1)S(1)} %get-tuple-element.37.refs_0_, bf16[512,256]{1,0:T(8,128)(2,1)S(1)} %collective-permute-done.27.refs_1_, ...), custom_call_target="tpu_custom_call", output_to_operand_aliasing={{0}: (4, {}), {1}: (5, {})} | custom-call | tf_op jit(solution)/shard_map/write_weights/pallas_call | solution.py:181
  (80 shorter events, 0.9 us)
Async XLA Ops:
  0.6 24.7 %copy-start = (f32[8,512]{1,0:T(8,128)S(1)}, f32[8,512]{1,0:T(8,128)}, u32[]{:S(2)}) copy-start(f32[8,512]{1,0:T(8,128)} %param.16) | copy-start | bytes 49156
  0.6 8.6 %collective-permute-start.2 = (bf16[128,512]{1,0:T(8,128)(2,1)}, bf16[128,512]{1,0:T(8,128)(2,1)S(1)}, u32[]{:S(2)}, u32[]{:S(2)}) collective-permute-start(bf16[128,512]{1,0:T(8,128)(2,1)} %param.10), channel_id=1, source_target_pairs={{0,24},{1,25},{2,26},{3,27},{4,28},{5,29},{6,30},{7,31},{8,16},{9,... | collective-permute-start | bytes 393224 | tf_op jit(solution)/shard_map/ppermute | solution.py:30
  4.6 6.5 %collective-permute-start.1 = (bf16[128,512]{1,0:T(8,128)(2,1)}, bf16[128,512]{1,0:T(8,128)(2,1)S(1)}, u32[]{:S(2)}, u32[]{:S(2)}) collective-permute-start(bf16[128,512]{1,0:T(8,128)(2,1)} %param.10), channel_id=1, source_target_pairs={{0,16},{1,9},{2,18},{3,11},{4,20},{5,13},{6,22},{7,15},{8,24},{9,1... | collective-permute-start | bytes 393224 | tf_op jit(solution)/shard_map/ppermute | solution.py:30
  5.1 6.3 %collective-permute-start = (bf16[128,512]{1,0:T(8,128)(2,1)}, bf16[128,512]{1,0:T(8,128)(2,1)S(1)}, u32[]{:S(2)}, u32[]{:S(2)}) collective-permute-start(bf16[128,512]{1,0:T(8,128)(2,1)} %param.10), channel_id=1, source_target_pairs={{0,8},{1,17},{2,10},{3,19},{4,12},{5,21},{6,14},{7,23},{8,0},{9,25... | collective-permute-start | bytes 393224 | tf_op jit(solution)/shard_map/ppermute | solution.py:30
  5.3 6.3 %collective-permute-start.4 = (bf16[128,512]{1,0:T(8,128)(2,1)}, bf16[128,512]{1,0:T(8,128)(2,1)S(1)}, u32[]{:S(2)}, u32[]{:S(2)}) collective-permute-start(bf16[128,512]{1,0:T(8,128)(2,1)} %param.10), channel_id=1, source_target_pairs={{0,1},{1,0},{2,3},{3,2},{4,5},{5,4},{6,7},{7,6},{8,9},{9,8},{10,11... | collective-permute-start | bytes 393224 | tf_op jit(solution)/shard_map/ppermute | solution.py:34
  5.9 3.3 %copy-start.4 = (bf16[128,512]{1,0:T(8,128)(2,1)S(1)}, bf16[128,512]{1,0:T(8,128)(2,1)}, u32[]{:S(2)}) copy-start(bf16[128,512]{1,0:T(8,128)(2,1)} %param.10) | copy-start | bytes 393220
  8.7 4.6 %collective-permute-start.3 = (bf16[512,1024]{1,0:T(8,128)(2,1)S(1)}, bf16[512,1024]{1,0:T(8,128)(2,1)S(1)}, u32[]{:S(2)}, u32[]{:S(2)}) collective-permute-start(bf16[512,1024]{1,0:T(8,128)(2,1)S(1)} %get-tuple-element.25), channel_id=1, source_target_pairs={{0,1},{1,0},{2,3},{3,2},{4,5},{5,4},{6,7},{7,6},{8,9},{9,8},{10,11... | collective-permute-start | bytes 3145736 | tf_op jit(solution)/shard_map/ppermute | solution.py:34
  11.4 1.8 %collective-permute-start.5 = (bf16[384,512]{1,0:T(8,128)(2,1)S(1)}, bf16[384,512]{1,0:T(8,128)(2,1)S(1)}, u32[]{:S(2)}, u32[]{:S(2)}) collective-permute-start(bf16[384,512]{1,0:T(8,128)(2,1)S(1)} %pad_maximum_fusion.1), channel_id=1, source_target_pairs={{0,1},{1,0},{2,3},{3,2},{4,5},{5,4},{6,7},{7,6},{8,9},{9,8},{10,11... | collective-permute-start | bytes 1179656 | tf_op jit(solution)/shard_map/ppermute | solution.py:34
  14.2 9.3 %collective-permute-start.6 = (bf16[256,512]{1,0:T(8,128)(2,1)S(1)}, bf16[256,512]{1,0:T(8,128)(2,1)S(1)}, u32[]{:S(2)}, u32[]{:S(2)}) collective-permute-start(bf16[256,512]{1,0:T(8,128)(2,1)S(1)} %fusion.2), channel_id=1, source_target_pairs={{0,4},{1,3},{2,6},{3,1},{4,0},{5,7},{6,2},{7,5},{8,12},{9,11},{10,... | collective-permute-start | bytes 786440 | tf_op jit(solution)/shard_map/ppermute | solution.py:30
  17.3 8.0 %copy-start.5 = (s32[128]{0:T(128)S(1)}, s32[128]{0:T(128)}, u32[]{:S(2)}) copy-start(s32[128]{0:T(128)} %param.15) | copy-start | bytes 1540
  17.3 12.4 %copy-start.1 = (bf16[512,1024]{1,0:T(8,128)(2,1)S(1)}, bf16[512,1024]{1,0:T(8,128)(2,1)}, u32[]{:S(2)}) copy-start(bf16[512,1024]{1,0:T(8,128)(2,1)} %w_ref.2) | copy-start | bytes 3145732
  17.3 12.4 %copy-start.2 = (bf16[1024,512]{1,0:T(8,128)(2,1)S(1)}, bf16[1024,512]{1,0:T(8,128)(2,1)}, u32[]{:S(2)}) copy-start(bf16[1024,512]{1,0:T(8,128)(2,1)} %w_ref.3) | copy-start | bytes 3145732
  17.3 12.4 %copy-start.3 = (bf16[128,512]{1,0:T(8,128)(2,1)S(1)}, bf16[128,512]{1,0:T(8,128)(2,1)}, u32[]{:S(2)}) copy-start(bf16[128,512]{1,0:T(8,128)(2,1)} %cot_ref.1) | copy-start | bytes 393220
  23.5 6.2 %collective-permute-start.7 = (bf16[128,512]{1,0:T(8,128)(2,1)S(1)}, bf16[128,512]{1,0:T(8,128)(2,1)S(1)}, u32[]{:S(2)}, u32[]{:S(2)}) collective-permute-start(bf16[128,512]{1,0:T(8,128)(2,1)S(1)} %get-tuple-element.27), channel_id=1, source_target_pairs={{0,2},{1,5},{2,0},{3,7},{4,6},{5,1},{6,4},{7,3},{8,10},{9,13},{10,... | collective-permute-start | bytes 393224 | tf_op jit(solution)/shard_map/ppermute | solution.py:30
  30.4 1.8 %collective-permute-start.8 = (bf16[128,1536]{1,0:T(8,128)(2,1)S(1)}, bf16[128,1536]{1,0:T(8,128)(2,1)S(1)}, u32[]{:S(2)}, u32[]{:S(2)}) collective-permute-start(bf16[128,1536]{1,0:T(8,128)(2,1)S(1)} %get-tuple-element.31), channel_id=1, source_target_pairs={{0,1},{1,0},{2,3},{3,2},{4,5},{5,4},{6,7},{7,6},{8,9},{9,8},{10,11... | collective-permute-start | bytes 1179656 | tf_op jit(solution)/shard_map/ppermute | solution.py:34
  32.7 6.8 %collective-permute-start.10 = (bf16[144,512]{1,0:T(8,128)(2,1)S(1)}, bf16[144,512]{1,0:T(8,128)(2,1)S(1)}, u32[]{:S(2)}, u32[]{:S(2)}) collective-permute-start(bf16[144,512]{1,0:T(8,128)(2,1)S(1)} %get-tuple-element.34), channel_id=1, source_target_pairs={{0,2},{1,5},{2,0},{3,7},{4,6},{5,1},{6,4},{7,3},{8,10},{9,13},{10,... | collective-permute-start | bytes 442376 | tf_op jit(solution)/shard_map/ppermute | solution.py:30
  33.4 7.7 %collective-permute-start.9 = (bf16[512,256]{1,0:T(8,128)(2,1)S(1)}, bf16[512,256]{1,0:T(8,128)(2,1)S(1)}, u32[]{:S(2)}, u32[]{:S(2)}) collective-permute-start(bf16[512,256]{1,0:T(8,128)(2,1)S(1)} %get-tuple-element.33), channel_id=1, source_target_pairs={{0,16},{1,9},{2,18},{3,11},{4,20},{5,13},{6,22},{7,15},{8,24},{9,1... | collective-permute-start | bytes 786440 | tf_op jit(solution)/shard_map/ppermute | solution.py:30
  35.4 7.4 %collective-permute-start.19 = (bf16[512,256]{1,0:T(8,128)(2,1)S(1)}, bf16[512,256]{1,0:T(8,128)(2,1)S(1)}, u32[]{:S(2)}, u32[]{:S(2)}) collective-permute-start(bf16[512,256]{1,0:T(8,128)(2,1)S(1)} %weight_blocks.5), channel_id=1, source_target_pairs={{0,16},{1,9},{2,18},{3,11},{4,20},{5,13},{6,22},{7,15},{8,24},{9,1... | collective-permute-start | bytes 786440 | tf_op jit(solution)/shard_map/ppermute | solution.py:30
  39.6 12.8 %collective-permute-start.11 = (bf16[272,512]{1,0:T(8,128)(2,1)S(1)}, bf16[272,512]{1,0:T(8,128)(2,1)S(1)}, u32[]{:S(2)}, u32[]{:S(2)}) collective-permute-start(bf16[272,512]{1,0:T(8,128)(2,1)S(1)} %pad_maximum_fusion.2), channel_id=1, source_target_pairs={{0,4},{1,3},{2,6},{3,1},{4,0},{5,7},{6,2},{7,5},{8,12},{9,11},{10,... | collective-permute-start | bytes 835592 | tf_op jit(solution)/shard_map/ppermute | solution.py:30
  41.2 5.0 %collective-permute-start.15 = (bf16[256,256]{1,0:T(8,128)(2,1)S(1)}, bf16[256,256]{1,0:T(8,128)(2,1)S(1)}, u32[]{:S(2)}, u32[]{:S(2)}) collective-permute-start(bf16[256,256]{1,0:T(8,128)(2,1)S(1)} %fusion.15), channel_id=1, source_target_pairs={{0,8},{1,17},{2,10},{3,19},{4,12},{5,21},{6,14},{7,23},{8,0},{9,25... | collective-permute-start | bytes 393224 | tf_op jit(solution)/shard_map/ppermute | solution.py:30
  42.9 5.9 %collective-permute-start.20 = (bf16[256,256]{1,0:T(8,128)(2,1)S(1)}, bf16[256,256]{1,0:T(8,128)(2,1)S(1)}, u32[]{:S(2)}, u32[]{:S(2)}) collective-permute-start(bf16[256,256]{1,0:T(8,128)(2,1)S(1)} %fusion.12), channel_id=1, source_target_pairs={{0,8},{1,17},{2,10},{3,19},{4,12},{5,21},{6,14},{7,23},{8,0},{9,25... | collective-permute-start | bytes 393224 | tf_op jit(solution)/shard_map/ppermute | solution.py:30
  46.3 7.1 %collective-permute-start.16 = (bf16[256,256]{1,0:T(8,128)(2,1)S(1)}, bf16[256,256]{1,0:T(8,128)(2,1)S(1)}, u32[]{:S(2)}, u32[]{:S(2)}) collective-permute-start(bf16[256,256]{1,0:T(8,128)(2,1)S(1)} %fusion.17), channel_id=1, source_target_pairs={{0,2},{1,5},{2,0},{3,7},{4,6},{5,1},{6,4},{7,3},{8,10},{9,13},{10,... | collective-permute-start | bytes 393224 | tf_op jit(solution)/shard_map/ppermute | solution.py:30
  48.9 8.1 %collective-permute-start.21 = (bf16[256,256]{1,0:T(8,128)(2,1)S(1)}, bf16[256,256]{1,0:T(8,128)(2,1)S(1)}, u32[]{:S(2)}, u32[]{:S(2)}) collective-permute-start(bf16[256,256]{1,0:T(8,128)(2,1)S(1)} %fusion.14.refs_0_), channel_id=1, source_target_pairs={{0,2},{1,5},{2,0},{3,7},{4,6},{5,1},{6,4},{7,3},{8,10},{9,13},{10,... | collective-permute-start | bytes 393224 | tf_op jit(solution)/shard_map/ppermute | solution.py:30
  52.9 2.0 %collective-permute-start.12 = (bf16[512,512]{1,0:T(8,128)(2,1)S(1)}, bf16[512,512]{1,0:T(8,128)(2,1)S(1)}, u32[]{:S(2)}, u32[]{:S(2)}) collective-permute-start(bf16[512,512]{1,0:T(8,128)(2,1)S(1)} %fusion), channel_id=1, source_target_pairs={{0,1},{1,0},{2,3},{3,2},{4,5},{5,4},{6,7},{7,6},{8,9},{9,8},{10,11... | collective-permute-start | bytes 1572872 | tf_op jit(solution)/shard_map/ppermute | solution.py:34
  53.5 6.0 %collective-permute-start.17 = (bf16[256,256]{1,0:T(8,128)(2,1)S(1)}, bf16[256,256]{1,0:T(8,128)(2,1)S(1)}, u32[]{:S(2)}, u32[]{:S(2)}) collective-permute-start(bf16[256,256]{1,0:T(8,128)(2,1)S(1)} %reduce-precision_convert_fusion.2), channel_id=1, source_target_pairs={{0,4},{1,3},{2,6},{3,1},{4,0},{5,7},{6,2},{7,5},{8,12},{9,11},{10,... | collective-permute-start | bytes 393224 | tf_op jit(solution)/shard_map/ppermute | solution.py:30
  55.4 9.9 %collective-permute-start.13 = (bf16[272,512]{1,0:T(8,128)(2,1)S(1)}, bf16[272,512]{1,0:T(8,128)(2,1)S(1)}, u32[]{:S(2)}, u32[]{:S(2)}) collective-permute-start(bf16[272,512]{1,0:T(8,128)(2,1)S(1)} %pad_maximum_fusion.3.refs_2_), channel_id=1, source_target_pairs={{0,16},{1,9},{2,18},{3,11},{4,20},{5,13},{6,22},{7,15},{8,24},{9,1... | collective-permute-start | bytes 835592 | tf_op jit(solution)/shard_map/ppermute | solution.py:30
  57.0 6.7 %collective-permute-start.22 = (bf16[256,256]{1,0:T(8,128)(2,1)S(1)}, bf16[256,256]{1,0:T(8,128)(2,1)S(1)}, u32[]{:S(2)}, u32[]{:S(2)}) collective-permute-start(bf16[256,256]{1,0:T(8,128)(2,1)S(1)} %added.3), channel_id=1, source_target_pairs={{0,4},{1,3},{2,6},{3,1},{4,0},{5,7},{6,2},{7,5},{8,12},{9,11},{10,... | collective-permute-start | bytes 393224 | tf_op jit(solution)/shard_map/ppermute | solution.py:30
  59.6 7.5 %collective-permute-start.18 = (bf16[256,256]{1,0:T(8,128)(2,1)S(1)}, bf16[256,256]{1,0:T(8,128)(2,1)S(1)}, u32[]{:S(2)}, u32[]{:S(2)}) collective-permute-start(bf16[256,256]{1,0:T(8,128)(2,1)S(1)} %reduce-precision_convert_fusion.1.refs_0_), channel_id=1, source_target_pairs={{0,8},{1,17},{2,10},{3,19},{4,12},{5,21},{6,14},{7,23},{8,0},{9,25... | collective-permute-start | bytes 393224 | tf_op jit(solution)/shard_map/ppermute | solution.py:30
  63.8 5.6 %collective-permute-start.23 = (bf16[256,256]{1,0:T(8,128)(2,1)S(1)}, bf16[256,256]{1,0:T(8,128)(2,1)S(1)}, u32[]{:S(2)}, u32[]{:S(2)}) collective-permute-start(bf16[256,256]{1,0:T(8,128)(2,1)S(1)} %reduce-precision_convert_fusion.refs_0_), channel_id=1, source_target_pairs={{0,8},{1,17},{2,10},{3,19},{4,12},{5,21},{6,14},{7,23},{8,0},{9,25... | collective-permute-start | bytes 393224 | tf_op jit(solution)/shard_map/ppermute | solution.py:30
  65.5 7.0 %collective-permute-start.14 = (bf16[144,512]{1,0:T(8,128)(2,1)S(1)}, bf16[144,512]{1,0:T(8,128)(2,1)S(1)}, u32[]{:S(2)}, u32[]{:S(2)}) collective-permute-start(bf16[144,512]{1,0:T(8,128)(2,1)S(1)} %pad_maximum_fusion.6.refs_3_), channel_id=1, source_target_pairs={{0,8},{1,17},{2,10},{3,19},{4,12},{5,21},{6,14},{7,23},{8,0},{9,25... | collective-permute-start | bytes 442376 | tf_op jit(solution)/shard_map/ppermute | solution.py:30
  67.1 6.4 %collective-permute-start.26 = (bf16[512,256]{1,0:T(8,128)(2,1)S(1)}, bf16[512,256]{1,0:T(8,128)(2,1)S(1)}, u32[]{:S(2)}, u32[]{:S(2)}) collective-permute-start(bf16[512,256]{1,0:T(8,128)(2,1)S(1)} %joined.2.refs_2_.refs_0_), channel_id=1, source_target_pairs={{0,16},{1,9},{2,18},{3,11},{4,20},{5,13},{6,22},{7,15},{8,24},{9,1... | collective-permute-start | bytes 786440 | tf_op jit(solution)/shard_map/ppermute | solution.py:30
  68.4 5.1 %collective-permute-start.24 = (bf16[512,256]{1,0:T(8,128)(2,1)S(1)}, bf16[512,256]{1,0:T(8,128)(2,1)S(1)}, u32[]{:S(2)}, u32[]{:S(2)}) collective-permute-start(bf16[512,256]{1,0:T(8,128)(2,1)S(1)} %joined.2.refs_2_.refs_0_), channel_id=1, source_target_pairs={{0,1},{1,0},{2,3},{3,2},{4,5},{5,4},{6,7},{7,6},{8,9},{9,8},{10,11... | collective-permute-start | bytes 786440 | tf_op jit(solution)/shard_map/ppermute | solution.py:34
  69.3 7.0 %collective-permute-start.27 = (bf16[512,256]{1,0:T(8,128)(2,1)S(1)}, bf16[512,256]{1,0:T(8,128)(2,1)S(1)}, u32[]{:S(2)}, u32[]{:S(2)}) collective-permute-start(bf16[512,256]{1,0:T(8,128)(2,1)S(1)} %joined.3.refs_1_), channel_id=1, source_target_pairs={{0,16},{1,9},{2,18},{3,11},{4,20},{5,13},{6,22},{7,15},{8,24},{9,1... | collective-permute-start | bytes 786440 | tf_op jit(solution)/shard_map/ppermute | solution.py:30
  70.3 3.2 %collective-permute-start.25 = (bf16[512,256]{1,0:T(8,128)(2,1)S(1)}, bf16[512,256]{1,0:T(8,128)(2,1)S(1)}, u32[]{:S(2)}, u32[]{:S(2)}) collective-permute-start(bf16[512,256]{1,0:T(8,128)(2,1)S(1)} %joined.3.refs_1_), channel_id=1, source_target_pairs={{0,1},{1,0},{2,3},{3,2},{4,5},{5,4},{6,7},{7,6},{8,9},{9,8},{10,11... | collective-permute-start | bytes 786440 | tf_op jit(solution)/shard_map/ppermute | solution.py:34
  75.0 2.9 %collective-permute-start.28 = (bf16[512,256]{1,0:T(8,128)(2,1)S(1)}, bf16[512,256]{1,0:T(8,128)(2,1)S(1)}, u32[]{:S(2)}, u32[]{:S(2)}) collective-permute-start(bf16[512,256]{1,0:T(8,128)(2,1)S(1)} %get-tuple-element.37.refs_0_), channel_id=1, source_target_pairs={{0,1},{1,0},{2,3},{3,2},{4,5},{5,4},{6,7},{7,6},{8,9},{9,8},{10,11... | collective-permute-start | bytes 786440 | tf_op jit(solution)/shard_map/ppermute | solution.py:34
  76.3 1.6 %collective-permute-start.29 = (bf16[512,256]{1,0:T(8,128)(2,1)S(1)}, bf16[512,256]{1,0:T(8,128)(2,1)S(1)}, u32[]{:S(2)}, u32[]{:S(2)}) collective-permute-start(bf16[512,256]{1,0:T(8,128)(2,1)S(1)} %collective-permute-done.27.refs_1_), channel_id=1, source_target_pairs={{0,1},{1,0},{2,3},{3,2},{4,5},{5,4},{6,7},{7,6},{8,9},{9,8},{10,11... | collective-permute-start | bytes 786440 | tf_op jit(solution)/shard_map/ppermute | solution.py:34
  76.3 1.6 %collective-permute-start.30 = (bf16[16,512]{1,0:T(8,128)(2,1)S(1)}, bf16[16,512]{1,0:T(8,128)(2,1)S(1)}, u32[]{:S(2)}, u32[]{:S(2)}) collective-permute-start(bf16[16,512]{1,0:T(8,128)(2,1)S(1)} %pad_maximum_fusion.7.refs_6_), channel_id=1, source_target_pairs={{0,1},{1,0},{2,3},{3,2},{4,5},{5,4},{6,7},{7,6},{8,9},{9,8},{10,11... | collective-permute-start | bytes 49160 | tf_op jit(solution)/shard_map/ppermute | solution.py:34

commit v5 on v4

--- a/solution.py
+++ b/solution.py
@@ -121,10 +121,11 @@
     )(tile_count, *(pltpu.with_memory_space_constraint(x, pltpu.HBM) for x in (tile_row, tile_col, tile_vals)))
 
 
-def write_weights(near, far, held, gains, first_place, first_lane, n_row, factor, through=()):
+def write_weights(near, far, held, gains, first_place, first_lane, n_row, factor, through=(), after=()):
     parts = len(near)
-    rows, lanes = near[0].shape
-    width = parts * lanes
+    rows = near[0].shape[0]
+    sizes = [x.shape[1] for x in near]
+    width = sum(sizes)
     span = 2 * F // n_row
     places = rows // span
     per = F // span
@@ -132,14 +133,16 @@
 
     def kernel(*refs):
         mine, there = refs[:parts], refs[parts : 2 * parts]
-        outs = refs[2 * parts + len(held) + len(gains) + len(through) :]
+        outs = refs[2 * parts + len(held) + len(gains) + len(through) + len(after) :]
         in_ref, out_ref = outs[:2]
         wide_in, wide_out, sems = refs[-3:]
         core, row = lax.axis_index("col") & 1, lax.axis_index("row")
 
         def put(sources, ref, at):
-            for i, x in enumerate(sources):
-                ref[at, i * lanes : (i + 1) * lanes] = x[at, :].astype(FP) * factor
+            start = 0
+            for x, size in zip(sources, sizes):
+                ref[at, start : start + size] = x[at, :].astype(FP) * factor
+                start += size
 
         copies = []
         for j in range(places):
@@ -183,7 +186,7 @@
         out_shape=(jax.ShapeDtypeStruct((F, 2 * F), FP), jax.ShapeDtypeStruct((2 * F, F), FP))
         + (jax.ShapeDtypeStruct((TYPES, F), FP),) * n_gain
         + tuple(jax.ShapeDtypeStruct(x.shape, x.dtype) for x in through),
-        in_specs=[vmem] * (2 * parts) + [hbm] * len(held) + [vmem] * len(gains) + [keep] * len(through),
+        in_specs=[vmem] * (2 * parts) + [hbm] * len(held) + [vmem] * len(gains) + [keep] * (len(through) + len(after)),
         out_specs=(hbm, hbm) + (vmem,) * n_gain + (keep,) * len(through),
         input_output_aliases=aliases,
         scratch_shapes=[
@@ -194,7 +197,7 @@
         compiler_params=pltpu.CompilerParams(vmem_limit_bytes=16 * 1024 * 1024),
         cost_estimate=pl.CostEstimate(flops=0, bytes_accessed=0, transcendentals=0),
         name="write_weights",
-    )(*near, *far, *held, *gains, *through)
+    )(*near, *far, *held, *gains, *through, *after)
 
 
 def node_gradients(grad_hidden, w_in, aggregate, gains, cotangent, picked):
@@ -233,16 +236,24 @@
     )(grad_hidden, w_in, aggregate, gains, cotangent, picked)
 
 
-def weight_blocks(mine, met, places, n_row, lanes, dtype, through=()):
+def weight_blocks(mine, met, places, n_row, lanes, dtype, through=(), mixing=()):
     span = 2 * F // n_row
     per = F // span
     rows = len(places) * span
     parts = len(lanes)
+    extra = 1 if mixing else 0
     low, high = lanes[0][0], lanes[-1][0] + lanes[-1][1]
 
     def kernel(mine_ref, met_ref, *refs):
-        outs = refs[len(through) : len(through) + parts]
+        outs = refs[len(through) + len(mixing) :][:parts]
         core, row = lax.axis_index("col") & 1, lax.axis_index("row")
+        if mixing:
+            aggregate, activated, w_out = refs[len(through) : len(through) + 3]
+            held, sem = refs[-2:]
+            branch = jnp.dot(activated[...], w_out[...], preferred_element_type=FP)
+            held[...] = (aggregate[...] + branch).astype(BF)
+            copy = pltpu.make_async_copy(held, refs[-3], sem)
+            copy.start()
 
         def block(left, right):
             total = None
@@ -272,37 +283,25 @@
                 left = pl.ds(pl.multiple_of(F + g * span, span), span)
                 put(j, block(left, slice(low, high)))
 
+        if mixing:
+            copy.wait()
+
+    vmem, keep = pl.BlockSpec(memory_space=pltpu.VMEM), pl.BlockSpec(memory_space=pl.ANY)
+    mixed = [jax.ShapeDtypeStruct(mixing[0].shape, BF)] if mixing else []
     return pl.pallas_call(
         kernel,
         out_shape=tuple(jax.ShapeDtypeStruct((rows, size), dtype) for _, size in lanes)
-        + tuple(jax.ShapeDtypeStruct(x.shape, x.dtype) for x in through),
-        in_specs=[pl.BlockSpec(memory_space=pltpu.VMEM)] * 2 + [pl.BlockSpec(memory_space=pl.ANY)] * len(through),
-        out_specs=(pl.BlockSpec(memory_space=pltpu.VMEM),) * parts
-        + (pl.BlockSpec(memory_space=pl.ANY),) * len(through),
+        + tuple(jax.ShapeDtypeStruct(x.shape, x.dtype) for x in (*through, *mixed)),
+        in_specs=[vmem] * 2 + [keep] * len(through) + [vmem] * len(mixing),
+        out_specs=(vmem,) * parts + (keep,) * len(through) + (pl.BlockSpec(memory_space=pltpu.HBM),) * extra,
         input_output_aliases={2 + i: parts + i for i in range(len(through))},
+        scratch_shapes=[pltpu.VMEM(x.shape, BF) for x in mixed] + [pltpu.SemaphoreType.DMA] * extra,
         compiler_params=pltpu.CompilerParams(vmem_limit_bytes=8 * 1024 * 1024),
         cost_estimate=pl.CostEstimate(
             flops=4 * TILE * rows * (high - low), bytes_accessed=8 * TILE * F + 4 * rows * F, transcendentals=0
         ),
         name="weight_blocks",
-    )(mine, met, *through)
-
-
-def mix(aggregate, activated, w_out, after):
-    def kernel(agg_ref, act_ref, w_ref, after_ref, out_ref):
-        branch = jnp.dot(act_ref[...], w_ref[...], preferred_element_type=FP)
-        out_ref[...] = (agg_ref[...] + branch).astype(BF)
-
-    vmem = pl.BlockSpec(memory_space=pltpu.VMEM)
-    return pl.pallas_call(
-        kernel,
-        out_shape=jax.ShapeDtypeStruct(aggregate.shape, BF),
-        in_specs=[vmem, vmem, vmem, pl.BlockSpec(memory_space=pl.ANY)],
-        out_specs=vmem,
-        compiler_params=pltpu.CompilerParams(vmem_limit_bytes=8 * 1024 * 1024),
-        cost_estimate=pl.CostEstimate(flops=0, bytes_accessed=0, transcendentals=0),
-        name="mix",
-    )(aggregate, activated, w_out, after)
+    )(mine, met, *through, *mixing)
 
 
 def small_call(kernel, name, outs, operands, after=()):
@@ -390,6 +389,29 @@
 
     outs = (jax.ShapeDtypeStruct((2 * n, lanes), BF),)
     return small_call(kernel, "joined", outs, (held, came), after)[0]
+
+
+def product(block, rows, first):
+    n = block.shape[0] - first
+
+    def kernel(block_ref, rows_ref, out_ref):
+        out_ref[...] = jnp.dot(block_ref[first:], rows_ref[...], preferred_element_type=FP)
+
+    return small_call(kernel, "product", (jax.ShapeDtypeStruct((n, F), FP),), (block, rows))[0]
+
+
+def stacked(pieces, after):
+    n = sum(x.shape[0] for x in pieces)
+
+    def kernel(*refs):
+        out_ref = refs[-1]
+        at = 0
+        for x in refs[:-1]:
+            out_ref[at : at + x.shape[0]] = x[...]
+            out_ref[n + at : n + at + x.shape[0]] = x[...]
+            at += x.shape[0]
+
+    return small_call(kernel, "stacked", (jax.ShapeDtypeStruct((2 * n, F), BF),), tuple(pieces), after)[0]
 
 
 def shards(
@@ -426,15 +448,17 @@
     here = [features]
     for q in range(1, n_row):
         here.append(exchange(features, n_row, n_col, (q, reversed_bits(q, row_bits)), (0, 0)))
-    there = [swap_cores(features, n_row, n_col), swap_cores(jnp.concatenate(here[1:], axis=0), n_row, n_col)]
+    there = [swap_cores(x, n_row, n_col) for x in here]
     near, far = build(tile_vals, tile_row, tile_col, tile_count, n_row, n_col)
     far = swap_cores(far, n_row, n_col)
     onehot = (node_type[:, None] == jnp.arange(TYPES, dtype=jnp.int32)[None, :]).astype(FP)
     gains = jnp.dot(onehot, type_gain, precision=lax.Precision.HIGHEST)
 
     mid = near.shape[0] // 2
-    here, there = jnp.concatenate(here + here, axis=0), jnp.concatenate(there + there, axis=0)
-    sent = rounded(dot(near[mid:], here, ((1,), (0,))) + dot(far[mid:], there, ((1,), (0,))))
+    here = jnp.concatenate(here + here, axis=0)
+    part = product(near, here, mid)
+    there = stacked(there, (part,))
+    sent = rounded(part + dot(far[mid:], there, ((1,), (0,))))
     total = dot(near[:mid], here, ((1,), (0,))) + dot(far[:mid], there, ((1,), (0,)))
     for step in reversed(range(z_bits)):
         came = z_step(sent, step)
@@ -445,11 +469,12 @@
     met = swap_cores(away, n_row, n_col)
     node_rows = node_gradients(grad_hidden, w_in, aggregate, gains, cotangent, onehot.T)
     parts = 2
-    lanes = [(i * F // parts, F // parts) for i in range(parts)]
+    sizes = (2 * TILE, 2 * TILE)
+    lanes = [(sum(sizes[:i]), sizes[i]) for i in range(parts)]
     ahead, behind = range(n_row // 2, n_row), range(n_row // 2)
     first, node_rows = weight_blocks(mine, met, ahead, n_row, lanes[:1], BF, (node_rows,))
     sent = [first] + [weight_blocks(mine, met, ahead, n_row, [x], BF)[0] for x in lanes[1:]]
-    sums = list(weight_blocks(mine, met, behind, n_row, lanes, FP))
+    *sums, mixed = weight_blocks(mine, met, behind, n_row, lanes, FP, (), (aggregate, activated, w_out))
 
     grad_rows, gain = node_rows[:TILE], node_rows[TILE:]
     for step in range(z_bits):
@@ -469,13 +494,10 @@
         low = low[:size] + came[:size].astype(FP)
     grad_x = low
 
-    mixed = None
     for step in reversed(range(row_bits)):
         for i in range(parts):
             mid = sums[i].shape[0] // 2
             came = row_step(sent[i], step)
-            if mixed is None:
-                mixed = mix(aggregate, activated, w_out, came)
             sums[i] = sums[i] + came.astype(FP)
             if step:
                 sums[i], sent[i] = sums[i][:mid], rounded(sums[i][mid:])
@@ -500,9 +522,12 @@
     factor = float(total_nodes) ** (-0.5)
     others = [swap_cores(x, n_row, n_col) for x in sent]
     gains = [gain, swap_cores(gain, n_row, n_col)]
-    *weights, came[0] = write_weights(sent, others, [], [], 0, 0, n_row, factor, came[:1])
+    half = n_row // 2
+    *weights, came[0] = write_weights(sent, others, [], [], 0, 0, n_row, factor, came[:1], [grad_x])
     others = [swap_cores(x, n_row, n_col) for x in came]
-    *weights, grad_gain = write_weights(came, others, weights, gains, n_row // 2, 0, n_row, factor)
+    for i in range(parts - 1):
+        weights = write_weights(came[i : i + 1], others[i : i + 1], weights, [], half, lanes[i][0], n_row, factor)
+    *weights, grad_gain = write_weights(came[-1:], others[-1:], weights, gains, half, lanes[-1][0], n_row, factor)
     grad_w_in, grad_w_out = weights
     return mixed, grad_x, grad_w_in, grad_w_out, grad_gain
 

time: 81.3 us -> 79.8 us (0.982)
  waiting for transfers between devices: 31.3 us -> 29.6 us
  starting transfers between devices: 31.8 us -> 32.7 us
    ppermute x10 -> x12, starting transfers between devices: 1.37 us -> 2.81 us  [swap_cores(): return lax.ppermute(x, AXES, [(i, i ^ 1) for i in range(rows * cols)])]
    ppermute x10 -> x12, waiting for transfers between devices: 3.42 us -> 2.02 us  [swap_cores(): return lax.ppermute(x, AXES, [(i, i ^ 1) for i in range(rows * cols)])]
    pallas_call x1 -> x0, Pallas kernels: 0.97 us -> none  [mix(): pl.pallas_call(kernel, out_shape=jax.ShapeDtypeStruct(aggregate.shape, BF...]
    pallas_call x2 -> x3, Pallas kernels: 3.46 us -> 4.12 us  [write_weights(): pl.pallas_call(kernel, out_shape=(jax.ShapeDtypeStruct((F, 2 * F), FP), j...]
    dot_general x6 -> x5, matrix products: 2.68 us -> 2.25 us  [dot(): return lax.dot_general(a, b, (dims, ((), ())), preferred_element_type=FP)]
  transfers between devices with their start and end apart: 31 -> 33, of which waited for: 18 -> 15; matrix products, arithmetic and copies ran while one was open for 5% -> 4% of each run, Pallas kernels for 9% -> 10%
where the time goes in v5:
time: 79.8 us; the launch traced here: 78.5 us
  starting transfers between devices  32.7 us (41%)
  waiting for transfers between devices  29.6 us (37%)
  Pallas kernels  11 us (14%)
  matrix products  2.56 us (3%)
  between operations  1.84 us (2%)
    ppermute x21, starting transfers between devices, exchange(): return lax.ppermute(x, AXES, pairs)  29.8 us
    ppermute x21, waiting for transfers between devices, exchange(): return lax.ppermute(x, AXES, pairs)  27.6 us
    pallas_call x3, Pallas kernels, write_weights(): pl.pallas_call(kernel, out_shape=(jax.ShapeDtypeStruct((F, 2 * F), FP), j...  4.12 us
    ppermute x12, starting transfers between devices, swap_cores(): return lax.ppermute(x, AXES, [(i, i ^ 1) for i in range(rows * cols)])  2.81 us
    pallas_call x1, Pallas kernels, build(): pl.pallas_call(kernel, out_shape=(result, result), in_specs=[pl.BlockSpec...  2.74 us
    dot_general x5, matrix products, dot(): return lax.dot_general(a, b, (dims, ((), ())), preferred_element_type=FP)  2.25 us
    ppermute x12, waiting for transfers between devices, swap_cores(): return lax.ppermute(x, AXES, [(i, i ^ 1) for i in range(rows * cols)])  2.02 us
    pallas_call x3, Pallas kernels, weight_blocks(): pl.pallas_call(kernel, out_shape=tuple((jax.ShapeDtypeStruct((rows, size)...  2.01 us
  transfers between devices with their start and end apart: 33, of which 15 were waited for; matrix products, arithmetic and copies ran while one was open for 4% of the time, Pallas kernels for 10%

profile of v5, /device:TPU:0, one launch (start us, length us, event | category | flops | bytes accessed | tf_op | source)
XLA Modules:
  0.0 78.5 jit_solution(3335486726957736720)
XLA Ops:
  0.6 3.0 %collective-permute-start = (bf16[128,512]{1,0:T(8,128)(2,1)}, bf16[128,512]{1,0:T(8,128)(2,1)S(1)}, u32[]{:S(2)}, u32[]{:S(2)}) collective-permute-start(bf16[128,512]{1,0:T(8,128)(2,1)} %param.10), channel_id=1, source_target_pairs={{0,8},{1,17},{2,10},{3,19},{4,12},{5,21},{6,14},{7,23},{8,0},{9,25... | collective-permute-start | bytes 393224 | tf_op jit(solution)/shard_map/ppermute | solution.py:30
  3.7 1.5 %collective-permute-start.1 = (bf16[128,512]{1,0:T(8,128)(2,1)}, bf16[128,512]{1,0:T(8,128)(2,1)S(1)}, u32[]{:S(2)}, u32[]{:S(2)}) collective-permute-start(bf16[128,512]{1,0:T(8,128)(2,1)} %param.10), channel_id=1, source_target_pairs={{0,16},{1,9},{2,18},{3,11},{4,20},{5,13},{6,22},{7,15},{8,24},{9,1... | collective-permute-start | bytes 393224 | tf_op jit(solution)/shard_map/ppermute | solution.py:30
  5.9 2.7 %build_dense.1 = (bf16[512,1024]{1,0:T(8,128)(2,1)S(1)}, bf16[512,1024]{1,0:T(8,128)(2,1)S(1)}) custom-call(s32[1,1]{1,0:T(1,128)S(6)} %copy.34.count_ref, s32[1,128]{1,0:T(1,128)} %rows_ref.1, s32[1,128]{1,0:T(1,128)} %cols_ref.1, bf16[1,128,128,128]{3,2,1,0:T(8,128)(2,1)} %vals_ref.1), custom_call_target="tpu_custom_call" | custom-call | flops 2097152 | bytes 6291456 | tf_op jit(solution)/shard_map/build_dense/pallas_call | solution.py:105
  8.6 0.6 collective-permute-start.3
  9.2 0.1 collective-permute-start.5
  9.3 2.3 %collective-permute-done.1 = bf16[128,512]{1,0:T(8,128)(2,1)S(1)} collective-permute-done((bf16[128,512]{1,0:T(8,128)(2,1)}, bf16[128,512]{1,0:T(8,128)(2,1)S(1)}, u32[]{:S(2)}, u32[]{:S(2)}) %collective-permute-start.1) | collective-permute-done | bytes 131104 | tf_op jit(solution)/shard_map/ppermute | solution.py:30
  11.6 0.5 collective-permute-start.7
  12.3 0.4 fusion.8
  12.7 0.4 product.1.refs_4_
  13.2 0.1 stacked.1
  13.3 0.4 fusion.2
  13.8 2.4 %collective-permute-start.8 = (bf16[256,512]{1,0:T(8,128)(2,1)S(1)}, bf16[256,512]{1,0:T(8,128)(2,1)S(1)}, u32[]{:S(2)}, u32[]{:S(2)}) collective-permute-start(bf16[256,512]{1,0:T(8,128)(2,1)S(1)} %fusion.2), channel_id=1, source_target_pairs={{0,4},{1,3},{2,6},{3,1},{4,0},{5,7},{6,2},{7,5},{8,12},{9,11},{10,... | collective-permute-start | bytes 786440 | tf_op jit(solution)/shard_map/ppermute | solution.py:30
  16.2 0.4 convolution_add_fusion.2.refs_0_
  16.7 6.5 %collective-permute-done.8.refs_1_ = bf16[256,512]{1,0:T(8,128)(2,1)S(1)} collective-permute-done((bf16[256,512]{1,0:T(8,128)(2,1)S(1)}, bf16[256,512]{1,0:T(8,128)(2,1)S(1)}, u32[]{:S(2)}, u32[]{:S(2)}) %collective-permute-start.8) | collective-permute-done | bytes 262176 | tf_op jit(solution)/shard_map/ppermute | solution.py:30
  23.2 1.5 %collective-permute-start.9 = (bf16[128,512]{1,0:T(8,128)(2,1)S(1)}, bf16[128,512]{1,0:T(8,128)(2,1)S(1)}, u32[]{:S(2)}, u32[]{:S(2)}) collective-permute-start(bf16[128,512]{1,0:T(8,128)(2,1)S(1)} %get-tuple-element.30), channel_id=1, source_target_pairs={{0,2},{1,5},{2,0},{3,7},{4,6},{5,1},{6,4},{7,3},{8,10},{9,13},{10,... | collective-permute-start | bytes 393224 | tf_op jit(solution)/shard_map/ppermute | solution.py:30
  24.8 0.3 fusion.17.refs_2_.gains_ref
  25.1 4.1 %collective-permute-done.9.refs_1_ = bf16[128,512]{1,0:T(8,128)(2,1)S(1)} collective-permute-done((bf16[128,512]{1,0:T(8,128)(2,1)S(1)}, bf16[128,512]{1,0:T(8,128)(2,1)S(1)}, u32[]{:S(2)}, u32[]{:S(2)}) %collective-permute-start.9) | collective-permute-done | bytes 131104 | tf_op jit(solution)/shard_map/ppermute | solution.py:30
  29.2 0.8 node_values.1
  30.0 0.1 collective-permute-start.10
  30.1 0.8 node_gradients.1.refs_0_
  30.8 0.9 %collective-permute-done.10.met_ref = bf16[128,1536]{1,0:T(8,128)(2,1)S(1)} collective-permute-done((bf16[128,1536]{1,0:T(8,128)(2,1)S(1)}, bf16[128,1536]{1,0:T(8,128)(2,1)S(1)}, u32[]{:S(2)}, u32[]{:S(2)}) %collective-permute-start.10) | collective-permute-done | bytes 393248 | tf_op jit(solution)/shard_map/ppermute | solution.py:34
  31.8 0.5 weight_blocks.4
  32.3 0.6 collective-permute-start.11
  32.9 1.9 %collective-permute-start.21 = (bf16[512,256]{1,0:T(8,128)(2,1)S(1)}, bf16[512,256]{1,0:T(8,128)(2,1)S(1)}, u32[]{:S(2)}, u32[]{:S(2)}) collective-permute-start(bf16[512,256]{1,0:T(8,128)(2,1)S(1)} %get-tuple-element.40), channel_id=1, source_target_pairs={{0,16},{1,9},{2,18},{3,11},{4,20},{5,13},{6,22},{7,15},{8,24},{9,1... | collective-permute-start | bytes 786440 | tf_op jit(solution)/shard_map/ppermute | solution.py:30
  34.9 0.5 weight_blocks.5
  35.4 0.2 collective-permute-start.16
  35.6 1.0 %weight_blocks.3 = (f32[512,256]{1,0:T(8,128)S(1)}, f32[512,256]{1,0:T(8,128)S(1)}, bf16[128,512]{1,0:T(8,128)(2,1)}) custom-call(bf16[128,1536]{1,0:T(8,128)(2,1)S(1)} %get-tuple-element.31.mine_ref, bf16[128,1536]{1,0:T(8,128)(2,1)S(1)} %collective-permute-done.10.met_ref, f32[128,512]{1,0:T(8,128)S(1)} %get-tuple-element.33.refs_0_.agg_ref, ...), custom_call_target="tpu_custom_call" | custom-call | flops 134217728 | bytes 1572864 | tf_op jit(solution)/shard_map/weight_blocks/pallas_call | solution.py:291
  36.6 2.5 %collective-permute-done.11 = bf16[144,512]{1,0:T(8,128)(2,1)S(1)} collective-permute-done((bf16[144,512]{1,0:T(8,128)(2,1)S(1)}, bf16[144,512]{1,0:T(8,128)(2,1)S(1)}, u32[]{:S(2)}, u32[]{:S(2)}) %collective-permute-start.11) | collective-permute-done | bytes 147488 | tf_op jit(solution)/shard_map/ppermute | solution.py:30
  39.1 1.3 %collective-permute-start.12 = (bf16[272,512]{1,0:T(8,128)(2,1)S(1)}, bf16[272,512]{1,0:T(8,128)(2,1)S(1)}, u32[]{:S(2)}, u32[]{:S(2)}) collective-permute-start(bf16[272,512]{1,0:T(8,128)(2,1)S(1)} %pad_maximum_fusion.1), channel_id=1, source_target_pairs={{0,4},{1,3},{2,6},{3,1},{4,0},{5,7},{6,2},{7,5},{8,12},{9,11},{10,... | collective-permute-start | bytes 835592 | tf_op jit(solution)/shard_map/ppermute | solution.py:30
  40.5 1.5 %collective-permute-start.22 = (bf16[256,256]{1,0:T(8,128)(2,1)S(1)}, bf16[256,256]{1,0:T(8,128)(2,1)S(1)}, u32[]{:S(2)}, u32[]{:S(2)}) collective-permute-start(bf16[256,256]{1,0:T(8,128)(2,1)S(1)} %fusion.10), channel_id=1, source_target_pairs={{0,8},{1,17},{2,10},{3,19},{4,12},{5,21},{6,14},{7,23},{8,0},{9,25... | collective-permute-start | bytes 393224 | tf_op jit(solution)/shard_map/ppermute | solution.py:30
  42.0 0.2 collective-permute-done.16
  42.2 0.1 convert_add_fusion.1
  42.3 1.5 %collective-permute-start.17 = (bf16[256,256]{1,0:T(8,128)(2,1)S(1)}, bf16[256,256]{1,0:T(8,128)(2,1)S(1)}, u32[]{:S(2)}, u32[]{:S(2)}) collective-permute-start(bf16[256,256]{1,0:T(8,128)(2,1)S(1)} %fusion.13), channel_id=1, source_target_pairs={{0,8},{1,17},{2,10},{3,19},{4,12},{5,21},{6,14},{7,23},{8,0},{9,25... | collective-permute-start | bytes 393224 | tf_op jit(solution)/shard_map/ppermute | solution.py:30
  43.8 1.7 %collective-permute-done.22 = bf16[256,256]{1,0:T(8,128)(2,1)S(1)} collective-permute-done((bf16[256,256]{1,0:T(8,128)(2,1)S(1)}, bf16[256,256]{1,0:T(8,128)(2,1)S(1)}, u32[]{:S(2)}, u32[]{:S(2)}) %collective-permute-start.22) | collective-permute-done | bytes 131104 | tf_op jit(solution)/shard_map/ppermute | solution.py:30
  45.6 2.6 %collective-permute-start.23 = (bf16[256,256]{1,0:T(8,128)(2,1)S(1)}, bf16[256,256]{1,0:T(8,128)(2,1)S(1)}, u32[]{:S(2)}, u32[]{:S(2)}) collective-permute-start(bf16[256,256]{1,0:T(8,128)(2,1)S(1)} %fusion.12), channel_id=1, source_target_pairs={{0,2},{1,5},{2,0},{3,7},{4,6},{5,1},{6,4},{7,3},{8,10},{9,13},{10,... | collective-permute-start | bytes 393224 | tf_op jit(solution)/shard_map/ppermute | solution.py:30
  48.2 1.6 %collective-permute-start.18 = (bf16[256,256]{1,0:T(8,128)(2,1)S(1)}, bf16[256,256]{1,0:T(8,128)(2,1)S(1)}, u32[]{:S(2)}, u32[]{:S(2)}) collective-permute-start(bf16[256,256]{1,0:T(8,128)(2,1)S(1)} %fusion.15.refs_0_), channel_id=1, source_target_pairs={{0,2},{1,5},{2,0},{3,7},{4,6},{5,1},{6,4},{7,3},{8,10},{9,13},{10,... | collective-permute-start | bytes 393224 | tf_op jit(solution)/shard_map/ppermute | solution.py:30
  49.8 2.4 %collective-permute-done.12 = bf16[272,512]{1,0:T(8,128)(2,1)S(1)} collective-permute-done((bf16[272,512]{1,0:T(8,128)(2,1)S(1)}, bf16[272,512]{1,0:T(8,128)(2,1)S(1)}, u32[]{:S(2)}, u32[]{:S(2)}) %collective-permute-start.12) | collective-permute-done | bytes 278560 | tf_op jit(solution)/shard_map/ppermute | solution.py:30
  52.2 0.5 fusion
  52.7 0.1 collective-permute-start.13
  52.9 0.8 collective-permute-start.24
  53.7 1.0 %collective-permute-done.13 = bf16[512,512]{1,0:T(8,128)(2,1)S(1)} collective-permute-done((bf16[512,512]{1,0:T(8,128)(2,1)S(1)}, bf16[512,512]{1,0:T(8,128)(2,1)S(1)}, u32[]{:S(2)}, u32[]{:S(2)}) %collective-permute-start.13) | collective-permute-done | bytes 524320 | tf_op jit(solution)/shard_map/ppermute | solution.py:34
  54.7 0.5 convolution_add_fusion
  55.2 1.8 %collective-permute-start.14 = (bf16[272,512]{1,0:T(8,128)(2,1)S(1)}, bf16[272,512]{1,0:T(8,128)(2,1)S(1)}, u32[]{:S(2)}, u32[]{:S(2)}) collective-permute-start(bf16[272,512]{1,0:T(8,128)(2,1)S(1)} %pad_maximum_fusion.2.refs_2_), channel_id=1, source_target_pairs={{0,16},{1,9},{2,18},{3,11},{4,20},{5,13},{6,22},{7,15},{8,24},{9,1... | collective-permute-start | bytes 835592 | tf_op jit(solution)/shard_map/ppermute | solution.py:30
  57.1 1.3 %collective-permute-start.19 = (bf16[256,256]{1,0:T(8,128)(2,1)S(1)}, bf16[256,256]{1,0:T(8,128)(2,1)S(1)}, u32[]{:S(2)}, u32[]{:S(2)}) collective-permute-start(bf16[256,256]{1,0:T(8,128)(2,1)S(1)} %added.3), channel_id=1, source_target_pairs={{0,4},{1,3},{2,6},{3,1},{4,0},{5,7},{6,2},{7,5},{8,12},{9,11},{10,... | collective-permute-start | bytes 393224 | tf_op jit(solution)/shard_map/ppermute | solution.py:30
  58.3 0.6 collective-permute-done.24
  59.0 1.5 %collective-permute-start.25 = (bf16[256,256]{1,0:T(8,128)(2,1)S(1)}, bf16[256,256]{1,0:T(8,128)(2,1)S(1)}, u32[]{:S(2)}, u32[]{:S(2)}) collective-permute-start(bf16[256,256]{1,0:T(8,128)(2,1)S(1)} %reduce-precision_convert_fusion.refs_0_), channel_id=1, source_target_pairs={{0,8},{1,17},{2,10},{3,19},{4,12},{5,21},{6,14},{7,23},{8,0},{9,25... | collective-permute-start | bytes 393224 | tf_op jit(solution)/shard_map/ppermute | solution.py:30
  60.4 3.0 %collective-permute-done.19 = bf16[256,256]{1,0:T(8,128)(2,1)S(1)} collective-permute-done((bf16[256,256]{1,0:T(8,128)(2,1)S(1)}, bf16[256,256]{1,0:T(8,128)(2,1)S(1)}, u32[]{:S(2)}, u32[]{:S(2)}) %collective-permute-start.19) | collective-permute-done | bytes 131104 | tf_op jit(solution)/shard_map/ppermute | solution.py:30
  63.4 1.3 %collective-permute-start.20 = (bf16[256,256]{1,0:T(8,128)(2,1)S(1)}, bf16[256,256]{1,0:T(8,128)(2,1)S(1)}, u32[]{:S(2)}, u32[]{:S(2)}) collective-permute-start(bf16[256,256]{1,0:T(8,128)(2,1)S(1)} %reduce-precision_convert_fusion.2.refs_0_), channel_id=1, source_target_pairs={{0,8},{1,17},{2,10},{3,19},{4,12},{5,21},{6,14},{7,23},{8,0},{9,25... | collective-permute-start | bytes 393224 | tf_op jit(solution)/shard_map/ppermute | solution.py:30
  64.8 0.1 slice_add_fusion
  64.9 0.9 %collective-permute-start.15 = (bf16[144,512]{1,0:T(8,128)(2,1)S(1)}, bf16[144,512]{1,0:T(8,128)(2,1)S(1)}, u32[]{:S(2)}, u32[]{:S(2)}) collective-permute-start(bf16[144,512]{1,0:T(8,128)(2,1)S(1)} %pad_maximum_fusion.5.refs_3_), channel_id=1, source_target_pairs={{0,8},{1,17},{2,10},{3,19},{4,12},{5,21},{6,14},{7,23},{8,0},{9,25... | collective-permute-start | bytes 442376 | tf_op jit(solution)/shard_map/ppermute | solution.py:30
  65.8 0.1 collective-permute-start.28
  65.9 1.3 %collective-permute-start.30 = (bf16[512,256]{1,0:T(8,128)(2,1)S(1)}, bf16[512,256]{1,0:T(8,128)(2,1)S(1)}, u32[]{:S(2)}, u32[]{:S(2)}) collective-permute-start(bf16[512,256]{1,0:T(8,128)(2,1)S(1)} %joined.2.refs_2_.refs_0_), channel_id=1, source_target_pairs={{0,16},{1,9},{2,18},{3,11},{4,20},{5,13},{6,22},{7,15},{8,24},{9,1... | collective-permute-start | bytes 786440 | tf_op jit(solution)/shard_map/ppermute | solution.py:30
  67.2 1.3 %collective-permute-done.20.refs_1_ = bf16[256,256]{1,0:T(8,128)(2,1)S(1)} collective-permute-done((bf16[256,256]{1,0:T(8,128)(2,1)S(1)}, bf16[256,256]{1,0:T(8,128)(2,1)S(1)}, u32[]{:S(2)}, u32[]{:S(2)}) %collective-permute-start.20) | collective-permute-done | bytes 131104 | tf_op jit(solution)/shard_map/ppermute | solution.py:30
  68.5 0.1 collective-permute-start.29
  68.6 1.3 %collective-permute-start.26 = (bf16[512,256]{1,0:T(8,128)(2,1)S(1)}, bf16[512,256]{1,0:T(8,128)(2,1)S(1)}, u32[]{:S(2)}, u32[]{:S(2)}) collective-permute-start(bf16[512,256]{1,0:T(8,128)(2,1)S(1)} %joined.3.refs_1_), channel_id=1, source_target_pairs={{0,16},{1,9},{2,18},{3,11},{4,20},{5,13},{6,22},{7,15},{8,24},{9,1... | collective-permute-start | bytes 786440 | tf_op jit(solution)/shard_map/ppermute | solution.py:30
  69.9 1.4 %collective-permute-done.15 = bf16[144,512]{1,0:T(8,128)(2,1)S(1)} collective-permute-done((bf16[144,512]{1,0:T(8,128)(2,1)S(1)}, bf16[144,512]{1,0:T(8,128)(2,1)S(1)}, u32[]{:S(2)}, u32[]{:S(2)}) %collective-permute-start.15) | collective-permute-done | bytes 147488 | tf_op jit(solution)/shard_map/ppermute | solution.py:30
  71.4 0.9 %collective-permute-done.30.refs_4_ = bf16[512,256]{1,0:T(8,128)(2,1)S(1)} collective-permute-done((bf16[512,256]{1,0:T(8,128)(2,1)S(1)}, bf16[512,256]{1,0:T(8,128)(2,1)S(1)}, u32[]{:S(2)}, u32[]{:S(2)}) %collective-permute-start.30) | collective-permute-done | bytes 262176 | tf_op jit(solution)/shard_map/ppermute | solution.py:30
  72.3 1.4 %write_weights.3 = (f32[512,1024]{1,0:T(8,128)}, f32[1024,512]{1,0:T(8,128)}, bf16[512,256]{1,0:T(8,128)(2,1)S(1)}) custom-call(bf16[512,256]{1,0:T(8,128)(2,1)S(1)} %joined.2.refs_2_.refs_0_, bf16[512,256]{1,0:T(8,128)(2,1)S(1)} %joined.3.refs_1_, bf16[512,256]{1,0:T(8,128)(2,1)S(1)} %collective-permute-done.28.refs_2_, ...), custom_call_target="tpu_custom_call", output_to_operand_aliasing={{2}: (4, {})} | custom-call | tf_op jit(solution)/shard_map/write_weights/pallas_call | solution.py:184
  73.7 0.8 collective-permute-start.31
  74.5 0.6 collective-permute-done.26.refs_0_
  75.1 0.4 collective-permute-start.27
  75.6 0.2 collective-permute-start.32
  75.7 1.0 %write_weights.4 = (f32[512,1024]{1,0:T(8,128)}, f32[1024,512]{1,0:T(8,128)}) custom-call(bf16[512,256]{1,0:T(8,128)(2,1)S(1)} %get-tuple-element.41.refs_0_, bf16[512,256]{1,0:T(8,128)(2,1)S(1)} %collective-permute-done.31.refs_1_, f32[512,1024]{1,0:T(8,128)} %get-tuple-element.42.refs_2_, ...), custom_call_target="tpu_custom_call", output_to_operand_aliasing={{0}: (2, {}), {1}: (3, {})} | custom-call | tf_op jit(solution)/shard_map/write_weights/pallas_call | solution.py:184
  76.8 1.6 %write_weights.5 = (f32[512,1024]{1,0:T(8,128)}, f32[1024,512]{1,0:T(8,128)}, f32[8,512]{1,0:T(8,128)}) custom-call(bf16[512,256]{1,0:T(8,128)(2,1)S(1)} %collective-permute-done.26.refs_0_, bf16[512,256]{1,0:T(8,128)(2,1)S(1)} %collective-permute-done.27.refs_1_, ...), custom_call_target="tpu_custom_call", output_to_operand_aliasing={{0}: (2, {}), {1}: (3, {})} | custom-call | tf_op jit(solution)/shard_map/write_weights/pallas_call | solution.py:184
  (82 shorter events, 0.9 us)
Async XLA Ops:
  0.6 24.1 %copy-start = (f32[8,512]{1,0:T(8,128)S(1)}, f32[8,512]{1,0:T(8,128)}, u32[]{:S(2)}) copy-start(f32[8,512]{1,0:T(8,128)} %param.16) | copy-start | bytes 49156
  0.6 8.6 %collective-permute-start = (bf16[128,512]{1,0:T(8,128)(2,1)}, bf16[128,512]{1,0:T(8,128)(2,1)S(1)}, u32[]{:S(2)}, u32[]{:S(2)}) collective-permute-start(bf16[128,512]{1,0:T(8,128)(2,1)} %param.10), channel_id=1, source_target_pairs={{0,8},{1,17},{2,10},{3,19},{4,12},{5,21},{6,14},{7,23},{8,0},{9,25... | collective-permute-start | bytes 393224 | tf_op jit(solution)/shard_map/ppermute | solution.py:30
  3.7 8.0 %collective-permute-start.1 = (bf16[128,512]{1,0:T(8,128)(2,1)}, bf16[128,512]{1,0:T(8,128)(2,1)S(1)}, u32[]{:S(2)}, u32[]{:S(2)}) collective-permute-start(bf16[128,512]{1,0:T(8,128)(2,1)} %param.10), channel_id=1, source_target_pairs={{0,16},{1,9},{2,18},{3,11},{4,20},{5,13},{6,22},{7,15},{8,24},{9,1... | collective-permute-start | bytes 393224 | tf_op jit(solution)/shard_map/ppermute | solution.py:30
  5.2 6.5 %collective-permute-start.2 = (bf16[128,512]{1,0:T(8,128)(2,1)}, bf16[128,512]{1,0:T(8,128)(2,1)S(1)}, u32[]{:S(2)}, u32[]{:S(2)}) collective-permute-start(bf16[128,512]{1,0:T(8,128)(2,1)} %param.10), channel_id=1, source_target_pairs={{0,24},{1,25},{2,26},{3,27},{4,28},{5,29},{6,30},{7,31},{8,16},{9,... | collective-permute-start | bytes 393224 | tf_op jit(solution)/shard_map/ppermute | solution.py:30
  5.2 8.0 %collective-permute-start.4 = (bf16[128,512]{1,0:T(8,128)(2,1)}, bf16[128,512]{1,0:T(8,128)(2,1)S(1)}, u32[]{:S(2)}, u32[]{:S(2)}) collective-permute-start(bf16[128,512]{1,0:T(8,128)(2,1)} %param.10), channel_id=1, source_target_pairs={{0,1},{1,0},{2,3},{3,2},{4,5},{5,4},{6,7},{7,6},{8,9},{9,8},{10,11... | collective-permute-start | bytes 393224 | tf_op jit(solution)/shard_map/ppermute | solution.py:34
  5.8 3.3 %copy-start.5 = (bf16[128,512]{1,0:T(8,128)(2,1)S(1)}, bf16[128,512]{1,0:T(8,128)(2,1)}, u32[]{:S(2)}) copy-start(bf16[128,512]{1,0:T(8,128)(2,1)} %param.10) | copy-start | bytes 393220
  8.6 4.7 %collective-permute-start.3 = (bf16[512,1024]{1,0:T(8,128)(2,1)S(1)}, bf16[512,1024]{1,0:T(8,128)(2,1)S(1)}, u32[]{:S(2)}, u32[]{:S(2)}) collective-permute-start(bf16[512,1024]{1,0:T(8,128)(2,1)S(1)} %get-tuple-element.28), channel_id=1, source_target_pairs={{0,1},{1,0},{2,3},{3,2},{4,5},{5,4},{6,7},{7,6},{8,9},{9,8},{10,11... | collective-permute-start | bytes 3145736 | tf_op jit(solution)/shard_map/ppermute | solution.py:34
  9.2 4.0 %collective-permute-start.5 = (bf16[128,512]{1,0:T(8,128)(2,1)S(1)}, bf16[128,512]{1,0:T(8,128)(2,1)S(1)}, u32[]{:S(2)}, u32[]{:S(2)}) collective-permute-start(bf16[128,512]{1,0:T(8,128)(2,1)S(1)} %collective-permute-done), channel_id=1, source_target_pairs={{0,1},{1,0},{2,3},{3,2},{4,5},{5,4},{6,7},{7,6},{8,9},{9,8},{10,11... | collective-permute-start | bytes 393224 | tf_op jit(solution)/shard_map/ppermute | solution.py:34
  11.6 1.6 %collective-permute-start.6 = (bf16[128,512]{1,0:T(8,128)(2,1)S(1)}, bf16[128,512]{1,0:T(8,128)(2,1)S(1)}, u32[]{:S(2)}, u32[]{:S(2)}) collective-permute-start(bf16[128,512]{1,0:T(8,128)(2,1)S(1)} %collective-permute-done.1), channel_id=1, source_target_pairs={{0,1},{1,0},{2,3},{3,2},{4,5},{5,4},{6,7},{7,6},{8,9},{9,8},{10,11... | collective-permute-start | bytes 393224 | tf_op jit(solution)/shard_map/ppermute | solution.py:34
  11.6 1.6 %collective-permute-start.7 = (bf16[128,512]{1,0:T(8,128)(2,1)S(1)}, bf16[128,512]{1,0:T(8,128)(2,1)S(1)}, u32[]{:S(2)}, u32[]{:S(2)}) collective-permute-start(bf16[128,512]{1,0:T(8,128)(2,1)S(1)} %collective-permute-done.2), channel_id=1, source_target_pairs={{0,1},{1,0},{2,3},{3,2},{4,5},{5,4},{6,7},{7,6},{8,9},{9,8},{10,11... | collective-permute-start | bytes 393224 | tf_op jit(solution)/shard_map/ppermute | solution.py:34
  13.7 11.0 %copy-start.6 = (s32[128]{0:T(128)S(1)}, s32[128]{0:T(128)}, u32[]{:S(2)}) copy-start(s32[128]{0:T(128)} %param.15) | copy-start | bytes 1540
  13.8 15.5 %copy-start.1 = (bf16[512,1024]{1,0:T(8,128)(2,1)S(1)}, bf16[512,1024]{1,0:T(8,128)(2,1)}, u32[]{:S(2)}) copy-start(bf16[512,1024]{1,0:T(8,128)(2,1)} %w_ref.1) | copy-start | bytes 3145732
  13.8 15.5 %copy-start.2 = (bf16[1024,512]{1,0:T(8,128)(2,1)S(1)}, bf16[1024,512]{1,0:T(8,128)(2,1)}, u32[]{:S(2)}) copy-start(bf16[1024,512]{1,0:T(8,128)(2,1)} %refs_2_.1) | copy-start | bytes 3145732
  13.8 15.4 %copy-start.4 = (bf16[128,512]{1,0:T(8,128)(2,1)S(1)}, bf16[128,512]{1,0:T(8,128)(2,1)}, u32[]{:S(2)}) copy-start(bf16[128,512]{1,0:T(8,128)(2,1)} %cot_ref.1) | copy-start | bytes 393220
  13.8 9.4 %collective-permute-start.8 = (bf16[256,512]{1,0:T(8,128)(2,1)S(1)}, bf16[256,512]{1,0:T(8,128)(2,1)S(1)}, u32[]{:S(2)}, u32[]{:S(2)}) collective-permute-start(bf16[256,512]{1,0:T(8,128)(2,1)S(1)} %fusion.2), channel_id=1, source_target_pairs={{0,4},{1,3},{2,6},{3,1},{4,0},{5,7},{6,2},{7,5},{8,12},{9,11},{10,... | collective-permute-start | bytes 786440 | tf_op jit(solution)/shard_map/ppermute | solution.py:30
  23.2 6.0 %collective-permute-start.9 = (bf16[128,512]{1,0:T(8,128)(2,1)S(1)}, bf16[128,512]{1,0:T(8,128)(2,1)S(1)}, u32[]{:S(2)}, u32[]{:S(2)}) collective-permute-start(bf16[128,512]{1,0:T(8,128)(2,1)S(1)} %get-tuple-element.30), channel_id=1, source_target_pairs={{0,2},{1,5},{2,0},{3,7},{4,6},{5,1},{6,4},{7,3},{8,10},{9,13},{10,... | collective-permute-start | bytes 393224 | tf_op jit(solution)/shard_map/ppermute | solution.py:30
  30.0 1.8 %collective-permute-start.10 = (bf16[128,1536]{1,0:T(8,128)(2,1)S(1)}, bf16[128,1536]{1,0:T(8,128)(2,1)S(1)}, u32[]{:S(2)}, u32[]{:S(2)}) collective-permute-start(bf16[128,1536]{1,0:T(8,128)(2,1)S(1)} %get-tuple-element.32), channel_id=1, source_target_pairs={{0,1},{1,0},{2,3},{3,2},{4,5},{5,4},{6,7},{7,6},{8,9},{9,8},{10,11... | collective-permute-start | bytes 1179656 | tf_op jit(solution)/shard_map/ppermute | solution.py:34
  32.3 6.7 %collective-permute-start.11 = (bf16[144,512]{1,0:T(8,128)(2,1)S(1)}, bf16[144,512]{1,0:T(8,128)(2,1)S(1)}, u32[]{:S(2)}, u32[]{:S(2)}) collective-permute-start(bf16[144,512]{1,0:T(8,128)(2,1)S(1)} %get-tuple-element.37), channel_id=1, source_target_pairs={{0,2},{1,5},{2,0},{3,7},{4,6},{5,1},{6,4},{7,3},{8,10},{9,13},{10,... | collective-permute-start | bytes 442376 | tf_op jit(solution)/shard_map/ppermute | solution.py:30
  32.9 7.5 %collective-permute-start.21 = (bf16[512,256]{1,0:T(8,128)(2,1)S(1)}, bf16[512,256]{1,0:T(8,128)(2,1)S(1)}, u32[]{:S(2)}, u32[]{:S(2)}) collective-permute-start(bf16[512,256]{1,0:T(8,128)(2,1)S(1)} %get-tuple-element.40), channel_id=1, source_target_pairs={{0,16},{1,9},{2,18},{3,11},{4,20},{5,13},{6,22},{7,15},{8,24},{9,1... | collective-permute-start | bytes 786440 | tf_op jit(solution)/shard_map/ppermute | solution.py:30
  35.4 6.8 %collective-permute-start.16 = (bf16[512,256]{1,0:T(8,128)(2,1)S(1)}, bf16[512,256]{1,0:T(8,128)(2,1)S(1)}, u32[]{:S(2)}, u32[]{:S(2)}) collective-permute-start(bf16[512,256]{1,0:T(8,128)(2,1)S(1)} %weight_blocks.5), channel_id=1, source_target_pairs={{0,16},{1,9},{2,18},{3,11},{4,20},{5,13},{6,22},{7,15},{8,24},{9,1... | collective-permute-start | bytes 786440 | tf_op jit(solution)/shard_map/ppermute | solution.py:30
  39.1 13.1 %collective-permute-start.12 = (bf16[272,512]{1,0:T(8,128)(2,1)S(1)}, bf16[272,512]{1,0:T(8,128)(2,1)S(1)}, u32[]{:S(2)}, u32[]{:S(2)}) collective-permute-start(bf16[272,512]{1,0:T(8,128)(2,1)S(1)} %pad_maximum_fusion.1), channel_id=1, source_target_pairs={{0,4},{1,3},{2,6},{3,1},{4,0},{5,7},{6,2},{7,5},{8,12},{9,11},{10,... | collective-permute-start | bytes 835592 | tf_op jit(solution)/shard_map/ppermute | solution.py:30
  40.5 5.0 %collective-permute-start.22 = (bf16[256,256]{1,0:T(8,128)(2,1)S(1)}, bf16[256,256]{1,0:T(8,128)(2,1)S(1)}, u32[]{:S(2)}, u32[]{:S(2)}) collective-permute-start(bf16[256,256]{1,0:T(8,128)(2,1)S(1)} %fusion.10), channel_id=1, source_target_pairs={{0,8},{1,17},{2,10},{3,19},{4,12},{5,21},{6,14},{7,23},{8,0},{9,25... | collective-permute-start | bytes 393224 | tf_op jit(solution)/shard_map/ppermute | solution.py:30
  42.3 5.9 %collective-permute-start.17 = (bf16[256,256]{1,0:T(8,128)(2,1)S(1)}, bf16[256,256]{1,0:T(8,128)(2,1)S(1)}, u32[]{:S(2)}, u32[]{:S(2)}) collective-permute-start(bf16[256,256]{1,0:T(8,128)(2,1)S(1)} %fusion.13), channel_id=1, source_target_pairs={{0,8},{1,17},{2,10},{3,19},{4,12},{5,21},{6,14},{7,23},{8,0},{9,25... | collective-permute-start | bytes 393224 | tf_op jit(solution)/shard_map/ppermute | solution.py:30
  45.6 7.3 %collective-permute-start.23 = (bf16[256,256]{1,0:T(8,128)(2,1)S(1)}, bf16[256,256]{1,0:T(8,128)(2,1)S(1)}, u32[]{:S(2)}, u32[]{:S(2)}) collective-permute-start(bf16[256,256]{1,0:T(8,128)(2,1)S(1)} %fusion.12), channel_id=1, source_target_pairs={{0,2},{1,5},{2,0},{3,7},{4,6},{5,1},{6,4},{7,3},{8,10},{9,13},{10,... | collective-permute-start | bytes 393224 | tf_op jit(solution)/shard_map/ppermute | solution.py:30
  48.2 8.8 %collective-permute-start.18 = (bf16[256,256]{1,0:T(8,128)(2,1)S(1)}, bf16[256,256]{1,0:T(8,128)(2,1)S(1)}, u32[]{:S(2)}, u32[]{:S(2)}) collective-permute-start(bf16[256,256]{1,0:T(8,128)(2,1)S(1)} %fusion.15.refs_0_), channel_id=1, source_target_pairs={{0,2},{1,5},{2,0},{3,7},{4,6},{5,1},{6,4},{7,3},{8,10},{9,13},{10,... | collective-permute-start | bytes 393224 | tf_op jit(solution)/shard_map/ppermute | solution.py:30
  52.7 2.0 %collective-permute-start.13 = (bf16[512,512]{1,0:T(8,128)(2,1)S(1)}, bf16[512,512]{1,0:T(8,128)(2,1)S(1)}, u32[]{:S(2)}, u32[]{:S(2)}) collective-permute-start(bf16[512,512]{1,0:T(8,128)(2,1)S(1)} %fusion), channel_id=1, source_target_pairs={{0,1},{1,0},{2,3},{3,2},{4,5},{5,4},{6,7},{7,6},{8,9},{9,8},{10,11... | collective-permute-start | bytes 1572872 | tf_op jit(solution)/shard_map/ppermute | solution.py:34
  52.9 6.0 %collective-permute-start.24 = (bf16[256,256]{1,0:T(8,128)(2,1)S(1)}, bf16[256,256]{1,0:T(8,128)(2,1)S(1)}, u32[]{:S(2)}, u32[]{:S(2)}) collective-permute-start(bf16[256,256]{1,0:T(8,128)(2,1)S(1)} %reduce-precision_convert_fusion.1), channel_id=1, source_target_pairs={{0,4},{1,3},{2,6},{3,1},{4,0},{5,7},{6,2},{7,5},{8,12},{9,11},{10,... | collective-permute-start | bytes 393224 | tf_op jit(solution)/shard_map/ppermute | solution.py:30
  55.2 9.5 %collective-permute-start.14 = (bf16[272,512]{1,0:T(8,128)(2,1)S(1)}, bf16[272,512]{1,0:T(8,128)(2,1)S(1)}, u32[]{:S(2)}, u32[]{:S(2)}) collective-permute-start(bf16[272,512]{1,0:T(8,128)(2,1)S(1)} %pad_maximum_fusion.2.refs_2_), channel_id=1, source_target_pairs={{0,16},{1,9},{2,18},{3,11},{4,20},{5,13},{6,22},{7,15},{8,24},{9,1... | collective-permute-start | bytes 835592 | tf_op jit(solution)/shard_map/ppermute | solution.py:30
  57.1 6.3 %collective-permute-start.19 = (bf16[256,256]{1,0:T(8,128)(2,1)S(1)}, bf16[256,256]{1,0:T(8,128)(2,1)S(1)}, u32[]{:S(2)}, u32[]{:S(2)}) collective-permute-start(bf16[256,256]{1,0:T(8,128)(2,1)S(1)} %added.3), channel_id=1, source_target_pairs={{0,4},{1,3},{2,6},{3,1},{4,0},{5,7},{6,2},{7,5},{8,12},{9,11},{10,... | collective-permute-start | bytes 393224 | tf_op jit(solution)/shard_map/ppermute | solution.py:30
  59.0 6.8 %collective-permute-start.25 = (bf16[256,256]{1,0:T(8,128)(2,1)S(1)}, bf16[256,256]{1,0:T(8,128)(2,1)S(1)}, u32[]{:S(2)}, u32[]{:S(2)}) collective-permute-start(bf16[256,256]{1,0:T(8,128)(2,1)S(1)} %reduce-precision_convert_fusion.refs_0_), channel_id=1, source_target_pairs={{0,8},{1,17},{2,10},{3,19},{4,12},{5,21},{6,14},{7,23},{8,0},{9,25... | collective-permute-start | bytes 393224 | tf_op jit(solution)/shard_map/ppermute | solution.py:30
  63.4 5.0 %collective-permute-start.20 = (bf16[256,256]{1,0:T(8,128)(2,1)S(1)}, bf16[256,256]{1,0:T(8,128)(2,1)S(1)}, u32[]{:S(2)}, u32[]{:S(2)}) collective-permute-start(bf16[256,256]{1,0:T(8,128)(2,1)S(1)} %reduce-precision_convert_fusion.2.refs_0_), channel_id=1, source_target_pairs={{0,8},{1,17},{2,10},{3,19},{4,12},{5,21},{6,14},{7,23},{8,0},{9,25... | collective-permute-start | bytes 393224 | tf_op jit(solution)/shard_map/ppermute | solution.py:30
  64.9 6.4 %collective-permute-start.15 = (bf16[144,512]{1,0:T(8,128)(2,1)S(1)}, bf16[144,512]{1,0:T(8,128)(2,1)S(1)}, u32[]{:S(2)}, u32[]{:S(2)}) collective-permute-start(bf16[144,512]{1,0:T(8,128)(2,1)S(1)} %pad_maximum_fusion.5.refs_3_), channel_id=1, source_target_pairs={{0,8},{1,17},{2,10},{3,19},{4,12},{5,21},{6,14},{7,23},{8,0},{9,25... | collective-permute-start | bytes 442376 | tf_op jit(solution)/shard_map/ppermute | solution.py:30
  65.8 5.6 %collective-permute-start.28 = (bf16[512,256]{1,0:T(8,128)(2,1)S(1)}, bf16[512,256]{1,0:T(8,128)(2,1)S(1)}, u32[]{:S(2)}, u32[]{:S(2)}) collective-permute-start(bf16[512,256]{1,0:T(8,128)(2,1)S(1)} %joined.2.refs_2_.refs_0_), channel_id=1, source_target_pairs={{0,1},{1,0},{2,3},{3,2},{4,5},{5,4},{6,7},{7,6},{8,9},{9,8},{10,11... | collective-permute-start | bytes 786440 | tf_op jit(solution)/shard_map/ppermute | solution.py:34
  65.9 6.4 %collective-permute-start.30 = (bf16[512,256]{1,0:T(8,128)(2,1)S(1)}, bf16[512,256]{1,0:T(8,128)(2,1)S(1)}, u32[]{:S(2)}, u32[]{:S(2)}) collective-permute-start(bf16[512,256]{1,0:T(8,128)(2,1)S(1)} %joined.2.refs_2_.refs_0_), channel_id=1, source_target_pairs={{0,16},{1,9},{2,18},{3,11},{4,20},{5,13},{6,22},{7,15},{8,24},{9,1... | collective-permute-start | bytes 786440 | tf_op jit(solution)/shard_map/ppermute | solution.py:30
  68.5 3.8 %collective-permute-start.29 = (bf16[512,256]{1,0:T(8,128)(2,1)S(1)}, bf16[512,256]{1,0:T(8,128)(2,1)S(1)}, u32[]{:S(2)}, u32[]{:S(2)}) collective-permute-start(bf16[512,256]{1,0:T(8,128)(2,1)S(1)} %joined.3.refs_1_), channel_id=1, source_target_pairs={{0,1},{1,0},{2,3},{3,2},{4,5},{5,4},{6,7},{7,6},{8,9},{9,8},{10,11... | collective-permute-start | bytes 786440 | tf_op jit(solution)/shard_map/ppermute | solution.py:34
  68.6 6.5 %collective-permute-start.26 = (bf16[512,256]{1,0:T(8,128)(2,1)S(1)}, bf16[512,256]{1,0:T(8,128)(2,1)S(1)}, u32[]{:S(2)}, u32[]{:S(2)}) collective-permute-start(bf16[512,256]{1,0:T(8,128)(2,1)S(1)} %joined.3.refs_1_), channel_id=1, source_target_pairs={{0,16},{1,9},{2,18},{3,11},{4,20},{5,13},{6,22},{7,15},{8,24},{9,1... | collective-permute-start | bytes 786440 | tf_op jit(solution)/shard_map/ppermute | solution.py:30
  71.4 5.4 %copy-start.3 = (f32[128,512]{1,0:T(8,128)}, f32[128,512]{1,0:T(8,128)S(1)}, u32[]{:S(2)}) copy-start(f32[128,512]{1,0:T(8,128)S(1)} %slice_add_fusion.3.refs_5_) | copy-start | bytes 786436
  73.7 2.0 %collective-permute-start.31 = (bf16[512,256]{1,0:T(8,128)(2,1)S(1)}, bf16[512,256]{1,0:T(8,128)(2,1)S(1)}, u32[]{:S(2)}, u32[]{:S(2)}) collective-permute-start(bf16[512,256]{1,0:T(8,128)(2,1)S(1)} %get-tuple-element.41.refs_0_), channel_id=1, source_target_pairs={{0,1},{1,0},{2,3},{3,2},{4,5},{5,4},{6,7},{7,6},{8,9},{9,8},{10,11... | collective-permute-start | bytes 786440 | tf_op jit(solution)/shard_map/ppermute | solution.py:34
  75.1 1.7 %collective-permute-start.27 = (bf16[512,256]{1,0:T(8,128)(2,1)S(1)}, bf16[512,256]{1,0:T(8,128)(2,1)S(1)}, u32[]{:S(2)}, u32[]{:S(2)}) collective-permute-start(bf16[512,256]{1,0:T(8,128)(2,1)S(1)} %collective-permute-done.26.refs_0_), channel_id=1, source_target_pairs={{0,1},{1,0},{2,3},{3,2},{4,5},{5,4},{6,7},{7,6},{8,9},{9,8},{10,11... | collective-permute-start | bytes 786440 | tf_op jit(solution)/shard_map/ppermute | solution.py:34
  75.6 1.2 %collective-permute-start.32 = (bf16[16,512]{1,0:T(8,128)(2,1)S(1)}, bf16[16,512]{1,0:T(8,128)(2,1)S(1)}, u32[]{:S(2)}, u32[]{:S(2)}) collective-permute-start(bf16[16,512]{1,0:T(8,128)(2,1)S(1)} %pad_maximum_fusion.6.refs_4_), channel_id=1, source_target_pairs={{0,1},{1,0},{2,3},{3,2},{4,5},{5,4},{6,7},{7,6},{8,9},{9,8},{10,11... | collective-permute-start | bytes 49160 | tf_op jit(solution)/shard_map/ppermute | solution.py:34

commit v6 on v5

--- a/solution.py
+++ b/solution.py
@@ -145,6 +145,12 @@
                 start += size
 
         copies = []
+        if gains:
+            one, two = (x[...].astype(FP) for x in refs[2 * parts + len(held) :][:2])
+            small = refs[-4]
+            small[...] = ((one[:TYPES] + one[TYPES:]) + (two[:TYPES] + two[TYPES:])) * factor
+            copies.append(pltpu.make_async_copy(small, outs[2], sems.at[2 * places]))
+            copies[-1].start()
         for j in range(places):
             q = first_place + j
             at = pl.ds(j * span, span)
@@ -170,9 +176,6 @@
             to = out_ref.at[pl.ds(pl.multiple_of(g * span, span), span), pl.ds(first_lane, width)]
             copies.append(pltpu.make_async_copy(wide_out.at[at], to, sems.at[2 * j + 1]))
             copies[-1].start()
-        if gains:
-            one, two = (x[...].astype(FP) for x in refs[2 * parts + len(held) :][:2])
-            outs[2][...] = ((one[:TYPES] + one[TYPES:]) + (two[:TYPES] + two[TYPES:])) * factor
         for copy in copies:
             copy.wait()
 
@@ -187,12 +190,13 @@
         + (jax.ShapeDtypeStruct((TYPES, F), FP),) * n_gain
         + tuple(jax.ShapeDtypeStruct(x.shape, x.dtype) for x in through),
         in_specs=[vmem] * (2 * parts) + [hbm] * len(held) + [vmem] * len(gains) + [keep] * (len(through) + len(after)),
-        out_specs=(hbm, hbm) + (vmem,) * n_gain + (keep,) * len(through),
+        out_specs=(hbm, hbm) + (hbm,) * n_gain + (keep,) * len(through),
         input_output_aliases=aliases,
-        scratch_shapes=[
+        scratch_shapes=[pltpu.VMEM((TYPES, F), FP)] * n_gain
+        + [
             pltpu.VMEM((rows, width), FP),
             pltpu.VMEM((rows, width), FP),
-            pltpu.SemaphoreType.DMA((2 * places,)),
+            pltpu.SemaphoreType.DMA((2 * places + n_gain,)),
         ],
         compiler_params=pltpu.CompilerParams(vmem_limit_bytes=16 * 1024 * 1024),
         cost_estimate=pl.CostEstimate(flops=0, bytes_accessed=0, transcendentals=0),
@@ -514,7 +518,7 @@
         for i in range(parts):
             came = row_step(sent[i], step)
             if step == row_bits - 2:
-                sent[i] = joined(sent[i], came, sent[:i] + (marks[-1:] if i == parts - 1 else []))
+                sent[i] = joined(sent[i], came, marks[-1:] if i == 0 else sent[:1])
             else:
                 sent[i] = jnp.concatenate([sent[i], came], axis=0)
     came = [row_step(x, row_bits - 1) for x in sent]
@@ -523,11 +527,11 @@
     others = [swap_cores(x, n_row, n_col) for x in sent]
     gains = [gain, swap_cores(gain, n_row, n_col)]
     half = n_row // 2
-    *weights, came[0] = write_weights(sent, others, [], [], 0, 0, n_row, factor, came[:1], [grad_x])
+    *weights, grad_gain, came[0] = write_weights(sent, others, [], gains, 0, 0, n_row, factor, came[:1], [grad_x])
     others = [swap_cores(x, n_row, n_col) for x in came]
     for i in range(parts - 1):
         weights = write_weights(came[i : i + 1], others[i : i + 1], weights, [], half, lanes[i][0], n_row, factor)
-    *weights, grad_gain = write_weights(came[-1:], others[-1:], weights, gains, half, lanes[-1][0], n_row, factor)
+    weights = write_weights(came[-1:], others[-1:], weights, [], half, lanes[-1][0], n_row, factor)
     grad_w_in, grad_w_out = weights
     return mixed, grad_x, grad_w_in, grad_w_out, grad_gain
 

time: 79.8 us -> 79.1 us (level)
    ppermute x12, waiting for transfers between devices: 2.02 us -> 3.26 us  [swap_cores(): return lax.ppermute(x, AXES, [(i, i ^ 1) for i in range(rows * cols)])]
    ppermute x21, waiting for transfers between devices: 27.6 us -> 26.5 us  [exchange(): return lax.ppermute(x, AXES, pairs)]
  transfers between devices with their start and end apart: 33 -> 33, of which waited for: 15 -> 16; matrix products, arithmetic and copies ran while one was open for 4% -> 4% of each run, Pallas kernels for 10% -> 10%
where the time goes in v6:
time: 79.1 us; the launch traced here: 77.8 us
  starting transfers between devices  32.4 us (41%)
  waiting for transfers between devices  29.8 us (38%)
  Pallas kernels  10.4 us (13%)
  matrix products  2.56 us (3%)
  between operations  1.86 us (2%)
    ppermute x21, starting transfers between devices, exchange(): return lax.ppermute(x, AXES, pairs)  29.8 us
    ppermute x21, waiting for transfers between devices, exchange(): return lax.ppermute(x, AXES, pairs)  26.5 us
    pallas_call x3, Pallas kernels, write_weights(): pl.pallas_call(kernel, out_shape=(jax.ShapeDtypeStruct((F, 2 * F), FP), j...  3.55 us
    ppermute x12, waiting for transfers between devices, swap_cores(): return lax.ppermute(x, AXES, [(i, i ^ 1) for i in range(rows * cols)])  3.26 us
    pallas_call x1, Pallas kernels, build(): pl.pallas_call(kernel, out_shape=(result, result), in_specs=[pl.BlockSpec...  2.74 us
    ppermute x12, starting transfers between devices, swap_cores(): return lax.ppermute(x, AXES, [(i, i ^ 1) for i in range(rows * cols)])  2.53 us
    dot_general x5, matrix products, dot(): return lax.dot_general(a, b, (dims, ((), ())), preferred_element_type=FP)  2.25 us
    pallas_call x3, Pallas kernels, weight_blocks(): pl.pallas_call(kernel, out_shape=tuple((jax.ShapeDtypeStruct((rows, size)...  2.01 us
  transfers between devices with their start and end apart: 33, of which 16 were waited for; matrix products, arithmetic and copies ran while one was open for 4% of the time, Pallas kernels for 10%

profile of v6, /device:TPU:0, one launch (start us, length us, event | category | flops | bytes accessed | tf_op | source)
XLA Modules:
  0.0 77.8 jit_solution(15742306306613935002)
XLA Ops:
  0.6 3.0 %collective-permute-start = (bf16[128,512]{1,0:T(8,128)(2,1)}, bf16[128,512]{1,0:T(8,128)(2,1)S(1)}, u32[]{:S(2)}, u32[]{:S(2)}) collective-permute-start(bf16[128,512]{1,0:T(8,128)(2,1)} %param.10), channel_id=1, source_target_pairs={{0,8},{1,17},{2,10},{3,19},{4,12},{5,21},{6,14},{7,23},{8,0},{9,25... | collective-permute-start | bytes 393224 | tf_op jit(solution)/shard_map/ppermute | solution.py:30
  3.7 1.5 %collective-permute-start.1 = (bf16[128,512]{1,0:T(8,128)(2,1)}, bf16[128,512]{1,0:T(8,128)(2,1)S(1)}, u32[]{:S(2)}, u32[]{:S(2)}) collective-permute-start(bf16[128,512]{1,0:T(8,128)(2,1)} %param.10), channel_id=1, source_target_pairs={{0,16},{1,9},{2,18},{3,11},{4,20},{5,13},{6,22},{7,15},{8,24},{9,1... | collective-permute-start | bytes 393224 | tf_op jit(solution)/shard_map/ppermute | solution.py:30
  5.9 2.7 %build_dense.1 = (bf16[512,1024]{1,0:T(8,128)(2,1)S(1)}, bf16[512,1024]{1,0:T(8,128)(2,1)S(1)}) custom-call(s32[1,1]{1,0:T(1,128)S(6)} %copy.34.count_ref, s32[1,128]{1,0:T(1,128)} %rows_ref.1, s32[1,128]{1,0:T(1,128)} %cols_ref.1, bf16[1,128,128,128]{3,2,1,0:T(8,128)(2,1)} %vals_ref.1), custom_call_target="tpu_custom_call" | custom-call | flops 2097152 | bytes 6291456 | tf_op jit(solution)/shard_map/build_dense/pallas_call | solution.py:105
  8.6 0.7 collective-permute-start.3
  9.3 0.1 collective-permute-start.5
  9.4 2.2 %collective-permute-done.1 = bf16[128,512]{1,0:T(8,128)(2,1)S(1)} collective-permute-done((bf16[128,512]{1,0:T(8,128)(2,1)}, bf16[128,512]{1,0:T(8,128)(2,1)S(1)}, u32[]{:S(2)}, u32[]{:S(2)}) %collective-permute-start.1) | collective-permute-done | bytes 131104 | tf_op jit(solution)/shard_map/ppermute | solution.py:30
  11.6 0.5 collective-permute-start.7
  12.3 0.4 fusion.8
  12.7 0.4 product.1.refs_4_
  13.2 0.1 stacked.1
  13.3 0.4 fusion.2
  13.8 2.4 %collective-permute-start.8 = (bf16[256,512]{1,0:T(8,128)(2,1)S(1)}, bf16[256,512]{1,0:T(8,128)(2,1)S(1)}, u32[]{:S(2)}, u32[]{:S(2)}) collective-permute-start(bf16[256,512]{1,0:T(8,128)(2,1)S(1)} %fusion.2), channel_id=1, source_target_pairs={{0,4},{1,3},{2,6},{3,1},{4,0},{5,7},{6,2},{7,5},{8,12},{9,11},{10,... | collective-permute-start | bytes 786440 | tf_op jit(solution)/shard_map/ppermute | solution.py:30
  16.2 0.4 convolution_add_fusion.2.refs_0_
  16.7 6.5 %collective-permute-done.8.refs_1_ = bf16[256,512]{1,0:T(8,128)(2,1)S(1)} collective-permute-done((bf16[256,512]{1,0:T(8,128)(2,1)S(1)}, bf16[256,512]{1,0:T(8,128)(2,1)S(1)}, u32[]{:S(2)}, u32[]{:S(2)}) %collective-permute-start.8) | collective-permute-done | bytes 262176 | tf_op jit(solution)/shard_map/ppermute | solution.py:30
  23.2 1.5 %collective-permute-start.9 = (bf16[128,512]{1,0:T(8,128)(2,1)S(1)}, bf16[128,512]{1,0:T(8,128)(2,1)S(1)}, u32[]{:S(2)}, u32[]{:S(2)}) collective-permute-start(bf16[128,512]{1,0:T(8,128)(2,1)S(1)} %get-tuple-element.30), channel_id=1, source_target_pairs={{0,2},{1,5},{2,0},{3,7},{4,6},{5,1},{6,4},{7,3},{8,10},{9,13},{10,... | collective-permute-start | bytes 393224 | tf_op jit(solution)/shard_map/ppermute | solution.py:30
  24.8 0.3 fusion.17.refs_2_.gains_ref
  25.1 4.1 %collective-permute-done.9.refs_1_ = bf16[128,512]{1,0:T(8,128)(2,1)S(1)} collective-permute-done((bf16[128,512]{1,0:T(8,128)(2,1)S(1)}, bf16[128,512]{1,0:T(8,128)(2,1)S(1)}, u32[]{:S(2)}, u32[]{:S(2)}) %collective-permute-start.9) | collective-permute-done | bytes 131104 | tf_op jit(solution)/shard_map/ppermute | solution.py:30
  29.2 0.8 node_values.1
  30.0 0.1 collective-permute-start.10
  30.1 0.8 node_gradients.1.refs_0_
  30.8 0.9 %collective-permute-done.10.met_ref = bf16[128,1536]{1,0:T(8,128)(2,1)S(1)} collective-permute-done((bf16[128,1536]{1,0:T(8,128)(2,1)S(1)}, bf16[128,1536]{1,0:T(8,128)(2,1)S(1)}, u32[]{:S(2)}, u32[]{:S(2)}) %collective-permute-start.10) | collective-permute-done | bytes 393248 | tf_op jit(solution)/shard_map/ppermute | solution.py:34
  31.8 0.5 weight_blocks.4
  32.3 0.6 collective-permute-start.11
  32.9 1.9 %collective-permute-start.21 = (bf16[512,256]{1,0:T(8,128)(2,1)S(1)}, bf16[512,256]{1,0:T(8,128)(2,1)S(1)}, u32[]{:S(2)}, u32[]{:S(2)}) collective-permute-start(bf16[512,256]{1,0:T(8,128)(2,1)S(1)} %get-tuple-element.40), channel_id=1, source_target_pairs={{0,16},{1,9},{2,18},{3,11},{4,20},{5,13},{6,22},{7,15},{8,24},{9,1... | collective-permute-start | bytes 786440 | tf_op jit(solution)/shard_map/ppermute | solution.py:30
  34.9 0.5 weight_blocks.5
  35.4 0.2 collective-permute-start.16
  35.6 1.0 %weight_blocks.3 = (f32[512,256]{1,0:T(8,128)S(1)}, f32[512,256]{1,0:T(8,128)S(1)}, bf16[128,512]{1,0:T(8,128)(2,1)}) custom-call(bf16[128,1536]{1,0:T(8,128)(2,1)S(1)} %get-tuple-element.31.mine_ref, bf16[128,1536]{1,0:T(8,128)(2,1)S(1)} %collective-permute-done.10.met_ref, f32[128,512]{1,0:T(8,128)S(1)} %get-tuple-element.33.refs_0_.agg_ref, ...), custom_call_target="tpu_custom_call" | custom-call | flops 134217728 | bytes 1572864 | tf_op jit(solution)/shard_map/weight_blocks/pallas_call | solution.py:295
  36.6 2.5 %collective-permute-done.11 = bf16[144,512]{1,0:T(8,128)(2,1)S(1)} collective-permute-done((bf16[144,512]{1,0:T(8,128)(2,1)S(1)}, bf16[144,512]{1,0:T(8,128)(2,1)S(1)}, u32[]{:S(2)}, u32[]{:S(2)}) %collective-permute-start.11) | collective-permute-done | bytes 147488 | tf_op jit(solution)/shard_map/ppermute | solution.py:30
  39.1 1.3 %collective-permute-start.12 = (bf16[272,512]{1,0:T(8,128)(2,1)S(1)}, bf16[272,512]{1,0:T(8,128)(2,1)S(1)}, u32[]{:S(2)}, u32[]{:S(2)}) collective-permute-start(bf16[272,512]{1,0:T(8,128)(2,1)S(1)} %pad_maximum_fusion.1), channel_id=1, source_target_pairs={{0,4},{1,3},{2,6},{3,1},{4,0},{5,7},{6,2},{7,5},{8,12},{9,11},{10,... | collective-permute-start | bytes 835592 | tf_op jit(solution)/shard_map/ppermute | solution.py:30
  40.5 1.5 %collective-permute-start.22 = (bf16[256,256]{1,0:T(8,128)(2,1)S(1)}, bf16[256,256]{1,0:T(8,128)(2,1)S(1)}, u32[]{:S(2)}, u32[]{:S(2)}) collective-permute-start(bf16[256,256]{1,0:T(8,128)(2,1)S(1)} %fusion.10), channel_id=1, source_target_pairs={{0,8},{1,17},{2,10},{3,19},{4,12},{5,21},{6,14},{7,23},{8,0},{9,25... | collective-permute-start | bytes 393224 | tf_op jit(solution)/shard_map/ppermute | solution.py:30
  42.0 0.2 collective-permute-done.16
  42.3 1.5 %collective-permute-start.17 = (bf16[256,256]{1,0:T(8,128)(2,1)S(1)}, bf16[256,256]{1,0:T(8,128)(2,1)S(1)}, u32[]{:S(2)}, u32[]{:S(2)}) collective-permute-start(bf16[256,256]{1,0:T(8,128)(2,1)S(1)} %fusion.13), channel_id=1, source_target_pairs={{0,8},{1,17},{2,10},{3,19},{4,12},{5,21},{6,14},{7,23},{8,0},{9,25... | collective-permute-start | bytes 393224 | tf_op jit(solution)/shard_map/ppermute | solution.py:30
  43.8 1.7 %collective-permute-done.22 = bf16[256,256]{1,0:T(8,128)(2,1)S(1)} collective-permute-done((bf16[256,256]{1,0:T(8,128)(2,1)S(1)}, bf16[256,256]{1,0:T(8,128)(2,1)S(1)}, u32[]{:S(2)}, u32[]{:S(2)}) %collective-permute-start.22) | collective-permute-done | bytes 131104 | tf_op jit(solution)/shard_map/ppermute | solution.py:30
  45.6 2.6 %collective-permute-start.23 = (bf16[256,256]{1,0:T(8,128)(2,1)S(1)}, bf16[256,256]{1,0:T(8,128)(2,1)S(1)}, u32[]{:S(2)}, u32[]{:S(2)}) collective-permute-start(bf16[256,256]{1,0:T(8,128)(2,1)S(1)} %fusion.12), channel_id=1, source_target_pairs={{0,2},{1,5},{2,0},{3,7},{4,6},{5,1},{6,4},{7,3},{8,10},{9,13},{10,... | collective-permute-start | bytes 393224 | tf_op jit(solution)/shard_map/ppermute | solution.py:30
  48.2 1.6 %collective-permute-start.18 = (bf16[256,256]{1,0:T(8,128)(2,1)S(1)}, bf16[256,256]{1,0:T(8,128)(2,1)S(1)}, u32[]{:S(2)}, u32[]{:S(2)}) collective-permute-start(bf16[256,256]{1,0:T(8,128)(2,1)S(1)} %fusion.15.refs_0_), channel_id=1, source_target_pairs={{0,2},{1,5},{2,0},{3,7},{4,6},{5,1},{6,4},{7,3},{8,10},{9,13},{10,... | collective-permute-start | bytes 393224 | tf_op jit(solution)/shard_map/ppermute | solution.py:30
  49.8 2.4 %collective-permute-done.12 = bf16[272,512]{1,0:T(8,128)(2,1)S(1)} collective-permute-done((bf16[272,512]{1,0:T(8,128)(2,1)S(1)}, bf16[272,512]{1,0:T(8,128)(2,1)S(1)}, u32[]{:S(2)}, u32[]{:S(2)}) %collective-permute-start.12) | collective-permute-done | bytes 278560 | tf_op jit(solution)/shard_map/ppermute | solution.py:30
  52.2 0.5 fusion
  52.7 0.1 collective-permute-start.13
  52.9 0.8 collective-permute-start.24
  53.7 1.0 %collective-permute-done.13 = bf16[512,512]{1,0:T(8,128)(2,1)S(1)} collective-permute-done((bf16[512,512]{1,0:T(8,128)(2,1)S(1)}, bf16[512,512]{1,0:T(8,128)(2,1)S(1)}, u32[]{:S(2)}, u32[]{:S(2)}) %collective-permute-start.13) | collective-permute-done | bytes 524320 | tf_op jit(solution)/shard_map/ppermute | solution.py:34
  54.7 0.5 convolution_add_fusion
  55.2 1.8 %collective-permute-start.14 = (bf16[272,512]{1,0:T(8,128)(2,1)S(1)}, bf16[272,512]{1,0:T(8,128)(2,1)S(1)}, u32[]{:S(2)}, u32[]{:S(2)}) collective-permute-start(bf16[272,512]{1,0:T(8,128)(2,1)S(1)} %pad_maximum_fusion.2.refs_2_), channel_id=1, source_target_pairs={{0,16},{1,9},{2,18},{3,11},{4,20},{5,13},{6,22},{7,15},{8,24},{9,1... | collective-permute-start | bytes 835592 | tf_op jit(solution)/shard_map/ppermute | solution.py:30
  57.1 1.3 %collective-permute-start.19 = (bf16[256,256]{1,0:T(8,128)(2,1)S(1)}, bf16[256,256]{1,0:T(8,128)(2,1)S(1)}, u32[]{:S(2)}, u32[]{:S(2)}) collective-permute-start(bf16[256,256]{1,0:T(8,128)(2,1)S(1)} %added.3), channel_id=1, source_target_pairs={{0,4},{1,3},{2,6},{3,1},{4,0},{5,7},{6,2},{7,5},{8,12},{9,11},{10,... | collective-permute-start | bytes 393224 | tf_op jit(solution)/shard_map/ppermute | solution.py:30
  58.3 0.6 collective-permute-done.24
  59.0 1.5 %collective-permute-start.25 = (bf16[256,256]{1,0:T(8,128)(2,1)S(1)}, bf16[256,256]{1,0:T(8,128)(2,1)S(1)}, u32[]{:S(2)}, u32[]{:S(2)}) collective-permute-start(bf16[256,256]{1,0:T(8,128)(2,1)S(1)} %reduce-precision_convert_fusion.refs_0_), channel_id=1, source_target_pairs={{0,8},{1,17},{2,10},{3,19},{4,12},{5,21},{6,14},{7,23},{8,0},{9,25... | collective-permute-start | bytes 393224 | tf_op jit(solution)/shard_map/ppermute | solution.py:30
  60.4 3.0 %collective-permute-done.19 = bf16[256,256]{1,0:T(8,128)(2,1)S(1)} collective-permute-done((bf16[256,256]{1,0:T(8,128)(2,1)S(1)}, bf16[256,256]{1,0:T(8,128)(2,1)S(1)}, u32[]{:S(2)}, u32[]{:S(2)}) %collective-permute-start.19) | collective-permute-done | bytes 131104 | tf_op jit(solution)/shard_map/ppermute | solution.py:30
  63.4 1.3 %collective-permute-start.20 = (bf16[256,256]{1,0:T(8,128)(2,1)S(1)}, bf16[256,256]{1,0:T(8,128)(2,1)S(1)}, u32[]{:S(2)}, u32[]{:S(2)}) collective-permute-start(bf16[256,256]{1,0:T(8,128)(2,1)S(1)} %reduce-precision_convert_fusion.2.refs_0_), channel_id=1, source_target_pairs={{0,8},{1,17},{2,10},{3,19},{4,12},{5,21},{6,14},{7,23},{8,0},{9,25... | collective-permute-start | bytes 393224 | tf_op jit(solution)/shard_map/ppermute | solution.py:30
  64.8 0.1 slice_add_fusion
  64.9 0.9 %collective-permute-start.15 = (bf16[144,512]{1,0:T(8,128)(2,1)S(1)}, bf16[144,512]{1,0:T(8,128)(2,1)S(1)}, u32[]{:S(2)}, u32[]{:S(2)}) collective-permute-start(bf16[144,512]{1,0:T(8,128)(2,1)S(1)} %pad_maximum_fusion.5.refs_2_), channel_id=1, source_target_pairs={{0,8},{1,17},{2,10},{3,19},{4,12},{5,21},{6,14},{7,23},{8,0},{9,25... | collective-permute-start | bytes 442376 | tf_op jit(solution)/shard_map/ppermute | solution.py:30
  65.8 0.1 collective-permute-start.28
  65.9 1.3 %collective-permute-start.31 = (bf16[512,256]{1,0:T(8,128)(2,1)S(1)}, bf16[512,256]{1,0:T(8,128)(2,1)S(1)}, u32[]{:S(2)}, u32[]{:S(2)}) collective-permute-start(bf16[512,256]{1,0:T(8,128)(2,1)S(1)} %joined.2.refs_2_.refs_0_), channel_id=1, source_target_pairs={{0,16},{1,9},{2,18},{3,11},{4,20},{5,13},{6,22},{7,15},{8,24},{9,1... | collective-permute-start | bytes 786440 | tf_op jit(solution)/shard_map/ppermute | solution.py:30
  67.2 1.3 %collective-permute-done.20.refs_1_ = bf16[256,256]{1,0:T(8,128)(2,1)S(1)} collective-permute-done((bf16[256,256]{1,0:T(8,128)(2,1)S(1)}, bf16[256,256]{1,0:T(8,128)(2,1)S(1)}, u32[]{:S(2)}, u32[]{:S(2)}) %collective-permute-start.20) | collective-permute-done | bytes 131104 | tf_op jit(solution)/shard_map/ppermute | solution.py:30
  68.5 0.1 collective-permute-start.29
  68.6 1.3 %collective-permute-start.26 = (bf16[512,256]{1,0:T(8,128)(2,1)S(1)}, bf16[512,256]{1,0:T(8,128)(2,1)S(1)}, u32[]{:S(2)}, u32[]{:S(2)}) collective-permute-start(bf16[512,256]{1,0:T(8,128)(2,1)S(1)} %joined.3.refs_1_), channel_id=1, source_target_pairs={{0,16},{1,9},{2,18},{3,11},{4,20},{5,13},{6,22},{7,15},{8,24},{9,1... | collective-permute-start | bytes 786440 | tf_op jit(solution)/shard_map/ppermute | solution.py:30
  69.9 1.4 %collective-permute-done.15 = bf16[144,512]{1,0:T(8,128)(2,1)S(1)} collective-permute-done((bf16[144,512]{1,0:T(8,128)(2,1)S(1)}, bf16[144,512]{1,0:T(8,128)(2,1)S(1)}, u32[]{:S(2)}, u32[]{:S(2)}) %collective-permute-start.15) | collective-permute-done | bytes 147488 | tf_op jit(solution)/shard_map/ppermute | solution.py:30
  71.4 0.1 collective-permute-start.30
  71.5 1.1 %collective-permute-done.30.refs_5_ = bf16[16,512]{1,0:T(8,128)(2,1)S(1)} collective-permute-done((bf16[16,512]{1,0:T(8,128)(2,1)S(1)}, bf16[16,512]{1,0:T(8,128)(2,1)S(1)}, u32[]{:S(2)}, u32[]{:S(2)}) %collective-permute-start.30) | collective-permute-done | bytes 16416 | tf_op jit(solution)/shard_map/ppermute | solution.py:34
  72.6 1.4 %write_weights.3 = (f32[512,1024]{1,0:T(8,128)}, f32[1024,512]{1,0:T(8,128)}, f32[8,512]{1,0:T(8,128)}, bf16[512,256]{1,0:T(8,128)(2,1)S(1)}) custom-call(bf16[512,256]{1,0:T(8,128)(2,1)S(1)} %joined.2.refs_2_.refs_0_, bf16[512,256]{1,0:T(8,128)(2,1)S(1)} %joined.3.refs_1_, ...), custom_call_target="tpu_custom_call", output_to_operand_aliasing={{3}: (6, {})} | custom-call | tf_op jit(solution)/shard_map/write_weights/pallas_call | solution.py:187
  74.1 0.5 collective-permute-start.32
  74.5 0.6 collective-permute-done.26.refs_0_
  75.1 0.4 collective-permute-start.27
  75.5 0.2 collective-permute-done.32.refs_1_
  75.7 1.0 %write_weights.4 = (f32[512,1024]{1,0:T(8,128)}, f32[1024,512]{1,0:T(8,128)}) custom-call(bf16[512,256]{1,0:T(8,128)(2,1)S(1)} %get-tuple-element.41.refs_0_, bf16[512,256]{1,0:T(8,128)(2,1)S(1)} %collective-permute-done.32.refs_1_, f32[512,1024]{1,0:T(8,128)} %get-tuple-element.42.refs_2_, ...), custom_call_target="tpu_custom_call", output_to_operand_aliasing={{0}: (2, {}), {1}: (3, {})} | custom-call | tf_op jit(solution)/shard_map/write_weights/pallas_call | solution.py:187
  76.8 1.1 %write_weights.5 = (f32[512,1024]{1,0:T(8,128)}, f32[1024,512]{1,0:T(8,128)}) custom-call(bf16[512,256]{1,0:T(8,128)(2,1)S(1)} %collective-permute-done.26.refs_0_, bf16[512,256]{1,0:T(8,128)(2,1)S(1)} %collective-permute-done.27.refs_1_, f32[512,1024]{1,0:T(8,128)} %get-tuple-element.44.refs_2_, ...), custom_call_target="tpu_custom_call", output_to_operand_aliasing={{0}: (2, {}), {1}: (3, {})} | custom-call | tf_op jit(solution)/shard_map/write_weights/pallas_call | solution.py:187
  (82 shorter events, 0.9 us)
Async XLA Ops:
  0.6 24.1 %copy-start = (f32[8,512]{1,0:T(8,128)S(1)}, f32[8,512]{1,0:T(8,128)}, u32[]{:S(2)}) copy-start(f32[8,512]{1,0:T(8,128)} %param.16) | copy-start | bytes 49156
  0.6 8.7 %collective-permute-start = (bf16[128,512]{1,0:T(8,128)(2,1)}, bf16[128,512]{1,0:T(8,128)(2,1)S(1)}, u32[]{:S(2)}, u32[]{:S(2)}) collective-permute-start(bf16[128,512]{1,0:T(8,128)(2,1)} %param.10), channel_id=1, source_target_pairs={{0,8},{1,17},{2,10},{3,19},{4,12},{5,21},{6,14},{7,23},{8,0},{9,25... | collective-permute-start | bytes 393224 | tf_op jit(solution)/shard_map/ppermute | solution.py:30
  3.7 8.0 %collective-permute-start.1 = (bf16[128,512]{1,0:T(8,128)(2,1)}, bf16[128,512]{1,0:T(8,128)(2,1)S(1)}, u32[]{:S(2)}, u32[]{:S(2)}) collective-permute-start(bf16[128,512]{1,0:T(8,128)(2,1)} %param.10), channel_id=1, source_target_pairs={{0,16},{1,9},{2,18},{3,11},{4,20},{5,13},{6,22},{7,15},{8,24},{9,1... | collective-permute-start | bytes 393224 | tf_op jit(solution)/shard_map/ppermute | solution.py:30
  5.2 6.5 %collective-permute-start.2 = (bf16[128,512]{1,0:T(8,128)(2,1)}, bf16[128,512]{1,0:T(8,128)(2,1)S(1)}, u32[]{:S(2)}, u32[]{:S(2)}) collective-permute-start(bf16[128,512]{1,0:T(8,128)(2,1)} %param.10), channel_id=1, source_target_pairs={{0,24},{1,25},{2,26},{3,27},{4,28},{5,29},{6,30},{7,31},{8,16},{9,... | collective-permute-start | bytes 393224 | tf_op jit(solution)/shard_map/ppermute | solution.py:30
  5.2 8.0 %collective-permute-start.4 = (bf16[128,512]{1,0:T(8,128)(2,1)}, bf16[128,512]{1,0:T(8,128)(2,1)S(1)}, u32[]{:S(2)}, u32[]{:S(2)}) collective-permute-start(bf16[128,512]{1,0:T(8,128)(2,1)} %param.10), channel_id=1, source_target_pairs={{0,1},{1,0},{2,3},{3,2},{4,5},{5,4},{6,7},{7,6},{8,9},{9,8},{10,11... | collective-permute-start | bytes 393224 | tf_op jit(solution)/shard_map/ppermute | solution.py:34
  5.8 3.5 %copy-start.5 = (bf16[128,512]{1,0:T(8,128)(2,1)S(1)}, bf16[128,512]{1,0:T(8,128)(2,1)}, u32[]{:S(2)}) copy-start(bf16[128,512]{1,0:T(8,128)(2,1)} %param.10) | copy-start | bytes 393220
  8.6 4.7 %collective-permute-start.3 = (bf16[512,1024]{1,0:T(8,128)(2,1)S(1)}, bf16[512,1024]{1,0:T(8,128)(2,1)S(1)}, u32[]{:S(2)}, u32[]{:S(2)}) collective-permute-start(bf16[512,1024]{1,0:T(8,128)(2,1)S(1)} %get-tuple-element.28), channel_id=1, source_target_pairs={{0,1},{1,0},{2,3},{3,2},{4,5},{5,4},{6,7},{7,6},{8,9},{9,8},{10,11... | collective-permute-start | bytes 3145736 | tf_op jit(solution)/shard_map/ppermute | solution.py:34
  9.3 3.9 %collective-permute-start.5 = (bf16[128,512]{1,0:T(8,128)(2,1)S(1)}, bf16[128,512]{1,0:T(8,128)(2,1)S(1)}, u32[]{:S(2)}, u32[]{:S(2)}) collective-permute-start(bf16[128,512]{1,0:T(8,128)(2,1)S(1)} %collective-permute-done), channel_id=1, source_target_pairs={{0,1},{1,0},{2,3},{3,2},{4,5},{5,4},{6,7},{7,6},{8,9},{9,8},{10,11... | collective-permute-start | bytes 393224 | tf_op jit(solution)/shard_map/ppermute | solution.py:34
  11.6 1.6 %collective-permute-start.6 = (bf16[128,512]{1,0:T(8,128)(2,1)S(1)}, bf16[128,512]{1,0:T(8,128)(2,1)S(1)}, u32[]{:S(2)}, u32[]{:S(2)}) collective-permute-start(bf16[128,512]{1,0:T(8,128)(2,1)S(1)} %collective-permute-done.1), channel_id=1, source_target_pairs={{0,1},{1,0},{2,3},{3,2},{4,5},{5,4},{6,7},{7,6},{8,9},{9,8},{10,11... | collective-permute-start | bytes 393224 | tf_op jit(solution)/shard_map/ppermute | solution.py:34
  11.6 1.6 %collective-permute-start.7 = (bf16[128,512]{1,0:T(8,128)(2,1)S(1)}, bf16[128,512]{1,0:T(8,128)(2,1)S(1)}, u32[]{:S(2)}, u32[]{:S(2)}) collective-permute-start(bf16[128,512]{1,0:T(8,128)(2,1)S(1)} %collective-permute-done.2), channel_id=1, source_target_pairs={{0,1},{1,0},{2,3},{3,2},{4,5},{5,4},{6,7},{7,6},{8,9},{9,8},{10,11... | collective-permute-start | bytes 393224 | tf_op jit(solution)/shard_map/ppermute | solution.py:34
  13.7 11.0 %copy-start.6 = (s32[128]{0:T(128)S(1)}, s32[128]{0:T(128)}, u32[]{:S(2)}) copy-start(s32[128]{0:T(128)} %param.15) | copy-start | bytes 1540
  13.8 15.5 %copy-start.1 = (bf16[512,1024]{1,0:T(8,128)(2,1)S(1)}, bf16[512,1024]{1,0:T(8,128)(2,1)}, u32[]{:S(2)}) copy-start(bf16[512,1024]{1,0:T(8,128)(2,1)} %w_ref.1) | copy-start | bytes 3145732
  13.8 15.5 %copy-start.2 = (bf16[1024,512]{1,0:T(8,128)(2,1)S(1)}, bf16[1024,512]{1,0:T(8,128)(2,1)}, u32[]{:S(2)}) copy-start(bf16[1024,512]{1,0:T(8,128)(2,1)} %refs_2_.1) | copy-start | bytes 3145732
  13.8 15.4 %copy-start.4 = (bf16[128,512]{1,0:T(8,128)(2,1)S(1)}, bf16[128,512]{1,0:T(8,128)(2,1)}, u32[]{:S(2)}) copy-start(bf16[128,512]{1,0:T(8,128)(2,1)} %cot_ref.1) | copy-start | bytes 393220
  13.8 9.4 %collective-permute-start.8 = (bf16[256,512]{1,0:T(8,128)(2,1)S(1)}, bf16[256,512]{1,0:T(8,128)(2,1)S(1)}, u32[]{:S(2)}, u32[]{:S(2)}) collective-permute-start(bf16[256,512]{1,0:T(8,128)(2,1)S(1)} %fusion.2), channel_id=1, source_target_pairs={{0,4},{1,3},{2,6},{3,1},{4,0},{5,7},{6,2},{7,5},{8,12},{9,11},{10,... | collective-permute-start | bytes 786440 | tf_op jit(solution)/shard_map/ppermute | solution.py:30
  23.2 6.0 %collective-permute-start.9 = (bf16[128,512]{1,0:T(8,128)(2,1)S(1)}, bf16[128,512]{1,0:T(8,128)(2,1)S(1)}, u32[]{:S(2)}, u32[]{:S(2)}) collective-permute-start(bf16[128,512]{1,0:T(8,128)(2,1)S(1)} %get-tuple-element.30), channel_id=1, source_target_pairs={{0,2},{1,5},{2,0},{3,7},{4,6},{5,1},{6,4},{7,3},{8,10},{9,13},{10,... | collective-permute-start | bytes 393224 | tf_op jit(solution)/shard_map/ppermute | solution.py:30
  30.0 1.8 %collective-permute-start.10 = (bf16[128,1536]{1,0:T(8,128)(2,1)S(1)}, bf16[128,1536]{1,0:T(8,128)(2,1)S(1)}, u32[]{:S(2)}, u32[]{:S(2)}) collective-permute-start(bf16[128,1536]{1,0:T(8,128)(2,1)S(1)} %get-tuple-element.32), channel_id=1, source_target_pairs={{0,1},{1,0},{2,3},{3,2},{4,5},{5,4},{6,7},{7,6},{8,9},{9,8},{10,11... | collective-permute-start | bytes 1179656 | tf_op jit(solution)/shard_map/ppermute | solution.py:34
  32.3 6.7 %collective-permute-start.11 = (bf16[144,512]{1,0:T(8,128)(2,1)S(1)}, bf16[144,512]{1,0:T(8,128)(2,1)S(1)}, u32[]{:S(2)}, u32[]{:S(2)}) collective-permute-start(bf16[144,512]{1,0:T(8,128)(2,1)S(1)} %get-tuple-element.37), channel_id=1, source_target_pairs={{0,2},{1,5},{2,0},{3,7},{4,6},{5,1},{6,4},{7,3},{8,10},{9,13},{10,... | collective-permute-start | bytes 442376 | tf_op jit(solution)/shard_map/ppermute | solution.py:30
  32.9 7.5 %collective-permute-start.21 = (bf16[512,256]{1,0:T(8,128)(2,1)S(1)}, bf16[512,256]{1,0:T(8,128)(2,1)S(1)}, u32[]{:S(2)}, u32[]{:S(2)}) collective-permute-start(bf16[512,256]{1,0:T(8,128)(2,1)S(1)} %get-tuple-element.40), channel_id=1, source_target_pairs={{0,16},{1,9},{2,18},{3,11},{4,20},{5,13},{6,22},{7,15},{8,24},{9,1... | collective-permute-start | bytes 786440 | tf_op jit(solution)/shard_map/ppermute | solution.py:30
  35.4 6.8 %collective-permute-start.16 = (bf16[512,256]{1,0:T(8,128)(2,1)S(1)}, bf16[512,256]{1,0:T(8,128)(2,1)S(1)}, u32[]{:S(2)}, u32[]{:S(2)}) collective-permute-start(bf16[512,256]{1,0:T(8,128)(2,1)S(1)} %weight_blocks.5), channel_id=1, source_target_pairs={{0,16},{1,9},{2,18},{3,11},{4,20},{5,13},{6,22},{7,15},{8,24},{9,1... | collective-permute-start | bytes 786440 | tf_op jit(solution)/shard_map/ppermute | solution.py:30
  39.1 13.1 %collective-permute-start.12 = (bf16[272,512]{1,0:T(8,128)(2,1)S(1)}, bf16[272,512]{1,0:T(8,128)(2,1)S(1)}, u32[]{:S(2)}, u32[]{:S(2)}) collective-permute-start(bf16[272,512]{1,0:T(8,128)(2,1)S(1)} %pad_maximum_fusion.1), channel_id=1, source_target_pairs={{0,4},{1,3},{2,6},{3,1},{4,0},{5,7},{6,2},{7,5},{8,12},{9,11},{10,... | collective-permute-start | bytes 835592 | tf_op jit(solution)/shard_map/ppermute | solution.py:30
  40.5 5.0 %collective-permute-start.22 = (bf16[256,256]{1,0:T(8,128)(2,1)S(1)}, bf16[256,256]{1,0:T(8,128)(2,1)S(1)}, u32[]{:S(2)}, u32[]{:S(2)}) collective-permute-start(bf16[256,256]{1,0:T(8,128)(2,1)S(1)} %fusion.10), channel_id=1, source_target_pairs={{0,8},{1,17},{2,10},{3,19},{4,12},{5,21},{6,14},{7,23},{8,0},{9,25... | collective-permute-start | bytes 393224 | tf_op jit(solution)/shard_map/ppermute | solution.py:30
  42.3 5.9 %collective-permute-start.17 = (bf16[256,256]{1,0:T(8,128)(2,1)S(1)}, bf16[256,256]{1,0:T(8,128)(2,1)S(1)}, u32[]{:S(2)}, u32[]{:S(2)}) collective-permute-start(bf16[256,256]{1,0:T(8,128)(2,1)S(1)} %fusion.13), channel_id=1, source_target_pairs={{0,8},{1,17},{2,10},{3,19},{4,12},{5,21},{6,14},{7,23},{8,0},{9,25... | collective-permute-start | bytes 393224 | tf_op jit(solution)/shard_map/ppermute | solution.py:30
  45.6 7.3 %collective-permute-start.23 = (bf16[256,256]{1,0:T(8,128)(2,1)S(1)}, bf16[256,256]{1,0:T(8,128)(2,1)S(1)}, u32[]{:S(2)}, u32[]{:S(2)}) collective-permute-start(bf16[256,256]{1,0:T(8,128)(2,1)S(1)} %fusion.12), channel_id=1, source_target_pairs={{0,2},{1,5},{2,0},{3,7},{4,6},{5,1},{6,4},{7,3},{8,10},{9,13},{10,... | collective-permute-start | bytes 393224 | tf_op jit(solution)/shard_map/ppermute | solution.py:30
  48.2 8.8 %collective-permute-start.18 = (bf16[256,256]{1,0:T(8,128)(2,1)S(1)}, bf16[256,256]{1,0:T(8,128)(2,1)S(1)}, u32[]{:S(2)}, u32[]{:S(2)}) collective-permute-start(bf16[256,256]{1,0:T(8,128)(2,1)S(1)} %fusion.15.refs_0_), channel_id=1, source_target_pairs={{0,2},{1,5},{2,0},{3,7},{4,6},{5,1},{6,4},{7,3},{8,10},{9,13},{10,... | collective-permute-start | bytes 393224 | tf_op jit(solution)/shard_map/ppermute | solution.py:30
  52.7 2.0 %collective-permute-start.13 = (bf16[512,512]{1,0:T(8,128)(2,1)S(1)}, bf16[512,512]{1,0:T(8,128)(2,1)S(1)}, u32[]{:S(2)}, u32[]{:S(2)}) collective-permute-start(bf16[512,512]{1,0:T(8,128)(2,1)S(1)} %fusion), channel_id=1, source_target_pairs={{0,1},{1,0},{2,3},{3,2},{4,5},{5,4},{6,7},{7,6},{8,9},{9,8},{10,11... | collective-permute-start | bytes 1572872 | tf_op jit(solution)/shard_map/ppermute | solution.py:34
  52.9 6.0 %collective-permute-start.24 = (bf16[256,256]{1,0:T(8,128)(2,1)S(1)}, bf16[256,256]{1,0:T(8,128)(2,1)S(1)}, u32[]{:S(2)}, u32[]{:S(2)}) collective-permute-start(bf16[256,256]{1,0:T(8,128)(2,1)S(1)} %reduce-precision_convert_fusion.1), channel_id=1, source_target_pairs={{0,4},{1,3},{2,6},{3,1},{4,0},{5,7},{6,2},{7,5},{8,12},{9,11},{10,... | collective-permute-start | bytes 393224 | tf_op jit(solution)/shard_map/ppermute | solution.py:30
  55.2 9.5 %collective-permute-start.14 = (bf16[272,512]{1,0:T(8,128)(2,1)S(1)}, bf16[272,512]{1,0:T(8,128)(2,1)S(1)}, u32[]{:S(2)}, u32[]{:S(2)}) collective-permute-start(bf16[272,512]{1,0:T(8,128)(2,1)S(1)} %pad_maximum_fusion.2.refs_2_), channel_id=1, source_target_pairs={{0,16},{1,9},{2,18},{3,11},{4,20},{5,13},{6,22},{7,15},{8,24},{9,1... | collective-permute-start | bytes 835592 | tf_op jit(solution)/shard_map/ppermute | solution.py:30
  57.1 6.3 %collective-permute-start.19 = (bf16[256,256]{1,0:T(8,128)(2,1)S(1)}, bf16[256,256]{1,0:T(8,128)(2,1)S(1)}, u32[]{:S(2)}, u32[]{:S(2)}) collective-permute-start(bf16[256,256]{1,0:T(8,128)(2,1)S(1)} %added.3), channel_id=1, source_target_pairs={{0,4},{1,3},{2,6},{3,1},{4,0},{5,7},{6,2},{7,5},{8,12},{9,11},{10,... | collective-permute-start | bytes 393224 | tf_op jit(solution)/shard_map/ppermute | solution.py:30
  59.0 6.8 %collective-permute-start.25 = (bf16[256,256]{1,0:T(8,128)(2,1)S(1)}, bf16[256,256]{1,0:T(8,128)(2,1)S(1)}, u32[]{:S(2)}, u32[]{:S(2)}) collective-permute-start(bf16[256,256]{1,0:T(8,128)(2,1)S(1)} %reduce-precision_convert_fusion.refs_0_), channel_id=1, source_target_pairs={{0,8},{1,17},{2,10},{3,19},{4,12},{5,21},{6,14},{7,23},{8,0},{9,25... | collective-permute-start | bytes 393224 | tf_op jit(solution)/shard_map/ppermute | solution.py:30
  63.4 5.0 %collective-permute-start.20 = (bf16[256,256]{1,0:T(8,128)(2,1)S(1)}, bf16[256,256]{1,0:T(8,128)(2,1)S(1)}, u32[]{:S(2)}, u32[]{:S(2)}) collective-permute-start(bf16[256,256]{1,0:T(8,128)(2,1)S(1)} %reduce-precision_convert_fusion.2.refs_0_), channel_id=1, source_target_pairs={{0,8},{1,17},{2,10},{3,19},{4,12},{5,21},{6,14},{7,23},{8,0},{9,25... | collective-permute-start | bytes 393224 | tf_op jit(solution)/shard_map/ppermute | solution.py:30
  64.9 6.4 %collective-permute-start.15 = (bf16[144,512]{1,0:T(8,128)(2,1)S(1)}, bf16[144,512]{1,0:T(8,128)(2,1)S(1)}, u32[]{:S(2)}, u32[]{:S(2)}) collective-permute-start(bf16[144,512]{1,0:T(8,128)(2,1)S(1)} %pad_maximum_fusion.5.refs_2_), channel_id=1, source_target_pairs={{0,8},{1,17},{2,10},{3,19},{4,12},{5,21},{6,14},{7,23},{8,0},{9,25... | collective-permute-start | bytes 442376 | tf_op jit(solution)/shard_map/ppermute | solution.py:30
  65.8 6.8 %collective-permute-start.28 = (bf16[512,256]{1,0:T(8,128)(2,1)S(1)}, bf16[512,256]{1,0:T(8,128)(2,1)S(1)}, u32[]{:S(2)}, u32[]{:S(2)}) collective-permute-start(bf16[512,256]{1,0:T(8,128)(2,1)S(1)} %joined.2.refs_2_.refs_0_), channel_id=1, source_target_pairs={{0,1},{1,0},{2,3},{3,2},{4,5},{5,4},{6,7},{7,6},{8,9},{9,8},{10,11... | collective-permute-start | bytes 786440 | tf_op jit(solution)/shard_map/ppermute | solution.py:34
  65.9 6.7 %collective-permute-start.31 = (bf16[512,256]{1,0:T(8,128)(2,1)S(1)}, bf16[512,256]{1,0:T(8,128)(2,1)S(1)}, u32[]{:S(2)}, u32[]{:S(2)}) collective-permute-start(bf16[512,256]{1,0:T(8,128)(2,1)S(1)} %joined.2.refs_2_.refs_0_), channel_id=1, source_target_pairs={{0,16},{1,9},{2,18},{3,11},{4,20},{5,13},{6,22},{7,15},{8,24},{9,1... | collective-permute-start | bytes 786440 | tf_op jit(solution)/shard_map/ppermute | solution.py:30
  68.5 4.1 %collective-permute-start.29 = (bf16[512,256]{1,0:T(8,128)(2,1)S(1)}, bf16[512,256]{1,0:T(8,128)(2,1)S(1)}, u32[]{:S(2)}, u32[]{:S(2)}) collective-permute-start(bf16[512,256]{1,0:T(8,128)(2,1)S(1)} %joined.3.refs_1_), channel_id=1, source_target_pairs={{0,1},{1,0},{2,3},{3,2},{4,5},{5,4},{6,7},{7,6},{8,9},{9,8},{10,11... | collective-permute-start | bytes 786440 | tf_op jit(solution)/shard_map/ppermute | solution.py:34
  68.6 6.5 %collective-permute-start.26 = (bf16[512,256]{1,0:T(8,128)(2,1)S(1)}, bf16[512,256]{1,0:T(8,128)(2,1)S(1)}, u32[]{:S(2)}, u32[]{:S(2)}) collective-permute-start(bf16[512,256]{1,0:T(8,128)(2,1)S(1)} %joined.3.refs_1_), channel_id=1, source_target_pairs={{0,16},{1,9},{2,18},{3,11},{4,20},{5,13},{6,22},{7,15},{8,24},{9,1... | collective-permute-start | bytes 786440 | tf_op jit(solution)/shard_map/ppermute | solution.py:30
  71.4 1.2 %collective-permute-start.30 = (bf16[16,512]{1,0:T(8,128)(2,1)S(1)}, bf16[16,512]{1,0:T(8,128)(2,1)S(1)}, u32[]{:S(2)}, u32[]{:S(2)}) collective-permute-start(bf16[16,512]{1,0:T(8,128)(2,1)S(1)} %pad_maximum_fusion.6.refs_4_), channel_id=1, source_target_pairs={{0,1},{1,0},{2,3},{3,2},{4,5},{5,4},{6,7},{7,6},{8,9},{9,8},{10,11... | collective-permute-start | bytes 49160 | tf_op jit(solution)/shard_map/ppermute | solution.py:34
  71.5 5.3 %copy-start.3 = (f32[128,512]{1,0:T(8,128)}, f32[128,512]{1,0:T(8,128)S(1)}, u32[]{:S(2)}) copy-start(f32[128,512]{1,0:T(8,128)S(1)} %slice_add_fusion.3.refs_7_) | copy-start | bytes 786436
  74.1 1.6 %collective-permute-start.32 = (bf16[512,256]{1,0:T(8,128)(2,1)S(1)}, bf16[512,256]{1,0:T(8,128)(2,1)S(1)}, u32[]{:S(2)}, u32[]{:S(2)}) collective-permute-start(bf16[512,256]{1,0:T(8,128)(2,1)S(1)} %get-tuple-element.41.refs_0_), channel_id=1, source_target_pairs={{0,1},{1,0},{2,3},{3,2},{4,5},{5,4},{6,7},{7,6},{8,9},{9,8},{10,11... | collective-permute-start | bytes 786440 | tf_op jit(solution)/shard_map/ppermute | solution.py:34
  75.1 1.6 %collective-permute-start.27 = (bf16[512,256]{1,0:T(8,128)(2,1)S(1)}, bf16[512,256]{1,0:T(8,128)(2,1)S(1)}, u32[]{:S(2)}, u32[]{:S(2)}) collective-permute-start(bf16[512,256]{1,0:T(8,128)(2,1)S(1)} %collective-permute-done.26.refs_0_), channel_id=1, source_target_pairs={{0,1},{1,0},{2,3},{3,2},{4,5},{5,4},{6,7},{7,6},{8,9},{9,8},{10,11... | collective-permute-start | bytes 786440 | tf_op jit(solution)/shard_map/ppermute | solution.py:34

commit v7 on v6

--- a/solution.py
+++ b/solution.py
@@ -490,13 +490,13 @@
     came = swap_cores(rounded(dot(far[:, :own], grad_rows, ((0,), (0,)))), n_row, n_col)
     low = dot(near[:, :own], grad_rows, ((0,), (0,))) + came.astype(FP)
     marks = []
-    for step in reversed(range(row_bits)):
-        size = low.shape[0] // 2
-        marks.append(jnp.concatenate([rounded(low[size:]), gain], axis=0))
+    tiles = [low[q * TILE : (q + 1) * TILE] for q in range(n_row)]
+    for step in range(row_bits):
+        marks.append(jnp.concatenate([rounded(x) for x in tiles[1::2]] + [gain], axis=0))
         came = row_step(marks[-1], step)
-        gain = split(whole(gain) + whole(came[size:]))
-        low = low[:size] + came[:size].astype(FP)
-    grad_x = low
+        tiles = [x + came[i * TILE : (i + 1) * TILE].astype(FP) for i, x in enumerate(tiles[0::2])]
+        gain = split(whole(gain) + whole(came[len(tiles) * TILE :]))
+    grad_x = tiles[0]
 
     for step in reversed(range(row_bits)):
         for i in range(parts):

time: 79.1 us -> 78.7 us (level)
  waiting for transfers between devices: 29.8 us -> 31.1 us
  starting transfers between devices: 32.4 us -> 31.4 us
    ppermute x21, waiting for transfers between devices: 26.5 us -> 27.5 us  [exchange(): return lax.ppermute(x, AXES, pairs)]
    ppermute x12, starting transfers between devices: 2.53 us -> 1.61 us  [swap_cores(): return lax.ppermute(x, AXES, [(i, i ^ 1) for i in range(rows * cols)])]
  transfers between devices with their start and end apart: 33 -> 33, of which waited for: 16 -> 17; matrix products, arithmetic and copies ran while one was open for 4% -> 4% of each run, Pallas kernels for 10% -> 10%
where the time goes in v7:
time: 78.7 us; the launch traced here: 78 us
  starting transfers between devices  31.4 us (40%)
  waiting for transfers between devices  31.1 us (40%)
  Pallas kernels  10.4 us (13%)
  matrix products  2.55 us (3%)
  between operations  1.86 us (2%)
    ppermute x21, starting transfers between devices, exchange(): return lax.ppermute(x, AXES, pairs)  29.8 us
    ppermute x21, waiting for transfers between devices, exchange(): return lax.ppermute(x, AXES, pairs)  27.5 us
    pallas_call x3, Pallas kernels, write_weights(): pl.pallas_call(kernel, out_shape=(jax.ShapeDtypeStruct((F, 2 * F), FP), j...  3.52 us
    ppermute x12, waiting for transfers between devices, swap_cores(): return lax.ppermute(x, AXES, [(i, i ^ 1) for i in range(rows * cols)])  3.51 us
    pallas_call x1, Pallas kernels, build(): pl.pallas_call(kernel, out_shape=(result, result), in_specs=[pl.BlockSpec...  2.74 us
    dot_general x5, matrix products, dot(): return lax.dot_general(a, b, (dims, ((), ())), preferred_element_type=FP)  2.25 us
    pallas_call x3, Pallas kernels, weight_blocks(): pl.pallas_call(kernel, out_shape=tuple((jax.ShapeDtypeStruct((rows, size)...  2.01 us
    ppermute x12, starting transfers between devices, swap_cores(): return lax.ppermute(x, AXES, [(i, i ^ 1) for i in range(rows * cols)])  1.61 us
  transfers between devices with their start and end apart: 33, of which 17 were waited for; matrix products, arithmetic and copies ran while one was open for 4% of the time, Pallas kernels for 10%

profile of v7, /device:TPU:0, one launch (start us, length us, event | category | flops | bytes accessed | tf_op | source)
XLA Modules:
  0.0 78.0 jit_solution(15976893659892628748)
XLA Ops:
  0.6 3.0 %collective-permute-start = (bf16[128,512]{1,0:T(8,128)(2,1)}, bf16[128,512]{1,0:T(8,128)(2,1)S(1)}, u32[]{:S(2)}, u32[]{:S(2)}) collective-permute-start(bf16[128,512]{1,0:T(8,128)(2,1)} %param.10), channel_id=1, source_target_pairs={{0,8},{1,17},{2,10},{3,19},{4,12},{5,21},{6,14},{7,23},{8,0},{9,25... | collective-permute-start | bytes 393224 | tf_op jit(solution)/shard_map/ppermute | solution.py:30
  3.7 1.5 %collective-permute-start.1 = (bf16[128,512]{1,0:T(8,128)(2,1)}, bf16[128,512]{1,0:T(8,128)(2,1)S(1)}, u32[]{:S(2)}, u32[]{:S(2)}) collective-permute-start(bf16[128,512]{1,0:T(8,128)(2,1)} %param.10), channel_id=1, source_target_pairs={{0,16},{1,9},{2,18},{3,11},{4,20},{5,13},{6,22},{7,15},{8,24},{9,1... | collective-permute-start | bytes 393224 | tf_op jit(solution)/shard_map/ppermute | solution.py:30
  5.9 2.7 %build_dense.1 = (bf16[512,1024]{1,0:T(8,128)(2,1)S(1)}, bf16[512,1024]{1,0:T(8,128)(2,1)S(1)}) custom-call(s32[1,1]{1,0:T(1,128)S(6)} %copy.34.count_ref, s32[1,128]{1,0:T(1,128)} %rows_ref.1, s32[1,128]{1,0:T(1,128)} %cols_ref.1, bf16[1,128,128,128]{3,2,1,0:T(8,128)(2,1)} %vals_ref.1), custom_call_target="tpu_custom_call" | custom-call | flops 2097152 | bytes 6291456 | tf_op jit(solution)/shard_map/build_dense/pallas_call | solution.py:105
  8.6 0.6 collective-permute-start.3
  9.2 0.1 collective-permute-start.5
  9.3 2.3 %collective-permute-done.1 = bf16[128,512]{1,0:T(8,128)(2,1)S(1)} collective-permute-done((bf16[128,512]{1,0:T(8,128)(2,1)}, bf16[128,512]{1,0:T(8,128)(2,1)S(1)}, u32[]{:S(2)}, u32[]{:S(2)}) %collective-permute-start.1) | collective-permute-done | bytes 131104 | tf_op jit(solution)/shard_map/ppermute | solution.py:30
  11.6 0.5 collective-permute-start.7
  12.3 0.4 fusion.7
  12.7 0.4 product.1.refs_4_
  13.2 0.1 stacked.1
  13.3 0.4 fusion.2
  13.8 2.4 %collective-permute-start.8 = (bf16[256,512]{1,0:T(8,128)(2,1)S(1)}, bf16[256,512]{1,0:T(8,128)(2,1)S(1)}, u32[]{:S(2)}, u32[]{:S(2)}) collective-permute-start(bf16[256,512]{1,0:T(8,128)(2,1)S(1)} %fusion.2), channel_id=1, source_target_pairs={{0,4},{1,3},{2,6},{3,1},{4,0},{5,7},{6,2},{7,5},{8,12},{9,11},{10,... | collective-permute-start | bytes 786440 | tf_op jit(solution)/shard_map/ppermute | solution.py:30
  16.2 0.4 convolution_add_fusion.2.refs_0_
  16.7 6.5 %collective-permute-done.8.refs_1_ = bf16[256,512]{1,0:T(8,128)(2,1)S(1)} collective-permute-done((bf16[256,512]{1,0:T(8,128)(2,1)S(1)}, bf16[256,512]{1,0:T(8,128)(2,1)S(1)}, u32[]{:S(2)}, u32[]{:S(2)}) %collective-permute-start.8) | collective-permute-done | bytes 262176 | tf_op jit(solution)/shard_map/ppermute | solution.py:30
  23.2 1.5 %collective-permute-start.9 = (bf16[128,512]{1,0:T(8,128)(2,1)S(1)}, bf16[128,512]{1,0:T(8,128)(2,1)S(1)}, u32[]{:S(2)}, u32[]{:S(2)}) collective-permute-start(bf16[128,512]{1,0:T(8,128)(2,1)S(1)} %get-tuple-element.30), channel_id=1, source_target_pairs={{0,2},{1,5},{2,0},{3,7},{4,6},{5,1},{6,4},{7,3},{8,10},{9,13},{10,... | collective-permute-start | bytes 393224 | tf_op jit(solution)/shard_map/ppermute | solution.py:30
  24.8 0.3 fusion.20.refs_2_.gains_ref
  25.1 4.1 %collective-permute-done.9.refs_1_ = bf16[128,512]{1,0:T(8,128)(2,1)S(1)} collective-permute-done((bf16[128,512]{1,0:T(8,128)(2,1)S(1)}, bf16[128,512]{1,0:T(8,128)(2,1)S(1)}, u32[]{:S(2)}, u32[]{:S(2)}) %collective-permute-start.9) | collective-permute-done | bytes 131104 | tf_op jit(solution)/shard_map/ppermute | solution.py:30
  29.2 0.8 node_values.1
  30.0 0.1 collective-permute-start.10
  30.1 0.8 node_gradients.1.refs_0_
  30.8 0.9 %collective-permute-done.10.met_ref = bf16[128,1536]{1,0:T(8,128)(2,1)S(1)} collective-permute-done((bf16[128,1536]{1,0:T(8,128)(2,1)S(1)}, bf16[128,1536]{1,0:T(8,128)(2,1)S(1)}, u32[]{:S(2)}, u32[]{:S(2)}) %collective-permute-start.10) | collective-permute-done | bytes 393248 | tf_op jit(solution)/shard_map/ppermute | solution.py:34
  31.8 0.5 weight_blocks.4
  32.3 0.6 collective-permute-start.11
  32.9 1.9 %collective-permute-start.21 = (bf16[512,256]{1,0:T(8,128)(2,1)S(1)}, bf16[512,256]{1,0:T(8,128)(2,1)S(1)}, u32[]{:S(2)}, u32[]{:S(2)}) collective-permute-start(bf16[512,256]{1,0:T(8,128)(2,1)S(1)} %get-tuple-element.40), channel_id=1, source_target_pairs={{0,16},{1,9},{2,18},{3,11},{4,20},{5,13},{6,22},{7,15},{8,24},{9,1... | collective-permute-start | bytes 786440 | tf_op jit(solution)/shard_map/ppermute | solution.py:30
  34.9 0.5 weight_blocks.5
  35.4 0.2 collective-permute-start.16
  35.6 1.0 %weight_blocks.3 = (f32[512,256]{1,0:T(8,128)S(1)}, f32[512,256]{1,0:T(8,128)S(1)}, bf16[128,512]{1,0:T(8,128)(2,1)}) custom-call(bf16[128,1536]{1,0:T(8,128)(2,1)S(1)} %get-tuple-element.31.mine_ref, bf16[128,1536]{1,0:T(8,128)(2,1)S(1)} %collective-permute-done.10.met_ref, f32[128,512]{1,0:T(8,128)S(1)} %get-tuple-element.33.refs_0_.agg_ref, ...), custom_call_target="tpu_custom_call" | custom-call | flops 134217728 | bytes 1572864 | tf_op jit(solution)/shard_map/weight_blocks/pallas_call | solution.py:295
  36.6 2.5 %collective-permute-done.11 = bf16[144,512]{1,0:T(8,128)(2,1)S(1)} collective-permute-done((bf16[144,512]{1,0:T(8,128)(2,1)S(1)}, bf16[144,512]{1,0:T(8,128)(2,1)S(1)}, u32[]{:S(2)}, u32[]{:S(2)}) %collective-permute-start.11) | collective-permute-done | bytes 147488 | tf_op jit(solution)/shard_map/ppermute | solution.py:30
  39.1 1.3 %collective-permute-start.12 = (bf16[272,512]{1,0:T(8,128)(2,1)S(1)}, bf16[272,512]{1,0:T(8,128)(2,1)S(1)}, u32[]{:S(2)}, u32[]{:S(2)}) collective-permute-start(bf16[272,512]{1,0:T(8,128)(2,1)S(1)} %pad_maximum_fusion.1), channel_id=1, source_target_pairs={{0,4},{1,3},{2,6},{3,1},{4,0},{5,7},{6,2},{7,5},{8,12},{9,11},{10,... | collective-permute-start | bytes 835592 | tf_op jit(solution)/shard_map/ppermute | solution.py:30
  40.4 0.1 convert_add_fusion
  40.5 1.5 %collective-permute-start.22 = (bf16[256,256]{1,0:T(8,128)(2,1)S(1)}, bf16[256,256]{1,0:T(8,128)(2,1)S(1)}, u32[]{:S(2)}, u32[]{:S(2)}) collective-permute-start(bf16[256,256]{1,0:T(8,128)(2,1)S(1)} %fusion.9), channel_id=1, source_target_pairs={{0,8},{1,17},{2,10},{3,19},{4,12},{5,21},{6,14},{7,23},{8,0},{9,25... | collective-permute-start | bytes 393224 | tf_op jit(solution)/shard_map/ppermute | solution.py:30
  42.0 0.2 collective-permute-done.16
  42.2 1.5 %collective-permute-start.17 = (bf16[256,256]{1,0:T(8,128)(2,1)S(1)}, bf16[256,256]{1,0:T(8,128)(2,1)S(1)}, u32[]{:S(2)}, u32[]{:S(2)}) collective-permute-start(bf16[256,256]{1,0:T(8,128)(2,1)S(1)} %fusion.12), channel_id=1, source_target_pairs={{0,8},{1,17},{2,10},{3,19},{4,12},{5,21},{6,14},{7,23},{8,0},{9,25... | collective-permute-start | bytes 393224 | tf_op jit(solution)/shard_map/ppermute | solution.py:30
  43.8 1.8 %collective-permute-done.22 = bf16[256,256]{1,0:T(8,128)(2,1)S(1)} collective-permute-done((bf16[256,256]{1,0:T(8,128)(2,1)S(1)}, bf16[256,256]{1,0:T(8,128)(2,1)S(1)}, u32[]{:S(2)}, u32[]{:S(2)}) %collective-permute-start.22) | collective-permute-done | bytes 131104 | tf_op jit(solution)/shard_map/ppermute | solution.py:30
  45.6 2.6 %collective-permute-start.23 = (bf16[256,256]{1,0:T(8,128)(2,1)S(1)}, bf16[256,256]{1,0:T(8,128)(2,1)S(1)}, u32[]{:S(2)}, u32[]{:S(2)}) collective-permute-start(bf16[256,256]{1,0:T(8,128)(2,1)S(1)} %fusion.11), channel_id=1, source_target_pairs={{0,2},{1,5},{2,0},{3,7},{4,6},{5,1},{6,4},{7,3},{8,10},{9,13},{10,... | collective-permute-start | bytes 393224 | tf_op jit(solution)/shard_map/ppermute | solution.py:30
  48.2 1.6 %collective-permute-start.18 = (bf16[256,256]{1,0:T(8,128)(2,1)S(1)}, bf16[256,256]{1,0:T(8,128)(2,1)S(1)}, u32[]{:S(2)}, u32[]{:S(2)}) collective-permute-start(bf16[256,256]{1,0:T(8,128)(2,1)S(1)} %fusion.14.refs_0_), channel_id=1, source_target_pairs={{0,2},{1,5},{2,0},{3,7},{4,6},{5,1},{6,4},{7,3},{8,10},{9,13},{10,... | collective-permute-start | bytes 393224 | tf_op jit(solution)/shard_map/ppermute | solution.py:30
  49.8 2.4 %collective-permute-done.12 = bf16[272,512]{1,0:T(8,128)(2,1)S(1)} collective-permute-done((bf16[272,512]{1,0:T(8,128)(2,1)S(1)}, bf16[272,512]{1,0:T(8,128)(2,1)S(1)}, u32[]{:S(2)}, u32[]{:S(2)}) %collective-permute-start.12) | collective-permute-done | bytes 278560 | tf_op jit(solution)/shard_map/ppermute | solution.py:30
  52.2 0.5 fusion
  52.7 0.1 collective-permute-start.13
  52.9 0.8 %collective-permute-start.24 = (bf16[256,256]{1,0:T(8,128)(2,1)S(1)}, bf16[256,256]{1,0:T(8,128)(2,1)S(1)}, u32[]{:S(2)}, u32[]{:S(2)}) collective-permute-start(bf16[256,256]{1,0:T(8,128)(2,1)S(1)} %reduce-precision_convert_fusion.1), channel_id=1, source_target_pairs={{0,4},{1,3},{2,6},{3,1},{4,0},{5,7},{6,2},{7,5},{8,12},{9,11},{10,... | collective-permute-start | bytes 393224 | tf_op jit(solution)/shard_map/ppermute | solution.py:30
  53.7 1.0 %collective-permute-done.13 = bf16[512,512]{1,0:T(8,128)(2,1)S(1)} collective-permute-done((bf16[512,512]{1,0:T(8,128)(2,1)S(1)}, bf16[512,512]{1,0:T(8,128)(2,1)S(1)}, u32[]{:S(2)}, u32[]{:S(2)}) %collective-permute-start.13) | collective-permute-done | bytes 524320 | tf_op jit(solution)/shard_map/ppermute | solution.py:34
  54.7 0.5 convolution_add_fusion
  55.2 1.5 %collective-permute-start.14 = (bf16[272,512]{1,0:T(8,128)(2,1)S(1)}, bf16[272,512]{1,0:T(8,128)(2,1)S(1)}, u32[]{:S(2)}, u32[]{:S(2)}) collective-permute-start(bf16[272,512]{1,0:T(8,128)(2,1)S(1)} %pad_maximum_fusion.2.refs_2_), channel_id=1, source_target_pairs={{0,8},{1,17},{2,10},{3,19},{4,12},{5,21},{6,14},{7,23},{8,0},{9,25... | collective-permute-start | bytes 835592 | tf_op jit(solution)/shard_map/ppermute | solution.py:30
  56.7 1.3 %collective-permute-start.19 = (bf16[256,256]{1,0:T(8,128)(2,1)S(1)}, bf16[256,256]{1,0:T(8,128)(2,1)S(1)}, u32[]{:S(2)}, u32[]{:S(2)}) collective-permute-start(bf16[256,256]{1,0:T(8,128)(2,1)S(1)} %added.3), channel_id=1, source_target_pairs={{0,4},{1,3},{2,6},{3,1},{4,0},{5,7},{6,2},{7,5},{8,12},{9,11},{10,... | collective-permute-start | bytes 393224 | tf_op jit(solution)/shard_map/ppermute | solution.py:30
  58.0 0.9 %collective-permute-done.24 = bf16[256,256]{1,0:T(8,128)(2,1)S(1)} collective-permute-done((bf16[256,256]{1,0:T(8,128)(2,1)S(1)}, bf16[256,256]{1,0:T(8,128)(2,1)S(1)}, u32[]{:S(2)}, u32[]{:S(2)}) %collective-permute-start.24) | collective-permute-done | bytes 131104 | tf_op jit(solution)/shard_map/ppermute | solution.py:30
  59.0 1.5 %collective-permute-start.25 = (bf16[256,256]{1,0:T(8,128)(2,1)S(1)}, bf16[256,256]{1,0:T(8,128)(2,1)S(1)}, u32[]{:S(2)}, u32[]{:S(2)}) collective-permute-start(bf16[256,256]{1,0:T(8,128)(2,1)S(1)} %reduce-precision_convert_fusion.refs_0_), channel_id=1, source_target_pairs={{0,8},{1,17},{2,10},{3,19},{4,12},{5,21},{6,14},{7,23},{8,0},{9,25... | collective-permute-start | bytes 393224 | tf_op jit(solution)/shard_map/ppermute | solution.py:30
  60.4 2.8 %collective-permute-done.19 = bf16[256,256]{1,0:T(8,128)(2,1)S(1)} collective-permute-done((bf16[256,256]{1,0:T(8,128)(2,1)S(1)}, bf16[256,256]{1,0:T(8,128)(2,1)S(1)}, u32[]{:S(2)}, u32[]{:S(2)}) %collective-permute-start.19) | collective-permute-done | bytes 131104 | tf_op jit(solution)/shard_map/ppermute | solution.py:30
  63.3 1.2 %collective-permute-start.20 = (bf16[256,256]{1,0:T(8,128)(2,1)S(1)}, bf16[256,256]{1,0:T(8,128)(2,1)S(1)}, u32[]{:S(2)}, u32[]{:S(2)}) collective-permute-start(bf16[256,256]{1,0:T(8,128)(2,1)S(1)} %reduce-precision_convert_fusion.2.refs_0_), channel_id=1, source_target_pairs={{0,8},{1,17},{2,10},{3,19},{4,12},{5,21},{6,14},{7,23},{8,0},{9,25... | collective-permute-start | bytes 393224 | tf_op jit(solution)/shard_map/ppermute | solution.py:30
  64.5 1.5 %collective-permute-start.15 = (bf16[144,512]{1,0:T(8,128)(2,1)S(1)}, bf16[144,512]{1,0:T(8,128)(2,1)S(1)}, u32[]{:S(2)}, u32[]{:S(2)}) collective-permute-start(bf16[144,512]{1,0:T(8,128)(2,1)S(1)} %pad_maximum_fusion.5.refs_2_), channel_id=1, source_target_pairs={{0,16},{1,9},{2,18},{3,11},{4,20},{5,13},{6,22},{7,15},{8,24},{9,1... | collective-permute-start | bytes 442376 | tf_op jit(solution)/shard_map/ppermute | solution.py:30
  66.1 0.1 collective-permute-start.28
  66.2 0.6 collective-permute-start.31
  66.8 1.5 %collective-permute-done.20.refs_1_ = bf16[256,256]{1,0:T(8,128)(2,1)S(1)} collective-permute-done((bf16[256,256]{1,0:T(8,128)(2,1)S(1)}, bf16[256,256]{1,0:T(8,128)(2,1)S(1)}, u32[]{:S(2)}, u32[]{:S(2)}) %collective-permute-start.20) | collective-permute-done | bytes 131104 | tf_op jit(solution)/shard_map/ppermute | solution.py:30
  68.3 0.1 collective-permute-start.29
  68.4 1.7 %collective-permute-start.26 = (bf16[512,256]{1,0:T(8,128)(2,1)S(1)}, bf16[512,256]{1,0:T(8,128)(2,1)S(1)}, u32[]{:S(2)}, u32[]{:S(2)}) collective-permute-start(bf16[512,256]{1,0:T(8,128)(2,1)S(1)} %joined.3.refs_1_), channel_id=1, source_target_pairs={{0,16},{1,9},{2,18},{3,11},{4,20},{5,13},{6,22},{7,15},{8,24},{9,1... | collective-permute-start | bytes 786440 | tf_op jit(solution)/shard_map/ppermute | solution.py:30
  70.2 0.1 collective-permute-start.30
  70.3 1.1 %collective-permute-done.30.refs_5_ = bf16[16,512]{1,0:T(8,128)(2,1)S(1)} collective-permute-done((bf16[16,512]{1,0:T(8,128)(2,1)S(1)}, bf16[16,512]{1,0:T(8,128)(2,1)S(1)}, u32[]{:S(2)}, u32[]{:S(2)}) %collective-permute-start.30) | collective-permute-done | bytes 16416 | tf_op jit(solution)/shard_map/ppermute | solution.py:34
  71.5 1.1 %collective-permute-done.31.refs_6_ = bf16[512,256]{1,0:T(8,128)(2,1)S(1)} collective-permute-done((bf16[512,256]{1,0:T(8,128)(2,1)S(1)}, bf16[512,256]{1,0:T(8,128)(2,1)S(1)}, u32[]{:S(2)}, u32[]{:S(2)}) %collective-permute-start.31) | collective-permute-done | bytes 262176 | tf_op jit(solution)/shard_map/ppermute | solution.py:30
  72.6 1.4 %write_weights.3 = (f32[512,1024]{1,0:T(8,128)}, f32[1024,512]{1,0:T(8,128)}, f32[8,512]{1,0:T(8,128)}, bf16[512,256]{1,0:T(8,128)(2,1)S(1)}) custom-call(bf16[512,256]{1,0:T(8,128)(2,1)S(1)} %joined.2.refs_2_.refs_0_, bf16[512,256]{1,0:T(8,128)(2,1)S(1)} %joined.3.refs_1_, ...), custom_call_target="tpu_custom_call", output_to_operand_aliasing={{3}: (6, {})} | custom-call | tf_op jit(solution)/shard_map/write_weights/pallas_call | solution.py:187
  74.0 0.1 collective-permute-start.32
  74.1 1.3 %collective-permute-done.26.refs_0_ = bf16[512,256]{1,0:T(8,128)(2,1)S(1)} collective-permute-done((bf16[512,256]{1,0:T(8,128)(2,1)S(1)}, bf16[512,256]{1,0:T(8,128)(2,1)S(1)}, u32[]{:S(2)}, u32[]{:S(2)}) %collective-permute-start.26) | collective-permute-done | bytes 262176 | tf_op jit(solution)/shard_map/ppermute | solution.py:30
  75.4 0.2 collective-permute-done.32.refs_1_
  75.6 1.0 %write_weights.4 = (f32[512,1024]{1,0:T(8,128)}, f32[1024,512]{1,0:T(8,128)}) custom-call(bf16[512,256]{1,0:T(8,128)(2,1)S(1)} %get-tuple-element.41.refs_0_, bf16[512,256]{1,0:T(8,128)(2,1)S(1)} %collective-permute-done.32.refs_1_, f32[512,1024]{1,0:T(8,128)} %get-tuple-element.42.refs_2_, ...), custom_call_target="tpu_custom_call", output_to_operand_aliasing={{0}: (2, {}), {1}: (3, {})} | custom-call | tf_op jit(solution)/shard_map/write_weights/pallas_call | solution.py:187
  76.7 0.2 collective-permute-done.27.refs_1_
  76.9 1.0 %write_weights.5 = (f32[512,1024]{1,0:T(8,128)}, f32[1024,512]{1,0:T(8,128)}) custom-call(bf16[512,256]{1,0:T(8,128)(2,1)S(1)} %collective-permute-done.26.refs_0_, bf16[512,256]{1,0:T(8,128)(2,1)S(1)} %collective-permute-done.27.refs_1_, f32[512,1024]{1,0:T(8,128)} %get-tuple-element.44.refs_2_, ...), custom_call_target="tpu_custom_call", output_to_operand_aliasing={{0}: (2, {}), {1}: (3, {})} | custom-call | tf_op jit(solution)/shard_map/write_weights/pallas_call | solution.py:187
  (81 shorter events, 0.9 us)
Async XLA Ops:
  0.6 24.1 %copy-start = (f32[8,512]{1,0:T(8,128)S(1)}, f32[8,512]{1,0:T(8,128)}, u32[]{:S(2)}) copy-start(f32[8,512]{1,0:T(8,128)} %param.16) | copy-start | bytes 49156
  0.6 8.6 %collective-permute-start = (bf16[128,512]{1,0:T(8,128)(2,1)}, bf16[128,512]{1,0:T(8,128)(2,1)S(1)}, u32[]{:S(2)}, u32[]{:S(2)}) collective-permute-start(bf16[128,512]{1,0:T(8,128)(2,1)} %param.10), channel_id=1, source_target_pairs={{0,8},{1,17},{2,10},{3,19},{4,12},{5,21},{6,14},{7,23},{8,0},{9,25... | collective-permute-start | bytes 393224 | tf_op jit(solution)/shard_map/ppermute | solution.py:30
  3.7 8.0 %collective-permute-start.1 = (bf16[128,512]{1,0:T(8,128)(2,1)}, bf16[128,512]{1,0:T(8,128)(2,1)S(1)}, u32[]{:S(2)}, u32[]{:S(2)}) collective-permute-start(bf16[128,512]{1,0:T(8,128)(2,1)} %param.10), channel_id=1, source_target_pairs={{0,16},{1,9},{2,18},{3,11},{4,20},{5,13},{6,22},{7,15},{8,24},{9,1... | collective-permute-start | bytes 393224 | tf_op jit(solution)/shard_map/ppermute | solution.py:30
  5.2 6.5 %collective-permute-start.2 = (bf16[128,512]{1,0:T(8,128)(2,1)}, bf16[128,512]{1,0:T(8,128)(2,1)S(1)}, u32[]{:S(2)}, u32[]{:S(2)}) collective-permute-start(bf16[128,512]{1,0:T(8,128)(2,1)} %param.10), channel_id=1, source_target_pairs={{0,24},{1,25},{2,26},{3,27},{4,28},{5,29},{6,30},{7,31},{8,16},{9,... | collective-permute-start | bytes 393224 | tf_op jit(solution)/shard_map/ppermute | solution.py:30
  5.2 8.0 %collective-permute-start.4 = (bf16[128,512]{1,0:T(8,128)(2,1)}, bf16[128,512]{1,0:T(8,128)(2,1)S(1)}, u32[]{:S(2)}, u32[]{:S(2)}) collective-permute-start(bf16[128,512]{1,0:T(8,128)(2,1)} %param.10), channel_id=1, source_target_pairs={{0,1},{1,0},{2,3},{3,2},{4,5},{5,4},{6,7},{7,6},{8,9},{9,8},{10,11... | collective-permute-start | bytes 393224 | tf_op jit(solution)/shard_map/ppermute | solution.py:34
  5.8 3.3 %copy-start.5 = (bf16[128,512]{1,0:T(8,128)(2,1)S(1)}, bf16[128,512]{1,0:T(8,128)(2,1)}, u32[]{:S(2)}) copy-start(bf16[128,512]{1,0:T(8,128)(2,1)} %param.10) | copy-start | bytes 393220
  8.6 4.7 %collective-permute-start.3 = (bf16[512,1024]{1,0:T(8,128)(2,1)S(1)}, bf16[512,1024]{1,0:T(8,128)(2,1)S(1)}, u32[]{:S(2)}, u32[]{:S(2)}) collective-permute-start(bf16[512,1024]{1,0:T(8,128)(2,1)S(1)} %get-tuple-element.28), channel_id=1, source_target_pairs={{0,1},{1,0},{2,3},{3,2},{4,5},{5,4},{6,7},{7,6},{8,9},{9,8},{10,11... | collective-permute-start | bytes 3145736 | tf_op jit(solution)/shard_map/ppermute | solution.py:34
  9.2 4.0 %collective-permute-start.5 = (bf16[128,512]{1,0:T(8,128)(2,1)S(1)}, bf16[128,512]{1,0:T(8,128)(2,1)S(1)}, u32[]{:S(2)}, u32[]{:S(2)}) collective-permute-start(bf16[128,512]{1,0:T(8,128)(2,1)S(1)} %collective-permute-done), channel_id=1, source_target_pairs={{0,1},{1,0},{2,3},{3,2},{4,5},{5,4},{6,7},{7,6},{8,9},{9,8},{10,11... | collective-permute-start | bytes 393224 | tf_op jit(solution)/shard_map/ppermute | solution.py:34
  11.6 1.6 %collective-permute-start.6 = (bf16[128,512]{1,0:T(8,128)(2,1)S(1)}, bf16[128,512]{1,0:T(8,128)(2,1)S(1)}, u32[]{:S(2)}, u32[]{:S(2)}) collective-permute-start(bf16[128,512]{1,0:T(8,128)(2,1)S(1)} %collective-permute-done.1), channel_id=1, source_target_pairs={{0,1},{1,0},{2,3},{3,2},{4,5},{5,4},{6,7},{7,6},{8,9},{9,8},{10,11... | collective-permute-start | bytes 393224 | tf_op jit(solution)/shard_map/ppermute | solution.py:34
  11.6 1.6 %collective-permute-start.7 = (bf16[128,512]{1,0:T(8,128)(2,1)S(1)}, bf16[128,512]{1,0:T(8,128)(2,1)S(1)}, u32[]{:S(2)}, u32[]{:S(2)}) collective-permute-start(bf16[128,512]{1,0:T(8,128)(2,1)S(1)} %collective-permute-done.2), channel_id=1, source_target_pairs={{0,1},{1,0},{2,3},{3,2},{4,5},{5,4},{6,7},{7,6},{8,9},{9,8},{10,11... | collective-permute-start | bytes 393224 | tf_op jit(solution)/shard_map/ppermute | solution.py:34
  13.7 11.0 %copy-start.6 = (s32[128]{0:T(128)S(1)}, s32[128]{0:T(128)}, u32[]{:S(2)}) copy-start(s32[128]{0:T(128)} %param.15) | copy-start | bytes 1540
  13.8 15.5 %copy-start.1 = (bf16[512,1024]{1,0:T(8,128)(2,1)S(1)}, bf16[512,1024]{1,0:T(8,128)(2,1)}, u32[]{:S(2)}) copy-start(bf16[512,1024]{1,0:T(8,128)(2,1)} %w_ref.1) | copy-start | bytes 3145732
  13.8 15.5 %copy-start.2 = (bf16[1024,512]{1,0:T(8,128)(2,1)S(1)}, bf16[1024,512]{1,0:T(8,128)(2,1)}, u32[]{:S(2)}) copy-start(bf16[1024,512]{1,0:T(8,128)(2,1)} %refs_2_.1) | copy-start | bytes 3145732
  13.8 15.4 %copy-start.4 = (bf16[128,512]{1,0:T(8,128)(2,1)S(1)}, bf16[128,512]{1,0:T(8,128)(2,1)}, u32[]{:S(2)}) copy-start(bf16[128,512]{1,0:T(8,128)(2,1)} %cot_ref.1) | copy-start | bytes 393220
  13.8 9.4 %collective-permute-start.8 = (bf16[256,512]{1,0:T(8,128)(2,1)S(1)}, bf16[256,512]{1,0:T(8,128)(2,1)S(1)}, u32[]{:S(2)}, u32[]{:S(2)}) collective-permute-start(bf16[256,512]{1,0:T(8,128)(2,1)S(1)} %fusion.2), channel_id=1, source_target_pairs={{0,4},{1,3},{2,6},{3,1},{4,0},{5,7},{6,2},{7,5},{8,12},{9,11},{10,... | collective-permute-start | bytes 786440 | tf_op jit(solution)/shard_map/ppermute | solution.py:30
  23.2 6.0 %collective-permute-start.9 = (bf16[128,512]{1,0:T(8,128)(2,1)S(1)}, bf16[128,512]{1,0:T(8,128)(2,1)S(1)}, u32[]{:S(2)}, u32[]{:S(2)}) collective-permute-start(bf16[128,512]{1,0:T(8,128)(2,1)S(1)} %get-tuple-element.30), channel_id=1, source_target_pairs={{0,2},{1,5},{2,0},{3,7},{4,6},{5,1},{6,4},{7,3},{8,10},{9,13},{10,... | collective-permute-start | bytes 393224 | tf_op jit(solution)/shard_map/ppermute | solution.py:30
  30.0 1.8 %collective-permute-start.10 = (bf16[128,1536]{1,0:T(8,128)(2,1)S(1)}, bf16[128,1536]{1,0:T(8,128)(2,1)S(1)}, u32[]{:S(2)}, u32[]{:S(2)}) collective-permute-start(bf16[128,1536]{1,0:T(8,128)(2,1)S(1)} %get-tuple-element.32), channel_id=1, source_target_pairs={{0,1},{1,0},{2,3},{3,2},{4,5},{5,4},{6,7},{7,6},{8,9},{9,8},{10,11... | collective-permute-start | bytes 1179656 | tf_op jit(solution)/shard_map/ppermute | solution.py:34
  32.3 6.7 %collective-permute-start.11 = (bf16[144,512]{1,0:T(8,128)(2,1)S(1)}, bf16[144,512]{1,0:T(8,128)(2,1)S(1)}, u32[]{:S(2)}, u32[]{:S(2)}) collective-permute-start(bf16[144,512]{1,0:T(8,128)(2,1)S(1)} %get-tuple-element.37), channel_id=1, source_target_pairs={{0,2},{1,5},{2,0},{3,7},{4,6},{5,1},{6,4},{7,3},{8,10},{9,13},{10,... | collective-permute-start | bytes 442376 | tf_op jit(solution)/shard_map/ppermute | solution.py:30
  32.9 7.5 %collective-permute-start.21 = (bf16[512,256]{1,0:T(8,128)(2,1)S(1)}, bf16[512,256]{1,0:T(8,128)(2,1)S(1)}, u32[]{:S(2)}, u32[]{:S(2)}) collective-permute-start(bf16[512,256]{1,0:T(8,128)(2,1)S(1)} %get-tuple-element.40), channel_id=1, source_target_pairs={{0,16},{1,9},{2,18},{3,11},{4,20},{5,13},{6,22},{7,15},{8,24},{9,1... | collective-permute-start | bytes 786440 | tf_op jit(solution)/shard_map/ppermute | solution.py:30
  35.4 6.8 %collective-permute-start.16 = (bf16[512,256]{1,0:T(8,128)(2,1)S(1)}, bf16[512,256]{1,0:T(8,128)(2,1)S(1)}, u32[]{:S(2)}, u32[]{:S(2)}) collective-permute-start(bf16[512,256]{1,0:T(8,128)(2,1)S(1)} %weight_blocks.5), channel_id=1, source_target_pairs={{0,16},{1,9},{2,18},{3,11},{4,20},{5,13},{6,22},{7,15},{8,24},{9,1... | collective-permute-start | bytes 786440 | tf_op jit(solution)/shard_map/ppermute | solution.py:30
  39.1 13.1 %collective-permute-start.12 = (bf16[272,512]{1,0:T(8,128)(2,1)S(1)}, bf16[272,512]{1,0:T(8,128)(2,1)S(1)}, u32[]{:S(2)}, u32[]{:S(2)}) collective-permute-start(bf16[272,512]{1,0:T(8,128)(2,1)S(1)} %pad_maximum_fusion.1), channel_id=1, source_target_pairs={{0,4},{1,3},{2,6},{3,1},{4,0},{5,7},{6,2},{7,5},{8,12},{9,11},{10,... | collective-permute-start | bytes 835592 | tf_op jit(solution)/shard_map/ppermute | solution.py:30
  40.5 5.0 %collective-permute-start.22 = (bf16[256,256]{1,0:T(8,128)(2,1)S(1)}, bf16[256,256]{1,0:T(8,128)(2,1)S(1)}, u32[]{:S(2)}, u32[]{:S(2)}) collective-permute-start(bf16[256,256]{1,0:T(8,128)(2,1)S(1)} %fusion.9), channel_id=1, source_target_pairs={{0,8},{1,17},{2,10},{3,19},{4,12},{5,21},{6,14},{7,23},{8,0},{9,25... | collective-permute-start | bytes 393224 | tf_op jit(solution)/shard_map/ppermute | solution.py:30
  42.2 5.9 %collective-permute-start.17 = (bf16[256,256]{1,0:T(8,128)(2,1)S(1)}, bf16[256,256]{1,0:T(8,128)(2,1)S(1)}, u32[]{:S(2)}, u32[]{:S(2)}) collective-permute-start(bf16[256,256]{1,0:T(8,128)(2,1)S(1)} %fusion.12), channel_id=1, source_target_pairs={{0,8},{1,17},{2,10},{3,19},{4,12},{5,21},{6,14},{7,23},{8,0},{9,25... | collective-permute-start | bytes 393224 | tf_op jit(solution)/shard_map/ppermute | solution.py:30
  45.6 7.3 %collective-permute-start.23 = (bf16[256,256]{1,0:T(8,128)(2,1)S(1)}, bf16[256,256]{1,0:T(8,128)(2,1)S(1)}, u32[]{:S(2)}, u32[]{:S(2)}) collective-permute-start(bf16[256,256]{1,0:T(8,128)(2,1)S(1)} %fusion.11), channel_id=1, source_target_pairs={{0,2},{1,5},{2,0},{3,7},{4,6},{5,1},{6,4},{7,3},{8,10},{9,13},{10,... | collective-permute-start | bytes 393224 | tf_op jit(solution)/shard_map/ppermute | solution.py:30
  48.2 8.5 %collective-permute-start.18 = (bf16[256,256]{1,0:T(8,128)(2,1)S(1)}, bf16[256,256]{1,0:T(8,128)(2,1)S(1)}, u32[]{:S(2)}, u32[]{:S(2)}) collective-permute-start(bf16[256,256]{1,0:T(8,128)(2,1)S(1)} %fusion.14.refs_0_), channel_id=1, source_target_pairs={{0,2},{1,5},{2,0},{3,7},{4,6},{5,1},{6,4},{7,3},{8,10},{9,13},{10,... | collective-permute-start | bytes 393224 | tf_op jit(solution)/shard_map/ppermute | solution.py:30
  52.7 2.0 %collective-permute-start.13 = (bf16[512,512]{1,0:T(8,128)(2,1)S(1)}, bf16[512,512]{1,0:T(8,128)(2,1)S(1)}, u32[]{:S(2)}, u32[]{:S(2)}) collective-permute-start(bf16[512,512]{1,0:T(8,128)(2,1)S(1)} %fusion), channel_id=1, source_target_pairs={{0,1},{1,0},{2,3},{3,2},{4,5},{5,4},{6,7},{7,6},{8,9},{9,8},{10,11... | collective-permute-start | bytes 1572872 | tf_op jit(solution)/shard_map/ppermute | solution.py:34
  52.9 6.0 %collective-permute-start.24 = (bf16[256,256]{1,0:T(8,128)(2,1)S(1)}, bf16[256,256]{1,0:T(8,128)(2,1)S(1)}, u32[]{:S(2)}, u32[]{:S(2)}) collective-permute-start(bf16[256,256]{1,0:T(8,128)(2,1)S(1)} %reduce-precision_convert_fusion.1), channel_id=1, source_target_pairs={{0,4},{1,3},{2,6},{3,1},{4,0},{5,7},{6,2},{7,5},{8,12},{9,11},{10,... | collective-permute-start | bytes 393224 | tf_op jit(solution)/shard_map/ppermute | solution.py:30
  55.2 9.2 %collective-permute-start.14 = (bf16[272,512]{1,0:T(8,128)(2,1)S(1)}, bf16[272,512]{1,0:T(8,128)(2,1)S(1)}, u32[]{:S(2)}, u32[]{:S(2)}) collective-permute-start(bf16[272,512]{1,0:T(8,128)(2,1)S(1)} %pad_maximum_fusion.2.refs_2_), channel_id=1, source_target_pairs={{0,8},{1,17},{2,10},{3,19},{4,12},{5,21},{6,14},{7,23},{8,0},{9,25... | collective-permute-start | bytes 835592 | tf_op jit(solution)/shard_map/ppermute | solution.py:30
  56.7 6.5 %collective-permute-start.19 = (bf16[256,256]{1,0:T(8,128)(2,1)S(1)}, bf16[256,256]{1,0:T(8,128)(2,1)S(1)}, u32[]{:S(2)}, u32[]{:S(2)}) collective-permute-start(bf16[256,256]{1,0:T(8,128)(2,1)S(1)} %added.3), channel_id=1, source_target_pairs={{0,4},{1,3},{2,6},{3,1},{4,0},{5,7},{6,2},{7,5},{8,12},{9,11},{10,... | collective-permute-start | bytes 393224 | tf_op jit(solution)/shard_map/ppermute | solution.py:30
  59.0 7.1 %collective-permute-start.25 = (bf16[256,256]{1,0:T(8,128)(2,1)S(1)}, bf16[256,256]{1,0:T(8,128)(2,1)S(1)}, u32[]{:S(2)}, u32[]{:S(2)}) collective-permute-start(bf16[256,256]{1,0:T(8,128)(2,1)S(1)} %reduce-precision_convert_fusion.refs_0_), channel_id=1, source_target_pairs={{0,8},{1,17},{2,10},{3,19},{4,12},{5,21},{6,14},{7,23},{8,0},{9,25... | collective-permute-start | bytes 393224 | tf_op jit(solution)/shard_map/ppermute | solution.py:30
  63.3 5.0 %collective-permute-start.20 = (bf16[256,256]{1,0:T(8,128)(2,1)S(1)}, bf16[256,256]{1,0:T(8,128)(2,1)S(1)}, u32[]{:S(2)}, u32[]{:S(2)}) collective-permute-start(bf16[256,256]{1,0:T(8,128)(2,1)S(1)} %reduce-precision_convert_fusion.2.refs_0_), channel_id=1, source_target_pairs={{0,8},{1,17},{2,10},{3,19},{4,12},{5,21},{6,14},{7,23},{8,0},{9,25... | collective-permute-start | bytes 393224 | tf_op jit(solution)/shard_map/ppermute | solution.py:30
  64.5 5.6 %collective-permute-start.15 = (bf16[144,512]{1,0:T(8,128)(2,1)S(1)}, bf16[144,512]{1,0:T(8,128)(2,1)S(1)}, u32[]{:S(2)}, u32[]{:S(2)}) collective-permute-start(bf16[144,512]{1,0:T(8,128)(2,1)S(1)} %pad_maximum_fusion.5.refs_2_), channel_id=1, source_target_pairs={{0,16},{1,9},{2,18},{3,11},{4,20},{5,13},{6,22},{7,15},{8,24},{9,1... | collective-permute-start | bytes 442376 | tf_op jit(solution)/shard_map/ppermute | solution.py:30
  66.1 5.4 %collective-permute-start.28 = (bf16[512,256]{1,0:T(8,128)(2,1)S(1)}, bf16[512,256]{1,0:T(8,128)(2,1)S(1)}, u32[]{:S(2)}, u32[]{:S(2)}) collective-permute-start(bf16[512,256]{1,0:T(8,128)(2,1)S(1)} %joined.2.refs_2_.refs_0_), channel_id=1, source_target_pairs={{0,1},{1,0},{2,3},{3,2},{4,5},{5,4},{6,7},{7,6},{8,9},{9,8},{10,11... | collective-permute-start | bytes 786440 | tf_op jit(solution)/shard_map/ppermute | solution.py:34
  66.2 6.4 %collective-permute-start.31 = (bf16[512,256]{1,0:T(8,128)(2,1)S(1)}, bf16[512,256]{1,0:T(8,128)(2,1)S(1)}, u32[]{:S(2)}, u32[]{:S(2)}) collective-permute-start(bf16[512,256]{1,0:T(8,128)(2,1)S(1)} %joined.2.refs_2_.refs_0_), channel_id=1, source_target_pairs={{0,16},{1,9},{2,18},{3,11},{4,20},{5,13},{6,22},{7,15},{8,24},{9,1... | collective-permute-start | bytes 786440 | tf_op jit(solution)/shard_map/ppermute | solution.py:30
  68.3 3.1 %collective-permute-start.29 = (bf16[512,256]{1,0:T(8,128)(2,1)S(1)}, bf16[512,256]{1,0:T(8,128)(2,1)S(1)}, u32[]{:S(2)}, u32[]{:S(2)}) collective-permute-start(bf16[512,256]{1,0:T(8,128)(2,1)S(1)} %joined.3.refs_1_), channel_id=1, source_target_pairs={{0,1},{1,0},{2,3},{3,2},{4,5},{5,4},{6,7},{7,6},{8,9},{9,8},{10,11... | collective-permute-start | bytes 786440 | tf_op jit(solution)/shard_map/ppermute | solution.py:34
  68.4 7.0 %collective-permute-start.26 = (bf16[512,256]{1,0:T(8,128)(2,1)S(1)}, bf16[512,256]{1,0:T(8,128)(2,1)S(1)}, u32[]{:S(2)}, u32[]{:S(2)}) collective-permute-start(bf16[512,256]{1,0:T(8,128)(2,1)S(1)} %joined.3.refs_1_), channel_id=1, source_target_pairs={{0,16},{1,9},{2,18},{3,11},{4,20},{5,13},{6,22},{7,15},{8,24},{9,1... | collective-permute-start | bytes 786440 | tf_op jit(solution)/shard_map/ppermute | solution.py:30
  70.2 1.2 %collective-permute-start.30 = (bf16[16,512]{1,0:T(8,128)(2,1)S(1)}, bf16[16,512]{1,0:T(8,128)(2,1)S(1)}, u32[]{:S(2)}, u32[]{:S(2)}) collective-permute-start(bf16[16,512]{1,0:T(8,128)(2,1)S(1)} %pad_maximum_fusion.6.refs_4_), channel_id=1, source_target_pairs={{0,1},{1,0},{2,3},{3,2},{4,5},{5,4},{6,7},{7,6},{8,9},{9,8},{10,11... | collective-permute-start | bytes 49160 | tf_op jit(solution)/shard_map/ppermute | solution.py:34
  70.3 6.4 %copy-start.3 = (f32[128,512]{1,0:T(8,128)}, f32[128,512]{1,0:T(8,128)S(1)}, u32[]{:S(2)}) copy-start(f32[128,512]{1,0:T(8,128)S(1)} %fusion.19.refs_7_) | copy-start | bytes 786436
  74.0 1.6 %collective-permute-start.32 = (bf16[512,256]{1,0:T(8,128)(2,1)S(1)}, bf16[512,256]{1,0:T(8,128)(2,1)S(1)}, u32[]{:S(2)}, u32[]{:S(2)}) collective-permute-start(bf16[512,256]{1,0:T(8,128)(2,1)S(1)} %get-tuple-element.41.refs_0_), channel_id=1, source_target_pairs={{0,1},{1,0},{2,3},{3,2},{4,5},{5,4},{6,7},{7,6},{8,9},{9,8},{10,11... | collective-permute-start | bytes 786440 | tf_op jit(solution)/shard_map/ppermute | solution.py:34
  75.4 1.5 %collective-permute-start.27 = (bf16[512,256]{1,0:T(8,128)(2,1)S(1)}, bf16[512,256]{1,0:T(8,128)(2,1)S(1)}, u32[]{:S(2)}, u32[]{:S(2)}) collective-permute-start(bf16[512,256]{1,0:T(8,128)(2,1)S(1)} %collective-permute-done.26.refs_0_), channel_id=1, source_target_pairs={{0,1},{1,0},{2,3},{3,2},{4,5},{5,4},{6,7},{7,6},{8,9},{9,8},{10,11... | collective-permute-start | bytes 786440 | tf_op jit(solution)/shard_map/ppermute | solution.py:34

commit v8 on v7

--- a/solution.py
+++ b/solution.py
@@ -509,7 +509,7 @@
         for i in range(parts):
             if step == 0:
                 sent[i] = rounded(sums[i])
-            came = z_step(sent[i], step)
+            came = z_step(sent[i], z_bits - 1 - step)
             if step == 0 and i == parts - 1:
                 sent[i] = added(sent[i], came, False, marks[:1])[0]
             else:

time: 78.7 us -> 78.9 us (level)
  starting transfers between devices: 31.4 us -> 33.4 us
  waiting for transfers between devices: 31.1 us -> 29.8 us
    ppermute x21, starting transfers between devices: 29.8 us -> 31.8 us  [exchange(): return lax.ppermute(x, AXES, pairs)]
    ppermute x12, waiting for transfers between devices: 3.51 us -> 2.55 us  [swap_cores(): return lax.ppermute(x, AXES, [(i, i ^ 1) for i in range(rows * cols)])]
where the time goes in v8:
time: 78.9 us; the launch traced here: 78.8 us
  starting transfers between devices  33.4 us (42%)
  waiting for transfers between devices  29.8 us (38%)
  Pallas kernels  10.4 us (13%)
  matrix products  2.56 us (3%)
  between operations  1.86 us (2%)
    ppermute x21, starting transfers between devices, exchange(): return lax.ppermute(x, AXES, pairs)  31.8 us
    ppermute x21, waiting for transfers between devices, exchange(): return lax.ppermute(x, AXES, pairs)  27.3 us
    pallas_call x3, Pallas kernels, write_weights(): pl.pallas_call(kernel, out_shape=(jax.ShapeDtypeStruct((F, 2 * F), FP), j...  3.52 us
    pallas_call x1, Pallas kernels, build(): pl.pallas_call(kernel, out_shape=(result, result), in_specs=[pl.BlockSpec...  2.74 us
    ppermute x12, waiting for transfers between devices, swap_cores(): return lax.ppermute(x, AXES, [(i, i ^ 1) for i in range(rows * cols)])  2.55 us
    dot_general x5, matrix products, dot(): return lax.dot_general(a, b, (dims, ((), ())), preferred_element_type=FP)  2.25 us
    pallas_call x3, Pallas kernels, weight_blocks(): pl.pallas_call(kernel, out_shape=tuple((jax.ShapeDtypeStruct((rows, size)...  2.01 us
    ppermute x12, starting transfers between devices, swap_cores(): return lax.ppermute(x, AXES, [(i, i ^ 1) for i in range(rows * cols)])  1.61 us
  transfers between devices with their start and end apart: 33, of which 17 were waited for; matrix products, arithmetic and copies ran while one was open for 4% of the time, Pallas kernels for 10%

profile of v8, /device:TPU:0, one launch (start us, length us, event | category | flops | bytes accessed | tf_op | source)
XLA Modules:
  0.0 78.8 jit_solution(956757875382791505)
XLA Ops:
  0.6 3.0 %collective-permute-start = (bf16[128,512]{1,0:T(8,128)(2,1)}, bf16[128,512]{1,0:T(8,128)(2,1)S(1)}, u32[]{:S(2)}, u32[]{:S(2)}) collective-permute-start(bf16[128,512]{1,0:T(8,128)(2,1)} %param.10), channel_id=1, source_target_pairs={{0,8},{1,17},{2,10},{3,19},{4,12},{5,21},{6,14},{7,23},{8,0},{9,25... | collective-permute-start | bytes 393224 | tf_op jit(solution)/shard_map/ppermute | solution.py:30
  3.7 1.5 %collective-permute-start.1 = (bf16[128,512]{1,0:T(8,128)(2,1)}, bf16[128,512]{1,0:T(8,128)(2,1)S(1)}, u32[]{:S(2)}, u32[]{:S(2)}) collective-permute-start(bf16[128,512]{1,0:T(8,128)(2,1)} %param.10), channel_id=1, source_target_pairs={{0,16},{1,9},{2,18},{3,11},{4,20},{5,13},{6,22},{7,15},{8,24},{9,1... | collective-permute-start | bytes 393224 | tf_op jit(solution)/shard_map/ppermute | solution.py:30
  5.9 2.7 %build_dense.1 = (bf16[512,1024]{1,0:T(8,128)(2,1)S(1)}, bf16[512,1024]{1,0:T(8,128)(2,1)S(1)}) custom-call(s32[1,1]{1,0:T(1,128)S(6)} %copy.34.count_ref, s32[1,128]{1,0:T(1,128)} %rows_ref.1, s32[1,128]{1,0:T(1,128)} %cols_ref.1, bf16[1,128,128,128]{3,2,1,0:T(8,128)(2,1)} %vals_ref.1), custom_call_target="tpu_custom_call" | custom-call | flops 2097152 | bytes 6291456 | tf_op jit(solution)/shard_map/build_dense/pallas_call | solution.py:105
  8.6 0.6 collective-permute-start.3
  9.2 0.1 collective-permute-start.5
  9.3 2.3 %collective-permute-done.1 = bf16[128,512]{1,0:T(8,128)(2,1)S(1)} collective-permute-done((bf16[128,512]{1,0:T(8,128)(2,1)}, bf16[128,512]{1,0:T(8,128)(2,1)S(1)}, u32[]{:S(2)}, u32[]{:S(2)}) %collective-permute-start.1) | collective-permute-done | bytes 131104 | tf_op jit(solution)/shard_map/ppermute | solution.py:30
  11.6 0.5 collective-permute-start.7
  12.3 0.4 fusion.7
  12.7 0.4 product.1.refs_4_
  13.2 0.1 stacked.1
  13.3 0.4 fusion.2
  13.8 2.4 %collective-permute-start.8 = (bf16[256,512]{1,0:T(8,128)(2,1)S(1)}, bf16[256,512]{1,0:T(8,128)(2,1)S(1)}, u32[]{:S(2)}, u32[]{:S(2)}) collective-permute-start(bf16[256,512]{1,0:T(8,128)(2,1)S(1)} %fusion.2), channel_id=1, source_target_pairs={{0,4},{1,3},{2,6},{3,1},{4,0},{5,7},{6,2},{7,5},{8,12},{9,11},{10,... | collective-permute-start | bytes 786440 | tf_op jit(solution)/shard_map/ppermute | solution.py:30
  16.2 0.4 convolution_add_fusion.2.refs_0_
  16.7 6.5 %collective-permute-done.8.refs_1_ = bf16[256,512]{1,0:T(8,128)(2,1)S(1)} collective-permute-done((bf16[256,512]{1,0:T(8,128)(2,1)S(1)}, bf16[256,512]{1,0:T(8,128)(2,1)S(1)}, u32[]{:S(2)}, u32[]{:S(2)}) %collective-permute-start.8) | collective-permute-done | bytes 262176 | tf_op jit(solution)/shard_map/ppermute | solution.py:30
  23.2 1.5 %collective-permute-start.9 = (bf16[128,512]{1,0:T(8,128)(2,1)S(1)}, bf16[128,512]{1,0:T(8,128)(2,1)S(1)}, u32[]{:S(2)}, u32[]{:S(2)}) collective-permute-start(bf16[128,512]{1,0:T(8,128)(2,1)S(1)} %get-tuple-element.30), channel_id=1, source_target_pairs={{0,2},{1,5},{2,0},{3,7},{4,6},{5,1},{6,4},{7,3},{8,10},{9,13},{10,... | collective-permute-start | bytes 393224 | tf_op jit(solution)/shard_map/ppermute | solution.py:30
  24.8 0.3 fusion.20.refs_2_.gains_ref
  25.1 4.1 %collective-permute-done.9.refs_1_ = bf16[128,512]{1,0:T(8,128)(2,1)S(1)} collective-permute-done((bf16[128,512]{1,0:T(8,128)(2,1)S(1)}, bf16[128,512]{1,0:T(8,128)(2,1)S(1)}, u32[]{:S(2)}, u32[]{:S(2)}) %collective-permute-start.9) | collective-permute-done | bytes 131104 | tf_op jit(solution)/shard_map/ppermute | solution.py:30
  29.2 0.8 node_values.1
  30.0 0.1 collective-permute-start.10
  30.1 0.8 node_gradients.1.refs_0_
  30.8 0.9 %collective-permute-done.10.met_ref = bf16[128,1536]{1,0:T(8,128)(2,1)S(1)} collective-permute-done((bf16[128,1536]{1,0:T(8,128)(2,1)S(1)}, bf16[128,1536]{1,0:T(8,128)(2,1)S(1)}, u32[]{:S(2)}, u32[]{:S(2)}) %collective-permute-start.10) | collective-permute-done | bytes 393248 | tf_op jit(solution)/shard_map/ppermute | solution.py:34
  31.8 0.5 weight_blocks.4
  32.3 0.6 collective-permute-start.11
  32.9 1.9 %collective-permute-start.21 = (bf16[512,256]{1,0:T(8,128)(2,1)S(1)}, bf16[512,256]{1,0:T(8,128)(2,1)S(1)}, u32[]{:S(2)}, u32[]{:S(2)}) collective-permute-start(bf16[512,256]{1,0:T(8,128)(2,1)S(1)} %get-tuple-element.40), channel_id=1, source_target_pairs={{0,16},{1,9},{2,18},{3,11},{4,20},{5,13},{6,22},{7,15},{8,24},{9,1... | collective-permute-start | bytes 786440 | tf_op jit(solution)/shard_map/ppermute | solution.py:30
  34.9 0.5 weight_blocks.5
  35.4 0.2 collective-permute-start.16
  35.6 1.0 %weight_blocks.3 = (f32[512,256]{1,0:T(8,128)S(1)}, f32[512,256]{1,0:T(8,128)S(1)}, bf16[128,512]{1,0:T(8,128)(2,1)}) custom-call(bf16[128,1536]{1,0:T(8,128)(2,1)S(1)} %get-tuple-element.31.mine_ref, bf16[128,1536]{1,0:T(8,128)(2,1)S(1)} %collective-permute-done.10.met_ref, f32[128,512]{1,0:T(8,128)S(1)} %get-tuple-element.33.refs_0_.agg_ref, ...), custom_call_target="tpu_custom_call" | custom-call | flops 134217728 | bytes 1572864 | tf_op jit(solution)/shard_map/weight_blocks/pallas_call | solution.py:295
  36.6 2.5 %collective-permute-done.11 = bf16[144,512]{1,0:T(8,128)(2,1)S(1)} collective-permute-done((bf16[144,512]{1,0:T(8,128)(2,1)S(1)}, bf16[144,512]{1,0:T(8,128)(2,1)S(1)}, u32[]{:S(2)}, u32[]{:S(2)}) %collective-permute-start.11) | collective-permute-done | bytes 147488 | tf_op jit(solution)/shard_map/ppermute | solution.py:30
  39.1 1.3 %collective-permute-start.12 = (bf16[272,512]{1,0:T(8,128)(2,1)S(1)}, bf16[272,512]{1,0:T(8,128)(2,1)S(1)}, u32[]{:S(2)}, u32[]{:S(2)}) collective-permute-start(bf16[272,512]{1,0:T(8,128)(2,1)S(1)} %pad_maximum_fusion.1), channel_id=1, source_target_pairs={{0,4},{1,3},{2,6},{3,1},{4,0},{5,7},{6,2},{7,5},{8,12},{9,11},{10,... | collective-permute-start | bytes 835592 | tf_op jit(solution)/shard_map/ppermute | solution.py:30
  40.4 0.1 convert_add_fusion
  40.5 1.5 %collective-permute-start.22 = (bf16[256,256]{1,0:T(8,128)(2,1)S(1)}, bf16[256,256]{1,0:T(8,128)(2,1)S(1)}, u32[]{:S(2)}, u32[]{:S(2)}) collective-permute-start(bf16[256,256]{1,0:T(8,128)(2,1)S(1)} %fusion.9), channel_id=1, source_target_pairs={{0,8},{1,17},{2,10},{3,19},{4,12},{5,21},{6,14},{7,23},{8,0},{9,25... | collective-permute-start | bytes 393224 | tf_op jit(solution)/shard_map/ppermute | solution.py:30
  42.0 0.2 collective-permute-done.16
  42.2 1.5 %collective-permute-start.17 = (bf16[256,256]{1,0:T(8,128)(2,1)S(1)}, bf16[256,256]{1,0:T(8,128)(2,1)S(1)}, u32[]{:S(2)}, u32[]{:S(2)}) collective-permute-start(bf16[256,256]{1,0:T(8,128)(2,1)S(1)} %fusion.12), channel_id=1, source_target_pairs={{0,8},{1,17},{2,10},{3,19},{4,12},{5,21},{6,14},{7,23},{8,0},{9,25... | collective-permute-start | bytes 393224 | tf_op jit(solution)/shard_map/ppermute | solution.py:30
  43.8 1.7 %collective-permute-done.22 = bf16[256,256]{1,0:T(8,128)(2,1)S(1)} collective-permute-done((bf16[256,256]{1,0:T(8,128)(2,1)S(1)}, bf16[256,256]{1,0:T(8,128)(2,1)S(1)}, u32[]{:S(2)}, u32[]{:S(2)}) %collective-permute-start.22) | collective-permute-done | bytes 131104 | tf_op jit(solution)/shard_map/ppermute | solution.py:30
  45.6 2.2 %collective-permute-start.23 = (bf16[256,256]{1,0:T(8,128)(2,1)S(1)}, bf16[256,256]{1,0:T(8,128)(2,1)S(1)}, u32[]{:S(2)}, u32[]{:S(2)}) collective-permute-start(bf16[256,256]{1,0:T(8,128)(2,1)S(1)} %fusion.11), channel_id=1, source_target_pairs={{0,4},{1,3},{2,6},{3,1},{4,0},{5,7},{6,2},{7,5},{8,12},{9,11},{10,... | collective-permute-start | bytes 393224 | tf_op jit(solution)/shard_map/ppermute | solution.py:30
  47.8 3.0 %collective-permute-start.18 = (bf16[256,256]{1,0:T(8,128)(2,1)S(1)}, bf16[256,256]{1,0:T(8,128)(2,1)S(1)}, u32[]{:S(2)}, u32[]{:S(2)}) collective-permute-start(bf16[256,256]{1,0:T(8,128)(2,1)S(1)} %fusion.14.refs_0_), channel_id=1, source_target_pairs={{0,4},{1,3},{2,6},{3,1},{4,0},{5,7},{6,2},{7,5},{8,12},{9,11},{10,... | collective-permute-start | bytes 393224 | tf_op jit(solution)/shard_map/ppermute | solution.py:30
  50.8 0.5 fusion
  51.3 0.1 collective-permute-start.13
  51.4 0.1 collective-permute-done.23
  51.6 2.7 %collective-permute-start.24 = (bf16[256,256]{1,0:T(8,128)(2,1)S(1)}, bf16[256,256]{1,0:T(8,128)(2,1)S(1)}, u32[]{:S(2)}, u32[]{:S(2)}) collective-permute-start(bf16[256,256]{1,0:T(8,128)(2,1)S(1)} %reduce-precision_convert_fusion.1), channel_id=1, source_target_pairs={{0,2},{1,5},{2,0},{3,7},{4,6},{5,1},{6,4},{7,3},{8,10},{9,13},{10,... | collective-permute-start | bytes 393224 | tf_op jit(solution)/shard_map/ppermute | solution.py:30
  54.2 0.5 convolution_add_fusion
  54.8 1.5 %collective-permute-start.14 = (bf16[272,512]{1,0:T(8,128)(2,1)S(1)}, bf16[272,512]{1,0:T(8,128)(2,1)S(1)}, u32[]{:S(2)}, u32[]{:S(2)}) collective-permute-start(bf16[272,512]{1,0:T(8,128)(2,1)S(1)} %pad_maximum_fusion.2.refs_2_), channel_id=1, source_target_pairs={{0,8},{1,17},{2,10},{3,19},{4,12},{5,21},{6,14},{7,23},{8,0},{9,25... | collective-permute-start | bytes 835592 | tf_op jit(solution)/shard_map/ppermute | solution.py:30
  56.3 2.3 %collective-permute-done.18.refs_1_ = bf16[256,256]{1,0:T(8,128)(2,1)S(1)} collective-permute-done((bf16[256,256]{1,0:T(8,128)(2,1)S(1)}, bf16[256,256]{1,0:T(8,128)(2,1)S(1)}, u32[]{:S(2)}, u32[]{:S(2)}) %collective-permute-start.18) | collective-permute-done | bytes 131104 | tf_op jit(solution)/shard_map/ppermute | solution.py:30
  58.7 0.1 collective-permute-start.19
  58.8 1.4 %collective-permute-done.24 = bf16[256,256]{1,0:T(8,128)(2,1)S(1)} collective-permute-done((bf16[256,256]{1,0:T(8,128)(2,1)S(1)}, bf16[256,256]{1,0:T(8,128)(2,1)S(1)}, u32[]{:S(2)}, u32[]{:S(2)}) %collective-permute-start.24) | collective-permute-done | bytes 131104 | tf_op jit(solution)/shard_map/ppermute | solution.py:30
  60.2 1.1 %collective-permute-start.25 = (bf16[256,256]{1,0:T(8,128)(2,1)S(1)}, bf16[256,256]{1,0:T(8,128)(2,1)S(1)}, u32[]{:S(2)}, u32[]{:S(2)}) collective-permute-start(bf16[256,256]{1,0:T(8,128)(2,1)S(1)} %reduce-precision_convert_fusion.refs_0_), channel_id=1, source_target_pairs={{0,8},{1,17},{2,10},{3,19},{4,12},{5,21},{6,14},{7,23},{8,0},{9,25... | collective-permute-start | bytes 393224 | tf_op jit(solution)/shard_map/ppermute | solution.py:30
  61.3 2.4 %collective-permute-done.19 = bf16[256,256]{1,0:T(8,128)(2,1)S(1)} collective-permute-done((bf16[256,256]{1,0:T(8,128)(2,1)S(1)}, bf16[256,256]{1,0:T(8,128)(2,1)S(1)}, u32[]{:S(2)}, u32[]{:S(2)}) %collective-permute-start.19) | collective-permute-done | bytes 131104 | tf_op jit(solution)/shard_map/ppermute | solution.py:30
  63.7 1.5 %collective-permute-start.20 = (bf16[256,256]{1,0:T(8,128)(2,1)S(1)}, bf16[256,256]{1,0:T(8,128)(2,1)S(1)}, u32[]{:S(2)}, u32[]{:S(2)}) collective-permute-start(bf16[256,256]{1,0:T(8,128)(2,1)S(1)} %reduce-precision_convert_fusion.2.refs_0_), channel_id=1, source_target_pairs={{0,8},{1,17},{2,10},{3,19},{4,12},{5,21},{6,14},{7,23},{8,0},{9,25... | collective-permute-start | bytes 393224 | tf_op jit(solution)/shard_map/ppermute | solution.py:30
  65.3 1.4 %collective-permute-start.15 = (bf16[144,512]{1,0:T(8,128)(2,1)S(1)}, bf16[144,512]{1,0:T(8,128)(2,1)S(1)}, u32[]{:S(2)}, u32[]{:S(2)}) collective-permute-start(bf16[144,512]{1,0:T(8,128)(2,1)S(1)} %pad_maximum_fusion.5.refs_2_), channel_id=1, source_target_pairs={{0,16},{1,9},{2,18},{3,11},{4,20},{5,13},{6,22},{7,15},{8,24},{9,1... | collective-permute-start | bytes 442376 | tf_op jit(solution)/shard_map/ppermute | solution.py:30
  66.7 0.1 collective-permute-start.28
  66.8 0.8 collective-permute-start.31
  67.6 1.5 %collective-permute-done.20.refs_1_ = bf16[256,256]{1,0:T(8,128)(2,1)S(1)} collective-permute-done((bf16[256,256]{1,0:T(8,128)(2,1)S(1)}, bf16[256,256]{1,0:T(8,128)(2,1)S(1)}, u32[]{:S(2)}, u32[]{:S(2)}) %collective-permute-start.20) | collective-permute-done | bytes 131104 | tf_op jit(solution)/shard_map/ppermute | solution.py:30
  69.1 0.1 collective-permute-start.29
  69.2 2.1 %collective-permute-start.26 = (bf16[512,256]{1,0:T(8,128)(2,1)S(1)}, bf16[512,256]{1,0:T(8,128)(2,1)S(1)}, u32[]{:S(2)}, u32[]{:S(2)}) collective-permute-start(bf16[512,256]{1,0:T(8,128)(2,1)S(1)} %joined.3.refs_1_), channel_id=1, source_target_pairs={{0,16},{1,9},{2,18},{3,11},{4,20},{5,13},{6,22},{7,15},{8,24},{9,1... | collective-permute-start | bytes 786440 | tf_op jit(solution)/shard_map/ppermute | solution.py:30
  71.3 0.1 collective-permute-start.30
  71.4 1.1 %collective-permute-done.30.refs_5_ = bf16[16,512]{1,0:T(8,128)(2,1)S(1)} collective-permute-done((bf16[16,512]{1,0:T(8,128)(2,1)S(1)}, bf16[16,512]{1,0:T(8,128)(2,1)S(1)}, u32[]{:S(2)}, u32[]{:S(2)}) %collective-permute-start.30) | collective-permute-done | bytes 16416 | tf_op jit(solution)/shard_map/ppermute | solution.py:34
  72.6 0.8 %collective-permute-done.31.refs_6_ = bf16[512,256]{1,0:T(8,128)(2,1)S(1)} collective-permute-done((bf16[512,256]{1,0:T(8,128)(2,1)S(1)}, bf16[512,256]{1,0:T(8,128)(2,1)S(1)}, u32[]{:S(2)}, u32[]{:S(2)}) %collective-permute-start.31) | collective-permute-done | bytes 262176 | tf_op jit(solution)/shard_map/ppermute | solution.py:30
  73.4 1.4 %write_weights.3 = (f32[512,1024]{1,0:T(8,128)}, f32[1024,512]{1,0:T(8,128)}, f32[8,512]{1,0:T(8,128)}, bf16[512,256]{1,0:T(8,128)(2,1)S(1)}) custom-call(bf16[512,256]{1,0:T(8,128)(2,1)S(1)} %joined.2.refs_2_.refs_0_, bf16[512,256]{1,0:T(8,128)(2,1)S(1)} %joined.3.refs_1_, ...), custom_call_target="tpu_custom_call", output_to_operand_aliasing={{3}: (6, {})} | custom-call | tf_op jit(solution)/shard_map/write_weights/pallas_call | solution.py:187
  74.8 0.1 collective-permute-start.32
  74.9 1.3 %collective-permute-done.26.refs_0_ = bf16[512,256]{1,0:T(8,128)(2,1)S(1)} collective-permute-done((bf16[512,256]{1,0:T(8,128)(2,1)S(1)}, bf16[512,256]{1,0:T(8,128)(2,1)S(1)}, u32[]{:S(2)}, u32[]{:S(2)}) %collective-permute-start.26) | collective-permute-done | bytes 262176 | tf_op jit(solution)/shard_map/ppermute | solution.py:30
  76.2 0.2 collective-permute-done.32.refs_1_
  76.4 1.0 %write_weights.4 = (f32[512,1024]{1,0:T(8,128)}, f32[1024,512]{1,0:T(8,128)}) custom-call(bf16[512,256]{1,0:T(8,128)(2,1)S(1)} %get-tuple-element.41.refs_0_, bf16[512,256]{1,0:T(8,128)(2,1)S(1)} %collective-permute-done.32.refs_1_, f32[512,1024]{1,0:T(8,128)} %get-tuple-element.42.refs_2_, ...), custom_call_target="tpu_custom_call", output_to_operand_aliasing={{0}: (2, {}), {1}: (3, {})} | custom-call | tf_op jit(solution)/shard_map/write_weights/pallas_call | solution.py:187
  77.5 0.2 collective-permute-done.27.refs_1_
  77.7 1.0 %write_weights.5 = (f32[512,1024]{1,0:T(8,128)}, f32[1024,512]{1,0:T(8,128)}) custom-call(bf16[512,256]{1,0:T(8,128)(2,1)S(1)} %collective-permute-done.26.refs_0_, bf16[512,256]{1,0:T(8,128)(2,1)S(1)} %collective-permute-done.27.refs_1_, f32[512,1024]{1,0:T(8,128)} %get-tuple-element.44.refs_2_, ...), custom_call_target="tpu_custom_call", output_to_operand_aliasing={{0}: (2, {}), {1}: (3, {})} | custom-call | tf_op jit(solution)/shard_map/write_weights/pallas_call | solution.py:187
  (81 shorter events, 0.9 us)
Async XLA Ops:
  0.6 24.1 %copy-start = (f32[8,512]{1,0:T(8,128)S(1)}, f32[8,512]{1,0:T(8,128)}, u32[]{:S(2)}) copy-start(f32[8,512]{1,0:T(8,128)} %param.16) | copy-start | bytes 49156
  0.6 8.6 %collective-permute-start = (bf16[128,512]{1,0:T(8,128)(2,1)}, bf16[128,512]{1,0:T(8,128)(2,1)S(1)}, u32[]{:S(2)}, u32[]{:S(2)}) collective-permute-start(bf16[128,512]{1,0:T(8,128)(2,1)} %param.10), channel_id=1, source_target_pairs={{0,8},{1,17},{2,10},{3,19},{4,12},{5,21},{6,14},{7,23},{8,0},{9,25... | collective-permute-start | bytes 393224 | tf_op jit(solution)/shard_map/ppermute | solution.py:30
  3.7 8.0 %collective-permute-start.1 = (bf16[128,512]{1,0:T(8,128)(2,1)}, bf16[128,512]{1,0:T(8,128)(2,1)S(1)}, u32[]{:S(2)}, u32[]{:S(2)}) collective-permute-start(bf16[128,512]{1,0:T(8,128)(2,1)} %param.10), channel_id=1, source_target_pairs={{0,16},{1,9},{2,18},{3,11},{4,20},{5,13},{6,22},{7,15},{8,24},{9,1... | collective-permute-start | bytes 393224 | tf_op jit(solution)/shard_map/ppermute | solution.py:30
  5.2 6.5 %collective-permute-start.2 = (bf16[128,512]{1,0:T(8,128)(2,1)}, bf16[128,512]{1,0:T(8,128)(2,1)S(1)}, u32[]{:S(2)}, u32[]{:S(2)}) collective-permute-start(bf16[128,512]{1,0:T(8,128)(2,1)} %param.10), channel_id=1, source_target_pairs={{0,24},{1,25},{2,26},{3,27},{4,28},{5,29},{6,30},{7,31},{8,16},{9,... | collective-permute-start | bytes 393224 | tf_op jit(solution)/shard_map/ppermute | solution.py:30
  5.2 8.0 %collective-permute-start.4 = (bf16[128,512]{1,0:T(8,128)(2,1)}, bf16[128,512]{1,0:T(8,128)(2,1)S(1)}, u32[]{:S(2)}, u32[]{:S(2)}) collective-permute-start(bf16[128,512]{1,0:T(8,128)(2,1)} %param.10), channel_id=1, source_target_pairs={{0,1},{1,0},{2,3},{3,2},{4,5},{5,4},{6,7},{7,6},{8,9},{9,8},{10,11... | collective-permute-start | bytes 393224 | tf_op jit(solution)/shard_map/ppermute | solution.py:34
  5.8 3.3 %copy-start.5 = (bf16[128,512]{1,0:T(8,128)(2,1)S(1)}, bf16[128,512]{1,0:T(8,128)(2,1)}, u32[]{:S(2)}) copy-start(bf16[128,512]{1,0:T(8,128)(2,1)} %param.10) | copy-start | bytes 393220
  8.6 4.7 %collective-permute-start.3 = (bf16[512,1024]{1,0:T(8,128)(2,1)S(1)}, bf16[512,1024]{1,0:T(8,128)(2,1)S(1)}, u32[]{:S(2)}, u32[]{:S(2)}) collective-permute-start(bf16[512,1024]{1,0:T(8,128)(2,1)S(1)} %get-tuple-element.28), channel_id=1, source_target_pairs={{0,1},{1,0},{2,3},{3,2},{4,5},{5,4},{6,7},{7,6},{8,9},{9,8},{10,11... | collective-permute-start | bytes 3145736 | tf_op jit(solution)/shard_map/ppermute | solution.py:34
  9.2 4.0 %collective-permute-start.5 = (bf16[128,512]{1,0:T(8,128)(2,1)S(1)}, bf16[128,512]{1,0:T(8,128)(2,1)S(1)}, u32[]{:S(2)}, u32[]{:S(2)}) collective-permute-start(bf16[128,512]{1,0:T(8,128)(2,1)S(1)} %collective-permute-done), channel_id=1, source_target_pairs={{0,1},{1,0},{2,3},{3,2},{4,5},{5,4},{6,7},{7,6},{8,9},{9,8},{10,11... | collective-permute-start | bytes 393224 | tf_op jit(solution)/shard_map/ppermute | solution.py:34
  11.6 1.6 %collective-permute-start.6 = (bf16[128,512]{1,0:T(8,128)(2,1)S(1)}, bf16[128,512]{1,0:T(8,128)(2,1)S(1)}, u32[]{:S(2)}, u32[]{:S(2)}) collective-permute-start(bf16[128,512]{1,0:T(8,128)(2,1)S(1)} %collective-permute-done.1), channel_id=1, source_target_pairs={{0,1},{1,0},{2,3},{3,2},{4,5},{5,4},{6,7},{7,6},{8,9},{9,8},{10,11... | collective-permute-start | bytes 393224 | tf_op jit(solution)/shard_map/ppermute | solution.py:34
  11.6 1.6 %collective-permute-start.7 = (bf16[128,512]{1,0:T(8,128)(2,1)S(1)}, bf16[128,512]{1,0:T(8,128)(2,1)S(1)}, u32[]{:S(2)}, u32[]{:S(2)}) collective-permute-start(bf16[128,512]{1,0:T(8,128)(2,1)S(1)} %collective-permute-done.2), channel_id=1, source_target_pairs={{0,1},{1,0},{2,3},{3,2},{4,5},{5,4},{6,7},{7,6},{8,9},{9,8},{10,11... | collective-permute-start | bytes 393224 | tf_op jit(solution)/shard_map/ppermute | solution.py:34
  13.7 11.0 %copy-start.6 = (s32[128]{0:T(128)S(1)}, s32[128]{0:T(128)}, u32[]{:S(2)}) copy-start(s32[128]{0:T(128)} %param.15) | copy-start | bytes 1540
  13.8 15.5 %copy-start.1 = (bf16[512,1024]{1,0:T(8,128)(2,1)S(1)}, bf16[512,1024]{1,0:T(8,128)(2,1)}, u32[]{:S(2)}) copy-start(bf16[512,1024]{1,0:T(8,128)(2,1)} %w_ref.1) | copy-start | bytes 3145732
  13.8 15.5 %copy-start.2 = (bf16[1024,512]{1,0:T(8,128)(2,1)S(1)}, bf16[1024,512]{1,0:T(8,128)(2,1)}, u32[]{:S(2)}) copy-start(bf16[1024,512]{1,0:T(8,128)(2,1)} %refs_2_.1) | copy-start | bytes 3145732
  13.8 15.4 %copy-start.4 = (bf16[128,512]{1,0:T(8,128)(2,1)S(1)}, bf16[128,512]{1,0:T(8,128)(2,1)}, u32[]{:S(2)}) copy-start(bf16[128,512]{1,0:T(8,128)(2,1)} %cot_ref.1) | copy-start | bytes 393220
  13.8 9.4 %collective-permute-start.8 = (bf16[256,512]{1,0:T(8,128)(2,1)S(1)}, bf16[256,512]{1,0:T(8,128)(2,1)S(1)}, u32[]{:S(2)}, u32[]{:S(2)}) collective-permute-start(bf16[256,512]{1,0:T(8,128)(2,1)S(1)} %fusion.2), channel_id=1, source_target_pairs={{0,4},{1,3},{2,6},{3,1},{4,0},{5,7},{6,2},{7,5},{8,12},{9,11},{10,... | collective-permute-start | bytes 786440 | tf_op jit(solution)/shard_map/ppermute | solution.py:30
  23.2 6.0 %collective-permute-start.9 = (bf16[128,512]{1,0:T(8,128)(2,1)S(1)}, bf16[128,512]{1,0:T(8,128)(2,1)S(1)}, u32[]{:S(2)}, u32[]{:S(2)}) collective-permute-start(bf16[128,512]{1,0:T(8,128)(2,1)S(1)} %get-tuple-element.30), channel_id=1, source_target_pairs={{0,2},{1,5},{2,0},{3,7},{4,6},{5,1},{6,4},{7,3},{8,10},{9,13},{10,... | collective-permute-start | bytes 393224 | tf_op jit(solution)/shard_map/ppermute | solution.py:30
  30.0 1.8 %collective-permute-start.10 = (bf16[128,1536]{1,0:T(8,128)(2,1)S(1)}, bf16[128,1536]{1,0:T(8,128)(2,1)S(1)}, u32[]{:S(2)}, u32[]{:S(2)}) collective-permute-start(bf16[128,1536]{1,0:T(8,128)(2,1)S(1)} %get-tuple-element.32), channel_id=1, source_target_pairs={{0,1},{1,0},{2,3},{3,2},{4,5},{5,4},{6,7},{7,6},{8,9},{9,8},{10,11... | collective-permute-start | bytes 1179656 | tf_op jit(solution)/shard_map/ppermute | solution.py:34
  32.3 6.7 %collective-permute-start.11 = (bf16[144,512]{1,0:T(8,128)(2,1)S(1)}, bf16[144,512]{1,0:T(8,128)(2,1)S(1)}, u32[]{:S(2)}, u32[]{:S(2)}) collective-permute-start(bf16[144,512]{1,0:T(8,128)(2,1)S(1)} %get-tuple-element.37), channel_id=1, source_target_pairs={{0,2},{1,5},{2,0},{3,7},{4,6},{5,1},{6,4},{7,3},{8,10},{9,13},{10,... | collective-permute-start | bytes 442376 | tf_op jit(solution)/shard_map/ppermute | solution.py:30
  32.9 7.5 %collective-permute-start.21 = (bf16[512,256]{1,0:T(8,128)(2,1)S(1)}, bf16[512,256]{1,0:T(8,128)(2,1)S(1)}, u32[]{:S(2)}, u32[]{:S(2)}) collective-permute-start(bf16[512,256]{1,0:T(8,128)(2,1)S(1)} %get-tuple-element.40), channel_id=1, source_target_pairs={{0,16},{1,9},{2,18},{3,11},{4,20},{5,13},{6,22},{7,15},{8,24},{9,1... | collective-permute-start | bytes 786440 | tf_op jit(solution)/shard_map/ppermute | solution.py:30
  35.4 6.8 %collective-permute-start.16 = (bf16[512,256]{1,0:T(8,128)(2,1)S(1)}, bf16[512,256]{1,0:T(8,128)(2,1)S(1)}, u32[]{:S(2)}, u32[]{:S(2)}) collective-permute-start(bf16[512,256]{1,0:T(8,128)(2,1)S(1)} %weight_blocks.5), channel_id=1, source_target_pairs={{0,16},{1,9},{2,18},{3,11},{4,20},{5,13},{6,22},{7,15},{8,24},{9,1... | collective-permute-start | bytes 786440 | tf_op jit(solution)/shard_map/ppermute | solution.py:30
  39.1 11.6 %collective-permute-start.12 = (bf16[272,512]{1,0:T(8,128)(2,1)S(1)}, bf16[272,512]{1,0:T(8,128)(2,1)S(1)}, u32[]{:S(2)}, u32[]{:S(2)}) collective-permute-start(bf16[272,512]{1,0:T(8,128)(2,1)S(1)} %pad_maximum_fusion.1), channel_id=1, source_target_pairs={{0,4},{1,3},{2,6},{3,1},{4,0},{5,7},{6,2},{7,5},{8,12},{9,11},{10,... | collective-permute-start | bytes 835592 | tf_op jit(solution)/shard_map/ppermute | solution.py:30
  40.5 5.0 %collective-permute-start.22 = (bf16[256,256]{1,0:T(8,128)(2,1)S(1)}, bf16[256,256]{1,0:T(8,128)(2,1)S(1)}, u32[]{:S(2)}, u32[]{:S(2)}) collective-permute-start(bf16[256,256]{1,0:T(8,128)(2,1)S(1)} %fusion.9), channel_id=1, source_target_pairs={{0,8},{1,17},{2,10},{3,19},{4,12},{5,21},{6,14},{7,23},{8,0},{9,25... | collective-permute-start | bytes 393224 | tf_op jit(solution)/shard_map/ppermute | solution.py:30
  42.2 5.5 %collective-permute-start.17 = (bf16[256,256]{1,0:T(8,128)(2,1)S(1)}, bf16[256,256]{1,0:T(8,128)(2,1)S(1)}, u32[]{:S(2)}, u32[]{:S(2)}) collective-permute-start(bf16[256,256]{1,0:T(8,128)(2,1)S(1)} %fusion.12), channel_id=1, source_target_pairs={{0,8},{1,17},{2,10},{3,19},{4,12},{5,21},{6,14},{7,23},{8,0},{9,25... | collective-permute-start | bytes 393224 | tf_op jit(solution)/shard_map/ppermute | solution.py:30
  45.6 6.0 %collective-permute-start.23 = (bf16[256,256]{1,0:T(8,128)(2,1)S(1)}, bf16[256,256]{1,0:T(8,128)(2,1)S(1)}, u32[]{:S(2)}, u32[]{:S(2)}) collective-permute-start(bf16[256,256]{1,0:T(8,128)(2,1)S(1)} %fusion.11), channel_id=1, source_target_pairs={{0,4},{1,3},{2,6},{3,1},{4,0},{5,7},{6,2},{7,5},{8,12},{9,11},{10,... | collective-permute-start | bytes 393224 | tf_op jit(solution)/shard_map/ppermute | solution.py:30
  47.8 10.9 %collective-permute-start.18 = (bf16[256,256]{1,0:T(8,128)(2,1)S(1)}, bf16[256,256]{1,0:T(8,128)(2,1)S(1)}, u32[]{:S(2)}, u32[]{:S(2)}) collective-permute-start(bf16[256,256]{1,0:T(8,128)(2,1)S(1)} %fusion.14.refs_0_), channel_id=1, source_target_pairs={{0,4},{1,3},{2,6},{3,1},{4,0},{5,7},{6,2},{7,5},{8,12},{9,11},{10,... | collective-permute-start | bytes 393224 | tf_op jit(solution)/shard_map/ppermute | solution.py:30
  51.3 3.0 %collective-permute-start.13 = (bf16[512,512]{1,0:T(8,128)(2,1)S(1)}, bf16[512,512]{1,0:T(8,128)(2,1)S(1)}, u32[]{:S(2)}, u32[]{:S(2)}) collective-permute-start(bf16[512,512]{1,0:T(8,128)(2,1)S(1)} %fusion), channel_id=1, source_target_pairs={{0,1},{1,0},{2,3},{3,2},{4,5},{5,4},{6,7},{7,6},{8,9},{9,8},{10,11... | collective-permute-start | bytes 1572872 | tf_op jit(solution)/shard_map/ppermute | solution.py:34
  51.6 8.6 %collective-permute-start.24 = (bf16[256,256]{1,0:T(8,128)(2,1)S(1)}, bf16[256,256]{1,0:T(8,128)(2,1)S(1)}, u32[]{:S(2)}, u32[]{:S(2)}) collective-permute-start(bf16[256,256]{1,0:T(8,128)(2,1)S(1)} %reduce-precision_convert_fusion.1), channel_id=1, source_target_pairs={{0,2},{1,5},{2,0},{3,7},{4,6},{5,1},{6,4},{7,3},{8,10},{9,13},{10,... | collective-permute-start | bytes 393224 | tf_op jit(solution)/shard_map/ppermute | solution.py:30
  54.8 10.5 %collective-permute-start.14 = (bf16[272,512]{1,0:T(8,128)(2,1)S(1)}, bf16[272,512]{1,0:T(8,128)(2,1)S(1)}, u32[]{:S(2)}, u32[]{:S(2)}) collective-permute-start(bf16[272,512]{1,0:T(8,128)(2,1)S(1)} %pad_maximum_fusion.2.refs_2_), channel_id=1, source_target_pairs={{0,8},{1,17},{2,10},{3,19},{4,12},{5,21},{6,14},{7,23},{8,0},{9,25... | collective-permute-start | bytes 835592 | tf_op jit(solution)/shard_map/ppermute | solution.py:30
  58.7 5.0 %collective-permute-start.19 = (bf16[256,256]{1,0:T(8,128)(2,1)S(1)}, bf16[256,256]{1,0:T(8,128)(2,1)S(1)}, u32[]{:S(2)}, u32[]{:S(2)}) collective-permute-start(bf16[256,256]{1,0:T(8,128)(2,1)S(1)} %added.3), channel_id=1, source_target_pairs={{0,2},{1,5},{2,0},{3,7},{4,6},{5,1},{6,4},{7,3},{8,10},{9,13},{10,... | collective-permute-start | bytes 393224 | tf_op jit(solution)/shard_map/ppermute | solution.py:30
  60.2 6.5 %collective-permute-start.25 = (bf16[256,256]{1,0:T(8,128)(2,1)S(1)}, bf16[256,256]{1,0:T(8,128)(2,1)S(1)}, u32[]{:S(2)}, u32[]{:S(2)}) collective-permute-start(bf16[256,256]{1,0:T(8,128)(2,1)S(1)} %reduce-precision_convert_fusion.refs_0_), channel_id=1, source_target_pairs={{0,8},{1,17},{2,10},{3,19},{4,12},{5,21},{6,14},{7,23},{8,0},{9,25... | collective-permute-start | bytes 393224 | tf_op jit(solution)/shard_map/ppermute | solution.py:30
  63.7 5.3 %collective-permute-start.20 = (bf16[256,256]{1,0:T(8,128)(2,1)S(1)}, bf16[256,256]{1,0:T(8,128)(2,1)S(1)}, u32[]{:S(2)}, u32[]{:S(2)}) collective-permute-start(bf16[256,256]{1,0:T(8,128)(2,1)S(1)} %reduce-precision_convert_fusion.2.refs_0_), channel_id=1, source_target_pairs={{0,8},{1,17},{2,10},{3,19},{4,12},{5,21},{6,14},{7,23},{8,0},{9,25... | collective-permute-start | bytes 393224 | tf_op jit(solution)/shard_map/ppermute | solution.py:30
  65.3 5.9 %collective-permute-start.15 = (bf16[144,512]{1,0:T(8,128)(2,1)S(1)}, bf16[144,512]{1,0:T(8,128)(2,1)S(1)}, u32[]{:S(2)}, u32[]{:S(2)}) collective-permute-start(bf16[144,512]{1,0:T(8,128)(2,1)S(1)} %pad_maximum_fusion.5.refs_2_), channel_id=1, source_target_pairs={{0,16},{1,9},{2,18},{3,11},{4,20},{5,13},{6,22},{7,15},{8,24},{9,1... | collective-permute-start | bytes 442376 | tf_op jit(solution)/shard_map/ppermute | solution.py:30
  66.7 5.8 %collective-permute-start.28 = (bf16[512,256]{1,0:T(8,128)(2,1)S(1)}, bf16[512,256]{1,0:T(8,128)(2,1)S(1)}, u32[]{:S(2)}, u32[]{:S(2)}) collective-permute-start(bf16[512,256]{1,0:T(8,128)(2,1)S(1)} %joined.2.refs_2_.refs_0_), channel_id=1, source_target_pairs={{0,1},{1,0},{2,3},{3,2},{4,5},{5,4},{6,7},{7,6},{8,9},{9,8},{10,11... | collective-permute-start | bytes 786440 | tf_op jit(solution)/shard_map/ppermute | solution.py:34
  66.8 6.5 %collective-permute-start.31 = (bf16[512,256]{1,0:T(8,128)(2,1)S(1)}, bf16[512,256]{1,0:T(8,128)(2,1)S(1)}, u32[]{:S(2)}, u32[]{:S(2)}) collective-permute-start(bf16[512,256]{1,0:T(8,128)(2,1)S(1)} %joined.2.refs_2_.refs_0_), channel_id=1, source_target_pairs={{0,16},{1,9},{2,18},{3,11},{4,20},{5,13},{6,22},{7,15},{8,24},{9,1... | collective-permute-start | bytes 786440 | tf_op jit(solution)/shard_map/ppermute | solution.py:30
  69.1 3.5 %collective-permute-start.29 = (bf16[512,256]{1,0:T(8,128)(2,1)S(1)}, bf16[512,256]{1,0:T(8,128)(2,1)S(1)}, u32[]{:S(2)}, u32[]{:S(2)}) collective-permute-start(bf16[512,256]{1,0:T(8,128)(2,1)S(1)} %joined.3.refs_1_), channel_id=1, source_target_pairs={{0,1},{1,0},{2,3},{3,2},{4,5},{5,4},{6,7},{7,6},{8,9},{9,8},{10,11... | collective-permute-start | bytes 786440 | tf_op jit(solution)/shard_map/ppermute | solution.py:34
  69.2 7.0 %collective-permute-start.26 = (bf16[512,256]{1,0:T(8,128)(2,1)S(1)}, bf16[512,256]{1,0:T(8,128)(2,1)S(1)}, u32[]{:S(2)}, u32[]{:S(2)}) collective-permute-start(bf16[512,256]{1,0:T(8,128)(2,1)S(1)} %joined.3.refs_1_), channel_id=1, source_target_pairs={{0,16},{1,9},{2,18},{3,11},{4,20},{5,13},{6,22},{7,15},{8,24},{9,1... | collective-permute-start | bytes 786440 | tf_op jit(solution)/shard_map/ppermute | solution.py:30
  71.3 1.2 %collective-permute-start.30 = (bf16[16,512]{1,0:T(8,128)(2,1)S(1)}, bf16[16,512]{1,0:T(8,128)(2,1)S(1)}, u32[]{:S(2)}, u32[]{:S(2)}) collective-permute-start(bf16[16,512]{1,0:T(8,128)(2,1)S(1)} %pad_maximum_fusion.6.refs_4_), channel_id=1, source_target_pairs={{0,1},{1,0},{2,3},{3,2},{4,5},{5,4},{6,7},{7,6},{8,9},{9,8},{10,11... | collective-permute-start | bytes 49160 | tf_op jit(solution)/shard_map/ppermute | solution.py:34
  71.4 6.0 %copy-start.3 = (f32[128,512]{1,0:T(8,128)}, f32[128,512]{1,0:T(8,128)S(1)}, u32[]{:S(2)}) copy-start(f32[128,512]{1,0:T(8,128)S(1)} %fusion.19.refs_7_) | copy-start | bytes 786436
  74.8 1.6 %collective-permute-start.32 = (bf16[512,256]{1,0:T(8,128)(2,1)S(1)}, bf16[512,256]{1,0:T(8,128)(2,1)S(1)}, u32[]{:S(2)}, u32[]{:S(2)}) collective-permute-start(bf16[512,256]{1,0:T(8,128)(2,1)S(1)} %get-tuple-element.41.refs_0_), channel_id=1, source_target_pairs={{0,1},{1,0},{2,3},{3,2},{4,5},{5,4},{6,7},{7,6},{8,9},{9,8},{10,11... | collective-permute-start | bytes 786440 | tf_op jit(solution)/shard_map/ppermute | solution.py:34
  76.2 1.5 %collective-permute-start.27 = (bf16[512,256]{1,0:T(8,128)(2,1)S(1)}, bf16[512,256]{1,0:T(8,128)(2,1)S(1)}, u32[]{:S(2)}, u32[]{:S(2)}) collective-permute-start(bf16[512,256]{1,0:T(8,128)(2,1)S(1)} %collective-permute-done.26.refs_0_), channel_id=1, source_target_pairs={{0,1},{1,0},{2,3},{3,2},{4,5},{5,4},{6,7},{7,6},{8,9},{9,8},{10,11... | collective-permute-start | bytes 786440 | tf_op jit(solution)/shard_map/ppermute | solution.py:34
